TPU v7x, 32 devices: a whole 2x2x4 slice. The times are simulated.
32 devices in a mesh: seq: 4 (over y, core), head: 8 (over z, x).
Axes of the slice: x: 2, y: 2, z: 4, core: 2. Of those that a mesh axis runs over, the one named last changes fastest.
Arguments:
- tokens: bfloat16 [4096, 2048], P(('seq', 'head')), may hold values from -6 to 6
- w_qkvg: bfloat16 [2048, 12288], P('seq', 'head'), may hold values from -0.125 to 0.125
- w_rates: bfloat16 [2048, 32], P('seq', 'head'), may hold values from -0.125 to 0.125
- conv_weight: float32 [4, 8192], P(None, 'head'), may hold values from -3 to 3
- head_bias: float32 [2, 16], P(None, 'head'), may hold values from -12 to -1.5, as said below
- norm_gain: float32 [2048], replicated, may hold values from 0.25 to 1.75
- head_gain: float32 [256], replicated, may hold values from 0.25 to 1.75
- mlp_gain: float32 [2048], replicated, may hold values from 0.25 to 1.75
- w_out: bfloat16 [4096, 2048], P('head', 'seq'), may hold values from -0.09375 to 0.09375
- w_ff_gate: bfloat16 [5632, 2048], P('head', 'seq'), may hold values from -0.125 to 0.125
- w_ff_up: bfloat16 [5632, 2048], P('head', 'seq'), may hold values from -0.125 to 0.125
- w_ff_down: bfloat16 [5632, 2048], P('head', 'seq'), may hold values from -0.078125 to 0.078125
- cotangent: bfloat16 [4096, 2048], P(('seq', 'head')), may hold values from -6 to 6
Outputs:
- output: bfloat16 [4096, 2048], P(('seq', 'head'))
- tokens_grad: float32 [4096, 2048], P(('seq', 'head'))
- w_qkvg_grad: float32 [2048, 12288], P('seq', 'head')
- w_rates_grad: float32 [2048, 32], P('seq', 'head')
- conv_weight_grad: float32 [4, 8192], P(None, 'head')
- head_bias_grad: float32 [2, 16], P(None, 'head')
- norm_gain_grad: float32 [2048], replicated
- head_gain_grad: float32 [256], replicated
- mlp_gain_grad: float32 [2048], replicated
- w_out_grad: float32 [4096, 2048], P('head', 'seq')
- w_ff_gate_grad: float32 [5632, 2048], P('head', 'seq')
- w_ff_up_grad: float32 [5632, 2048], P('head', 'seq')
- w_ff_down_grad: float32 [5632, 2048], P('head', 'seq')
Inputs may be any that keep to these rules, and one draw needn't show every extreme that they name: `head_bias`: row 0 shifts each head's decay logit, row 1 its update-strength logit.
All inputs are finite; a program needn't handle non-finite values.
Results may differ from a plain program's by a relative error of at most 0.025.
Values may be sent and summed in bfloat16 or wider, within the bound.
No kernel may reach another device: no remote copies, remote signals or barrier semaphores. Data moves between devices by JAX's collectives and lax.ppermute only.
A program may use at most 320 MiB of HBM per device.

v0:
```python
import jax
import jax.numpy as jnp
from jax import lax
from jax.sharding import PartitionSpec as P

DK = 128
DV = 256
CONV = 4
BLOCK = 64


epsilon = 1e-06
highest = lax.Precision.HIGHEST


def shifted(value, axis, steps):
    count = lax.axis_size(axis)
    leading, last = (max(0, -steps), min(count, count - steps))
    return lax.ppermute(value, axis, [(source, source + steps) for source in range(leading, last)])


def entering(shard, axis, combine, identity):
    peers, position = (lax.axis_size(axis), lax.axis_index(axis))
    everything = jax.tree.map(lambda part: lax.all_gather(part, axis), shard)
    start = jax.tree.map(
        lambda part, zero: jnp.broadcast_to(jnp.asarray(zero, part.dtype), part.shape),
        shard,
        identity,
    )

    def turn(k, before):
        reached = k < position
        new = combine(before, jax.tree.map(lambda part: part[k], everything))
        return jax.tree.map(lambda a, b: jnp.where(reached, a, b), new, before)

    return lax.fori_loop(0, peers, turn, start)


def prefix(shard, axis, join, neutral):
    count = lax.axis_size(axis)
    place = lax.axis_index(axis)
    ahead = count - 1 - place
    gathered = jax.tree.map(
        lambda a, kind: lax.all_gather(a.astype(kind), axis), shard, (jnp.bfloat16, jnp.bfloat16)
    )
    state = jax.tree.map(lambda a, e: jnp.zeros_like(a) + jnp.asarray(e, a.dtype), shard, neutral)

    def one(turn, state):
        source = count - 1 - turn
        return join(
            state,
            jax.tree.map(
                lambda a, own: lax.dynamic_index_in_dim(a, source, 0, False).astype(own.dtype),
                gathered,
                shard,
            ),
        )

    return lax.fori_loop(0, ahead, one, state)


def exact_product(form, left, right):
    return jnp.einsum(form, left, right, precision=highest)


def unit_lower_inverse(lower_part):
    full_size = lower_part.shape[1]
    identity = jnp.eye(full_size, dtype=jnp.float32)
    result = identity - lower_part
    power = lower_part
    span = 2
    while span < full_size:
        power = exact_product("bij,bjk->bik", power, power)
        result = exact_product("bij,bjk->bik", result, identity + power)
        span = 2 * span
    return result


def unit_rows(matrix):
    return matrix * lax.rsqrt(jnp.sum(matrix * matrix, axis=-1, keepdims=True) + epsilon)


def compose(earlier, later):
    return (
        exact_product("hij,hjk->hik", earlier[0], later[0]),
        exact_product("hvj,hjk->hvk", earlier[1], later[0]) + later[1],
    )


def head_mixer(extended, rate_logits, conv_taps, biases):
    row_count = rate_logits.shape[0]
    mixed_rows = jax.nn.silu(
        sum(
            (
                conv_taps[tap_index] * extended[tap_index : tap_index + row_count]
                for tap_index in range(CONV)
            )
        )
    )
    blocks = row_count // BLOCK
    queries = (unit_rows(mixed_rows[:, :DK]) * DK ** (-0.5)).reshape(blocks, BLOCK, DK)
    key_rows = unit_rows(mixed_rows[:, DK : 2 * DK]).reshape(blocks, BLOCK, DK)
    values = mixed_rows[:, 2 * DK :]
    augmented = jnp.concatenate([values, jnp.zeros((row_count, DK), jnp.float32)], axis=1).reshape(
        blocks, BLOCK, DV + DK
    )
    log_decay = -jax.nn.softplus(rate_logits[:, 0] + biases[0])
    strength = jax.nn.sigmoid(rate_logits[:, 1] + biases[1]).reshape(blocks, BLOCK)
    cumulative = jnp.cumsum(log_decay.reshape(blocks, BLOCK), axis=1)
    final_decay = cumulative[:, -1]
    positions = jnp.arange(BLOCK)
    included = positions[:, None] >= positions[None, :]
    strictly = positions[:, None] > positions[None, :]
    difference = cumulative[:, :, None] - cumulative[:, None, :]
    decays = jnp.where(included, jnp.exp(jnp.where(included, difference, 0.0)), 0.0)
    key_gram = exact_product("cik,cjk->cij", key_rows, key_rows)
    lower_part = jnp.where(strictly, strength[:, :, None] * decays * key_gram, 0.0)
    inverse = unit_lower_inverse(lower_part)
    updates = exact_product("cij,cjw->ciw", inverse, strength[:, :, None] * augmented)
    weighted = exact_product(
        "cij,cjw->ciw", inverse, (strength * jnp.exp(cumulative))[:, :, None] * key_rows
    )
    key_tails = key_rows * jnp.exp(final_decay[:, None] - cumulative)[:, :, None]
    transitions = jnp.exp(final_decay)[:, None, None] * jnp.eye(
        DK, dtype=jnp.float32
    ) - exact_product("cti,ctj->cij", weighted, key_tails)
    injections = exact_product("ctv,ctk->cvk", updates, key_tails)
    prefix_maps, prefix_adds = lax.associative_scan(compose, (transitions, injections))
    start_state = jnp.concatenate(
        [jnp.zeros((DV, DK), jnp.float32), jnp.eye(DK, dtype=jnp.float32)], axis=0
    )
    end_states = exact_product("vj,cjk->cvk", start_state, prefix_maps) + prefix_adds
    starts = jnp.concatenate([start_state[None], end_states[:-1]], axis=0)
    errors = updates - exact_product("ctk,cvk->ctv", weighted, starts)
    scores = exact_product("cik,cjk->cij", queries, key_rows) * decays
    outputs = exact_product(
        "ctk,cvk->ctv", queries * jnp.exp(cumulative)[:, :, None], starts
    ) + exact_product("cij,cjv->civ", scores, errors)
    return (outputs.reshape(row_count, DV + DK), end_states[-1])


def per_device(
    tokens,
    w_qkvg,
    w_rates,
    conv_weight,
    head_bias,
    norm_gain,
    head_gain,
    mlp_gain,
    w_out,
    w_ff_gate,
    w_ff_up,
    w_ff_down,
    cotangent,
):
    heads_here = head_bias.shape[1]
    per_head = 2 * DK + 2 * DV
    mixed_width = 2 * DK + DV
    contract = (((1,), (1,)), ((), ()))
    rows_first = (((0,), (0,)), ((), ()))
    head_index = lax.axis_index("head")
    inputs = tokens.astype(jnp.float32)
    inverse_one = lax.rsqrt(jnp.mean(inputs * inputs, axis=-1, keepdims=True) + epsilon)
    norm_normed = inputs * inverse_one
    block_tokens, block_cotangent = (
        lax.all_gather(tokens, "head", axis=0, tiled=True),
        lax.all_gather(cotangent, "head", axis=0, tiled=True),
    )
    seq_rows = block_tokens.shape[0]
    block_inputs = block_tokens.astype(jnp.float32)
    block_rows = (
        block_inputs
        * lax.rsqrt(jnp.mean(block_inputs * block_inputs, axis=-1, keepdims=True) + epsilon)
        * norm_gain
    ).astype(jnp.bfloat16)
    w_mix, w_rate, out_rows, ff_gate_rows, ff_up_rows, ff_down_rows = (
        lax.all_gather(w_qkvg, "seq", axis=0, tiled=True),
        lax.all_gather(w_rates, "seq", axis=0, tiled=True),
        lax.all_gather(w_out, "seq", axis=1, tiled=True),
        lax.all_gather(w_ff_gate, "seq", axis=1, tiled=True),
        lax.all_gather(w_ff_up, "seq", axis=1, tiled=True),
        lax.all_gather(w_ff_down, "seq", axis=1, tiled=True),
    )
    projected = (
        jnp.dot(block_rows, w_mix, preferred_element_type=jnp.float32)
        .astype(jnp.bfloat16)
        .reshape(seq_rows, heads_here, per_head)
    )
    rate_logits = jnp.dot(block_rows, w_rate, preferred_element_type=jnp.float32).reshape(
        seq_rows, heads_here, 2
    )
    mixer_in = projected[:, :, :mixed_width]
    halo_rows = shifted(mixer_in[seq_rows - (CONV - 1) :], "seq", 1)
    extended = jnp.concatenate([halo_rows, mixer_in], axis=0).astype(jnp.float32)
    conv_taps = conv_weight.reshape(CONV, heads_here, mixed_width)
    mixer_all = jax.vmap(head_mixer, in_axes=(1, 1, 1, 1), out_axes=(1, 0))
    (outputs, end_state), mixer_pull = jax.vjp(
        mixer_all, extended, rate_logits, conv_taps, head_bias
    )
    transfer = end_state[:, DV:, :]
    injected = end_state[:, :DV, :]
    identity = (
        jnp.broadcast_to(jnp.eye(DK, dtype=jnp.float32), transfer.shape),
        jnp.zeros_like(injected),
    )
    prefix_map, incoming = entering((transfer, injected), "seq", compose, identity)
    attended = outputs[:, :, :DV] + exact_product("thk,hvk->thv", outputs[:, :, DV:], incoming)
    mixer_val = lax.optimization_barrier(attended.astype(jnp.bfloat16)).astype(jnp.float32)
    gate_val = projected[:, :, mixed_width:].astype(jnp.float32)
    head_inverse = lax.rsqrt(jnp.mean(mixer_val * mixer_val, axis=-1, keepdims=True) + epsilon)
    head_normed = mixer_val * head_inverse
    gate_sigmoid = jax.nn.sigmoid(gate_val)
    gate_silu = gate_val * gate_sigmoid
    gated_rows = (
        (head_normed * head_gain * gate_silu)
        .astype(jnp.bfloat16)
        .reshape(seq_rows, heads_here * DV)
    )
    residual = inputs + lax.psum_scatter(
        jnp.dot(gated_rows, out_rows, preferred_element_type=jnp.float32).astype(jnp.bfloat16),
        "head",
        scatter_dimension=0,
        tiled=True,
    ).astype(jnp.float32)
    own_inverse = lax.rsqrt(jnp.mean(residual * residual, axis=-1, keepdims=True) + epsilon)
    mlp_own = (residual * own_inverse * mlp_gain).astype(jnp.bfloat16)
    mlp_all = lax.all_gather(mlp_own, "head", axis=0, tiled=True)
    inverse_two = lax.rsqrt(jnp.mean(residual * residual, axis=-1, keepdims=True) + epsilon)
    mlp_normed = residual * inverse_two
    gate_pre = lax.dot_general(mlp_all, ff_gate_rows, contract, preferred_element_type=jnp.float32)
    up_pre = lax.dot_general(mlp_all, ff_up_rows, contract, preferred_element_type=jnp.float32)
    ff_sigmoid = jax.nn.sigmoid(gate_pre)
    ff_silu = gate_pre * ff_sigmoid
    hidden = (ff_silu * up_pre).astype(jnp.bfloat16)
    output = (
        residual
        + lax.psum_scatter(
            jnp.dot(hidden, ff_down_rows, preferred_element_type=jnp.float32).astype(jnp.bfloat16),
            "head",
            scatter_dimension=0,
            tiled=True,
        ).astype(jnp.float32)
    ).astype(jnp.bfloat16)
    grad_down = lax.dot_general(
        hidden, block_cotangent, rows_first, preferred_element_type=jnp.float32
    )
    grad_hidden = lax.dot_general(
        block_cotangent, ff_down_rows, contract, preferred_element_type=jnp.float32
    )
    ff_slope = ff_sigmoid * (1.0 + gate_pre * (1.0 - ff_sigmoid))
    grad_gate_pre = (grad_hidden * up_pre * ff_slope).astype(jnp.bfloat16)
    grad_up_pre = (grad_hidden * ff_silu).astype(jnp.bfloat16)
    grad_gate_w = lax.dot_general(
        grad_gate_pre, mlp_all, rows_first, preferred_element_type=jnp.float32
    )
    grad_up_w = lax.dot_general(
        grad_up_pre, mlp_all, rows_first, preferred_element_type=jnp.float32
    )
    grad_mlp_in = lax.psum_scatter(
        (
            jnp.dot(grad_gate_pre, ff_gate_rows, preferred_element_type=jnp.float32)
            + jnp.dot(grad_up_pre, ff_up_rows, preferred_element_type=jnp.float32)
        ).astype(jnp.bfloat16),
        "head",
        scatter_dimension=0,
        tiled=True,
    ).astype(jnp.float32)
    mlp_gain_part = jnp.sum(grad_mlp_in * mlp_normed, axis=0)
    scaled_two = grad_mlp_in * mlp_gain
    grad_residual = cotangent.astype(jnp.float32) + inverse_two * (
        scaled_two - mlp_normed * jnp.mean(scaled_two * mlp_normed, axis=-1, keepdims=True)
    )
    grad_branch = grad_residual.astype(jnp.bfloat16)
    branch_block = lax.all_gather(grad_branch, "head", axis=0, tiled=True)
    grad_out_w = lax.dot_general(
        gated_rows, branch_block, rows_first, preferred_element_type=jnp.float32
    )
    grad_gated = lax.dot_general(
        branch_block, out_rows, contract, preferred_element_type=jnp.float32
    ).reshape(seq_rows, heads_here, DV)
    grad_normed_head = grad_gated * gate_silu
    gate_slope = gate_sigmoid * (1.0 + gate_val * (1.0 - gate_sigmoid))
    grad_gate_mix = (grad_gated * head_normed * head_gain * gate_slope).astype(jnp.bfloat16)
    head_gain_part = jnp.sum(grad_normed_head * head_normed, axis=(0, 1))
    scaled_head = grad_normed_head * head_gain
    grad_mixer = (
        head_inverse
        * (scaled_head - head_normed * jnp.mean(scaled_head * head_normed, axis=-1, keepdims=True))
    ).astype(jnp.bfloat16)
    grad_attended = grad_mixer.astype(jnp.float32)
    local_grad = exact_product("thv,thk->hvk", grad_attended, outputs[:, :, DV:])
    transposed = jnp.swapaxes(transfer, 1, 2)
    suffix_map, grad_end = prefix((transposed, local_grad), "seq", compose, identity)
    grad_outputs = jnp.concatenate(
        [grad_attended, exact_product("thv,hvk->thk", grad_attended, incoming)], axis=2
    )
    grad_final = jnp.concatenate(
        [grad_end, exact_product("hvk,hvj->hkj", incoming, grad_end)], axis=1
    )
    grad_extended, grad_rates, grad_taps, grad_biases = mixer_pull((grad_outputs, grad_final))
    halo_grad = shifted(grad_extended[: CONV - 1], "seq", -1)
    grad_mixed = grad_extended[CONV - 1 :]
    grad_mixed = jnp.concatenate(
        [grad_mixed[: seq_rows - (CONV - 1)], grad_mixed[seq_rows - (CONV - 1) :] + halo_grad],
        axis=0,
    )
    grad_projected = (
        jnp.concatenate([grad_mixed, grad_gate_mix.astype(jnp.float32)], axis=2)
        .astype(jnp.bfloat16)
        .reshape(seq_rows, heads_here * per_head)
    )
    grad_rate_low = grad_rates.reshape(seq_rows, heads_here * 2).astype(jnp.bfloat16)
    grad_w_mix = lax.dot_general(
        block_rows, grad_projected, rows_first, preferred_element_type=jnp.float32
    )
    grad_w_rate = lax.dot_general(
        block_rows, grad_rate_low, rows_first, preferred_element_type=jnp.float32
    )
    grad_w_mix_s, grad_w_rate_s, grad_out_s, grad_gate_s, grad_up_s, grad_down_s = (
        lax.psum_scatter(
            grad_w_mix.astype(jnp.bfloat16), "seq", scatter_dimension=0, tiled=True
        ).astype(jnp.float32),
        lax.psum_scatter(
            grad_w_rate.astype(jnp.bfloat16), "seq", scatter_dimension=0, tiled=True
        ).astype(jnp.float32),
        lax.psum_scatter(
            grad_out_w.astype(jnp.bfloat16), "seq", scatter_dimension=1, tiled=True
        ).astype(jnp.float32),
        lax.psum_scatter(
            grad_gate_w.astype(jnp.bfloat16), "seq", scatter_dimension=1, tiled=True
        ).astype(jnp.float32),
        lax.psum_scatter(
            grad_up_w.astype(jnp.bfloat16), "seq", scatter_dimension=1, tiled=True
        ).astype(jnp.float32),
        lax.psum_scatter(
            grad_down.astype(jnp.bfloat16), "seq", scatter_dimension=1, tiled=True
        ).astype(jnp.float32),
    )
    grad_normed = lax.psum_scatter(
        (
            lax.dot_general(grad_projected, w_mix, contract, preferred_element_type=jnp.float32)
            + lax.dot_general(grad_rate_low, w_rate, contract, preferred_element_type=jnp.float32)
        ).astype(jnp.bfloat16),
        "head",
        scatter_dimension=0,
        tiled=True,
    ).astype(jnp.float32)
    norm_gain_part = jnp.sum(grad_normed * norm_normed, axis=0)
    scaled_one = grad_normed * norm_gain
    grad_input = grad_residual + inverse_one * (
        scaled_one - norm_normed * jnp.mean(scaled_one * norm_normed, axis=-1, keepdims=True)
    )
    head_groups = lax.axis_size("head")
    taps_full = jnp.zeros((CONV, head_groups, heads_here * mixed_width), jnp.float32)
    taps_full = lax.dynamic_update_slice_in_dim(
        taps_full, grad_taps.reshape(CONV, 1, heads_here * mixed_width), head_index, 1
    )
    bias_full = jnp.zeros((2, head_groups, heads_here), jnp.float32)
    bias_full = lax.dynamic_update_slice_in_dim(
        bias_full, grad_biases.reshape(2, 1, heads_here), head_index, 1
    )
    taps_sum, bias_sum, norm_gain_grad, mlp_gain_grad, head_gain_grad = lax.psum(
        (taps_full, bias_full, norm_gain_part, mlp_gain_part, head_gain_part), ("seq", "head")
    )
    conv_grad = lax.dynamic_index_in_dim(taps_sum, head_index, 1, False)
    bias_grad = lax.dynamic_index_in_dim(bias_sum, head_index, 1, False)
    return (
        output,
        grad_input,
        grad_w_mix_s,
        grad_w_rate_s,
        conv_grad,
        bias_grad,
        norm_gain_grad,
        head_gain_grad,
        mlp_gain_grad,
        grad_out_s,
        grad_gate_s,
        grad_up_s,
        grad_down_s,
    )


def solution(mesh):
    in_specs = (
        P(("seq", "head"), None),
        P("seq", "head"),
        P("seq", "head"),
        P(None, "head"),
        P(None, "head"),
        P(),
        P(),
        P(),
        P("head", "seq"),
        P("head", "seq"),
        P("head", "seq"),
        P("head", "seq"),
        P(("seq", "head"), None),
    )
    out_specs = (
        P(("seq", "head"), None),
        P(("seq", "head"), None),
        P("seq", "head"),
        P("seq", "head"),
        P(None, "head"),
        P(None, "head"),
        P(),
        P(),
        P(),
        P("head", "seq"),
        P("head", "seq"),
        P("head", "seq"),
        P("head", "seq"),
    )
    return jax.shard_map(
        per_device, mesh=mesh, in_specs=in_specs, out_specs=out_specs, check_vma=False
    )
```

profile of v0, /device:TPU:0, one launch (start us, length us, event | category | flops | bytes accessed | tf_op | source)
XLA Modules:
  0.0 1815.7 jit_solution(9491780598576695689)
XLA Ops:
  19.2 67.0 %all-gather.15.cloned.1.call-done = bf16[1024,2048]{1,0:T(8,128)(2,1)} async-done(((bf16[128,2048]{1,0:T(8,128)(2,1)}), bf16[1024,2048]{1,0:T(8,128)(2,1)}) %all-gather.15.cloned.1.call-update) | async-done | bytes 4194320 | tf_op jit(solution)/shard_map/all_gather | solution.py:167
  92.9 39.6 %all-gather.17.cloned.1.call-done = bf16[2048,1536]{1,0:T(8,128)(2,1)} async-done(((bf16[512,1536]{1,0:T(8,128)(2,1)}), bf16[2048,1536]{1,0:T(8,128)(2,1)}) %all-gather.17.cloned.1.call-update) | async-done | bytes 6291472 | tf_op jit(solution)/shard_map/all_gather | solution.py:178
  132.5 11.7 convolution_convert_fusion.1
  238.7 10.2 pad.285
  255.7 10.9 fusion.169
  308.0 10.3 pad.284
  333.3 12.5 pad.293
  353.2 12.6 pad.292
  365.8 10.3 bitcast_add_fusion
  394.8 7.4 fusion.72
  405.7 10.8 all-gather
  444.5 87.6 %reduce-scatter.13.cloned.1.call-done = bf16[128,2048]{1,0:T(8,128)(2,1)} async-done(((bf16[1024,2048]{1,0:T(8,128)(2,1)}), bf16[128,2048]{1,0:T(8,128)(2,1)}) %reduce-scatter.13.cloned.1.call-update) | async-done | bytes 524304 | tf_op jit(solution)/shard_map/reduce_scatter | solution.py:220
  537.7 22.6 %all-gather.25.cloned.1.call-done = bf16[704,2048]{1,0:T(8,128)(2,1)} async-done(((bf16[704,512]{1,0:T(8,128)(2,1)}), bf16[704,2048]{1,0:T(8,128)(2,1)}) %all-gather.25.cloned.1.call-update) | async-done | bytes 2883600 | tf_op jit(solution)/shard_map/all_gather | solution.py:182
  560.4 76.3 %all-gather.21.cloned.1.call-done = bf16[1024,2048]{1,0:T(8,128)(2,1)} async-done(((bf16[128,2048]{1,0:T(8,128)(2,1)}), bf16[1024,2048]{1,0:T(8,128)(2,1)}) %all-gather.21.cloned.1.call-update) | async-done | bytes 4194320 | tf_op jit(solution)/shard_map/all_gather | solution.py:228
  636.7 7.8 fusion.354
  644.6 19.1 %all-gather.23.cloned.1.call-done = bf16[704,2048]{1,0:T(8,128)(2,1)} async-done(((bf16[704,512]{1,0:T(8,128)(2,1)}), bf16[704,2048]{1,0:T(8,128)(2,1)}) %all-gather.23.cloned.1.call-update) | async-done | bytes 2883600 | tf_op jit(solution)/shard_map/all_gather | solution.py:181
  663.7 7.9 fusion.353
  671.6 20.8 %all-gather.27.cloned.1.call-done = bf16[704,2048]{1,0:T(8,128)(2,1)} async-done(((bf16[704,512]{1,0:T(8,128)(2,1)}), bf16[704,2048]{1,0:T(8,128)(2,1)}) %all-gather.27.cloned.1.call-update) | async-done | bytes 2883600 | tf_op jit(solution)/shard_map/all_gather | solution.py:183
  692.4 75.6 %all-gather.29.cloned.1.call-done = bf16[1024,2048]{1,0:T(8,128)(2,1)} async-done(((bf16[128,2048]{1,0:T(8,128)(2,1)}), bf16[1024,2048]{1,0:T(8,128)(2,1)}) %all-gather.29.cloned.1.call-update) | async-done | bytes 4194320 | tf_op jit(solution)/shard_map/all_gather | solution.py:168
  768.1 10.0 multiply_convert_fusion
  787.6 86.5 %reduce-scatter.17.cloned.1.call-done = bf16[128,2048]{1,0:T(8,128)(2,1)} async-done(((bf16[1024,2048]{1,0:T(8,128)(2,1)}), bf16[128,2048]{1,0:T(8,128)(2,1)}) %reduce-scatter.17.cloned.1.call-update) | async-done | bytes 524304 | tf_op jit(solution)/shard_map/reduce_scatter | solution.py:260
  878.8 7.4 convolution_convert_fusion.4
  886.3 7.6 convolution_convert_fusion.5
  901.0 7.4 convolution_convert_fusion.6
  908.4 43.6 %all-gather.31.cloned.1.call-done = bf16[1024,2048]{1,0:T(8,128)(2,1)} async-done(((bf16[128,2048]{1,0:T(8,128)(2,1)}), bf16[1024,2048]{1,0:T(8,128)(2,1)}) %all-gather.31.cloned.1.call-update) | async-done | bytes 4194320 | tf_op jit(solution)/shard_map/all_gather | solution.py:275
  972.4 10.9 all-gather.3
  984.0 11.9 while.28
  1002.0 7.5 fusion.358
  1009.5 10.4 multiply_reduce_fusion.7
  1023.4 11.0 fusion.155
  1034.4 9.8 fusion.26
  1044.2 11.0 fusion.30
  1185.1 12.5 pad.319
  1197.6 12.4 pad.320
  1210.0 11.5 pad.298
  1221.4 10.9 add_add_fusion
  1232.4 9.4 fusion.359
  1241.8 10.8 convolution_add_fusion
  1255.3 9.0 pad.324
  1270.8 8.3 fusion.95
  1406.5 9.8 fusion.366
  1429.8 11.6 convolution_convert_fusion
  1450.6 76.4 %all-reduce.73.cloned.1.call-done = f32[4,8,1024]{2,0,1:T(4,128)} async-done(((f32[4,8,1024]{2,0,1:T(4,128)}), f32[4,8,1024]{2,0,1:T(4,128)}) %all-reduce.73.cloned.1.call-update) | async-done | bytes 131088 | tf_op jit(solution)/shard_map/psum | solution.py:363
  1528.3 31.6 %reduce-scatter.23.cloned.1.call-done = bf16[512,512]{1,0:T(8,128)(2,1)} async-done(((bf16[512,2048]{1,0:T(8,128)(2,1)}), bf16[512,512]{1,0:T(8,128)(2,1)}) %reduce-scatter.23.cloned.1.call-update) | async-done | bytes 524304 | tf_op jit(solution)/shard_map/reduce_scatter | solution.py:327
  1562.0 89.8 %reduce-scatter.19.cloned.1.call-done = bf16[128,2048]{1,0:T(8,128)(2,1)} async-done(((bf16[1024,2048]{1,0:T(8,128)(2,1)}), bf16[128,2048]{1,0:T(8,128)(2,1)}) %reduce-scatter.19.cloned.1.call-update) | async-done | bytes 524304 | tf_op jit(solution)/shard_map/reduce_scatter | solution.py:340
  1653.4 43.0 %all-reduce.70 = (f32[2,8,2]{2,0,1:T(2,128)S(1)}, f32[2048]{0:T(1024)}, f32[256]{0:T(256)}, f32[2048]{0:T(1024)}) all-reduce(f32[2,8,2]{2,0,1:T(2,128)S(1)} %bitcast_dynamic-update-slice_fusion, f32[2048]{0:T(1024)S(1)} %get-tuple-element.273, f32[256]{0:T(256)S(1)} %copy-done.208, ...), channel_id=1, replica_groups=mesh['seq'=4,'head'=8] {'seq','head'}, use_global_device_ids=true, to_apply=%region_39.40 | all-reduce | flops 4384 | bytes 35072 | tf_op jit(solution)/shard_map/psum | solution.py:363
  1697.0 47.3 %reduce-scatter.15.cloned.1.call-done = bf16[128,2048]{1,0:T(8,128)(2,1)} async-done(((bf16[1024,2048]{1,0:T(8,128)(2,1)}), bf16[128,2048]{1,0:T(8,128)(2,1)}) %reduce-scatter.15.cloned.1.call-update) | async-done | bytes 524304 | tf_op jit(solution)/shard_map/reduce_scatter | solution.py:238
  1747.5 57.6 %reduce-scatter.21.cloned.1.call-done = bf16[512,1536]{1,0:T(8,128)(2,1)} async-done(((bf16[2048,1536]{1,0:T(8,128)(2,1)}), bf16[512,1536]{1,0:T(8,128)(2,1)}) %reduce-scatter.21.cloned.1.call-update) | async-done | bytes 1572880 | tf_op jit(solution)/shard_map/reduce_scatter | solution.py:321
  (856 shorter events, 607.8 us)
Async XLA Ops:
  7.2 79.1 %all-gather.15.cloned.1.call-start = ((), (), s32[]{:S(2)}) async-start(), calls=%async_computation.10 | async-start | bytes 4718592 | tf_op jit(solution)/shard_map/all_gather | solution.py:167
  7.2 82.3 %copy-start.195 = (f32[2048]{0:T(1024)S(1)}, f32[2048]{0:T(1024)}, u32[]{:S(2)}) copy-start(f32[2048]{0:T(1024)} %param.22) | copy-start | bytes 24580
  7.9 124.6 %all-gather.17.cloned.1.call-start = ((), (), s32[]{:S(2)}) async-start(), calls=%async_computation.11 | async-start | bytes 7864320 | tf_op jit(solution)/shard_map/all_gather | solution.py:178
  8.7 414.2 %all-gather.33.cloned.1.call-start = ((), (), s32[]{:S(2)}) async-start(), calls=%async_computation.29 | async-start | bytes 1310720 | tf_op jit(solution)/shard_map/all_gather | solution.py:24
  18.4 72.6 %copy-start.185 = (bf16[2048,4]{0,1:T(4,128)(2,1)}, bf16[2048,4]{0,1:T(4,128)(2,1)S(1)}, u32[]{:S(2)}) copy-start(bf16[2048,4]{0,1:T(4,128)(2,1)S(1)} %all_gather.56) | copy-start | bytes 49156
  18.4 167.7 %copy-start.150 = (pred[64,64]{0,1:T(8,128)(4,1)}, pred[64,64]{0,1:T(8,128)(4,1)S(1)}, u32[]{:S(2)}) copy-start(pred[64,64]{0,1:T(8,128)(4,1)S(1)} %iota_compare_fusion.1) | copy-start | bytes 12292
  18.4 167.7 %copy-start.170 = (pred[64,64]{0,1:T(8,128)(4,1)}, pred[64,64]{0,1:T(8,128)(4,1)S(1)}, u32[]{:S(2)}) copy-start(pred[64,64]{0,1:T(8,128)(4,1)S(1)} %iota_compare_fusion.2) | copy-start | bytes 12292
  18.4 175.1 %copy-start.126 = (f32[64,64]{0,1:T(8,128)}, f32[64,64]{0,1:T(8,128)S(1)}, u32[]{:S(2)}) copy-start(f32[64,64]{0,1:T(8,128)S(1)} %fusion.283) | copy-start | bytes 49156
  18.5 181.1 %copy-start.129 = (f32[128,128]{1,0:T(8,128)}, f32[128,128]{1,0:T(8,128)S(1)}, u32[]{:S(2)}) copy-start(f32[128,128]{1,0:T(8,128)S(1)} %fusion.280) | copy-start | bytes 196612
  19.2 72.1 %copy-start.204 = (f32[2]{0:T(128)}, f32[2]{0:T(128)S(1)}, u32[]{:S(2)}) copy-start(f32[2]{0:T(128)S(1)} %get-tuple-element.361) | copy-start | bytes 28
  19.2 72.9 %copy-start.202 = (f32[2]{0:T(128)}, f32[2]{0:T(128)S(1)}, u32[]{:S(2)}) copy-start(f32[2]{0:T(128)S(1)} %get-tuple-element.360) | copy-start | bytes 28
  92.1 107.4 %copy-start.154 = (f32[2,16,64]{2,1,0:T(8,128)}, f32[2,16,64]{2,1,0:T(8,128)S(1)}, u32[]{:S(2)}) copy-start(f32[2,16,64]{2,1,0:T(8,128)S(1)} %subtract_exponential_fusion) | copy-start | bytes 24580
  148.5 10.1 collective-permute-start
  167.4 223.4 %copy-start.1 = (f32[2,1024,128]{2,1,0:T(8,128)}, f32[2,1024,128]{2,1,0:T(8,128)S(1)}, u32[]{:S(2)}) copy-start(f32[2,1024,128]{2,1,0:T(8,128)S(1)} %get-tuple-element.334) | copy-start | bytes 3145732
  203.8 71.6 %copy-start.4 = (f32[2,16,128,128]{3,2,1,0:T(8,128)}, f32[2,16,128,128]{3,2,1,0:T(8,128)S(1)}, u32[]{:S(2)}) copy-start(f32[2,16,128,128]{3,2,1,0:T(8,128)S(1)} %multiply_subtract_fusion) | copy-start | bytes 6291460
  207.0 77.9 %copy-start.106 = (f32[2,2,128,128]{3,2,1,0:T(8,128)}, f32[2,2,128,128]{3,2,1,0:T(8,128)S(1)}, u32[]{:S(2)}) copy-start(f32[2,2,128,128]{3,2,1,0:T(8,128)S(1)} %fusion.262) | copy-start | bytes 786436
  379.6 57.2 %all-gather.19.cloned.1.call-start = ((), (), s32[]{:S(2)}) async-start(), calls=%async_computation.12 | async-start | bytes 2621440 | tf_op jit(solution)/shard_map/all_gather | solution.py:180
  380.2 151.9 %reduce-scatter.13.cloned.1.call-start = ((), (), s32[]{:S(2)}) async-start(), calls=%async_computation.13 | async-start | bytes 4718592 | tf_op jit(solution)/shard_map/reduce_scatter | solution.py:220
  443.8 88.2 %copy-start.47 = (bf16[128,2048]{1,0:T(8,128)(2,1)S(1)}, bf16[128,2048]{1,0:T(8,128)(2,1)}, u32[]{:S(2)}) copy-start(bf16[128,2048]{1,0:T(8,128)(2,1)} %param.17) | copy-start | bytes 1572868
  443.8 89.6 %copy-start.172 = (f32[2048]{0:T(1024)S(1)}, f32[2048]{0:T(1024)}, u32[]{:S(2)}) copy-start(f32[2048]{0:T(1024)} %param.24) | copy-start | bytes 24580
  443.8 116.5 %all-gather.25.cloned.1.call-start = ((), (), s32[]{:S(2)}) async-start(), calls=%async_computation.16 | async-start | bytes 3604480 | tf_op jit(solution)/shard_map/all_gather | solution.py:182
  444.4 192.3 %all-gather.21.cloned.1.call-start = ((), (), s32[]{:S(2)}) async-start(), calls=%async_computation.14 | async-start | bytes 4718592 | tf_op jit(solution)/shard_map/all_gather | solution.py:228
  533.4 342.9 %copy-start.199 = (f32[128]{0:T(128)}, f32[128]{0:T(128)S(1)}, u32[]{:S(2)}) copy-start(f32[128]{0:T(128)S(1)} %add_rsqrt_fusion.5) | copy-start | bytes 1540
  535.4 128.3 %all-gather.23.cloned.1.call-start = ((), (), s32[]{:S(2)}) async-start(), calls=%async_computation.15 | async-start | bytes 3604480 | tf_op jit(solution)/shard_map/all_gather | solution.py:181
  536.2 156.2 %all-gather.27.cloned.1.call-start = ((), (), s32[]{:S(2)}) async-start(), calls=%async_computation.17 | async-start | bytes 3604480 | tf_op jit(solution)/shard_map/all_gather | solution.py:183
  536.9 231.1 %all-gather.29.cloned.1.call-start = ((), (), s32[]{:S(2)}) async-start(), calls=%async_computation.19 | async-start | bytes 4718592 | tf_op jit(solution)/shard_map/all_gather | solution.py:168
  537.5 336.5 %reduce-scatter.17.cloned.1.call-start = ((), (), s32[]{:S(2)}) async-start(), calls=%async_computation.20 | async-start | bytes 4718592 | tf_op jit(solution)/shard_map/reduce_scatter | solution.py:260
  787.5 86.5 %copy-start.68 = (bf16[128,2048]{1,0:T(8,128)(2,1)S(1)}, bf16[128,2048]{1,0:T(8,128)(2,1)}, u32[]{:S(2)}) copy-start(bf16[128,2048]{1,0:T(8,128)(2,1)} %reduce-scatter.13.cloned.1.call-done) | copy-start | bytes 1572868
  787.5 164.5 %all-gather.31.cloned.1.call-start = ((), (), s32[]{:S(2)}) async-start(), calls=%async_computation.21 | async-start | bytes 4718592 | tf_op jit(solution)/shard_map/all_gather | solution.py:275
  878.7 562.8 %reduce-scatter.29.cloned.1.call-start = ((), (), s32[]{:S(2)}) async-start(), calls=%async_computation.28 | async-start | bytes 3604480 | tf_op jit(solution)/shard_map/reduce_scatter | solution.py:336
  886.2 557.8 %reduce-scatter.27.cloned.1.call-start = ((), (), s32[]{:S(2)}) async-start(), calls=%async_computation.27 | async-start | bytes 3604480 | tf_op jit(solution)/shard_map/reduce_scatter | solution.py:333
  893.9 552.6 %reduce-scatter.25.cloned.1.call-start = ((), (), s32[]{:S(2)}) async-start(), calls=%async_computation.26 | async-start | bytes 3604480 | tf_op jit(solution)/shard_map/reduce_scatter | solution.py:330
  908.4 540.6 %reduce-scatter.31.cloned.1.call-start = ((), (), s32[]{:S(2)}) async-start(), calls=%async_computation.30 | async-start | bytes 655360
  1378.6 148.4 %all-reduce.73.cloned.1.call-start = ((), (), s32[]{:S(2)}) async-start(), calls=%async_computation.24 | async-start | bytes 262144 | tf_op jit(solution)/shard_map/psum | solution.py:363
  1379.5 180.4 %reduce-scatter.23.cloned.1.call-start = ((), (), s32[]{:S(2)}) async-start(), calls=%async_computation.25 | async-start | bytes 2621440 | tf_op jit(solution)/shard_map/reduce_scatter | solution.py:327
  1385.5 266.4 %reduce-scatter.19.cloned.1.call-start = ((), (), s32[]{:S(2)}) async-start(), calls=%async_computation.22 | async-start | bytes 4718592 | tf_op jit(solution)/shard_map/reduce_scatter | solution.py:340
  1392.6 9.5 collective-permute-start.1
  1419.7 324.6 %reduce-scatter.15.cloned.1.call-start = ((), (), s32[]{:S(2)}) async-start(), calls=%async_computation.18 | async-start | bytes 4718592 | tf_op jit(solution)/shard_map/reduce_scatter | solution.py:238
  1427.9 377.2 %reduce-scatter.21.cloned.1.call-start = ((), (), s32[]{:S(2)}) async-start(), calls=%async_computation.23 | async-start | bytes 7864320 | tf_op jit(solution)/shard_map/reduce_scatter | solution.py:321
  1443.9 208.0 %copy-start.48 = (bf16[128,2048]{1,0:T(8,128)(2,1)S(1)}, bf16[128,2048]{1,0:T(8,128)(2,1)}, u32[]{:S(2)}) copy-start(bf16[128,2048]{1,0:T(8,128)(2,1)} %param.17) | copy-start | bytes 1572868
  1443.9 209.5 %copy-start.197 = (f32[2048]{0:T(1024)S(1)}, f32[2048]{0:T(1024)}, u32[]{:S(2)}) copy-start(f32[2048]{0:T(1024)} %get-tuple-element.271) | copy-start | bytes 24580
  1443.9 209.5 %copy-start.208 = (f32[256]{0:T(256)S(1)}, f32[256]{0:T(256)}, u32[]{:S(2)}) copy-start(f32[256]{0:T(256)} %get-tuple-element.265) | copy-start | bytes 3076
  1443.9 300.4 %copy-start.69 = (bf16[128,2048]{1,0:T(8,128)(2,1)S(1)}, bf16[128,2048]{1,0:T(8,128)(2,1)}, u32[]{:S(2)}) copy-start(bf16[128,2048]{1,0:T(8,128)(2,1)} %reduce-scatter.13.cloned.1.call-done) | copy-start | bytes 1572868
  1443.9 300.4 %copy-start.110 = (bf16[128,2048]{1,0:T(8,128)(2,1)S(1)}, bf16[128,2048]{1,0:T(8,128)(2,1)}, u32[]{:S(2)}) copy-start(bf16[128,2048]{1,0:T(8,128)(2,1)} %reduce-scatter.17.cloned.1.call-done) | copy-start | bytes 1572868
  1443.9 300.4 %copy-start.111 = (bf16[128,2048]{1,0:T(8,128)(2,1)S(1)}, bf16[128,2048]{1,0:T(8,128)(2,1)}, u32[]{:S(2)}) copy-start(bf16[128,2048]{1,0:T(8,128)(2,1)} %param.29) | copy-start | bytes 1572868
  1443.9 300.4 %copy-start.173 = (f32[2048]{0:T(1024)S(1)}, f32[2048]{0:T(1024)}, u32[]{:S(2)}) copy-start(f32[2048]{0:T(1024)} %param.24) | copy-start | bytes 24580
  1443.9 300.4 %copy-start.200 = (f32[128]{0:T(128)S(1)}, f32[128]{0:T(128)}, u32[]{:S(2)}) copy-start(f32[128]{0:T(128)} %copy-done.199) | copy-start | bytes 1540
  1443.9 300.4 %copy-start.210 = (f32[128]{0:T(128)S(1)}, f32[128]{0:T(128)}, u32[]{:S(2)}) copy-start(f32[128]{0:T(128)} %copy-done.209) | copy-start | bytes 1540
  (207 other events, 1255.0 us)
Sparse Core Ops, SparseCore 0:
  10.1 76.0 all-gather.14
  87.8 44.6 all-gather.16
  379.7 16.7 all-gather.32
  398.0 25.3 all-gather.18
  444.0 88.0 reduce-scatter.12
  533.5 26.7 all-gather.24
  563.3 73.3 all-gather.20
  638.4 25.3 all-gather.22
  665.4 27.0 all-gather.26
  694.6 73.3 all-gather.28
  787.7 86.3 reduce-scatter.16
  878.8 73.1 all-gather.30
  954.5 37.4 reduce-scatter.28
  994.6 36.3 reduce-scatter.26
  1033.3 36.3 reduce-scatter.24
  1378.8 19.7 reduce-scatter.30
  1404.5 122.4 all-reduce.72
  1529.4 30.4 reduce-scatter.22
  1564.0 87.8 reduce-scatter.18
  1655.4 88.8 reduce-scatter.14
  1747.0 58.0 reduce-scatter.20
where the time goes:
time: 1830 us; the launch traced here: 1820 us
  waiting for transfers between devices  846 us (46%)
  matrix products  442 us (24%)
  local copies, waits for them, and re-layouts  311 us (17%)
  other arithmetic  116 us (6%)
  blocking collectives  77.3 us (4%)
    dot_general x112, matrix products, exact_product(): return jnp.einsum(form, left, right, precision=highest)  318 us
    pad x34, local copies, waits for them, and re-layouts, head_mixer(): lax.associative_scan(compose, (transitions, injections))  194 us
    reduce_scatter x1, waiting for transfers between devices, per_device(): lax.psum_scatter((lax.dot_general(grad_projected, w_mix, contract, prefer...  89.8 us
    reduce_scatter x1, waiting for transfers between devices, per_device(): lax.psum_scatter(jnp.dot(gated_rows, out_rows, preferred_element_type=jnp...  87.6 us
    reduce_scatter x1, waiting for transfers between devices, per_device(): lax.psum_scatter((jnp.dot(grad_gate_pre, ff_gate_rows, preferred_element_...  86.5 us
    psum x1, waiting for transfers between devices, per_device(): lax.psum((taps_full, bias_full, norm_gain_part, mlp_gain_part, head_gain_...  76.4 us
    all_gather x1, waiting for transfers between devices, per_device(): mlp_all = lax.all_gather(mlp_own, 'head', axis=0, tiled=True)  76.3 us
    all_gather x1, waiting for transfers between devices, per_device(): lax.all_gather(cotangent, 'head', axis=0, tiled=True)  75.6 us
  transfers between devices with their start and end apart: 23, of which 15 were waited for; matrix products, arithmetic and copies ran while one was open for 32% of the time, Pallas kernels for 0%

commit v1 on v0

--- a/solution.py
+++ b/solution.py
@@ -1,16 +1,24 @@
+import functools
 import jax
 import jax.numpy as jnp
 from jax import lax
+from jax.experimental import pallas as pl
+from jax.experimental.pallas import tpu as pltpu
 from jax.sharding import PartitionSpec as P
 
 DK = 128
 DV = 256
 CONV = 4
-BLOCK = 64
-
-
+CHUNK = 128
+MIX = 2 * DK + DV
+PER = 2 * DK + 2 * DV
+GROUP = 4
 epsilon = 1e-06
 highest = lax.Precision.HIGHEST
+F32 = jnp.float32
+BF16 = jnp.bfloat16
+HALO = 16
+VMEM_LIMIT = 56 * 1024 * 1024
 
 
 def shifted(value, axis, steps):
@@ -63,23 +71,6 @@
     return jnp.einsum(form, left, right, precision=highest)
 
 
-def unit_lower_inverse(lower_part):
-    full_size = lower_part.shape[1]
-    identity = jnp.eye(full_size, dtype=jnp.float32)
-    result = identity - lower_part
-    power = lower_part
-    span = 2
-    while span < full_size:
-        power = exact_product("bij,bjk->bik", power, power)
-        result = exact_product("bij,bjk->bik", result, identity + power)
-        span = 2 * span
-    return result
-
-
-def unit_rows(matrix):
-    return matrix * lax.rsqrt(jnp.sum(matrix * matrix, axis=-1, keepdims=True) + epsilon)
-
-
 def compose(earlier, later):
     return (
         exact_product("hij,hjk->hik", earlier[0], later[0]),
@@ -87,56 +78,418 @@
     )
 
 
-def head_mixer(extended, rate_logits, conv_taps, biases):
-    row_count = rate_logits.shape[0]
-    mixed_rows = jax.nn.silu(
-        sum(
-            (
-                conv_taps[tap_index] * extended[tap_index : tap_index + row_count]
-                for tap_index in range(CONV)
+def mm(a, b, ca=1, cb=0):
+    return lax.dot_general(
+        a.astype(BF16), b.astype(BF16), (((ca,), (cb,)), ((), ())), preferred_element_type=F32
+    )
+
+
+def mmx(a, b, ca=1, cb=0):
+    return lax.dot_general(
+        a, b, (((ca,), (cb,)), ((), ())), preferred_element_type=F32, precision=lax.Precision.HIGHEST
+    )
+
+
+def softplus(x):
+    return jnp.maximum(x, 0.0) + jnp.log1p(jnp.exp(-jnp.abs(x)))
+
+
+def sigmoid(x):
+    return 1.0 / (1.0 + jnp.exp(-x))
+
+
+def iotas(n):
+    return (
+        lax.broadcasted_iota(jnp.int32, (n, n), 0),
+        lax.broadcasted_iota(jnp.int32, (n, n), 1),
+    )
+
+
+def inverse_parts(mats, rows, cols):
+    base = 16
+    near = (rows // base) == (cols // base)
+    diag = [jnp.where(near, a, 0.0) for a in mats]
+    result = [-d for d in diag]
+    power = [mm(d, d) for d in diag]
+    span = 2
+    while True:
+        result = [r + p + mm(r, p) for r, p in zip(result, power)]
+        span *= 2
+        if span >= base:
+            break
+        power = [mm(p, p) for p in power]
+    size = base
+    n = mats[0].shape[0]
+    while size < n:
+        cross = ((rows // (2 * size)) == (cols // (2 * size))) & ((rows // size) != (cols // size))
+        off = [jnp.where(cross, a, 0.0) for a in mats]
+        left = [o + mm(r, o) for o, r in zip(off, result)]
+        result = [r - x - mm(x, r) for r, x in zip(result, left)]
+        size *= 2
+    return result
+
+
+def conv_scratch(first, proj_ref, prev_ref, halo_ref, x_ref, heads, rows):
+    for h in range(heads):
+        cols = slice(h * PER, h * PER + MIX)
+        before = jnp.where(first, halo_ref[:, cols].astype(F32), prev_ref[:, cols].astype(F32))
+        x_ref[0:8, h * MIX : (h + 1) * MIX] = before[HALO - 8 :]
+        x_ref[8 : 8 + rows, h * MIX : (h + 1) * MIX] = proj_ref[:, cols].astype(F32)
+
+
+def conv_pre(x_ref, taps_ref, h, row):
+    cols = slice(h * MIX, (h + 1) * MIX)
+    total = None
+    for i in range(CONV):
+        part = taps_ref[i : i + 1, cols] * x_ref[pl.ds(row + 8 - (CONV - 1) + i, CHUNK), cols]
+        total = part if total is None else total + part
+    return total
+
+
+def unit(a):
+    r = lax.rsqrt(jnp.sum(a * a, axis=-1, keepdims=True) + epsilon)
+    return a * r, r
+
+
+def forward_kernel(
+    heads, group,
+    proj_ref, prev_ref, halo_ref, rates_ref, bias_ref, taps_ref,
+    olocal_ref, qmap_ref, state_ref, uw_ref, inv_ref, trans_ref, qe_ref, end_ref,
+    x_ref, carry_ref, n_ref,
+):
+    step = pl.program_id(0)
+    rows_here = CHUNK * group
+    conv_scratch(step == 0, proj_ref, prev_ref, halo_ref, x_ref, heads, rows_here)
+    ri, ci = iotas(CHUNK)
+    included = ri >= ci
+    strictly = ri > ci
+    lower = jnp.where(included, 1.0, 0.0)
+    upper = jnp.where(ri <= ci, 1.0, 0.0)
+
+    @pl.when(step == 0)
+    def _():
+        for h in range(heads):
+            carry_ref[h, :DV, :] = jnp.zeros((DV, DK), F32)
+            carry_ref[h, DV:, :] = jnp.where(ri == ci, 1.0, 0.0)
+
+    pairs = [(g, h) for g in range(group) for h in range(heads)]
+    logits = rates_ref[...] + bias_ref[...]
+    log_decay = -softplus(logits)
+    strength = sigmoid(logits)
+    cums, cum_rows = [], []
+    for g in range(group):
+        part = log_decay[g * CHUNK : (g + 1) * CHUNK]
+        cums.append(mmx(lower, part))
+        cum_rows.append(mmx(part, upper, 0, 0))
+    mats, scores, rhs, tails, scaled_q, finals = [], [], [], [], [], []
+    for g, h in pairs:
+        pre = conv_pre(x_ref, taps_ref, h, g * CHUNK)
+        mixed = pre * sigmoid(pre)
+        q = unit(mixed[:, :DK])[0] * DK ** (-0.5)
+        k = unit(mixed[:, DK : 2 * DK])[0]
+        v = mixed[:, 2 * DK :]
+        cum = cums[g][:, 2 * h : 2 * h + 1]
+        cum_row = cum_rows[g][2 * h : 2 * h + 1, :]
+        beta = strength[g * CHUNK : (g + 1) * CHUNK, 2 * h + 1 : 2 * h + 2]
+        growth = jnp.exp(cum)
+        decays = jnp.where(included, jnp.exp(jnp.where(included, cum - cum_row, 0.0)), 0.0)
+        grams = mm(jnp.concatenate([q, k], axis=0), k, 1, 1)
+        scores.append(grams[:CHUNK] * decays)
+        mats.append(jnp.where(strictly, beta * decays * grams[CHUNK:], 0.0))
+        rhs.append(jnp.concatenate([beta * v, beta * growth * k], axis=1))
+        last = cum[CHUNK - 1 : CHUNK, :]
+        tails.append(k * jnp.exp(last - cum))
+        scaled_q.append(growth * q)
+        finals.append(jnp.exp(last))
+    inverses = inverse_parts(mats, ri, ci)
+    solved = [b + mm(r, b) for r, b in zip(inverses, rhs)]
+    mixes = [mm(p, u) for p, u in zip(scores, solved)]
+    adds = [mm(u, t, 0, 0) for u, t in zip(solved, tails)]
+    for j, (g, h) in enumerate(pairs):
+        inv_ref[h, g] = inverses[j].astype(BF16)
+        uw_ref[h, g] = solved[j].astype(BF16)
+        qe_ref[h, g] = (scaled_q[j] - mixes[j][:, DV:]).astype(BF16)
+        trans_ref[h, g] = (-adds[j][DV:]).astype(BF16)
+        olocal_ref[g * CHUNK : (g + 1) * CHUNK, h * DV : (h + 1) * DV] = mixes[j][:, :DV]
+    for h in range(heads):
+        now = carry_ref[h]
+        for g in range(group):
+            j = pairs.index((g, h))
+            low = now.astype(BF16)
+            state_ref[h, g] = low
+            moved = finals[j] * now + mm(low, trans_ref[h, g])
+            now = jnp.concatenate([moved[:DV] + adds[j][:DV], moved[DV:]], axis=0)
+        carry_ref[h] = now
+        end_ref[h] = now
+    for j, (g, h) in enumerate(pairs):
+        both = mm(qe_ref[h, g], state_ref[h, g], 1, 1)
+        rows = slice(g * CHUNK, (g + 1) * CHUNK)
+        olocal_ref[rows, h * DV : (h + 1) * DV] += both[:, :DV]
+        qmap_ref[rows, h * DK : (h + 1) * DK] = both[:, DV:].astype(BF16)
+
+
+def mixer_forward(projected, halo, rates, bias_row, taps, group):
+    total = projected.shape[0]
+    heads = rates.shape[1] // 2
+    rows = CHUNK * group
+    steps = total // rows
+    chunks = total // CHUNK
+    whole = lambda i: (0, 0)
+    saved = lambda a, b: (
+        jax.ShapeDtypeStruct((heads, chunks, a, b), BF16),
+        pl.BlockSpec((heads, group, a, b), lambda i: (0, i, 0, 0)),
+    )
+    outs = [
+        (jax.ShapeDtypeStruct((total, heads * DV), F32), pl.BlockSpec((rows, heads * DV), lambda i: (i, 0))),
+        (jax.ShapeDtypeStruct((total, heads * DK), BF16), pl.BlockSpec((rows, heads * DK), lambda i: (i, 0))),
+        saved(DV + DK, DK),
+        saved(CHUNK, DV + DK),
+        saved(CHUNK, CHUNK),
+        saved(DK, DK),
+        saved(CHUNK, DK),
+        (jax.ShapeDtypeStruct((heads, DV + DK, DK), F32), pl.BlockSpec((heads, DV + DK, DK), lambda i: (0, 0, 0))),
+    ]
+    return pl.pallas_call(
+        functools.partial(forward_kernel, heads, group),
+        grid=(steps,),
+        in_specs=[
+            pl.BlockSpec((rows, heads * PER), lambda i: (i, 0)),
+            pl.BlockSpec((HALO, heads * PER), lambda i: (jnp.maximum(i * (rows // HALO) - 1, 0), 0)),
+            pl.BlockSpec((HALO, heads * PER), whole),
+            pl.BlockSpec((rows, 2 * heads), lambda i: (i, 0)),
+            pl.BlockSpec((1, 2 * heads), whole),
+            pl.BlockSpec((CONV, heads * MIX), whole),
+        ],
+        out_shape=[o[0] for o in outs],
+        out_specs=[o[1] for o in outs],
+        scratch_shapes=[
+            pltpu.VMEM((rows + 8, heads * MIX), F32),
+            pltpu.VMEM((heads, DV + DK, DK), F32),
+            pltpu.VMEM((8, 128), F32),
+        ],
+        compiler_params=pltpu.CompilerParams(vmem_limit_bytes=VMEM_LIMIT),
+        cost_estimate=pl.CostEstimate(flops=40_000_000_000, bytes_accessed=16_000_000, transcendentals=0),
+    )(projected, projected, halo, rates, bias_row, taps)
+
+
+def backward_kernel(
+    heads, group, steps,
+    proj_ref, prev_ref, halo_ref, rates_ref, bias_ref, taps_ref,
+    state_ref, uw_ref, inv_ref, trans_ref, qe_ref,
+    dout_ref, ggate_ref, incoming_ref, dend_ref,
+    gp_ref, grates_ref, gtaps_ref, gbias_ref, tail_ref, lead_ref,
+    x_ref, d_ref, carry_ref, next_ref,
+):
+    step = pl.program_id(0)
+    rows_here = CHUNK * group
+    conv_scratch(step == steps - 1, proj_ref, prev_ref, halo_ref, x_ref, heads, rows_here)
+    ri, ci = iotas(CHUNK)
+    included = ri >= ci
+    strictly = ri > ci
+    lower = jnp.where(included, 1.0, 0.0)
+    upper = jnp.where(ri <= ci, 1.0, 0.0)
+
+    @pl.when(step == 0)
+    def _():
+        for h in range(heads):
+            carry_ref[h] = dend_ref[h]
+        d_ref[rows_here : rows_here + 8, :] = jnp.zeros((8, heads * MIX), F32)
+        gtaps_ref[...] = jnp.zeros_like(gtaps_ref)
+        gbias_ref[...] = jnp.zeros_like(gbias_ref)
+
+    @pl.when(step > 0)
+    def _():
+        d_ref[rows_here : rows_here + 8, :] = d_ref[0:8, :]
+
+    pairs = [(g, h) for g in range(group) for h in range(heads)]
+    logits = rates_ref[...] + bias_ref[...]
+    log_decay = -softplus(logits)
+    strength = sigmoid(logits)
+    cums, cum_rows = [], []
+    for g in range(group):
+        part = log_decay[g * CHUNK : (g + 1) * CHUNK]
+        cums.append(mmx(lower, part))
+        cum_rows.append(mmx(part, upper, 0, 0))
+    douts, injections = [], []
+    for g, h in pairs:
+        do = dout_ref[g * CHUNK : (g + 1) * CHUNK, h * DV : (h + 1) * DV]
+        douts.append(do)
+        injections.append(mm(do, qe_ref[h, g], 0, 0))
+    for h in range(heads):
+        now = carry_ref[h]
+        for g in reversed(range(group)):
+            j = pairs.index((g, h))
+            last = cums[g][CHUNK - 1 : CHUNK, 2 * h : 2 * h + 1]
+            next_ref[h, g] = now
+            now = jnp.exp(last) * now + mm(now, trans_ref[h, g], 1, 1) + injections[j]
+        carry_ref[h] = now
+    lane = lax.broadcasted_iota(jnp.int32, (CHUNK, 2 * heads), 1)
+    row_col = lax.broadcasted_iota(jnp.int32, (CHUNK, 1), 0)
+    dcums = [jnp.zeros((CHUNK, 2 * heads), F32) for _ in range(group)]
+    dbetas = [jnp.zeros((CHUNK, 2 * heads), F32) for _ in range(group)]
+    for j, (g, h) in enumerate(pairs):
+        pre = conv_pre(x_ref, taps_ref, h, g * CHUNK)
+        sig = sigmoid(pre)
+        mixed = pre * sig
+        slope = sig * (1.0 + pre * (1.0 - sig))
+        uq, rq = unit(mixed[:, :DK])
+        q = uq * DK ** (-0.5)
+        k, rk = unit(mixed[:, DK : 2 * DK])
+        v = mixed[:, 2 * DK :]
+        cum = cums[g][:, 2 * h : 2 * h + 1]
+        cum_row = cum_rows[g][2 * h : 2 * h + 1, :]
+        beta = strength[g * CHUNK : (g + 1) * CHUNK, 2 * h + 1 : 2 * h + 2]
+        growth = jnp.exp(cum)
+        decays = jnp.where(included, jnp.exp(jnp.where(included, cum - cum_row, 0.0)), 0.0)
+        qb, kb = q.astype(BF16), k.astype(BF16)
+        grams = mm(jnp.concatenate([qb, kb], axis=0), kb, 1, 1)
+        scores = grams[:CHUNK] * decays
+        dk_gram = decays * grams[CHUNK:]
+        last = cum[CHUNK - 1 : CHUNK, :]
+        fade = jnp.exp(last - cum)
+        tail = k * fade
+        sl = state_ref[h, g]
+        state = sl[:DV].astype(F32) + mm(incoming_ref[h], sl[DV:])
+        after = next_ref[h, g]
+        afterb = after.astype(BF16)
+        stateb = state.astype(BF16)
+        uw = uw_ref[h, g]
+        errors = uw[:, :DV].astype(F32) - mm(uw[:, DV:], stateb, 1, 1)
+        eb = errors.astype(BF16)
+        do = douts[j]
+        de = mm(scores, do, 0, 0) + mm(tail, afterb, 1, 1)
+        db = de + mm(inv_ref[h, g], de, 0, 0)
+        dbb = db.astype(BF16)
+        stacked = jnp.concatenate([do, dbb], axis=0)
+        against_e = mm(stacked, eb, 1, 1)
+        against_s = mm(stacked, stateb)
+        dp = against_e[:CHUNK]
+        da = jnp.where(strictly, -against_e[CHUNK:], 0.0)
+        dos = against_s[:CHUNK]
+        dbs = against_s[CHUNK:]
+        dpd = dp * decays
+        dg = da * beta * decays
+        crossed = dp * scores + da * beta * dk_gram
+        dtail = mm(eb, afterb)
+        dq = mm(dpd, kb) + growth * dos
+        sym = dg + dg.T
+        dk = (
+            mm(jnp.concatenate([dpd.T, sym], axis=1), jnp.concatenate([qb, kb], axis=0))
+            - beta * growth * dbs
+            + fade * dtail
+        )
+        dv = beta * db
+        kdbs = jnp.sum(k * dbs, axis=1, keepdims=True)
+        dbeta = (
+            jnp.sum(db * v, axis=1, keepdims=True)
+            - growth * kdbs
+            + jnp.sum(da * dk_gram, axis=1, keepdims=True)
+        )
+        tdot = jnp.sum(tail * dtail, axis=1, keepdims=True)
+        dcum = (
+            jnp.sum(crossed - crossed.T, axis=1, keepdims=True)
+            + growth * jnp.sum(q * dos, axis=1, keepdims=True)
+            - beta * growth * kdbs
+            - tdot
+        )
+        at_end = jnp.exp(last) * jnp.sum(jnp.sum(after * state, axis=1, keepdims=True), axis=0, keepdims=True) + jnp.sum(
+            tdot, axis=0, keepdims=True
+        )
+        dcum = dcum + jnp.where(row_col == CHUNK - 1, at_end, 0.0)
+        dcums[g] = jnp.where(lane == 2 * h, dcum, dcums[g])
+        dbetas[g] = jnp.where(lane == 2 * h + 1, dbeta, dbetas[g])
+        dq = dq * DK ** (-0.5)
+        dmq = rq * (dq - uq * jnp.sum(uq * dq, axis=1, keepdims=True))
+        dmk = rk * (dk - k * jnp.sum(k * dk, axis=1, keepdims=True))
+        d_ref[g * CHUNK : (g + 1) * CHUNK, h * MIX : (h + 1) * MIX] = (
+            jnp.concatenate([dmq, dmk, dv], axis=1) * slope
+        )
+    for g in range(group):
+        rows = slice(g * CHUNK, (g + 1) * CHUNK)
+        s = strength[rows]
+        dld = mmx(upper, dcums[g])
+        drate = jnp.where(lane % 2 == 0, -sigmoid(logits[rows]) * dld, s * (1.0 - s) * dbetas[g])
+        grates_ref[rows, :] = drate
+        gbias_ref[...] += jnp.sum(drate, axis=0, keepdims=True)
+    for g, h in pairs:
+        cols = slice(h * MIX, (h + 1) * MIX)
+        row = g * CHUNK
+        dpre = d_ref[pl.ds(row, CHUNK), cols]
+        total = None
+        for i in range(CONV):
+            gtaps_ref[i : i + 1, cols] += jnp.sum(
+                dpre * x_ref[pl.ds(row + 8 - (CONV - 1) + i, CHUNK), cols], axis=0, keepdims=True
             )
-        )
-    )
-    blocks = row_count // BLOCK
-    queries = (unit_rows(mixed_rows[:, :DK]) * DK ** (-0.5)).reshape(blocks, BLOCK, DK)
-    key_rows = unit_rows(mixed_rows[:, DK : 2 * DK]).reshape(blocks, BLOCK, DK)
-    values = mixed_rows[:, 2 * DK :]
-    augmented = jnp.concatenate([values, jnp.zeros((row_count, DK), jnp.float32)], axis=1).reshape(
-        blocks, BLOCK, DV + DK
-    )
-    log_decay = -jax.nn.softplus(rate_logits[:, 0] + biases[0])
-    strength = jax.nn.sigmoid(rate_logits[:, 1] + biases[1]).reshape(blocks, BLOCK)
-    cumulative = jnp.cumsum(log_decay.reshape(blocks, BLOCK), axis=1)
-    final_decay = cumulative[:, -1]
-    positions = jnp.arange(BLOCK)
-    included = positions[:, None] >= positions[None, :]
-    strictly = positions[:, None] > positions[None, :]
-    difference = cumulative[:, :, None] - cumulative[:, None, :]
-    decays = jnp.where(included, jnp.exp(jnp.where(included, difference, 0.0)), 0.0)
-    key_gram = exact_product("cik,cjk->cij", key_rows, key_rows)
-    lower_part = jnp.where(strictly, strength[:, :, None] * decays * key_gram, 0.0)
-    inverse = unit_lower_inverse(lower_part)
-    updates = exact_product("cij,cjw->ciw", inverse, strength[:, :, None] * augmented)
-    weighted = exact_product(
-        "cij,cjw->ciw", inverse, (strength * jnp.exp(cumulative))[:, :, None] * key_rows
-    )
-    key_tails = key_rows * jnp.exp(final_decay[:, None] - cumulative)[:, :, None]
-    transitions = jnp.exp(final_decay)[:, None, None] * jnp.eye(
-        DK, dtype=jnp.float32
-    ) - exact_product("cti,ctj->cij", weighted, key_tails)
-    injections = exact_product("ctv,ctk->cvk", updates, key_tails)
-    prefix_maps, prefix_adds = lax.associative_scan(compose, (transitions, injections))
-    start_state = jnp.concatenate(
-        [jnp.zeros((DV, DK), jnp.float32), jnp.eye(DK, dtype=jnp.float32)], axis=0
-    )
-    end_states = exact_product("vj,cjk->cvk", start_state, prefix_maps) + prefix_adds
-    starts = jnp.concatenate([start_state[None], end_states[:-1]], axis=0)
-    errors = updates - exact_product("ctk,cvk->ctv", weighted, starts)
-    scores = exact_product("cik,cjk->cij", queries, key_rows) * decays
-    outputs = exact_product(
-        "ctk,cvk->ctv", queries * jnp.exp(cumulative)[:, :, None], starts
-    ) + exact_product("cij,cjv->civ", scores, errors)
-    return (outputs.reshape(row_count, DV + DK), end_states[-1])
+            part = taps_ref[i : i + 1, cols] * d_ref[pl.ds(row + CONV - 1 - i, CHUNK), cols]
+            total = part if total is None else total + part
+        gp_ref[row : row + CHUNK, h * PER : h * PER + MIX] = total.astype(BF16)
+        gp_ref[row : row + CHUNK, h * PER + MIX : (h + 1) * PER] = ggate_ref[
+            row : row + CHUNK, h * DV : (h + 1) * DV
+        ]
+        if g == group - 1:
+            @pl.when(step == 0)
+            def _(total=total, cols=cols):
+                tail_ref[:, cols] = total[CHUNK - HALO :]
+
+    @pl.when(step == steps - 1)
+    def _():
+        lead_ref[...] = d_ref[0:8, :]
+
+
+def mixer_backward(projected, halo, rates, bias_row, taps, saved, dout, ggate, incoming, dend, group):
+    state, uw, inv, trans, qe = saved
+    total = projected.shape[0]
+    heads = rates.shape[1] // 2
+    rows = CHUNK * group
+    steps = total // rows
+    whole = lambda i: (0, 0)
+    flip = lambda i: (steps - 1 - i, 0)
+    keep = lambda a, b: pl.BlockSpec((heads, group, a, b), lambda i: (0, steps - 1 - i, 0, 0))
+    return pl.pallas_call(
+        functools.partial(backward_kernel, heads, group, steps),
+        grid=(steps,),
+        in_specs=[
+            pl.BlockSpec((rows, heads * PER), flip),
+            pl.BlockSpec((HALO, heads * PER), lambda i: (jnp.maximum((steps - 1 - i) * (rows // HALO) - 1, 0), 0)),
+            pl.BlockSpec((HALO, heads * PER), whole),
+            pl.BlockSpec((rows, 2 * heads), flip),
+            pl.BlockSpec((1, 2 * heads), whole),
+            pl.BlockSpec((CONV, heads * MIX), whole),
+            keep(DV + DK, DK),
+            keep(CHUNK, DV + DK),
+            keep(CHUNK, CHUNK),
+            keep(DK, DK),
+            keep(CHUNK, DK),
+            pl.BlockSpec((rows, heads * DV), flip),
+            pl.BlockSpec((rows, heads * DV), flip),
+            pl.BlockSpec((heads, DV, DK), lambda i: (0, 0, 0)),
+            pl.BlockSpec((heads, DV, DK), lambda i: (0, 0, 0)),
+        ],
+        out_shape=[
+            jax.ShapeDtypeStruct((total, heads * PER), BF16),
+            jax.ShapeDtypeStruct((total, 2 * heads), F32),
+            jax.ShapeDtypeStruct((CONV, heads * MIX), F32),
+            jax.ShapeDtypeStruct((1, 2 * heads), F32),
+            jax.ShapeDtypeStruct((HALO, heads * MIX), F32),
+            jax.ShapeDtypeStruct((8, heads * MIX), F32),
+        ],
+        out_specs=[
+            pl.BlockSpec((rows, heads * PER), flip),
+            pl.BlockSpec((rows, 2 * heads), flip),
+            pl.BlockSpec((CONV, heads * MIX), whole),
+            pl.BlockSpec((1, 2 * heads), whole),
+            pl.BlockSpec((HALO, heads * MIX), whole),
+            pl.BlockSpec((8, heads * MIX), whole),
+        ],
+        scratch_shapes=[
+            pltpu.VMEM((rows + 8, heads * MIX), F32),
+            pltpu.VMEM((rows + 8, heads * MIX), F32),
+            pltpu.VMEM((heads, DV, DK), F32),
+            pltpu.VMEM((heads, group, DV, DK), F32),
+        ],
+        compiler_params=pltpu.CompilerParams(vmem_limit_bytes=VMEM_LIMIT),
+        cost_estimate=pl.CostEstimate(flops=60_000_000_000, bytes_accessed=20_000_000, transcendentals=0),
+    )(projected, projected, halo, rates, bias_row, taps, state, uw, inv, trans, qe, dout, ggate, incoming, dend)
 
 
 def per_device(
@@ -190,14 +543,14 @@
     rate_logits = jnp.dot(block_rows, w_rate, preferred_element_type=jnp.float32).reshape(
         seq_rows, heads_here, 2
     )
-    mixer_in = projected[:, :, :mixed_width]
-    halo_rows = shifted(mixer_in[seq_rows - (CONV - 1) :], "seq", 1)
-    extended = jnp.concatenate([halo_rows, mixer_in], axis=0).astype(jnp.float32)
-    conv_taps = conv_weight.reshape(CONV, heads_here, mixed_width)
-    mixer_all = jax.vmap(head_mixer, in_axes=(1, 1, 1, 1), out_axes=(1, 0))
-    (outputs, end_state), mixer_pull = jax.vjp(
-        mixer_all, extended, rate_logits, conv_taps, head_bias
-    )
+    flat_projected = projected.reshape(seq_rows, heads_here * per_head)
+    flat_rates = rate_logits.reshape(seq_rows, heads_here * 2)
+    bias_row = head_bias.T.reshape(1, 2 * heads_here)
+    halo_rows = shifted(flat_projected[seq_rows - HALO :], "seq", 1)
+    out_local, query_map, *saved, end_state = mixer_forward(
+        flat_projected, halo_rows, flat_rates, bias_row, conv_weight, GROUP
+    )
+    query_map = query_map.reshape(seq_rows, heads_here, DK)
     transfer = end_state[:, DV:, :]
     injected = end_state[:, :DV, :]
     identity = (
@@ -205,7 +558,9 @@
         jnp.zeros_like(injected),
     )
     prefix_map, incoming = entering((transfer, injected), "seq", compose, identity)
-    attended = outputs[:, :, :DV] + exact_product("thk,hvk->thv", outputs[:, :, DV:], incoming)
+    attended = out_local.reshape(seq_rows, heads_here, DV) + jnp.einsum(
+        "thk,hvk->thv", query_map, incoming.astype(BF16), preferred_element_type=F32
+    )
     mixer_val = lax.optimization_barrier(attended.astype(jnp.bfloat16)).astype(jnp.float32)
     gate_val = projected[:, :, mixed_width:].astype(jnp.float32)
     head_inverse = lax.rsqrt(jnp.mean(mixer_val * mixer_val, axis=-1, keepdims=True) + epsilon)
@@ -288,29 +643,35 @@
         head_inverse
         * (scaled_head - head_normed * jnp.mean(scaled_head * head_normed, axis=-1, keepdims=True))
     ).astype(jnp.bfloat16)
-    grad_attended = grad_mixer.astype(jnp.float32)
-    local_grad = exact_product("thv,thk->hvk", grad_attended, outputs[:, :, DV:])
+    local_grad = jnp.einsum("thv,thk->hvk", grad_mixer, query_map, preferred_element_type=F32)
     transposed = jnp.swapaxes(transfer, 1, 2)
     suffix_map, grad_end = prefix((transposed, local_grad), "seq", compose, identity)
-    grad_outputs = jnp.concatenate(
-        [grad_attended, exact_product("thv,hvk->thk", grad_attended, incoming)], axis=2
-    )
-    grad_final = jnp.concatenate(
-        [grad_end, exact_product("hvk,hvj->hkj", incoming, grad_end)], axis=1
-    )
-    grad_extended, grad_rates, grad_taps, grad_biases = mixer_pull((grad_outputs, grad_final))
-    halo_grad = shifted(grad_extended[: CONV - 1], "seq", -1)
-    grad_mixed = grad_extended[CONV - 1 :]
-    grad_mixed = jnp.concatenate(
-        [grad_mixed[: seq_rows - (CONV - 1)], grad_mixed[seq_rows - (CONV - 1) :] + halo_grad],
-        axis=0,
-    )
-    grad_projected = (
-        jnp.concatenate([grad_mixed, grad_gate_mix.astype(jnp.float32)], axis=2)
-        .astype(jnp.bfloat16)
-        .reshape(seq_rows, heads_here * per_head)
-    )
-    grad_rate_low = grad_rates.reshape(seq_rows, heads_here * 2).astype(jnp.bfloat16)
+    grad_projected, grad_rates, grad_taps, grad_bias_row, tail_rows, lead_rows = mixer_backward(
+        flat_projected,
+        halo_rows,
+        flat_rates,
+        bias_row,
+        conv_weight,
+        saved,
+        grad_mixer.reshape(seq_rows, heads_here * DV),
+        grad_gate_mix.reshape(seq_rows, heads_here * DV),
+        incoming,
+        grad_end,
+        GROUP,
+    )
+    grad_biases = grad_bias_row.reshape(heads_here, 2).T
+    later_rows = shifted(lead_rows, "seq", -1)
+    padded = jnp.concatenate([jnp.zeros((HALO, heads_here * mixed_width), F32), later_rows])
+    last_rows = tail_rows + sum(
+        conv_weight[i] * padded[CONV - 1 - i : CONV - 1 - i + HALO] for i in range(CONV)
+    )
+    for h in range(heads_here):
+        grad_projected = lax.dynamic_update_slice(
+            grad_projected,
+            last_rows[:, h * mixed_width : (h + 1) * mixed_width].astype(BF16),
+            (seq_rows - HALO, h * per_head),
+        )
+    grad_rate_low = grad_rates.astype(jnp.bfloat16)
     grad_w_mix = lax.dot_general(
         block_rows, grad_projected, rows_first, preferred_element_type=jnp.float32
     )

time: 1830 us -> 1290 us (0.70)
  matrix products: 442 us -> 134 us
  local copies, waits for them, and re-layouts: 311 us -> 32 us
  waiting for transfers between devices: 846 us -> 949 us
  other arithmetic: 116 us -> 36 us
  Pallas kernels: 0 us -> 45.3 us
    dot_general x112 -> x7, matrix products: 318 us -> 2.71 us  [exact_product(): return jnp.einsum(form, left, right, precision=highest)]
    pad x34 -> x0, local copies, waits for them, and re-layouts: 194 us -> none  [head_mixer(): lax.associative_scan(compose, (transitions, injections))]
    psum x1, waiting for transfers between devices: 76.4 us -> 127 us  [per_device(): lax.psum((taps_full, bias_full, norm_gain_part, mlp_gain_part, head_gain_...]
    pallas_call x0 -> x2, Pallas kernels: none -> 45.3 us  [the longest x1 30.8 us: mixer_backward(): pl.pallas_call(functools.partial(backward_kernel, heads, group, steps), g...]
    unnamed x457 -> x78, local copies, waits for them, and re-layouts: 44.4 us -> 7.31 us
    add_any x19 -> x0, other arithmetic: 29.8 us -> none  [the longest x11 20.6 us: head_mixer(): lax.associative_scan(compose, (transitions, injections))]
    unnamed x22, waiting for transfers between devices: 4.57 us -> 25.5 us
    slice x28 -> x1, local copies, waits for them, and re-layouts: 19.4 us -> 0.01 us  [per_device(): halo_rows = shifted(flat_projected[seq_rows - HALO:], 'seq', 1)]
  transfers between devices with their start and end apart: 23 -> 23, of which waited for: 15 -> 20; matrix products, arithmetic and copies ran while one was open for 32% -> 11% of each run, Pallas kernels for 0% -> 2%
where the time goes in v1:
time: 1290 us
  waiting for transfers between devices  949 us (74%)
  matrix products  134 us (10%)
  blocking collectives  74.8 us (6%)
  Pallas kernels  45.3 us (4%)
  other arithmetic  36 us (3%)
  local copies, waits for them, and re-layouts  32 us (2%)
  between operations  15.2 us (1%)
    psum x1, waiting for transfers between devices, per_device(): lax.psum((taps_full, bias_full, norm_gain_part, mlp_gain_part, head_gain_...  127 us
    reduce_scatter x1, waiting for transfers between devices, per_device(): lax.psum_scatter((lax.dot_general(grad_projected, w_mix, contract, prefer...  89.8 us
    reduce_scatter x1, waiting for transfers between devices, per_device(): lax.psum_scatter(jnp.dot(gated_rows, out_rows, preferred_element_type=jnp...  87.6 us
    reduce_scatter x1, waiting for transfers between devices, per_device(): lax.psum_scatter((jnp.dot(grad_gate_pre, ff_gate_rows, preferred_element_...  86.4 us
    all_gather x1, waiting for transfers between devices, per_device(): mlp_all = lax.all_gather(mlp_own, 'head', axis=0, tiled=True)  76.3 us
    all_gather x1, waiting for transfers between devices, per_device(): lax.all_gather(cotangent, 'head', axis=0, tiled=True)  75.6 us
    all_gather x1, waiting for transfers between devices, per_device(): lax.all_gather(tokens, 'head', axis=0, tiled=True)  69.8 us
    reduce_scatter x1, waiting for transfers between devices, per_device(): lax.psum_scatter(grad_w_mix.astype(jnp.bfloat16), 'seq', scatter_dimensio...  57.7 us
  transfers between devices with their start and end apart: 23, of which 20 were waited for; matrix products, arithmetic and copies ran while one was open for 11% of the time, Pallas kernels for 2%

profile of v1, /device:TPU:0, one launch (start us, length us, event | category | flops | bytes accessed | tf_op | source)
XLA Modules:
  0.0 1290.9 jit_solution(12902938740527779236)
XLA Ops:
  10.1 6.3 all_gather.56
  16.4 69.8 %all-gather.15.cloned.1.call-done = bf16[1024,2048]{1,0:T(8,128)(2,1)} async-done(((bf16[128,2048]{1,0:T(8,128)(2,1)}), bf16[1024,2048]{1,0:T(8,128)(2,1)}) %all-gather.15.cloned.1.call-update) | async-done | bytes 4194320 | tf_op jit(solution)/shard_map/all_gather | solution.py:520
  86.3 3.1 fusion.13
  89.4 43.1 %all-gather.17.cloned.1.call-done = bf16[2048,1536]{1,0:T(8,128)(2,1)} async-done(((bf16[512,1536]{1,0:T(8,128)(2,1)}), bf16[2048,1536]{1,0:T(8,128)(2,1)}) %all-gather.17.cloned.1.call-update) | async-done | bytes 6291472 | tf_op jit(solution)/shard_map/all_gather | solution.py:531
  132.5 10.7 convolution_convert_fusion.1.proj_ref.prev_ref
  148.2 14.4 %shard_map.228 = (f32[1024,512]{1,0:T(8,128)}, bf16[1024,256]{1,0:T(8,128)(2,1)}, bf16[2,8,384,128]{3,2,1,0:T(8,128)(2,1)}, bf16[2,8,128,384]{3,2,1,0:T(8,128)(2...) custom-call(bf16[1024,1536]{1,0:T(8,128)(2,1)} %copy-done.9, ...), custom_call_target="tpu_custom_call" | custom-call | flops 40000000000 | bytes 16000000 | tf_op jit(solution)/shard_map/pallas_call | solution.py:252
  164.9 4.7 copy.69
  169.7 2.9 copy.68
  172.6 10.5 all-gather
  185.1 6.4 while.29
  196.2 12.9 %all-gather.19.cloned.1.call-done = bf16[512,2048]{1,0:T(8,128)(2,1)} async-done(((bf16[512,512]{1,0:T(8,128)(2,1)}), bf16[512,2048]{1,0:T(8,128)(2,1)}) %all-gather.19.cloned.1.call-update) | async-done | bytes 2097168 | tf_op jit(solution)/shard_map/all_gather | solution.py:533
  209.1 6.0 convolution_convert_fusion.3
  215.8 87.6 %reduce-scatter.13.cloned.1.call-done = bf16[128,2048]{1,0:T(8,128)(2,1)} async-done(((bf16[1024,2048]{1,0:T(8,128)(2,1)}), bf16[128,2048]{1,0:T(8,128)(2,1)}) %reduce-scatter.13.cloned.1.call-update) | async-done | bytes 524304 | tf_op jit(solution)/shard_map/reduce_scatter | solution.py:575
  308.9 22.8 %all-gather.25.cloned.1.call-done = bf16[704,2048]{1,0:T(8,128)(2,1)} async-done(((bf16[704,512]{1,0:T(8,128)(2,1)}), bf16[704,2048]{1,0:T(8,128)(2,1)}) %all-gather.25.cloned.1.call-update) | async-done | bytes 2883600 | tf_op jit(solution)/shard_map/all_gather | solution.py:535
  331.7 76.3 %all-gather.21.cloned.1.call-done = bf16[1024,2048]{1,0:T(8,128)(2,1)} async-done(((bf16[128,2048]{1,0:T(8,128)(2,1)}), bf16[1024,2048]{1,0:T(8,128)(2,1)}) %all-gather.21.cloned.1.call-update) | async-done | bytes 4194320 | tf_op jit(solution)/shard_map/all_gather | solution.py:583
  408.1 7.9 fusion.82
  416.0 19.1 %all-gather.23.cloned.1.call-done = bf16[704,2048]{1,0:T(8,128)(2,1)} async-done(((bf16[704,512]{1,0:T(8,128)(2,1)}), bf16[704,2048]{1,0:T(8,128)(2,1)}) %all-gather.23.cloned.1.call-update) | async-done | bytes 2883600 | tf_op jit(solution)/shard_map/all_gather | solution.py:534
  435.1 7.8 fusion.81
  442.9 20.9 %all-gather.27.cloned.1.call-done = bf16[704,2048]{1,0:T(8,128)(2,1)} async-done(((bf16[704,512]{1,0:T(8,128)(2,1)}), bf16[704,2048]{1,0:T(8,128)(2,1)}) %all-gather.27.cloned.1.call-update) | async-done | bytes 2883600 | tf_op jit(solution)/shard_map/all_gather | solution.py:536
  463.8 75.6 %all-gather.29.cloned.1.call-done = bf16[1024,2048]{1,0:T(8,128)(2,1)} async-done(((bf16[128,2048]{1,0:T(8,128)(2,1)}), bf16[1024,2048]{1,0:T(8,128)(2,1)}) %all-gather.29.cloned.1.call-update) | async-done | bytes 4194320 | tf_op jit(solution)/shard_map/all_gather | solution.py:521
  539.4 10.0 multiply_convert_fusion
  549.5 3.5 fusion.83
  553.1 17.1 %add_convert_fusion.1 = bf16[1024,2048]{1,0:T(8,128)(2,1)} fusion(f32[1024,2048]{1,0:T(8,128)S(1)} %fusion.83, bf16[1024,704]{0,1:T(8,128)(2,1)S(1)} %get-tuple-element.292, bf16[704,2048]{1,0:T(8,128)(2,1)S(1)} %copy-done.29), kind=kOutput, calls=%fused_computation.23 | convolution fusion | flops 2956984320 | bytes 16908288 | tf_op jit(solution)/shard_map/dot_general | solution.py:618
  570.2 86.4 %reduce-scatter.17.cloned.1.call-done = bf16[128,2048]{1,0:T(8,128)(2,1)} async-done(((bf16[1024,2048]{1,0:T(8,128)(2,1)}), bf16[128,2048]{1,0:T(8,128)(2,1)}) %reduce-scatter.17.cloned.1.call-update) | async-done | bytes 524304 | tf_op jit(solution)/shard_map/reduce_scatter | solution.py:615
  660.6 7.3 convolution_convert_fusion.4
  668.0 7.6 convolution_convert_fusion.5
  675.8 5.8 all-gather.2
  682.5 7.4 convolution_convert_fusion.6
  690.0 43.9 %all-gather.31.cloned.1.call-done = bf16[1024,2048]{1,0:T(8,128)(2,1)} async-done(((bf16[128,2048]{1,0:T(8,128)(2,1)}), bf16[1024,2048]{1,0:T(8,128)(2,1)}) %all-gather.31.cloned.1.call-update) | async-done | bytes 4194320 | tf_op jit(solution)/shard_map/all_gather | solution.py:630
  733.9 5.4 fusion.84
  740.8 2.5 fusion.30
  749.2 9.0 all-gather.3
  760.7 30.8 %shard_map.229 = (bf16[1024,1536]{1,0:T(8,128)(2,1)}, f32[1024,4]{1,0:T(8,128)}, f32[4,1024]{1,0:T(4,128)}, f32[1,4]{1,0:T(1,128)}, f32[16,1024]{1,0:T(8,128)}, /*index=5*/f32[8,1024]{1,0:T(8,128)}) custom-call(bf16[1024,1536]{1,0:T(8,128)(2,1)} %copy-done.9, bf16[1024,1536]{1,0:T(8,128)(2,1)} %copy-done.9, bf16[16,1536]{1,0:T(8,128)(2,1)} %copy-done.31, ...), custom_call_target="tpu_custom_call" | custom-call | flops 60000002048 | bytes 20000000 | tf_op jit(solution)/shard_map/pallas_call | solution.py:448
  795.8 6.2 convolution_convert_fusion.7
  807.4 8.3 add_convert_fusion
  815.7 7.7 convolution_convert_fusion.2
  823.5 11.8 convolution_convert_fusion
  835.3 2.4 convert_element_type.182
  840.2 8.9 reduce-scatter.25.cloned.1.call-done
  852.9 20.9 %reduce-scatter.31.cloned.1.call-done = bf16[512,4]{1,0:T(8,128)(2,1)} async-done(((bf16[2048,4]{1,0:T(8,128)(2,1)}), bf16[512,4]{1,0:T(8,128)(2,1)}) %reduce-scatter.31.cloned.1.call-update) | async-done | bytes 4112
  875.4 126.8 %all-reduce.4.cloned.1.call-done = f32[4,8,1024]{2,0,1:T(4,128)} async-done(((f32[4,8,1024]{2,0,1:T(4,128)}), f32[4,8,1024]{2,0,1:T(4,128)}) %all-reduce.4.cloned.1.call-update) | async-done | bytes 131088 | tf_op jit(solution)/shard_map/psum | solution.py:724
  1003.6 31.6 %reduce-scatter.23.cloned.1.call-done = bf16[512,512]{1,0:T(8,128)(2,1)} async-done(((bf16[512,2048]{1,0:T(8,128)(2,1)}), bf16[512,512]{1,0:T(8,128)(2,1)}) %reduce-scatter.23.cloned.1.call-update) | async-done | bytes 524304 | tf_op jit(solution)/shard_map/reduce_scatter | solution.py:688
  1037.3 89.8 %reduce-scatter.19.cloned.1.call-done = bf16[128,2048]{1,0:T(8,128)(2,1)} async-done(((bf16[1024,2048]{1,0:T(8,128)(2,1)}), bf16[128,2048]{1,0:T(8,128)(2,1)}) %reduce-scatter.19.cloned.1.call-update) | async-done | bytes 524304 | tf_op jit(solution)/shard_map/reduce_scatter | solution.py:701
  1128.6 43.0 %all-reduce.1 = (f32[2,8,2]{2,0,1:T(2,128)S(1)}, f32[2048]{0:T(1024)}, f32[256]{0:T(256)}, f32[2048]{0:T(1024)}) all-reduce(f32[2,8,2]{2,0,1:T(2,128)S(1)} %constant_dynamic-update-slice_fusion, f32[2048]{0:T(1024)S(1)} %get-tuple-element.263, f32[256]{0:T(256)S(1)} %get-tuple-element.259, ...), channel_id=1, replica_groups=mesh['seq'=4,'head'=8] {'seq','head'}, use_global_device_ids=true, to_apply=%region_18.19 | all-reduce | flops 4384 | bytes 35072 | tf_op jit(solution)/shard_map/psum | solution.py:724
  1172.2 47.3 %reduce-scatter.15.cloned.1.call-done = bf16[128,2048]{1,0:T(8,128)(2,1)} async-done(((bf16[1024,2048]{1,0:T(8,128)(2,1)}), bf16[128,2048]{1,0:T(8,128)(2,1)}) %reduce-scatter.15.cloned.1.call-update) | async-done | bytes 524304 | tf_op jit(solution)/shard_map/reduce_scatter | solution.py:593
  1219.5 3.2 fusion.46
  1222.7 57.7 %reduce-scatter.21.cloned.1.call-done = bf16[512,1536]{1,0:T(8,128)(2,1)} async-done(((bf16[2048,1536]{1,0:T(8,128)(2,1)}), bf16[512,1536]{1,0:T(8,128)(2,1)}) %reduce-scatter.21.cloned.1.call-update) | async-done | bytes 1572880 | tf_op jit(solution)/shard_map/reduce_scatter | solution.py:682
  1280.4 3.5 convert_element_type.172
  (209 shorter events, 68.2 us)
Async XLA Ops:
  7.2 79.1 %all-gather.15.cloned.1.call-start = ((), (), s32[]{:S(2)}) async-start(), calls=%async_computation.10 | async-start | bytes 4718592 | tf_op jit(solution)/shard_map/all_gather | solution.py:520
  7.9 124.6 %copy-start.20 = (f32[2048]{0:T(1024)S(1)}, f32[2048]{0:T(1024)}, u32[]{:S(2)}) copy-start(f32[2048]{0:T(1024)} %param.22) | copy-start | bytes 24580
  7.9 124.6 %all-gather.17.cloned.1.call-start = ((), (), s32[]{:S(2)}) async-start(), calls=%async_computation.11 | async-start | bytes 7864320 | tf_op jit(solution)/shard_map/all_gather | solution.py:531
  8.7 176.4 %all-gather.33.cloned.1.call-start = ((), (), s32[]{:S(2)}) async-start(), calls=%async_computation.29 | async-start | bytes 1310720 | tf_op jit(solution)/shard_map/all_gather | solution.py:32
  16.4 129.0 %copy-start.17 = (bf16[2048,4]{0,1:T(4,128)(2,1)}, bf16[2048,4]{0,1:T(4,128)(2,1)S(1)}, u32[]{:S(2)}) copy-start(bf16[2048,4]{0,1:T(4,128)(2,1)S(1)} %all_gather.56) | copy-start | bytes 49156
  89.3 56.0 %copy-start.25 = (f32[1024]{0:T(1024)}, f32[1024]{0:T(1024)S(1)}, u32[]{:S(2)}) copy-start(f32[1024]{0:T(1024)S(1)} %add_rsqrt_fusion.1) | copy-start | bytes 12292
  132.5 12.9 copy-start.6
  143.2 4.3 copy-start.9
  143.2 4.3 collective-permute-start
  164.3 44.8 %all-gather.19.cloned.1.call-start = ((), (), s32[]{:S(2)}) async-start(), calls=%async_computation.12 | async-start | bytes 2621440 | tf_op jit(solution)/shard_map/all_gather | solution.py:533
  164.9 138.5 %reduce-scatter.13.cloned.1.call-start = ((), (), s32[]{:S(2)}) async-start(), calls=%async_computation.13 | async-start | bytes 4718592 | tf_op jit(solution)/shard_map/reduce_scatter | solution.py:575
  164.9 4.7 copy-start.12
  185.1 6.4 copy-start.14
  196.2 12.9 %copy-start.11 = (bf16[1024,2,256]{0,2,1:T(8,128)(2,1)}, bf16[1024,2,256]{0,2,1:T(8,128)(2,1)S(1)}, u32[]{:S(2)}) copy-start(bf16[1024,2,256]{0,2,1:T(8,128)(2,1)S(1)} %fusion.23) | copy-start | bytes 3145732
  215.1 88.2 %copy-start = (bf16[128,2048]{1,0:T(8,128)(2,1)S(1)}, bf16[128,2048]{1,0:T(8,128)(2,1)}, u32[]{:S(2)}) copy-start(bf16[128,2048]{1,0:T(8,128)(2,1)} %param.17) | copy-start | bytes 1572868
  215.1 89.6 %copy-start.16 = (f32[2048]{0:T(1024)S(1)}, f32[2048]{0:T(1024)}, u32[]{:S(2)}) copy-start(f32[2048]{0:T(1024)} %param.24) | copy-start | bytes 24580
  215.2 116.6 %all-gather.25.cloned.1.call-start = ((), (), s32[]{:S(2)}) async-start(), calls=%async_computation.16 | async-start | bytes 3604480 | tf_op jit(solution)/shard_map/all_gather | solution.py:535
  215.8 192.3 %all-gather.21.cloned.1.call-start = ((), (), s32[]{:S(2)}) async-start(), calls=%async_computation.14 | async-start | bytes 4718592 | tf_op jit(solution)/shard_map/all_gather | solution.py:583
  306.8 128.3 %all-gather.23.cloned.1.call-start = ((), (), s32[]{:S(2)}) async-start(), calls=%async_computation.15 | async-start | bytes 3604480 | tf_op jit(solution)/shard_map/all_gather | solution.py:534
  307.5 156.3 %all-gather.27.cloned.1.call-start = ((), (), s32[]{:S(2)}) async-start(), calls=%async_computation.17 | async-start | bytes 3604480 | tf_op jit(solution)/shard_map/all_gather | solution.py:536
  308.3 231.2 %all-gather.29.cloned.1.call-start = ((), (), s32[]{:S(2)}) async-start(), calls=%async_computation.19 | async-start | bytes 4718592 | tf_op jit(solution)/shard_map/all_gather | solution.py:521
  308.8 347.8 %reduce-scatter.17.cloned.1.call-start = ((), (), s32[]{:S(2)}) async-start(), calls=%async_computation.20 | async-start | bytes 4718592 | tf_op jit(solution)/shard_map/reduce_scatter | solution.py:615
  539.4 10.1 copy-start.30
  570.2 86.5 %copy-start.1 = (bf16[128,2048]{1,0:T(8,128)(2,1)S(1)}, bf16[128,2048]{1,0:T(8,128)(2,1)}, u32[]{:S(2)}) copy-start(bf16[128,2048]{1,0:T(8,128)(2,1)} %reduce-scatter.13.cloned.1.call-done) | copy-start | bytes 1572868
  570.2 88.1 %copy-start.5 = (bf16[128,2048]{1,0:T(8,128)(2,1)S(1)}, bf16[128,2048]{1,0:T(8,128)(2,1)}, u32[]{:S(2)}) copy-start(bf16[128,2048]{1,0:T(8,128)(2,1)} %param.29) | copy-start | bytes 1572868
  570.2 163.7 %all-gather.31.cloned.1.call-start = ((), (), s32[]{:S(2)}) async-start(), calls=%async_computation.21 | async-start | bytes 4718592 | tf_op jit(solution)/shard_map/all_gather | solution.py:630
  660.6 174.8 %reduce-scatter.29.cloned.1.call-start = ((), (), s32[]{:S(2)}) async-start(), calls=%async_computation.28 | async-start | bytes 3604480 | tf_op jit(solution)/shard_map/reduce_scatter | solution.py:697
  667.9 169.8 %reduce-scatter.27.cloned.1.call-start = ((), (), s32[]{:S(2)}) async-start(), calls=%async_computation.27 | async-start | bytes 3604480 | tf_op jit(solution)/shard_map/reduce_scatter | solution.py:694
  675.6 173.5 %reduce-scatter.25.cloned.1.call-start = ((), (), s32[]{:S(2)}) async-start(), calls=%async_computation.26 | async-start | bytes 3604480 | tf_op jit(solution)/shard_map/reduce_scatter | solution.py:691
  689.9 183.9 %reduce-scatter.31.cloned.1.call-start = ((), (), s32[]{:S(2)}) async-start(), calls=%async_computation.30 | async-start | bytes 655360
  733.9 5.4 copy-start.2
  760.7 30.8 %copy-start.7 = (bf16[1024,2048]{1,0:T(8,128)(2,1)S(1)}, bf16[1024,2048]{1,0:T(8,128)(2,1)}, u32[]{:S(2)}) copy-start(bf16[1024,2048]{1,0:T(8,128)(2,1)} %all-gather.15.cloned.1.call-done) | copy-start | bytes 12582916
  760.7 30.9 %copy-start.21 = (f32[2048]{0:T(1024)S(1)}, f32[2048]{0:T(1024)}, u32[]{:S(2)}) copy-start(f32[2048]{0:T(1024)} %param.22) | copy-start | bytes 24580
  760.7 30.9 %copy-start.26 = (f32[1024]{0:T(1024)S(1)}, f32[1024]{0:T(1024)}, u32[]{:S(2)}) copy-start(f32[1024]{0:T(1024)} %copy-done.25) | copy-start | bytes 12292
  794.9 207.4 %all-reduce.4.cloned.1.call-start = ((), (), s32[]{:S(2)}) async-start(), calls=%async_computation.24 | async-start | bytes 262144 | tf_op jit(solution)/shard_map/psum | solution.py:724
  795.7 6.4 copy-start.22
  795.7 6.4 copy-start.32
  795.7 8.0 copy-start.10
  795.7 8.0 copy-start.18
  795.7 239.4 %reduce-scatter.23.cloned.1.call-start = ((), (), s32[]{:S(2)}) async-start(), calls=%async_computation.25 | async-start | bytes 2621440 | tf_op jit(solution)/shard_map/reduce_scatter | solution.py:688
  802.0 325.2 %reduce-scatter.19.cloned.1.call-start = ((), (), s32[]{:S(2)}) async-start(), calls=%async_computation.22 | async-start | bytes 4718592 | tf_op jit(solution)/shard_map/reduce_scatter | solution.py:701
  802.1 5.3 slice-start
  802.1 5.2 slice-start.1
  802.1 3.5 collective-permute-start.1
  815.7 403.9 %reduce-scatter.15.cloned.1.call-start = ((), (), s32[]{:S(2)}) async-start(), calls=%async_computation.18 | async-start | bytes 4718592 | tf_op jit(solution)/shard_map/reduce_scatter | solution.py:593
  823.4 456.9 %reduce-scatter.21.cloned.1.call-start = ((), (), s32[]{:S(2)}) async-start(), calls=%async_computation.23 | async-start | bytes 7864320 | tf_op jit(solution)/shard_map/reduce_scatter | solution.py:682
  835.3 16.7 %copy-start.33 = (f32[1,4]{1,0:T(1,128)S(1)}, f32[1,4]{1,0:T(1,128)}, u32[]{:S(2)}) copy-start(f32[1,4]{1,0:T(1,128)} %get-tuple-element.220) | copy-start | bytes 52
  840.2 379.4 %copy-start.4 = (bf16[128,2048]{1,0:T(8,128)(2,1)S(1)}, bf16[128,2048]{1,0:T(8,128)(2,1)}, u32[]{:S(2)}) copy-start(bf16[128,2048]{1,0:T(8,128)(2,1)} %reduce-scatter.17.cloned.1.call-done) | copy-start | bytes 1572868
  (13 other events, 31.1 us)
Sparse Core Ops, SparseCore 0:
  10.1 76.0 all-gather.14
  87.8 44.6 all-gather.16
  164.4 20.5 all-gather.32
  186.5 22.5 all-gather.18
  215.3 88.0 reduce-scatter.12
  304.9 26.8 all-gather.24
  334.7 73.3 all-gather.20
  409.7 25.3 all-gather.22
  436.7 27.0 all-gather.26
  466.0 73.3 all-gather.28
  570.3 86.3 reduce-scatter.16
  660.7 73.1 all-gather.30
  736.4 35.7 reduce-scatter.28
  774.7 35.5 reduce-scatter.26
  812.7 36.3 reduce-scatter.24
  852.2 21.6 reduce-scatter.30
  879.8 122.4 all-reduce.3
  1004.6 30.4 reduce-scatter.22
  1039.2 87.8 reduce-scatter.18
  1130.6 88.8 reduce-scatter.14
  1222.2 58.0 reduce-scatter.20

commit v2 on v1

v2 whole, which is shorter than its diff:
```python
import functools
import jax
import jax.numpy as jnp
from jax import lax
from jax.experimental import pallas as pl
from jax.experimental.pallas import tpu as pltpu
from jax.sharding import PartitionSpec as P

DK = 128
DV = 256
CONV = 4
CHUNK = 128
MIX = 2 * DK + DV
PER = 2 * DK + 2 * DV
GROUP = 4
epsilon = 1e-06
F32 = jnp.float32
BF16 = jnp.bfloat16
HALO = 16
VMEM_LIMIT = 56 * 1024 * 1024


def shifted(value, axis, steps):
    count = lax.axis_size(axis)
    leading, last = (max(0, -steps), min(count, count - steps))
    return lax.ppermute(value, axis, [(source, source + steps) for source in range(leading, last)])


def mm(a, b, ca=1, cb=0):
    return lax.dot_general(
        a.astype(BF16), b.astype(BF16), (((ca,), (cb,)), ((), ())), preferred_element_type=F32
    )


def mmx(a, b, ca=1, cb=0):
    return lax.dot_general(
        a, b, (((ca,), (cb,)), ((), ())), preferred_element_type=F32, precision=lax.Precision.HIGHEST
    )


def softplus(x):
    return jnp.maximum(x, 0.0) + jnp.log1p(jnp.exp(-jnp.abs(x)))


def sigmoid(x):
    return 1.0 / (1.0 + jnp.exp(-x))


def iotas(n):
    return (
        lax.broadcasted_iota(jnp.int32, (n, n), 0),
        lax.broadcasted_iota(jnp.int32, (n, n), 1),
    )


def inverse_parts(mats, rows, cols):
    base = 16
    near = (rows // base) == (cols // base)
    diag = [jnp.where(near, a, 0.0) for a in mats]
    result = [-d for d in diag]
    power = [mm(d, d) for d in diag]
    span = 2
    while True:
        result = [r + p + mm(r, p) for r, p in zip(result, power)]
        span *= 2
        if span >= base:
            break
        power = [mm(p, p) for p in power]
    size = base
    n = mats[0].shape[0]
    while size < n:
        cross = ((rows // (2 * size)) == (cols // (2 * size))) & ((rows // size) != (cols // size))
        off = [jnp.where(cross, a, 0.0) for a in mats]
        left = [o + mm(r, o) for o, r in zip(off, result)]
        result = [r - x - mm(x, r) for r, x in zip(result, left)]
        size *= 2
    return result


def conv_scratch(first, proj_ref, prev_ref, halo_ref, x_ref, heads, rows):
    for h in range(heads):
        cols = slice(h * PER, h * PER + MIX)
        before = jnp.where(first, halo_ref[:, cols].astype(F32), prev_ref[:, cols].astype(F32))
        x_ref[0:8, h * MIX : (h + 1) * MIX] = before[HALO - 8 :]
        x_ref[8 : 8 + rows, h * MIX : (h + 1) * MIX] = proj_ref[:, cols].astype(F32)


def conv_pre(x_ref, taps_ref, h, row):
    cols = slice(h * MIX, (h + 1) * MIX)
    total = None
    for i in range(CONV):
        part = taps_ref[i : i + 1, cols] * x_ref[pl.ds(row + 8 - (CONV - 1) + i, CHUNK), cols]
        total = part if total is None else total + part
    return total


def unit(a):
    r = lax.rsqrt(jnp.sum(a * a, axis=-1, keepdims=True) + epsilon)
    return a * r, r


def forward_kernel(
    heads, group,
    proj_ref, prev_ref, halo_ref, rates_ref, bias_ref, taps_ref,
    olocal_ref, qmap_ref, state_ref, uw_ref, inv_ref, trans_ref, qe_ref, end_ref,
    x_ref, carry_ref,
):
    step = pl.program_id(0)
    rows_here = CHUNK * group
    conv_scratch(step == 0, proj_ref, prev_ref, halo_ref, x_ref, heads, rows_here)
    ri, ci = iotas(CHUNK)
    included = ri >= ci
    strictly = ri > ci
    lower = jnp.where(included, 1.0, 0.0)
    upper = jnp.where(ri <= ci, 1.0, 0.0)

    @pl.when(step == 0)
    def _():
        for h in range(heads):
            carry_ref[h, :DV, :] = jnp.zeros((DV, DK), F32)
            carry_ref[h, DV:, :] = jnp.where(ri == ci, 1.0, 0.0)

    pairs = [(g, h) for g in range(group) for h in range(heads)]
    logits = rates_ref[...] + bias_ref[...]
    log_decay = -softplus(logits)
    strength = sigmoid(logits)
    cums, cum_rows = [], []
    for g in range(group):
        part = log_decay[g * CHUNK : (g + 1) * CHUNK]
        cums.append(mmx(lower, part))
        cum_rows.append(mmx(part, upper, 0, 0))
    mats, scores, rhs, tails, scaled_q, finals = [], [], [], [], [], []
    for g, h in pairs:
        pre = conv_pre(x_ref, taps_ref, h, g * CHUNK)
        mixed = pre * sigmoid(pre)
        q = unit(mixed[:, :DK])[0] * DK ** (-0.5)
        k = unit(mixed[:, DK : 2 * DK])[0]
        v = mixed[:, 2 * DK :]
        cum = cums[g][:, 2 * h : 2 * h + 1]
        cum_row = cum_rows[g][2 * h : 2 * h + 1, :]
        beta = strength[g * CHUNK : (g + 1) * CHUNK, 2 * h + 1 : 2 * h + 2]
        growth = jnp.exp(cum)
        decays = jnp.where(included, jnp.exp(jnp.where(included, cum - cum_row, 0.0)), 0.0)
        grams = mm(jnp.concatenate([q, k], axis=0), k, 1, 1)
        scores.append(grams[:CHUNK] * decays)
        mats.append(jnp.where(strictly, beta * decays * grams[CHUNK:], 0.0))
        rhs.append(jnp.concatenate([beta * v, beta * growth * k], axis=1))
        last = cum[CHUNK - 1 : CHUNK, :]
        tails.append(k * jnp.exp(last - cum))
        scaled_q.append(growth * q)
        finals.append(jnp.exp(last))
    inverses = inverse_parts(mats, ri, ci)
    solved = [b + mm(r, b) for r, b in zip(inverses, rhs)]
    mixes = [mm(p, u) for p, u in zip(scores, solved)]
    adds = [mm(u, t, 0, 0) for u, t in zip(solved, tails)]
    for j, (g, h) in enumerate(pairs):
        inv_ref[h, g] = inverses[j].astype(BF16)
        uw_ref[h, g] = solved[j].astype(BF16)
        qe_ref[h, g] = (scaled_q[j] - mixes[j][:, DV:]).astype(BF16)
        trans_ref[h, g] = (-adds[j][DV:]).astype(BF16)
        olocal_ref[g * CHUNK : (g + 1) * CHUNK, h * DV : (h + 1) * DV] = mixes[j][:, :DV]
    for h in range(heads):
        now = carry_ref[h]
        for g in range(group):
            j = pairs.index((g, h))
            low = now.astype(BF16)
            state_ref[h, g] = low
            moved = finals[j] * now + mm(low, trans_ref[h, g])
            now = jnp.concatenate([moved[:DV] + adds[j][:DV], moved[DV:]], axis=0)
        carry_ref[h] = now
        end_ref[h] = now.astype(BF16)
    for j, (g, h) in enumerate(pairs):
        both = mm(qe_ref[h, g], state_ref[h, g], 1, 1)
        rows = slice(g * CHUNK, (g + 1) * CHUNK)
        olocal_ref[rows, h * DV : (h + 1) * DV] += both[:, :DV]
        qmap_ref[rows, h * DK : (h + 1) * DK] = both[:, DV:].astype(BF16)


def mixer_forward(projected, halo, rates, bias_row, taps, group):
    total = projected.shape[0]
    heads = rates.shape[1] // 2
    rows = CHUNK * group
    steps = total // rows
    chunks = total // CHUNK
    whole = lambda i: (0, 0)
    saved = lambda a, b: (
        jax.ShapeDtypeStruct((heads, chunks, a, b), BF16),
        pl.BlockSpec((heads, group, a, b), lambda i: (0, i, 0, 0)),
    )
    outs = [
        (jax.ShapeDtypeStruct((total, heads * DV), F32), pl.BlockSpec((rows, heads * DV), lambda i: (i, 0))),
        (jax.ShapeDtypeStruct((total, heads * DK), BF16), pl.BlockSpec((rows, heads * DK), lambda i: (i, 0))),
        saved(DV + DK, DK),
        saved(CHUNK, DV + DK),
        saved(CHUNK, CHUNK),
        saved(DK, DK),
        saved(CHUNK, DK),
        (jax.ShapeDtypeStruct((heads, DV + DK, DK), BF16), pl.BlockSpec((heads, DV + DK, DK), lambda i: (0, 0, 0))),
    ]
    return pl.pallas_call(
        functools.partial(forward_kernel, heads, group),
        grid=(steps,),
        in_specs=[
            pl.BlockSpec((rows, heads * PER), lambda i: (i, 0)),
            pl.BlockSpec((HALO, heads * PER), lambda i: (jnp.maximum(i * (rows // HALO) - 1, 0), 0)),
            pl.BlockSpec((HALO, heads * PER), whole),
            pl.BlockSpec((rows, 2 * heads), lambda i: (i, 0)),
            pl.BlockSpec((1, 2 * heads), whole),
            pl.BlockSpec((CONV, heads * MIX), whole),
        ],
        out_shape=[o[0] for o in outs],
        out_specs=[o[1] for o in outs],
        scratch_shapes=[
            pltpu.VMEM((rows + 8, heads * MIX), F32),
            pltpu.VMEM((heads, DV + DK, DK), F32),
        ],
        compiler_params=pltpu.CompilerParams(vmem_limit_bytes=VMEM_LIMIT),
        cost_estimate=pl.CostEstimate(flops=40_000_000_000, bytes_accessed=16_000_000, transcendentals=0),
    )(projected, projected, halo, rates, bias_row, taps)


def backward_kernel(
    heads, group, steps, peers,
    proj_ref, prev_ref, halo_ref, rates_ref, bias_ref, taps_ref,
    state_ref, uw_ref, inv_ref, trans_ref, qe_ref,
    dout_ref, ggate_ref, value_ref, incoming_ref, place_ref, maps_ref, local_ref,
    gp_ref, grates_ref, gtaps_ref, gbias_ref, tail_ref, lead_ref,
    x_ref, d_ref, carry_ref, next_ref,
):
    step = pl.program_id(0)
    rows_here = CHUNK * group
    conv_scratch(step == steps - 1, proj_ref, prev_ref, halo_ref, x_ref, heads, rows_here)
    ri, ci = iotas(CHUNK)
    included = ri >= ci
    strictly = ri > ci
    lower = jnp.where(included, 1.0, 0.0)
    upper = jnp.where(ri <= ci, 1.0, 0.0)

    @pl.when(step == 0)
    def _():
        for h in range(heads):
            grad = jnp.zeros((DV, DK), F32)
            for turn in range(peers - 1):
                source = peers - 1 - turn
                moved = mm(grad, maps_ref[source, h, DV:, :], 1, 1) + local_ref[source, h].astype(F32)
                grad = jnp.where(source > place_ref[0], moved, grad)
            carry_ref[h] = grad
        d_ref[rows_here : rows_here + 8, :] = jnp.zeros((8, heads * MIX), F32)
        gtaps_ref[...] = jnp.zeros_like(gtaps_ref)
        gbias_ref[...] = jnp.zeros_like(gbias_ref)

    @pl.when(step > 0)
    def _():
        d_ref[rows_here : rows_here + 8, :] = d_ref[0:8, :]

    pairs = [(g, h) for g in range(group) for h in range(heads)]
    logits = rates_ref[...] + bias_ref[...]
    log_decay = -softplus(logits)
    strength = sigmoid(logits)
    cums, cum_rows = [], []
    for g in range(group):
        part = log_decay[g * CHUNK : (g + 1) * CHUNK]
        cums.append(mmx(lower, part))
        cum_rows.append(mmx(part, upper, 0, 0))
    douts, injections = [], []
    for g, h in pairs:
        do = dout_ref[g * CHUNK : (g + 1) * CHUNK, h * DV : (h + 1) * DV]
        douts.append(do)
        injections.append(mm(do, qe_ref[h, g], 0, 0))
    for h in range(heads):
        now = carry_ref[h]
        for g in reversed(range(group)):
            j = pairs.index((g, h))
            last = cums[g][CHUNK - 1 : CHUNK, 2 * h : 2 * h + 1]
            next_ref[h, g] = now
            now = jnp.exp(last) * now + mm(now, trans_ref[h, g], 1, 1) + injections[j]
        carry_ref[h] = now
    lane = lax.broadcasted_iota(jnp.int32, (CHUNK, 2 * heads), 1)
    row_col = lax.broadcasted_iota(jnp.int32, (CHUNK, 1), 0)
    dcums = [jnp.zeros((CHUNK, 2 * heads), F32) for _ in range(group)]
    dlogits = [jnp.zeros((CHUNK, 2 * heads), F32) for _ in range(group)]
    for j, (g, h) in enumerate(pairs):
        pre = conv_pre(x_ref, taps_ref, h, g * CHUNK)
        sig = sigmoid(pre)
        mixed = pre * sig
        slope = sig * (1.0 + pre * (1.0 - sig))
        uq, rq = unit(mixed[:, :DK])
        q = uq * DK ** (-0.5)
        k, rk = unit(mixed[:, DK : 2 * DK])
        v = mixed[:, 2 * DK :]
        cum = cums[g][:, 2 * h : 2 * h + 1]
        cum_row = cum_rows[g][2 * h : 2 * h + 1, :]
        beta = strength[g * CHUNK : (g + 1) * CHUNK, 2 * h + 1 : 2 * h + 2]
        growth = jnp.exp(cum)
        decays = jnp.where(included, jnp.exp(jnp.where(included, cum - cum_row, 0.0)), 0.0)
        qb, kb = q.astype(BF16), k.astype(BF16)
        grams = mm(jnp.concatenate([qb, kb], axis=0), kb, 1, 1)
        scores = grams[:CHUNK] * decays
        last = cum[CHUNK - 1 : CHUNK, :]
        fade = jnp.exp(last - cum)
        tail = k * fade
        sl = state_ref[h, g]
        state = sl[:DV].astype(F32) + mm(incoming_ref[h], sl[DV:])
        after = next_ref[h, g]
        afterb = after.astype(BF16)
        stateb = state.astype(BF16)
        uw = uw_ref[h, g]
        errors = uw[:, :DV].astype(F32) - mm(uw[:, DV:], stateb, 1, 1)
        eb = errors.astype(BF16)
        do = douts[j]
        de = mm(scores, do, 0, 0) + mm(tail, afterb, 1, 1)
        db = de + mm(inv_ref[h, g], de, 0, 0)
        dbb = db.astype(BF16)
        stacked = jnp.concatenate([do, dbb], axis=0)
        against_e = mm(stacked, eb, 1, 1)
        against_s = mm(stacked, stateb)
        dp = against_e[:CHUNK]
        da = jnp.where(strictly, -against_e[CHUNK:], 0.0)
        dos = against_s[:CHUNK]
        dbs = against_s[CHUNK:]
        dpd = dp * decays
        dg = da * beta * decays
        dtail = mm(eb, afterb)
        dq = mm(dpd, kb) + growth * dos
        sym = dg + dg.T
        dk = (
            mm(jnp.concatenate([dpd.T, sym], axis=1), jnp.concatenate([qb, kb], axis=0))
            - beta * growth * dbs
            + fade * dtail
        )
        dv = beta * db
        dlogit = (1.0 - beta) * jnp.sum(db * errors, axis=1, keepdims=True)
        tdot = jnp.sum(tail * dtail, axis=1, keepdims=True)
        out = value_ref[g * CHUNK : (g + 1) * CHUNK, h * DV : (h + 1) * DV].astype(F32)
        dcum = jnp.sum(do.astype(F32) * out, axis=1, keepdims=True) - beta * jnp.sum(
            v * db, axis=1, keepdims=True
        )
        at_end = jnp.exp(last) * jnp.sum(jnp.sum(after * state, axis=1, keepdims=True), axis=0, keepdims=True) + jnp.sum(
            tdot, axis=0, keepdims=True
        )
        dcum = dcum + jnp.where(row_col == CHUNK - 1, at_end, 0.0)
        dcums[g] = jnp.where(lane == 2 * h, dcum, dcums[g])
        dlogits[g] = jnp.where(lane == 2 * h + 1, dlogit, dlogits[g])
        dq = dq * DK ** (-0.5)
        dmq = rq * (dq - uq * jnp.sum(uq * dq, axis=1, keepdims=True))
        dmk = rk * (dk - k * jnp.sum(k * dk, axis=1, keepdims=True))
        d_ref[g * CHUNK : (g + 1) * CHUNK, h * MIX : (h + 1) * MIX] = (
            jnp.concatenate([dmq, dmk, dv], axis=1) * slope
        )
    for g in range(group):
        rows = slice(g * CHUNK, (g + 1) * CHUNK)
        dld = mmx(upper, dcums[g])
        drate = jnp.where(lane % 2 == 0, -sigmoid(logits[rows]) * dld, dlogits[g])
        grates_ref[rows, :] = drate
        gbias_ref[...] += jnp.sum(drate, axis=0, keepdims=True)
    for g, h in pairs:
        cols = slice(h * MIX, (h + 1) * MIX)
        row = g * CHUNK
        dpre = d_ref[pl.ds(row, CHUNK), cols]
        total = None
        for i in range(CONV):
            gtaps_ref[i : i + 1, cols] += jnp.sum(
                dpre * x_ref[pl.ds(row + 8 - (CONV - 1) + i, CHUNK), cols], axis=0, keepdims=True
            )
            part = taps_ref[i : i + 1, cols] * d_ref[pl.ds(row + CONV - 1 - i, CHUNK), cols]
            total = part if total is None else total + part
        gp_ref[row : row + CHUNK, h * PER : h * PER + MIX] = total.astype(BF16)
        gp_ref[row : row + CHUNK, h * PER + MIX : (h + 1) * PER] = ggate_ref[
            row : row + CHUNK, h * DV : (h + 1) * DV
        ]
        if g == group - 1:
            @pl.when(step == 0)
            def _(total=total, cols=cols):
                tail_ref[:, cols] = total[CHUNK - HALO :]

    @pl.when(step == steps - 1)
    def _():
        lead_ref[...] = d_ref[0:8, :]


def mixer_backward(projected, halo, rates, bias_row, taps, saved, dout, ggate, value, incoming, place, maps, local, group):
    state, uw, inv, trans, qe = saved
    total = projected.shape[0]
    heads = rates.shape[1] // 2
    rows = CHUNK * group
    steps = total // rows
    whole = lambda i: (0, 0)
    flip = lambda i: (steps - 1 - i, 0)
    keep = lambda a, b: pl.BlockSpec((heads, group, a, b), lambda i: (0, steps - 1 - i, 0, 0))
    return pl.pallas_call(
        functools.partial(backward_kernel, heads, group, steps, maps.shape[0]),
        grid=(steps,),
        in_specs=[
            pl.BlockSpec((rows, heads * PER), flip),
            pl.BlockSpec((HALO, heads * PER), lambda i: (jnp.maximum((steps - 1 - i) * (rows // HALO) - 1, 0), 0)),
            pl.BlockSpec((HALO, heads * PER), whole),
            pl.BlockSpec((rows, 2 * heads), flip),
            pl.BlockSpec((1, 2 * heads), whole),
            pl.BlockSpec((CONV, heads * MIX), whole),
            keep(DV + DK, DK),
            keep(CHUNK, DV + DK),
            keep(CHUNK, CHUNK),
            keep(DK, DK),
            keep(CHUNK, DK),
            pl.BlockSpec((rows, heads * DV), flip),
            pl.BlockSpec((rows, heads * DV), flip),
            pl.BlockSpec((rows, heads * DV), flip),
            pl.BlockSpec(incoming.shape, lambda i: (0, 0, 0)),
            pl.BlockSpec(memory_space=pltpu.SMEM),
            pl.BlockSpec(maps.shape, lambda i: (0, 0, 0, 0)),
            pl.BlockSpec(local.shape, lambda i: (0, 0, 0, 0)),
        ],
        out_shape=[
            jax.ShapeDtypeStruct((total, heads * PER), BF16),
            jax.ShapeDtypeStruct((total, 2 * heads), F32),
            jax.ShapeDtypeStruct((CONV, heads * MIX), F32),
            jax.ShapeDtypeStruct((1, 2 * heads), F32),
            jax.ShapeDtypeStruct((HALO, heads * MIX), F32),
            jax.ShapeDtypeStruct((8, heads * MIX), F32),
        ],
        out_specs=[
            pl.BlockSpec((rows, heads * PER), flip),
            pl.BlockSpec((rows, 2 * heads), flip),
            pl.BlockSpec((CONV, heads * MIX), whole),
            pl.BlockSpec((1, 2 * heads), whole),
            pl.BlockSpec((HALO, heads * MIX), whole),
            pl.BlockSpec((8, heads * MIX), whole),
        ],
        scratch_shapes=[
            pltpu.VMEM((rows + 8, heads * MIX), F32),
            pltpu.VMEM((rows + 8, heads * MIX), F32),
            pltpu.VMEM((heads, DV, DK), F32),
            pltpu.VMEM((heads, group, DV, DK), F32),
        ],
        compiler_params=pltpu.CompilerParams(vmem_limit_bytes=VMEM_LIMIT),
        cost_estimate=pl.CostEstimate(flops=60_000_000_000, bytes_accessed=20_000_000, transcendentals=0),
    )(projected, projected, halo, rates, bias_row, taps, state, uw, inv, trans, qe, dout, ggate, value, incoming, place, maps, local)


def gate_kernel(
    heads, peers,
    ids_ref, place_ref, maps_ref, olocal_ref, qmap_ref, proj_ref, gain_ref, w_ref,
    value_ref, gated_ref, part_ref, incoming_ref,
):
    @pl.when(pl.program_id(0) == 0)
    def _():
        for h in range(heads):
            state = jnp.zeros((DV, DK), F32)
            for source in range(peers - 1):
                moved = mm(state, maps_ref[source, h, DV:, :]) + maps_ref[source, h, :DV, :].astype(F32)
                state = jnp.where(source < place_ref[0], moved, state)
            incoming_ref[h] = state.astype(BF16)

    for h in range(heads):
        cols = slice(h * DV, (h + 1) * DV)
        out = olocal_ref[:, cols] + mm(qmap_ref[:, h * DK : (h + 1) * DK], incoming_ref[h], 1, 1)
        low = out.astype(BF16)
        value_ref[:, cols] = low
        value = low.astype(F32)
        normed = value * lax.rsqrt(jnp.mean(value * value, axis=-1, keepdims=True) + epsilon)
        gate = proj_ref[:, h * PER + MIX : (h + 1) * PER].astype(F32)
        gated_ref[:, cols] = (normed * gain_ref[...] * (gate * sigmoid(gate))).astype(BF16)
    part_ref[...] = mm(gated_ref[...], w_ref[...]).astype(BF16)


def gate_output(ids, place, maps, out_local, query_map, projected, gain, w_out):
    heads = maps.shape[1]
    total = projected.shape[0]
    count = ids.shape[0]
    rows = total // count
    width = w_out.shape[1]
    theirs = lambda i, ids, place: (ids[i], 0)
    mine = lambda i, ids, place: (i, 0)
    whole = lambda i, ids, place: (0, 0)
    return pl.pallas_call(
        functools.partial(gate_kernel, heads, maps.shape[0]),
        grid_spec=pltpu.PrefetchScalarGridSpec(
            num_scalar_prefetch=2,
            grid=(count,),
            in_specs=[
                pl.BlockSpec(maps.shape, lambda i, ids, place: (0, 0, 0, 0)),
                pl.BlockSpec((rows, heads * DV), theirs),
                pl.BlockSpec((rows, heads * DK), theirs),
                pl.BlockSpec((rows, heads * PER), theirs),
                pl.BlockSpec((1, DV), whole),
                pl.BlockSpec(w_out.shape, whole),
            ],
            out_specs=[
                pl.BlockSpec((rows, heads * DV), theirs),
                pl.BlockSpec((rows, heads * DV), mine),
                pl.BlockSpec((rows, width), mine),
                pl.BlockSpec((heads, DV, DK), lambda i, ids, place: (0, 0, 0)),
            ],
        ),
        out_shape=[
            jax.ShapeDtypeStruct((total, heads * DV), BF16),
            jax.ShapeDtypeStruct((total, heads * DV), BF16),
            jax.ShapeDtypeStruct((total, width), BF16),
            jax.ShapeDtypeStruct((heads, DV, DK), BF16),
        ],
        compiler_params=pltpu.CompilerParams(vmem_limit_bytes=VMEM_LIMIT),
        cost_estimate=pl.CostEstimate(flops=8_000_000_000, bytes_accessed=16_000_000, transcendentals=0),
    )(ids, place, maps, out_local, query_map, projected, gain, w_out)


def gate_back_kernel(
    heads,
    ids_ref, branch_ref, w_ref, value_ref, proj_ref, qmap_ref, gain_ref,
    ggate_ref, dout_ref, gain_grad_ref, local_ref,
):
    @pl.when(pl.program_id(0) == 0)
    def _():
        gain_grad_ref[...] = jnp.zeros_like(gain_grad_ref)
        local_ref[...] = jnp.zeros_like(local_ref)

    grads = mm(branch_ref[...], w_ref[...], 1, 1)
    gain = gain_ref[...]
    for h in range(heads):
        cols = slice(h * DV, (h + 1) * DV)
        value = value_ref[:, cols].astype(F32)
        inverse = lax.rsqrt(jnp.mean(value * value, axis=-1, keepdims=True) + epsilon)
        normed = value * inverse
        gate = proj_ref[:, h * PER + MIX : (h + 1) * PER].astype(F32)
        sig = sigmoid(gate)
        grad = grads[:, cols]
        through = grad * (gate * sig)
        ggate_ref[:, cols] = (grad * normed * gain * (sig * (1.0 + gate * (1.0 - sig)))).astype(BF16)
        gain_grad_ref[...] += jnp.sum(through * normed, axis=0, keepdims=True)
        scaled = through * gain
        low = (inverse * (scaled - normed * jnp.mean(scaled * normed, axis=-1, keepdims=True))).astype(BF16)
        dout_ref[:, cols] = low
        local_ref[h] += mm(low, qmap_ref[:, h * DK : (h + 1) * DK], 0, 0)


def gate_backward(ids, branch, w_out, value, projected, query_map, gain, heads):
    total = projected.shape[0]
    count = ids.shape[0]
    rows = total // count
    theirs = lambda i, ids: (ids[i], 0)
    mine = lambda i, ids: (i, 0)
    whole = lambda i, ids: (0, 0)
    return pl.pallas_call(
        functools.partial(gate_back_kernel, heads),
        grid_spec=pltpu.PrefetchScalarGridSpec(
            num_scalar_prefetch=1,
            grid=(count,),
            in_specs=[
                pl.BlockSpec((rows, branch.shape[1]), mine),
                pl.BlockSpec(w_out.shape, whole),
                pl.BlockSpec((rows, heads * DV), theirs),
                pl.BlockSpec((rows, heads * PER), theirs),
                pl.BlockSpec((rows, heads * DK), theirs),
                pl.BlockSpec((1, DV), whole),
            ],
            out_specs=[
                pl.BlockSpec((rows, heads * DV), theirs),
                pl.BlockSpec((rows, heads * DV), theirs),
                pl.BlockSpec((1, DV), whole),
                pl.BlockSpec((heads, DV, DK), lambda i, ids: (0, 0, 0)),
            ],
        ),
        out_shape=[
            jax.ShapeDtypeStruct((total, heads * DV), BF16),
            jax.ShapeDtypeStruct((total, heads * DV), BF16),
            jax.ShapeDtypeStruct((1, DV), F32),
            jax.ShapeDtypeStruct((heads, DV, DK), F32),
        ],
        compiler_params=pltpu.CompilerParams(vmem_limit_bytes=VMEM_LIMIT),
        cost_estimate=pl.CostEstimate(flops=8_000_000_000, bytes_accessed=16_000_000, transcendentals=0),
    )(ids, branch, w_out, value, projected, query_map, gain)


def ring_order(count):
    return list(range(0, count, 2)) + list(range(1, count, 2))[::-1]


def ring_step(value, axis, step):
    order = ring_order(lax.axis_size(axis))
    count = len(order)
    return lax.ppermute(value, axis, [(order[i], order[(i + step) % count]) for i in range(count)])


def ring_ids(axis):
    order = ring_order(lax.axis_size(axis))
    count = len(order)
    place = {device: i for i, device in enumerate(order)}
    table = [[order[(place[device] + k) % count] for k in range(count)] for device in range(count)]
    return lax.dynamic_index_in_dim(jnp.array(table, jnp.int32), lax.axis_index(axis), 0, False)


def ring_gather(shard, axis):
    count = lax.axis_size(axis)
    half = shard.shape[0] // 2
    halves = []
    for part in range(2):
        piece = shard[part * half : (part + 1) * half]
        found = {0: piece}
        forward = backward = piece
        for s in range(1, count // 2):
            forward = ring_step(forward, axis, 1)
            backward = ring_step(backward, axis, -1)
            found[count - s] = forward
            found[s] = backward
        if count > 1:
            found[count // 2] = ring_step(forward if part == 0 else backward, axis, 1 if part == 0 else -1)
        halves.append(found)
    return halves


def gathered_near(halves):
    count = len(halves[0])
    return jnp.concatenate([found[k] for k in range(count) for found in halves], axis=0)


def gathered_whole(halves, ids):
    count = len(halves[0])
    half, width = halves[0][0].shape
    buffer = jnp.zeros((count * 2 * half, width), halves[0][0].dtype)
    for k in range(count):
        for part, found in enumerate(halves):
            buffer = lax.dynamic_update_slice(buffer, found[k], (ids[k] * (2 * half) + part * half, 0))
    return buffer


def ring_scatter(take, rows, axis):
    count = lax.axis_size(axis)
    half = rows // 2
    totals = []
    for part in range(2):
        piece = lambda k: take(k, part * half, half)
        forward = backward = None
        if count > 1:
            if part == 0:
                forward = ring_step(piece(count // 2), axis, 1)
            else:
                backward = ring_step(piece(count // 2), axis, -1)
        for s in range(count // 2 - 1, 0, -1):
            forward = piece(s) if forward is None else forward + piece(s)
            backward = piece(count - s) if backward is None else backward + piece(count - s)
            forward = ring_step(forward, axis, 1)
            backward = ring_step(backward, axis, -1)
        total = piece(0).astype(F32)
        for other in (forward, backward):
            if other is not None:
                total = total + other.astype(F32)
        totals.append(total)
    return jnp.concatenate(totals, axis=0)


def near_rows(array, rows):
    return lambda k, start, size: lax.slice_in_dim(array, k * rows + start, k * rows + start + size, axis=0)


def whole_rows(array, rows, ids):
    return lambda k, start, size: lax.dynamic_slice_in_dim(array, ids[k] * rows + start, size, 0)


def swap(value, axis, bit):
    count = lax.axis_size(axis)
    return lax.ppermute(value, axis, [(i, i ^ bit) for i in range(count)])


def pair_gather(shard, axis, dim):
    if lax.axis_size(axis) != 4:
        return lax.all_gather(shard, axis, axis=dim, tiled=True)
    me = lax.axis_index(axis)
    far = swap(shard, axis, 2)
    near = swap(shard, axis, 1)
    both = swap(far, axis, 1)
    size = shard.shape[dim]
    shape = list(shard.shape)
    shape[dim] = 4 * size
    buffer = jnp.zeros(shape, shard.dtype)
    for bit, piece in enumerate((shard, near, far, both)):
        buffer = lax.dynamic_update_slice_in_dim(buffer, piece, (me ^ bit) * size, dim)
    return buffer


def pair_scatter(array, axis, dim):
    if lax.axis_size(axis) != 4:
        return lax.psum_scatter(array, axis, scatter_dimension=dim, tiled=True).astype(F32)
    me = lax.axis_index(axis)
    size = array.shape[dim] // 4
    piece = lambda bit: lax.dynamic_slice_in_dim(array, (me ^ bit) * size, size, dim)
    across = swap(piece(3), axis, 1)
    near = swap(piece(1), axis, 1)
    far = swap(piece(2) + across, axis, 2)
    return piece(0).astype(F32) + near.astype(F32) + far.astype(F32)


def butterfly(value, axis):
    count = lax.axis_size(axis)
    bit = 1
    while bit < count:
        value = value + swap(value, axis, bit)
        bit *= 2
    return value


def after(value, *earlier):
    return lax.optimization_barrier((value, *earlier))[0]


def per_device(
    tokens,
    w_qkvg,
    w_rates,
    conv_weight,
    head_bias,
    norm_gain,
    head_gain,
    mlp_gain,
    w_out,
    w_ff_gate,
    w_ff_up,
    w_ff_down,
    cotangent,
):
    heads = head_bias.shape[1]
    own_rows = tokens.shape[0]
    contract = (((1,), (1,)), ((), ()))
    rows_first = (((0,), (0,)), ((), ()))
    dot = lambda a, b, dims: lax.dot_general(a, b, dims, preferred_element_type=F32)
    plain = (((1,), (0,)), ((), ()))
    ids = ring_ids("head")
    place = lax.axis_index("seq").reshape(1)
    gain_row = head_gain.reshape(1, DV)
    bias_row = head_bias.T.reshape(1, 2 * heads)

    inputs = tokens.astype(F32)
    inverse_one = lax.rsqrt(jnp.mean(inputs * inputs, axis=-1, keepdims=True) + epsilon)
    norm_normed = inputs * inverse_one
    normed_halves = ring_gather((norm_normed * norm_gain).astype(BF16), "head")
    w_mix = pair_gather(w_qkvg, "seq", 0)
    w_rate = pair_gather(w_rates.T, "seq", 1)
    out_rows = pair_gather(after(w_out, w_mix), "seq", 1)
    gate_w = pair_gather(after(w_ff_gate, out_rows), "seq", 1)
    up_w = pair_gather(after(w_ff_up, gate_w), "seq", 1)
    down_w = pair_gather(after(w_ff_down, up_w), "seq", 1)
    normed = gathered_whole(normed_halves, ids)
    seq_rows = normed.shape[0]
    cotangent_near = gathered_near(ring_gather(after(cotangent, normed), "head"))

    projected = dot(normed, w_mix, plain).astype(BF16)
    rates = dot(normed, w_rate, contract)
    halo_rows = shifted(projected[seq_rows - HALO :], "seq", 1)
    out_local, query_map, *saved, end_state = mixer_forward(
        projected, halo_rows, rates, bias_row, conv_weight, GROUP
    )
    maps = lax.all_gather(end_state, "seq")
    value, gated, branch_part, incoming = gate_output(
        ids, place, maps, out_local, query_map, projected, gain_row, out_rows
    )
    residual = inputs + ring_scatter(near_rows(branch_part, own_rows), own_rows, "head")
    inverse_two = lax.rsqrt(jnp.mean(residual * residual, axis=-1, keepdims=True) + epsilon)
    mlp_normed = residual * inverse_two
    mlp_near = gathered_near(ring_gather((mlp_normed * mlp_gain).astype(BF16), "head"))

    grad_hidden = dot(cotangent_near, down_w, contract)
    gate_pre = dot(mlp_near, gate_w, contract)
    up_pre = dot(mlp_near, up_w, contract)
    ff_sigmoid = jax.nn.sigmoid(gate_pre)
    ff_silu = gate_pre * ff_sigmoid
    hidden = (ff_silu * up_pre).astype(BF16)
    ff_slope = ff_sigmoid * (1.0 + gate_pre * (1.0 - ff_sigmoid))
    grad_gate_pre = (grad_hidden * up_pre * ff_slope).astype(BF16)
    grad_up_pre = (grad_hidden * ff_silu).astype(BF16)
    grad_mlp_part = (dot(grad_gate_pre, gate_w, plain) + dot(grad_up_pre, up_w, plain)).astype(BF16)
    grad_mlp_in = ring_scatter(near_rows(grad_mlp_part, own_rows), own_rows, "head")

    grad_down_s = pair_scatter(dot(hidden, cotangent_near, rows_first).astype(BF16), "seq", 1)
    grad_gate_s = pair_scatter(dot(grad_gate_pre, mlp_near, rows_first).astype(BF16), "seq", 1)
    grad_up_s = pair_scatter(dot(grad_up_pre, mlp_near, rows_first).astype(BF16), "seq", 1)

    mlp_gain_part = jnp.sum(grad_mlp_in * mlp_normed, axis=0)
    scaled_two = grad_mlp_in * mlp_gain
    grad_residual = cotangent.astype(F32) + inverse_two * (
        scaled_two - mlp_normed * jnp.mean(scaled_two * mlp_normed, axis=-1, keepdims=True)
    )
    branch_near = gathered_near(ring_gather(grad_residual.astype(BF16), "head"))
    grad_gate_mix, grad_mixer, head_gain_part, local_grad = gate_backward(
        ids, branch_near, out_rows, value, projected, query_map, gain_row, heads
    )
    locals_all = lax.all_gather(local_grad.astype(BF16), "seq")
    output_part = after(dot(hidden, down_w, plain).astype(BF16), branch_near)
    output = (residual + ring_scatter(near_rows(output_part, own_rows), own_rows, "head")).astype(BF16)
    grad_out_s = pair_scatter(dot(gated, branch_near, rows_first).astype(BF16), "seq", 1)

    grad_projected, grad_rates, grad_taps, grad_bias_row, tail_rows, lead_rows = mixer_backward(
        projected, halo_rows, rates, bias_row, conv_weight, saved,
        grad_mixer, grad_gate_mix, value, incoming, place, maps, locals_all, GROUP,
    )
    later_rows = shifted(lead_rows, "seq", -1)
    padded = jnp.concatenate([jnp.zeros((HALO, heads * MIX), F32), later_rows])
    last_rows = tail_rows + sum(
        conv_weight[i] * padded[CONV - 1 - i : CONV - 1 - i + HALO] for i in range(CONV)
    )
    for h in range(heads):
        grad_projected = lax.dynamic_update_slice(
            grad_projected, last_rows[:, h * MIX : (h + 1) * MIX].astype(BF16), (seq_rows - HALO, h * PER)
        )
    grad_rate_low = grad_rates.astype(BF16)
    grad_normed_part = (
        dot(grad_projected, w_mix, contract) + dot(grad_rate_low, w_rate, plain)
    ).astype(BF16)
    grad_normed = ring_scatter(whole_rows(grad_normed_part, own_rows, ids), own_rows, "head")
    grad_w_mix_s = pair_scatter(dot(normed, grad_projected, rows_first).astype(BF16), "seq", 0)
    grad_rate_t = dot(grad_rate_low, normed, rows_first)
    norm_gain_part = jnp.sum(grad_normed_part.astype(F32) * normed.astype(F32), axis=0) / norm_gain

    scaled_one = grad_normed * norm_gain
    grad_input = grad_residual + inverse_one * (
        scaled_one - norm_normed * jnp.mean(scaled_one * norm_normed, axis=-1, keepdims=True)
    )
    width = norm_gain.shape[0]
    flat = lambda a: jnp.pad(a.reshape(-1), (0, -a.size % 128)).reshape(-1, 128)
    seq_pack = [flat(a) for a in (grad_taps, grad_rate_t, grad_bias_row)]
    all_pack = [flat(a) for a in (norm_gain_part, mlp_gain_part, head_gain_part)]
    sizes = [a.shape[0] for a in seq_pack + all_pack]
    split = len(seq_pack)
    pack = butterfly(jnp.concatenate(seq_pack + all_pack, axis=0), "seq")
    cut = sum(sizes[:split])
    rest = butterfly(pack[cut:], "head")
    parts = []
    start = 0
    for i, size in enumerate(sizes):
        parts.append(pack[start : start + size] if i < split else rest[start - cut : start - cut + size])
        start += size
    conv_grad = parts[0].reshape(CONV, heads * MIX)
    rate_sum = parts[1].reshape(2 * heads, width)
    per_seq = w_rates.shape[0]
    grad_rates_s = lax.dynamic_slice_in_dim(rate_sum, lax.axis_index("seq") * per_seq, per_seq, 1).T
    bias_grad = parts[2].reshape(-1)[: 2 * heads].reshape(heads, 2).T
    return (
        output,
        grad_input,
        grad_w_mix_s,
        grad_rates_s,
        conv_grad,
        bias_grad,
        parts[3].reshape(width),
        parts[5].reshape(DV),
        parts[4].reshape(width),
        grad_out_s,
        grad_gate_s,
        grad_up_s,
        grad_down_s,
    )


def solution(mesh):
    in_specs = (
        P(("seq", "head"), None),
        P("seq", "head"),
        P("seq", "head"),
        P(None, "head"),
        P(None, "head"),
        P(),
        P(),
        P(),
        P("head", "seq"),
        P("head", "seq"),
        P("head", "seq"),
        P("head", "seq"),
        P(("seq", "head"), None),
    )
    out_specs = (
        P(("seq", "head"), None),
        P(("seq", "head"), None),
        P("seq", "head"),
        P("seq", "head"),
        P(None, "head"),
        P(None, "head"),
        P(),
        P(),
        P(),
        P("head", "seq"),
        P("head", "seq"),
        P("head", "seq"),
        P("head", "seq"),
    )
    return jax.shard_map(
        per_device, mesh=mesh, in_specs=in_specs, out_specs=out_specs, check_vma=False
    )
```

time: 1290 us -> 682 us (0.53)
  waiting for transfers between devices: 949 us -> 259 us
  starting transfers between devices: 4.56 us -> 153 us
  blocking collectives: 74.8 us -> 18.6 us
  matrix products: 134 us -> 85.5 us
  local copies, waits for them, and re-layouts: 32 us -> 55.8 us
  Pallas kernels: 45.3 us -> 67 us
    reduce_scatter x9 -> x0, waiting for transfers between devices: 409 us -> none  [the longest x1 89.8 us: per_device(): lax.psum_scatter((lax.dot_general(grad_projected, w_mix, contract, prefer...]
    all_gather x10 -> x0, waiting for transfers between devices: 387 us -> none  [the longest x1 76.3 us: per_device(): mlp_all = lax.all_gather(mlp_own, 'head', axis=0, tiled=True)]
    ppermute x0 -> x150, waiting for transfers between devices: none -> 259 us  [the longest x112 167 us: ring_step(): lax.ppermute(value, axis, [(order[i], order[(i + step) % count]) for i in...]
    ppermute x0 -> x150, starting transfers between devices: none -> 150 us  [the longest x112 125 us: ring_step(): lax.ppermute(value, axis, [(order[i], order[(i + step) % count]) for i in...]
    psum x1 -> x0, waiting for transfers between devices: 127 us -> none  [per_device(): lax.psum((taps_full, bias_full, norm_gain_part, mlp_gain_part, head_gain_...]
    dot_general x27 -> x16, matrix products: 134 us -> 85.5 us  [per_device(): lax.dot_general(a, b, dims, preferred_element_type=F32)]
    psum x1 -> x0, blocking collectives: 43 us -> none  [per_device(): lax.psum((taps_full, bias_full, norm_gain_part, mlp_gain_part, head_gain_...]
    unnamed x22 -> x0, waiting for transfers between devices: 25.5 us -> none
  transfers between devices with their start and end apart: 23 -> 152, of which waited for: 20 -> 87; matrix products, arithmetic and copies ran while one was open for 11% -> 16% of each run, Pallas kernels for 2% -> 4%
where the time goes in v2:
time: 682 us; the launch traced here: 674 us
  waiting for transfers between devices  259 us (38%)
  starting transfers between devices  153 us (22%)
  matrix products  85.5 us (13%)
  Pallas kernels  67 us (10%)
  local copies, waits for them, and re-layouts  55.8 us (8%)
  other arithmetic  27.2 us (4%)
  blocking collectives  18.6 us (3%)
  between operations  7.7 us (1%)
    ppermute x112, waiting for transfers between devices, ring_step(): lax.ppermute(value, axis, [(order[i], order[(i + step) % count]) for i in...  167 us
    ppermute x112, starting transfers between devices, ring_step(): lax.ppermute(value, axis, [(order[i], order[(i + step) % count]) for i in...  125 us
    ppermute x38, waiting for transfers between devices, swap(): return lax.ppermute(value, axis, [(i, i ^ bit) for i in range(count)])  92.6 us
    dot_general x16, matrix products, per_device(): lax.dot_general(a, b, dims, preferred_element_type=F32)  85.5 us
    pallas_call x1, Pallas kernels, mixer_backward(): pl.pallas_call(functools.partial(backward_kernel, heads, group, steps, ma...  27.1 us
    ppermute x38, starting transfers between devices, swap(): return lax.ppermute(value, axis, [(i, i ^ bit) for i in range(count)])  24.9 us
    pallas_call x1, Pallas kernels, mixer_forward(): pl.pallas_call(functools.partial(forward_kernel, heads, group), grid=(ste...  14.4 us
    unnamed x131, local copies, waits for them, and re-layouts  14.2 us
  transfers between devices with their start and end apart: 152, of which 87 were waited for; matrix products, arithmetic and copies ran while one was open for 16% of the time, Pallas kernels for 4%

profile of v2, /device:TPU:0, one launch (start us, length us, event | category | flops | bytes accessed | tf_op | source)
XLA Modules:
  0.0 673.8 jit_solution(18161551567156822964)
XLA Ops:
  18.2 3.1 broadcast_in_dim.11
  32.2 3.2 collective-permute-done.11
  39.2 4.1 collective-permute-done.3
  57.0 6.0 collective-permute-done.9
  72.5 4.2 fusion.34.rates_ref
  85.4 5.4 collective-permute-done.63
  102.6 3.6 collective-permute-done.69
  111.5 10.0 %convolution_convert_fusion.1.proj_ref.prev_ref = bf16[1024,1536]{1,0:T(8,128)(2,1)S(1)} fusion(bf16[1024,2048]{1,0:T(8,128)(2,1)} %constant_dynamic-update-slice_fusion.70, bf16[2048,1536]{1,0:T(8,128)(2,1)} %constant_dynamic-update-slice_fusion.66), kind=kOutput, calls=%fused_computation.4 | convolution fusion | flops 6444023808 | bytes 13631488 | tf_op jit(solution)/shard_map/dot_general | solution.py:723
  127.4 14.4 %shard_map.237 = (f32[1024,512]{1,0:T(8,128)}, bf16[1024,256]{1,0:T(8,128)(2,1)}, bf16[2,8,384,128]{3,2,1,0:T(8,128)(2,1)}, bf16[2,8,128,384]{3,2,1,0:T(8,128)(2...) custom-call(bf16[1024,1536]{1,0:T(8,128)(2,1)} %copy-done.38, ...), custom_call_target="tpu_custom_call" | custom-call | flops 40000000000 | bytes 16000000 | tf_op jit(solution)/shard_map/pallas_call | solution.py:200
  141.9 10.7 %all-gather = bf16[8,384,128]{2,1,0:T(8,128)(2,1)} all-gather(bf16[2,384,128]{2,1,0:T(8,128)(2,1)} %get-tuple-element.41), channel_id=2, replica_groups=mesh['seq'=4,'head'=8] {'seq'}, dimensions={0}, use_global_device_ids=true | all-gather | bytes 983040 | tf_op jit(solution)/shard_map/all_gather | solution.py:750
  154.2 11.8 %shard_map.238 = (bf16[1024,512]{1,0:T(8,128)(2,1)}, bf16[1024,512]{1,0:T(8,128)(2,1)}, bf16[1024,2048]{1,0:T(8,128)(2,1)}, bf16[2,256,128]{2,1,0:T(8,128)(2,1)}) custom-call(s32[8]{0:T(128)} %get-tuple-element.197.ids_ref, s32[1]{0:T(128)} %bitcast.1.place_ref, bf16[4,2,384,128]{3,2,1,0:T(8,128)(2,1)} %bitcast.69, ...), custom_call_target="tpu_custom_call" | custom-call | flops 8000000000 | bytes 16000000 | tf_op jit(solution)/shard_map/pallas_call | solution.py:475
  170.7 5.1 collective-permute-done.24
  182.8 3.8 collective-permute-done.25
  187.2 3.3 collective-permute-done.31
  196.5 3.7 collective-permute-done.26
  218.7 9.5 %collective-permute-done.53 = bf16[704,512]{1,0:T(8,128)(2,1)S(1)} collective-permute-done((bf16[704,512]{1,0:T(8,128)(2,1)S(1)}, bf16[704,512]{1,0:T(8,128)(2,1)S(1)}, u32[]{:S(2)}, u32[]{:S(2)}) %collective-permute-start.53) | collective-permute-done | bytes 720928 | tf_op jit(solution)/shard_map/ppermute | solution.py:660
  232.5 6.6 collective-permute-done.39
  245.8 4.7 collective-permute-done.41
  262.5 8.2 %collective-permute-done.47 = bf16[64,2048]{1,0:T(8,128)(2,1)S(1)} collective-permute-done((bf16[64,2048]{1,0:T(8,128)(2,1)S(1)}, bf16[64,2048]{1,0:T(8,128)(2,1)S(1)}, u32[]{:S(2)}, u32[]{:S(2)}) %collective-permute-start.47) | collective-permute-done | bytes 262176 | tf_op jit(solution)/shard_map/ppermute | solution.py:580
  275.5 16.6 %collective-permute-done.59 = bf16[704,512]{1,0:T(8,128)(2,1)S(1)} collective-permute-done((bf16[704,512]{1,0:T(8,128)(2,1)S(1)}, bf16[704,512]{1,0:T(8,128)(2,1)S(1)}, u32[]{:S(2)}, u32[]{:S(2)}) %collective-permute-start.59) | collective-permute-done | bytes 720928 | tf_op jit(solution)/shard_map/ppermute | solution.py:660
  292.1 3.3 fusion.35
  297.6 3.2 fusion.36
  300.8 5.7 multiply_convert_fusion.1
  306.5 3.4 convolution_convert_fusion.4
  309.9 5.7 fusion.37
  315.6 3.4 convolution_convert_fusion.5
  319.0 6.1 add_convert_fusion.1
  327.2 3.4 convolution_convert_fusion.3
  330.5 3.3 collective-permute-done.75
  339.5 3.7 convolution_convert_fusion.2
  355.0 4.6 collective-permute-done.77
  367.6 3.5 collective-permute-done.78
  380.0 6.2 collective-permute-done.89
  387.0 3.4 collective-permute-done.90
  396.4 12.6 %collective-permute-done.148 = bf16[704,512]{1,0:T(8,128)(2,1)S(1)} collective-permute-done((bf16[704,512]{1,0:T(8,128)(2,1)S(1)}, bf16[704,512]{1,0:T(8,128)(2,1)S(1)}, u32[]{:S(2)}, u32[]{:S(2)}) %collective-permute-start.148) | collective-permute-done | bytes 720928 | tf_op jit(solution)/shard_map/ppermute | solution.py:660
  414.5 8.8 %collective-permute-done.145 = bf16[704,512]{1,0:T(8,128)(2,1)S(1)} collective-permute-done((bf16[704,512]{1,0:T(8,128)(2,1)S(1)}, bf16[704,512]{1,0:T(8,128)(2,1)S(1)}, u32[]{:S(2)}, u32[]{:S(2)}) %collective-permute-start.145) | collective-permute-done | bytes 720928 | tf_op jit(solution)/shard_map/ppermute | solution.py:660
  428.9 6.7 collective-permute-done.97
  439.2 5.3 collective-permute-done.98
  446.9 13.7 %shard_map.239 = (bf16[1024,512]{1,0:T(8,128)(2,1)}, bf16[1024,512]{1,0:T(8,128)(2,1)}, f32[1,256]{1,0:T(1,128)}, f32[2,256,128]{2,1,0:T(8,128)}) custom-call(s32[8]{0:T(128)} %get-tuple-element.197.ids_ref, bf16[1024,2048]{1,0:T(8,128)(2,1)} %copy-done.25, bf16[512,2048]{1,0:T(8,128)(2,1)} %copy-done.10, bf16[1024,512]{1,0:T(8,128)(2,1)} %get-tuple-element.56.value_ref, ...), custom_call_target="tpu_custom_call" | custom-call | flops 8000000000 | bytes 16000000 | tf_op jit(solution)/shard_map/pallas_call | solution.py:542
  461.6 7.9 %all-gather.1 = bf16[8,256,128]{2,1,0:T(8,128)(2,1)} all-gather(bf16[2,256,128]{2,1,0:T(8,128)(2,1)S(1)} %convert_element_type.217), channel_id=3, replica_groups=mesh['seq'=4,'head'=8] {'seq'}, dimensions={0}, use_global_device_ids=true | all-gather | bytes 655360 | tf_op jit(solution)/shard_map/all_gather | solution.py:784
  469.5 27.1 %shard_map.240 = (bf16[1024,1536]{1,0:T(8,128)(2,1)}, f32[1024,4]{1,0:T(8,128)}, f32[4,1024]{1,0:T(4,128)}, f32[1,4]{1,0:T(1,128)}, f32[16,1024]{1,0:T(8,128)}, /*index=5*/f32[8,1024]{1,0:T(8,128)}) custom-call(bf16[1024,1536]{1,0:T(8,128)(2,1)} %copy-done.38, bf16[1024,1536]{1,0:T(8,128)(2,1)} %copy-done.38, bf16[16,1536]{1,0:T(8,128)(2,1)} %copy-done.39, ...), custom_call_target="tpu_custom_call" | custom-call | flops 60000002048 | bytes 20000000 | tf_op jit(solution)/shard_map/pallas_call | solution.py:390
  496.6 3.1 fusion.11
  499.7 4.5 fusion.13
  515.0 13.7 %multiply_reduce_fusion = (f32[2048]{0:T(1024)S(1)}, bf16[1024,2048]{1,0:T(8,128)(2,1)}) fusion(bf16[1024,2048]{1,0:T(8,128)(2,1)} %constant_dynamic-update-slice_fusion.70, f32[1024,2048]{1,0:T(8,128)} %fusion.13, bf16[1024,1536]{1,0:T(8,128)(2,1)} %slice_dynamic-update-slice_fusion, bf16[2048,1536]{1,0:T(8,128)(2,1)} %constant_dynamic-update-slice_fusion.66), kind=kOutput, calls=%fused_computation | convolution fusion | flops 6455031808 | bytes 26222592 | tf_op jit(solution)/shard_map/dot_general | solution.py:723
  530.4 9.8 %convolution_convert_fusion = bf16[2048,1536]{1,0:T(8,128)(2,1)S(1)} fusion(bf16[1024,2048]{1,0:T(8,128)(2,1)} %constant_dynamic-update-slice_fusion.70, bf16[1024,1536]{1,0:T(8,128)(2,1)} %slice_dynamic-update-slice_fusion), kind=kOutput, calls=%fused_computation.3 | convolution fusion | flops 6445596672 | bytes 13631488 | tf_op jit(solution)/shard_map/dot_general | solution.py:723
  577.0 3.2 collective-permute-done.110
  628.9 5.9 collective-permute-done.142
  643.6 27.7 %collective-permute-done.134 = bf16[512,1536]{1,0:T(8,128)(2,1)S(1)} collective-permute-done((bf16[512,1536]{1,0:T(8,128)(2,1)S(1)}, bf16[512,1536]{1,0:T(8,128)(2,1)S(1)}, u32[]{:S(2)}, u32[]{:S(2)}) %collective-permute-start.134) | collective-permute-done | bytes 1572896 | tf_op jit(solution)/shard_map/ppermute | solution.py:660
  (541 shorter events, 319.4 us)
Async XLA Ops:
  9.0 19.5 %collective-permute-start = (bf16[64,2048]{1,0:T(8,128)(2,1)S(1)}, bf16[64,2048]{1,0:T(8,128)(2,1)S(1)}, u32[]{:S(2)}, u32[]{:S(2)}) collective-permute-start(bf16[64,2048]{1,0:T(8,128)(2,1)S(1)} %get-tuple-element.189), channel_id=1, source_target_pairs={{0,1},{2,0},{4,2},{6,4},{7,6},{5,7},{3,5},{1,3},{8,9},{10,8},{12,1... | collective-permute-start | bytes 786440 | tf_op jit(solution)/shard_map/ppermute | solution.py:580
  12.0 19.7 %collective-permute-start.6 = (bf16[64,2048]{1,0:T(8,128)(2,1)S(1)}, bf16[64,2048]{1,0:T(8,128)(2,1)S(1)}, u32[]{:S(2)}, u32[]{:S(2)}) collective-permute-start(bf16[64,2048]{1,0:T(8,128)(2,1)S(1)} %get-tuple-element.189), channel_id=1, source_target_pairs={{0,2},{2,4},{4,6},{6,7},{7,5},{5,3},{3,1},{1,0},{8,10},{10,12},{12... | collective-permute-start | bytes 786440 | tf_op jit(solution)/shard_map/ppermute | solution.py:580
  12.1 14.6 %collective-permute-start.18 = (bf16[4,512]{1,0:T(4,128)(2,1)S(1)}, bf16[4,512]{1,0:T(4,128)(2,1)S(1)}, u32[]{:S(2)}, u32[]{:S(2)}) collective-permute-start(bf16[4,512]{1,0:T(4,128)(2,1)S(1)} %bitcast.77), channel_id=1, source_target_pairs={{0,8},{8,0},{16,24},{24,16},{1,9},{9,1},{17,25},{25,17},{2,10},{10... | collective-permute-start | bytes 12296 | tf_op jit(solution)/shard_map/ppermute | solution.py:660
  12.1 15.1 %collective-permute-start.19 = (bf16[4,512]{1,0:T(4,128)(2,1)S(1)}, bf16[4,512]{1,0:T(4,128)(2,1)S(1)}, u32[]{:S(2)}, u32[]{:S(2)}) collective-permute-start(bf16[4,512]{1,0:T(4,128)(2,1)S(1)} %bitcast.78), channel_id=1, source_target_pairs={{0,16},{8,24},{16,0},{24,8},{1,17},{9,25},{17,1},{25,9},{2,18},{10... | collective-permute-start | bytes 12296 | tf_op jit(solution)/shard_map/ppermute | solution.py:660
  14.0 16.1 %collective-permute-start.1 = (bf16[64,2048]{1,0:T(8,128)(2,1)S(1)}, bf16[64,2048]{1,0:T(8,128)(2,1)S(1)}, u32[]{:S(2)}, u32[]{:S(2)}) collective-permute-start(bf16[64,2048]{1,0:T(8,128)(2,1)S(1)} %get-tuple-element.187), channel_id=1, source_target_pairs={{0,1},{2,0},{4,2},{6,4},{7,6},{5,7},{3,5},{1,3},{8,9},{10,8},{12,1... | collective-permute-start | bytes 786440 | tf_op jit(solution)/shard_map/ppermute | solution.py:580
  28.4 66.9 %collective-permute-start.14 = (bf16[512,1536]{1,0:T(8,128)(2,1)S(1)}, bf16[512,1536]{1,0:T(8,128)(2,1)S(1)}, u32[]{:S(2)}, u32[]{:S(2)}) collective-permute-start(bf16[512,1536]{1,0:T(8,128)(2,1)S(1)} %copy-done.12), channel_id=1, source_target_pairs={{0,8},{8,0},{16,24},{24,16},{1,9},{9,1},{17,25},{25,17},{2,10},{10... | collective-permute-start | bytes 4718600 | tf_op jit(solution)/shard_map/ppermute | solution.py:660
  30.1 13.2 %collective-permute-start.3 = (bf16[64,2048]{1,0:T(8,128)(2,1)S(1)}, bf16[64,2048]{1,0:T(8,128)(2,1)S(1)}, u32[]{:S(2)}, u32[]{:S(2)}) collective-permute-start(bf16[64,2048]{1,0:T(8,128)(2,1)S(1)} %collective-permute-done.1), channel_id=1, source_target_pairs={{0,1},{2,0},{4,2},{6,4},{7,6},{5,7},{3,5},{1,3},{8,9},{10,8},{12,1... | collective-permute-start | bytes 786440 | tf_op jit(solution)/shard_map/ppermute | solution.py:580
  46.8 38.0 %collective-permute-start.15 = (bf16[512,1536]{1,0:T(8,128)(2,1)S(1)}, bf16[512,1536]{1,0:T(8,128)(2,1)S(1)}, u32[]{:S(2)}, u32[]{:S(2)}) collective-permute-start(bf16[512,1536]{1,0:T(8,128)(2,1)S(1)} %copy-done.12), channel_id=1, source_target_pairs={{0,16},{8,24},{16,0},{24,8},{1,17},{9,25},{17,1},{25,9},{2,18},{10... | collective-permute-start | bytes 4718600 | tf_op jit(solution)/shard_map/ppermute | solution.py:660
  49.0 16.2 %collective-permute-start.13 = (bf16[64,2048]{1,0:T(8,128)(2,1)S(1)}, bf16[64,2048]{1,0:T(8,128)(2,1)S(1)}, u32[]{:S(2)}, u32[]{:S(2)}) collective-permute-start(bf16[64,2048]{1,0:T(8,128)(2,1)S(1)} %collective-permute-done.12), channel_id=1, source_target_pairs={{0,2},{2,4},{4,6},{6,7},{7,5},{5,3},{3,1},{1,0},{8,10},{10,12},{12... | collective-permute-start | bytes 786440 | tf_op jit(solution)/shard_map/ppermute | solution.py:580
  84.8 23.4 %collective-permute-start.16 = (bf16[512,1536]{1,0:T(8,128)(2,1)S(1)}, bf16[512,1536]{1,0:T(8,128)(2,1)S(1)}, u32[]{:S(2)}, u32[]{:S(2)}) collective-permute-start(bf16[512,1536]{1,0:T(8,128)(2,1)S(1)} %collective-permute-done.15), channel_id=1, source_target_pairs={{0,8},{8,0},{16,24},{24,16},{1,9},{9,1},{17,25},{25,17},{2,10},{10... | collective-permute-start | bytes 4718600 | tf_op jit(solution)/shard_map/ppermute | solution.py:660
  93.8 14.5 %collective-permute-start.65 = (bf16[64,2048]{1,0:T(8,128)(2,1)S(1)}, bf16[64,2048]{1,0:T(8,128)(2,1)S(1)}, u32[]{:S(2)}, u32[]{:S(2)}) collective-permute-start(bf16[64,2048]{1,0:T(8,128)(2,1)S(1)} %collective-permute-done.63), channel_id=1, source_target_pairs={{0,1},{2,0},{4,2},{6,4},{7,6},{5,7},{3,5},{1,3},{8,9},{10,8},{12,1... | collective-permute-start | bytes 786440 | tf_op jit(solution)/shard_map/ppermute | solution.py:580
  100.0 82.1 %collective-permute-start.74 = (bf16[64,2048]{1,0:T(8,128)(2,1)S(1)}, bf16[64,2048]{1,0:T(8,128)(2,1)S(1)}, u32[]{:S(2)}, u32[]{:S(2)}) collective-permute-start(bf16[64,2048]{1,0:T(8,128)(2,1)S(1)} %collective-permute-done.73), channel_id=1, source_target_pairs={{0,2},{2,4},{4,6},{6,7},{7,5},{5,3},{3,1},{1,0},{8,10},{10,12},{12... | collective-permute-start | bytes 786440 | tf_op jit(solution)/shard_map/ppermute | solution.py:580
  106.2 63.1 %collective-permute-start.70 = (bf16[64,2048]{1,0:T(8,128)(2,1)S(1)}, bf16[64,2048]{1,0:T(8,128)(2,1)S(1)}, u32[]{:S(2)}, u32[]{:S(2)}) collective-permute-start(bf16[64,2048]{1,0:T(8,128)(2,1)S(1)} %collective-permute-done.69), channel_id=1, source_target_pairs={{0,2},{2,4},{4,6},{6,7},{7,5},{5,3},{3,1},{1,0},{8,10},{10,12},{12... | collective-permute-start | bytes 786440 | tf_op jit(solution)/shard_map/ppermute | solution.py:580
  106.6 63.4 %collective-permute-start.71 = (bf16[64,2048]{1,0:T(8,128)(2,1)S(1)}, bf16[64,2048]{1,0:T(8,128)(2,1)S(1)}, u32[]{:S(2)}, u32[]{:S(2)}) collective-permute-start(bf16[64,2048]{1,0:T(8,128)(2,1)S(1)} %collective-permute-done.66), channel_id=1, source_target_pairs={{0,1},{2,0},{4,2},{6,4},{7,6},{5,7},{3,5},{1,3},{8,9},{10,8},{12,1... | collective-permute-start | bytes 786440 | tf_op jit(solution)/shard_map/ppermute | solution.py:580
  123.2 29.4 %collective-permute-start.21 = (bf16[512,512]{1,0:T(8,128)(2,1)S(1)}, bf16[512,512]{1,0:T(8,128)(2,1)S(1)}, u32[]{:S(2)}, u32[]{:S(2)}) collective-permute-start(bf16[512,512]{1,0:T(8,128)(2,1)S(1)} %copy-done.18), channel_id=1, source_target_pairs={{0,8},{8,0},{16,24},{24,16},{1,9},{9,1},{17,25},{25,17},{2,10},{10... | collective-permute-start | bytes 1572872 | tf_op jit(solution)/shard_map/ppermute | solution.py:660
  124.8 17.0 %collective-permute-start.22 = (bf16[512,512]{1,0:T(8,128)(2,1)S(1)}, bf16[512,512]{1,0:T(8,128)(2,1)S(1)}, u32[]{:S(2)}, u32[]{:S(2)}) collective-permute-start(bf16[512,512]{1,0:T(8,128)(2,1)S(1)} %copy-done.18), channel_id=1, source_target_pairs={{0,16},{8,24},{16,0},{24,8},{1,17},{9,25},{17,1},{25,9},{2,18},{10... | collective-permute-start | bytes 1572872 | tf_op jit(solution)/shard_map/ppermute | solution.py:660
  209.6 18.6 %collective-permute-start.52 = (bf16[704,512]{1,0:T(8,128)(2,1)S(1)}, bf16[704,512]{1,0:T(8,128)(2,1)S(1)}, u32[]{:S(2)}, u32[]{:S(2)}) collective-permute-start(bf16[704,512]{1,0:T(8,128)(2,1)S(1)} %copy-done.15), channel_id=1, source_target_pairs={{0,8},{8,0},{16,24},{24,16},{1,9},{9,1},{17,25},{25,17},{2,10},{10... | collective-permute-start | bytes 2162696 | tf_op jit(solution)/shard_map/ppermute | solution.py:660
  211.9 16.2 %collective-permute-start.53 = (bf16[704,512]{1,0:T(8,128)(2,1)S(1)}, bf16[704,512]{1,0:T(8,128)(2,1)S(1)}, u32[]{:S(2)}, u32[]{:S(2)}) collective-permute-start(bf16[704,512]{1,0:T(8,128)(2,1)S(1)} %copy-done.15), channel_id=1, source_target_pairs={{0,16},{8,24},{16,0},{24,8},{1,17},{9,25},{17,1},{25,9},{2,18},{10... | collective-permute-start | bytes 2162696 | tf_op jit(solution)/shard_map/ppermute | solution.py:660
  217.9 14.3 %collective-permute-start.38 = (bf16[64,2048]{1,0:T(8,128)(2,1)S(1)}, bf16[64,2048]{1,0:T(8,128)(2,1)S(1)}, u32[]{:S(2)}, u32[]{:S(2)}) collective-permute-start(bf16[64,2048]{1,0:T(8,128)(2,1)S(1)} %get-tuple-element.186), channel_id=1, source_target_pairs={{0,1},{2,0},{4,2},{6,4},{7,6},{5,7},{3,5},{1,3},{8,9},{10,8},{12,1... | collective-permute-start | bytes 786440 | tf_op jit(solution)/shard_map/ppermute | solution.py:580
  228.1 16.6 %collective-permute-start.54 = (bf16[704,512]{1,0:T(8,128)(2,1)S(1)}, bf16[704,512]{1,0:T(8,128)(2,1)S(1)}, u32[]{:S(2)}, u32[]{:S(2)}) collective-permute-start(bf16[704,512]{1,0:T(8,128)(2,1)S(1)} %collective-permute-done.53), channel_id=1, source_target_pairs={{0,8},{8,0},{16,24},{24,16},{1,9},{9,1},{17,25},{25,17},{2,10},{10... | collective-permute-start | bytes 2162696 | tf_op jit(solution)/shard_map/ppermute | solution.py:660
  244.8 26.8 %collective-permute-start.55 = (bf16[704,512]{1,0:T(8,128)(2,1)S(1)}, bf16[704,512]{1,0:T(8,128)(2,1)S(1)}, u32[]{:S(2)}, u32[]{:S(2)}) collective-permute-start(bf16[704,512]{1,0:T(8,128)(2,1)S(1)} %copy-done.16), channel_id=1, source_target_pairs={{0,8},{8,0},{16,24},{24,16},{1,9},{9,1},{17,25},{25,17},{2,10},{10... | collective-permute-start | bytes 2162696 | tf_op jit(solution)/shard_map/ppermute | solution.py:660
  254.3 17.2 %collective-permute-start.56 = (bf16[704,512]{1,0:T(8,128)(2,1)S(1)}, bf16[704,512]{1,0:T(8,128)(2,1)S(1)}, u32[]{:S(2)}, u32[]{:S(2)}) collective-permute-start(bf16[704,512]{1,0:T(8,128)(2,1)S(1)} %copy-done.16), channel_id=1, source_target_pairs={{0,16},{8,24},{16,0},{24,8},{1,17},{9,25},{17,1},{25,9},{2,18},{10... | collective-permute-start | bytes 2162696 | tf_op jit(solution)/shard_map/ppermute | solution.py:660
  256.0 15.6 %collective-permute-start.51 = (bf16[64,2048]{1,0:T(8,128)(2,1)S(1)}, bf16[64,2048]{1,0:T(8,128)(2,1)S(1)}, u32[]{:S(2)}, u32[]{:S(2)}) collective-permute-start(bf16[64,2048]{1,0:T(8,128)(2,1)S(1)} %collective-permute-done.50), channel_id=1, source_target_pairs={{0,2},{2,4},{4,6},{6,7},{7,5},{5,3},{3,1},{1,0},{8,10},{10,12},{12... | collective-permute-start | bytes 786440 | tf_op jit(solution)/shard_map/ppermute | solution.py:580
  273.9 18.2 %collective-permute-start.59 = (bf16[704,512]{1,0:T(8,128)(2,1)S(1)}, bf16[704,512]{1,0:T(8,128)(2,1)S(1)}, u32[]{:S(2)}, u32[]{:S(2)}) collective-permute-start(bf16[704,512]{1,0:T(8,128)(2,1)S(1)} %copy-done.17), channel_id=1, source_target_pairs={{0,16},{8,24},{16,0},{24,8},{1,17},{9,25},{17,1},{25,9},{2,18},{10... | collective-permute-start | bytes 2162696 | tf_op jit(solution)/shard_map/ppermute | solution.py:660
  275.4 20.4 %collective-permute-start.58 = (bf16[704,512]{1,0:T(8,128)(2,1)S(1)}, bf16[704,512]{1,0:T(8,128)(2,1)S(1)}, u32[]{:S(2)}, u32[]{:S(2)}) collective-permute-start(bf16[704,512]{1,0:T(8,128)(2,1)S(1)} %copy-done.17), channel_id=1, source_target_pairs={{0,8},{8,0},{16,24},{24,16},{1,9},{9,1},{17,25},{25,17},{2,10},{10... | collective-permute-start | bytes 2162696 | tf_op jit(solution)/shard_map/ppermute | solution.py:660
  367.2 19.7 %collective-permute-start.149 = (bf16[704,512]{1,0:T(8,128)(2,1)S(1)}, bf16[704,512]{1,0:T(8,128)(2,1)S(1)}, u32[]{:S(2)}, u32[]{:S(2)}) collective-permute-start(bf16[704,512]{1,0:T(8,128)(2,1)S(1)} %get-tuple-element.173), channel_id=1, source_target_pairs={{0,8},{8,0},{16,24},{24,16},{1,9},{9,1},{17,25},{25,17},{2,10},{10... | collective-permute-start | bytes 2162696 | tf_op jit(solution)/shard_map/ppermute | solution.py:660
  371.7 24.0 %collective-permute-start.146 = (bf16[704,512]{1,0:T(8,128)(2,1)S(1)}, bf16[704,512]{1,0:T(8,128)(2,1)S(1)}, u32[]{:S(2)}, u32[]{:S(2)}) collective-permute-start(bf16[704,512]{1,0:T(8,128)(2,1)S(1)} %get-tuple-element.175), channel_id=1, source_target_pairs={{0,8},{8,0},{16,24},{24,16},{1,9},{9,1},{17,25},{25,17},{2,10},{10... | collective-permute-start | bytes 2162696 | tf_op jit(solution)/shard_map/ppermute | solution.py:660
  374.5 19.0 %collective-permute-start.151 = (bf16[704,512]{1,0:T(8,128)(2,1)S(1)}, bf16[704,512]{1,0:T(8,128)(2,1)S(1)}, u32[]{:S(2)}, u32[]{:S(2)}) collective-permute-start(bf16[704,512]{1,0:T(8,128)(2,1)S(1)} %dynamic-slice_add_fusion.1), channel_id=1, source_target_pairs={{0,16},{8,24},{16,0},{24,8},{1,17},{9,25},{17,1},{25,9},{2,18},{10... | collective-permute-start | bytes 2162696 | tf_op jit(solution)/shard_map/ppermute | solution.py:660
  386.3 22.8 %collective-permute-start.148 = (bf16[704,512]{1,0:T(8,128)(2,1)S(1)}, bf16[704,512]{1,0:T(8,128)(2,1)S(1)}, u32[]{:S(2)}, u32[]{:S(2)}) collective-permute-start(bf16[704,512]{1,0:T(8,128)(2,1)S(1)} %dynamic-slice_add_fusion.2), channel_id=1, source_target_pairs={{0,16},{8,24},{16,0},{24,8},{1,17},{9,25},{17,1},{25,9},{2,18},{10... | collective-permute-start | bytes 2162696 | tf_op jit(solution)/shard_map/ppermute | solution.py:660
  386.9 24.5 %collective-permute-start.143 = (bf16[704,512]{1,0:T(8,128)(2,1)S(1)}, bf16[704,512]{1,0:T(8,128)(2,1)S(1)}, u32[]{:S(2)}, u32[]{:S(2)}) collective-permute-start(bf16[704,512]{1,0:T(8,128)(2,1)S(1)} %get-tuple-element.177), channel_id=1, source_target_pairs={{0,8},{8,0},{16,24},{24,16},{1,9},{9,1},{17,25},{25,17},{2,10},{10... | collective-permute-start | bytes 2162696 | tf_op jit(solution)/shard_map/ppermute | solution.py:660
  390.4 32.9 %collective-permute-start.145 = (bf16[704,512]{1,0:T(8,128)(2,1)S(1)}, bf16[704,512]{1,0:T(8,128)(2,1)S(1)}, u32[]{:S(2)}, u32[]{:S(2)}) collective-permute-start(bf16[704,512]{1,0:T(8,128)(2,1)S(1)} %dynamic-slice_add_fusion.3), channel_id=1, source_target_pairs={{0,16},{8,24},{16,0},{24,8},{1,17},{9,25},{17,1},{25,9},{2,18},{10... | collective-permute-start | bytes 2162696 | tf_op jit(solution)/shard_map/ppermute | solution.py:660
  393.6 19.3 %collective-permute-start.95 = (bf16[64,2048]{1,0:T(8,128)(2,1)S(1)}, bf16[64,2048]{1,0:T(8,128)(2,1)S(1)}, u32[]{:S(2)}, u32[]{:S(2)}) collective-permute-start(bf16[64,2048]{1,0:T(8,128)(2,1)S(1)} %get-tuple-element.182), channel_id=1, source_target_pairs={{0,2},{2,4},{4,6},{6,7},{7,5},{5,3},{3,1},{1,0},{8,10},{10,12},{12... | collective-permute-start | bytes 786440 | tf_op jit(solution)/shard_map/ppermute | solution.py:580
  395.7 17.8 %collective-permute-start.100 = (bf16[64,2048]{1,0:T(8,128)(2,1)S(1)}, bf16[64,2048]{1,0:T(8,128)(2,1)S(1)}, u32[]{:S(2)}, u32[]{:S(2)}) collective-permute-start(bf16[64,2048]{1,0:T(8,128)(2,1)S(1)} %get-tuple-element.181), channel_id=1, source_target_pairs={{0,2},{2,4},{4,6},{6,7},{7,5},{5,3},{3,1},{1,0},{8,10},{10,12},{12... | collective-permute-start | bytes 786440 | tf_op jit(solution)/shard_map/ppermute | solution.py:580
  409.0 15.7 %collective-permute-start.91 = (bf16[64,2048]{1,0:T(8,128)(2,1)S(1)}, bf16[64,2048]{1,0:T(8,128)(2,1)S(1)}, u32[]{:S(2)}, u32[]{:S(2)}) collective-permute-start(bf16[64,2048]{1,0:T(8,128)(2,1)S(1)} %collective-permute-done.89), channel_id=1, source_target_pairs={{0,1},{2,0},{4,2},{6,4},{7,6},{5,7},{3,5},{1,3},{8,9},{10,8},{12,1... | collective-permute-start | bytes 786440 | tf_op jit(solution)/shard_map/ppermute | solution.py:580
  411.5 14.6 %collective-permute-start.92 = (bf16[64,2048]{1,0:T(8,128)(2,1)S(1)}, bf16[64,2048]{1,0:T(8,128)(2,1)S(1)}, u32[]{:S(2)}, u32[]{:S(2)}) collective-permute-start(bf16[64,2048]{1,0:T(8,128)(2,1)S(1)} %collective-permute-done.90), channel_id=1, source_target_pairs={{0,1},{2,0},{4,2},{6,4},{7,6},{5,7},{3,5},{1,3},{8,9},{10,8},{12,1... | collective-permute-start | bytes 786440 | tf_op jit(solution)/shard_map/ppermute | solution.py:580
  412.9 13.5 %collective-permute-start.96 = (bf16[64,2048]{1,0:T(8,128)(2,1)S(1)}, bf16[64,2048]{1,0:T(8,128)(2,1)S(1)}, u32[]{:S(2)}, u32[]{:S(2)}) collective-permute-start(bf16[64,2048]{1,0:T(8,128)(2,1)S(1)} %collective-permute-done.95), channel_id=1, source_target_pairs={{0,2},{2,4},{4,6},{6,7},{7,5},{5,3},{3,1},{1,0},{8,10},{10,12},{12... | collective-permute-start | bytes 786440 | tf_op jit(solution)/shard_map/ppermute | solution.py:580
  413.5 14.7 %collective-permute-start.101 = (bf16[64,2048]{1,0:T(8,128)(2,1)S(1)}, bf16[64,2048]{1,0:T(8,128)(2,1)S(1)}, u32[]{:S(2)}, u32[]{:S(2)}) collective-permute-start(bf16[64,2048]{1,0:T(8,128)(2,1)S(1)} %collective-permute-done.100), channel_id=1, source_target_pairs={{0,2},{2,4},{4,6},{6,7},{7,5},{5,3},{3,1},{1,0},{8,10},{10,12},{12... | collective-permute-start | bytes 786440 | tf_op jit(solution)/shard_map/ppermute | solution.py:580
  424.7 14.5 %collective-permute-start.93 = (bf16[64,2048]{1,0:T(8,128)(2,1)S(1)}, bf16[64,2048]{1,0:T(8,128)(2,1)S(1)}, u32[]{:S(2)}, u32[]{:S(2)}) collective-permute-start(bf16[64,2048]{1,0:T(8,128)(2,1)S(1)} %collective-permute-done.91), channel_id=1, source_target_pairs={{0,1},{2,0},{4,2},{6,4},{7,6},{5,7},{3,5},{1,3},{8,9},{10,8},{12,1... | collective-permute-start | bytes 786440 | tf_op jit(solution)/shard_map/ppermute | solution.py:580
  428.1 16.5 %collective-permute-start.102 = (bf16[64,2048]{1,0:T(8,128)(2,1)S(1)}, bf16[64,2048]{1,0:T(8,128)(2,1)S(1)}, u32[]{:S(2)}, u32[]{:S(2)}) collective-permute-start(bf16[64,2048]{1,0:T(8,128)(2,1)S(1)} %collective-permute-done.101), channel_id=1, source_target_pairs={{0,2},{2,4},{4,6},{6,7},{7,5},{5,3},{3,1},{1,0},{8,10},{10,12},{12... | collective-permute-start | bytes 786440 | tf_op jit(solution)/shard_map/ppermute | solution.py:580
  507.8 74.8 %collective-permute-start.141 = (bf16[512,512]{1,0:T(8,128)(2,1)}, bf16[512,512]{1,0:T(8,128)(2,1)S(1)}, u32[]{:S(2)}, u32[]{:S(2)}) collective-permute-start(bf16[512,512]{1,0:T(8,128)(2,1)} %get-tuple-element.180), channel_id=1, source_target_pairs={{0,8},{8,0},{16,24},{24,16},{1,9},{9,1},{17,25},{25,17},{2,10},{10... | collective-permute-start | bytes 1572872 | tf_op jit(solution)/shard_map/ppermute | solution.py:660
  510.8 53.0 %collective-permute-start.103 = (bf16[64,2048]{1,0:T(8,128)(2,1)}, bf16[64,2048]{1,0:T(8,128)(2,1)S(1)}, u32[]{:S(2)}, u32[]{:S(2)}) collective-permute-start(bf16[64,2048]{1,0:T(8,128)(2,1)} %get-tuple-element.139), channel_id=1, source_target_pairs={{0,2},{2,4},{4,6},{6,7},{7,5},{5,3},{3,1},{1,0},{8,10},{10,12},{12... | collective-permute-start | bytes 786440 | tf_op jit(solution)/shard_map/ppermute | solution.py:580
  512.5 51.2 %collective-permute-start.113 = (bf16[64,2048]{1,0:T(8,128)(2,1)}, bf16[64,2048]{1,0:T(8,128)(2,1)}, u32[]{:S(2)}, u32[]{:S(2)}) collective-permute-start(bf16[64,2048]{1,0:T(8,128)(2,1)} %get-tuple-element.140), channel_id=1, source_target_pairs={{0,1},{2,0},{4,2},{6,4},{7,6},{5,7},{3,5},{1,3},{8,9},{10,8},{12,1... | collective-permute-start | bytes 786440 | tf_op jit(solution)/shard_map/ppermute | solution.py:580
  548.4 19.0 %collective-permute-start.118 = (bf16[64,2048]{1,0:T(8,128)(2,1)}, bf16[64,2048]{1,0:T(8,128)(2,1)}, u32[]{:S(2)}, u32[]{:S(2)}) collective-permute-start(bf16[64,2048]{1,0:T(8,128)(2,1)} %get-tuple-element.123), channel_id=1, source_target_pairs={{0,2},{2,4},{4,6},{6,7},{7,5},{5,3},{3,1},{1,0},{8,10},{10,12},{12... | collective-permute-start | bytes 786440 | tf_op jit(solution)/shard_map/ppermute | solution.py:580
  582.6 43.8 %collective-permute-start.133 = (bf16[512,1536]{1,0:T(8,128)(2,1)S(1)}, bf16[512,1536]{1,0:T(8,128)(2,1)S(1)}, u32[]{:S(2)}, u32[]{:S(2)}) collective-permute-start(bf16[512,1536]{1,0:T(8,128)(2,1)S(1)} %copy-done.14), channel_id=1, source_target_pairs={{0,8},{8,0},{16,24},{24,16},{1,9},{9,1},{17,25},{25,17},{2,10},{10... | collective-permute-start | bytes 4718600 | tf_op jit(solution)/shard_map/ppermute | solution.py:660
  619.6 24.0 %collective-permute-start.132 = (bf16[512,1536]{1,0:T(8,128)(2,1)S(1)}, bf16[512,1536]{1,0:T(8,128)(2,1)S(1)}, u32[]{:S(2)}, u32[]{:S(2)}) collective-permute-start(bf16[512,1536]{1,0:T(8,128)(2,1)S(1)} %copy-done.13), channel_id=1, source_target_pairs={{0,8},{8,0},{16,24},{24,16},{1,9},{9,1},{17,25},{25,17},{2,10},{10... | collective-permute-start | bytes 4718600 | tf_op jit(solution)/shard_map/ppermute | solution.py:660
  621.6 13.2 %collective-permute-start.142 = (bf16[512,512]{1,0:T(8,128)(2,1)S(1)}, bf16[512,512]{1,0:T(8,128)(2,1)S(1)}, u32[]{:S(2)}, u32[]{:S(2)}) collective-permute-start(bf16[512,512]{1,0:T(8,128)(2,1)S(1)} %dynamic-slice_add_fusion.4), channel_id=1, source_target_pairs={{0,16},{8,24},{16,0},{24,8},{1,17},{9,25},{17,1},{25,9},{2,18},{10... | collective-permute-start | bytes 1572872 | tf_op jit(solution)/shard_map/ppermute | solution.py:660
  626.5 13.7 %collective-permute-start.124 = (bf16[64,2048]{1,0:T(8,128)(2,1)S(1)}, bf16[64,2048]{1,0:T(8,128)(2,1)S(1)}, u32[]{:S(2)}, u32[]{:S(2)}) collective-permute-start(bf16[64,2048]{1,0:T(8,128)(2,1)S(1)} %get-tuple-element.114), channel_id=1, source_target_pairs={{0,1},{2,0},{4,2},{6,4},{7,6},{5,7},{3,5},{1,3},{8,9},{10,8},{12,1... | collective-permute-start | bytes 786440 | tf_op jit(solution)/shard_map/ppermute | solution.py:580
  636.2 35.1 %collective-permute-start.134 = (bf16[512,1536]{1,0:T(8,128)(2,1)S(1)}, bf16[512,1536]{1,0:T(8,128)(2,1)S(1)}, u32[]{:S(2)}, u32[]{:S(2)}) collective-permute-start(bf16[512,1536]{1,0:T(8,128)(2,1)S(1)} %dynamic-slice_add_fusion), channel_id=1, source_target_pairs={{0,16},{8,24},{16,0},{24,8},{1,17},{9,25},{17,1},{25,9},{2,18},{10... | collective-permute-start | bytes 4718600 | tf_op jit(solution)/shard_map/ppermute | solution.py:660
  (149 other events, 1750.6 us)

commit v3 on v2

--- a/solution.py
+++ b/solution.py
@@ -18,6 +18,7 @@
 BF16 = jnp.bfloat16
 HALO = 16
 VMEM_LIMIT = 56 * 1024 * 1024
+LIGHT = pl.CostEstimate(flops=1, bytes_accessed=1, transcendentals=0)
 
 
 def shifted(value, axis, steps):
@@ -36,6 +37,10 @@
     return lax.dot_general(
         a, b, (((ca,), (cb,)), ((), ())), preferred_element_type=F32, precision=lax.Precision.HIGHEST
     )
+
+
+def block_columns(spots_ref, b, width):
+    return pl.ds(pl.multiple_of(spots_ref[b] * width, 128), width)
 
 
 def softplus(x):
@@ -215,16 +220,16 @@
             pltpu.VMEM((heads, DV + DK, DK), F32),
         ],
         compiler_params=pltpu.CompilerParams(vmem_limit_bytes=VMEM_LIMIT),
-        cost_estimate=pl.CostEstimate(flops=40_000_000_000, bytes_accessed=16_000_000, transcendentals=0),
+        cost_estimate=LIGHT,
     )(projected, projected, halo, rates, bias_row, taps)
 
 
 def backward_kernel(
-    heads, group, steps, peers,
+    heads, group, steps, peers, own,
     proj_ref, prev_ref, halo_ref, rates_ref, bias_ref, taps_ref,
     state_ref, uw_ref, inv_ref, trans_ref, qe_ref,
-    dout_ref, ggate_ref, value_ref, incoming_ref, place_ref, maps_ref, local_ref,
-    gp_ref, grates_ref, gtaps_ref, gbias_ref, tail_ref, lead_ref,
+    dout_ref, ggate_ref, value_ref, incoming_ref, place_ref, spots_ref, maps_ref, local_ref,
+    gp_ref, grates_ref, sums_ref, tail_ref, lead_ref,
     x_ref, d_ref, carry_ref, next_ref,
 ):
     step = pl.program_id(0)
@@ -246,12 +251,15 @@
                 grad = jnp.where(source > place_ref[0], moved, grad)
             carry_ref[h] = grad
         d_ref[rows_here : rows_here + 8, :] = jnp.zeros((8, heads * MIX), F32)
-        gtaps_ref[...] = jnp.zeros_like(gtaps_ref)
-        gbias_ref[...] = jnp.zeros_like(gbias_ref)
+        sums_ref[...] = jnp.zeros_like(sums_ref)
 
     @pl.when(step > 0)
     def _():
         d_ref[rows_here : rows_here + 8, :] = d_ref[0:8, :]
+
+    def near_row(g):
+        first = ((steps - 1 - step) * group + g) * CHUNK
+        return pl.multiple_of(spots_ref[first // own] * own + first % own, CHUNK)
 
     pairs = [(g, h) for g in range(group) for h in range(heads)]
     logits = rates_ref[...] + bias_ref[...]
@@ -351,21 +359,21 @@
         rows = slice(g * CHUNK, (g + 1) * CHUNK)
         dld = mmx(upper, dcums[g])
         drate = jnp.where(lane % 2 == 0, -sigmoid(logits[rows]) * dld, dlogits[g])
-        grates_ref[rows, :] = drate
-        gbias_ref[...] += jnp.sum(drate, axis=0, keepdims=True)
+        grates_ref[pl.ds(near_row(g), CHUNK), :] = drate
+        sums_ref[CONV : CONV + 1, : 2 * heads] += jnp.sum(drate, axis=0, keepdims=True)
     for g, h in pairs:
         cols = slice(h * MIX, (h + 1) * MIX)
         row = g * CHUNK
         dpre = d_ref[pl.ds(row, CHUNK), cols]
         total = None
         for i in range(CONV):
-            gtaps_ref[i : i + 1, cols] += jnp.sum(
+            sums_ref[i : i + 1, cols] += jnp.sum(
                 dpre * x_ref[pl.ds(row + 8 - (CONV - 1) + i, CHUNK), cols], axis=0, keepdims=True
             )
             part = taps_ref[i : i + 1, cols] * d_ref[pl.ds(row + CONV - 1 - i, CHUNK), cols]
             total = part if total is None else total + part
-        gp_ref[row : row + CHUNK, h * PER : h * PER + MIX] = total.astype(BF16)
-        gp_ref[row : row + CHUNK, h * PER + MIX : (h + 1) * PER] = ggate_ref[
+        gp_ref[pl.ds(near_row(g), CHUNK), h * PER : h * PER + MIX] = total.astype(BF16)
+        gp_ref[pl.ds(near_row(g), CHUNK), h * PER + MIX : (h + 1) * PER] = ggate_ref[
             row : row + CHUNK, h * DV : (h + 1) * DV
         ]
         if g == group - 1:
@@ -378,7 +386,7 @@
         lead_ref[...] = d_ref[0:8, :]
 
 
-def mixer_backward(projected, halo, rates, bias_row, taps, saved, dout, ggate, value, incoming, place, maps, local, group):
+def mixer_backward(projected, halo, rates, bias_row, taps, saved, dout, ggate, value, incoming, place, spots, maps, local, group):
     state, uw, inv, trans, qe = saved
     total = projected.shape[0]
     heads = rates.shape[1] // 2
@@ -388,7 +396,7 @@
     flip = lambda i: (steps - 1 - i, 0)
     keep = lambda a, b: pl.BlockSpec((heads, group, a, b), lambda i: (0, steps - 1 - i, 0, 0))
     return pl.pallas_call(
-        functools.partial(backward_kernel, heads, group, steps, maps.shape[0]),
+        functools.partial(backward_kernel, heads, group, steps, maps.shape[0], total // spots.shape[0]),
         grid=(steps,),
         in_specs=[
             pl.BlockSpec((rows, heads * PER), flip),
@@ -407,22 +415,21 @@
             pl.BlockSpec((rows, heads * DV), flip),
             pl.BlockSpec(incoming.shape, lambda i: (0, 0, 0)),
             pl.BlockSpec(memory_space=pltpu.SMEM),
+            pl.BlockSpec(memory_space=pltpu.SMEM),
             pl.BlockSpec(maps.shape, lambda i: (0, 0, 0, 0)),
             pl.BlockSpec(local.shape, lambda i: (0, 0, 0, 0)),
         ],
         out_shape=[
             jax.ShapeDtypeStruct((total, heads * PER), BF16),
             jax.ShapeDtypeStruct((total, 2 * heads), F32),
-            jax.ShapeDtypeStruct((CONV, heads * MIX), F32),
-            jax.ShapeDtypeStruct((1, 2 * heads), F32),
+            jax.ShapeDtypeStruct((8, heads * MIX), F32),
             jax.ShapeDtypeStruct((HALO, heads * MIX), F32),
             jax.ShapeDtypeStruct((8, heads * MIX), F32),
         ],
         out_specs=[
-            pl.BlockSpec((rows, heads * PER), flip),
-            pl.BlockSpec((rows, 2 * heads), flip),
-            pl.BlockSpec((CONV, heads * MIX), whole),
-            pl.BlockSpec((1, 2 * heads), whole),
+            pl.BlockSpec((total, heads * PER), whole),
+            pl.BlockSpec((total, 2 * heads), whole),
+            pl.BlockSpec((8, heads * MIX), whole),
             pl.BlockSpec((HALO, heads * MIX), whole),
             pl.BlockSpec((8, heads * MIX), whole),
         ],
@@ -433,15 +440,16 @@
             pltpu.VMEM((heads, group, DV, DK), F32),
         ],
         compiler_params=pltpu.CompilerParams(vmem_limit_bytes=VMEM_LIMIT),
-        cost_estimate=pl.CostEstimate(flops=60_000_000_000, bytes_accessed=20_000_000, transcendentals=0),
-    )(projected, projected, halo, rates, bias_row, taps, state, uw, inv, trans, qe, dout, ggate, value, incoming, place, maps, local)
+        cost_estimate=LIGHT,
+    )(projected, projected, halo, rates, bias_row, taps, state, uw, inv, trans, qe, dout, ggate, value, incoming, place, spots, maps, local)
 
 
 def gate_kernel(
     heads, peers,
-    ids_ref, place_ref, maps_ref, olocal_ref, qmap_ref, proj_ref, gain_ref, w_ref,
-    value_ref, gated_ref, part_ref, incoming_ref,
+    ids_ref, place_ref, maps_ref, olocal_ref, qmap_ref, proj_ref, gain_ref, *refs,
 ):
+    *w_refs, value_ref, gated_ref, part_ref, incoming_ref = refs
+
     @pl.when(pl.program_id(0) == 0)
     def _():
         for h in range(heads):
@@ -460,7 +468,7 @@
         normed = value * lax.rsqrt(jnp.mean(value * value, axis=-1, keepdims=True) + epsilon)
         gate = proj_ref[:, h * PER + MIX : (h + 1) * PER].astype(F32)
         gated_ref[:, cols] = (normed * gain_ref[...] * (gate * sigmoid(gate))).astype(BF16)
-    part_ref[...] = mm(gated_ref[...], w_ref[...]).astype(BF16)
+    part_ref[...] = mm(gated_ref[...], w_refs[0][...]).astype(BF16)
 
 
 def gate_output(ids, place, maps, out_local, query_map, projected, gain, w_out):
@@ -468,7 +476,7 @@
     total = projected.shape[0]
     count = ids.shape[0]
     rows = total // count
-    width = w_out.shape[1]
+    width = sum(w.shape[1] for w in w_out)
     theirs = lambda i, ids, place: (ids[i], 0)
     mine = lambda i, ids, place: (i, 0)
     whole = lambda i, ids, place: (0, 0)
@@ -483,7 +491,7 @@
                 pl.BlockSpec((rows, heads * DK), theirs),
                 pl.BlockSpec((rows, heads * PER), theirs),
                 pl.BlockSpec((1, DV), whole),
-                pl.BlockSpec(w_out.shape, whole),
+                *[pl.BlockSpec(w.shape, whole) for w in w_out],
             ],
             out_specs=[
                 pl.BlockSpec((rows, heads * DV), theirs),
@@ -499,21 +507,22 @@
             jax.ShapeDtypeStruct((heads, DV, DK), BF16),
         ],
         compiler_params=pltpu.CompilerParams(vmem_limit_bytes=VMEM_LIMIT),
-        cost_estimate=pl.CostEstimate(flops=8_000_000_000, bytes_accessed=16_000_000, transcendentals=0),
-    )(ids, place, maps, out_local, query_map, projected, gain, w_out)
+        cost_estimate=LIGHT,
+    )(ids, place, maps, out_local, query_map, projected, gain, *w_out)
 
 
 def gate_back_kernel(
     heads,
-    ids_ref, branch_ref, w_ref, value_ref, proj_ref, qmap_ref, gain_ref,
-    ggate_ref, dout_ref, gain_grad_ref, local_ref,
+    ids_ref, branch_ref, value_ref, proj_ref, qmap_ref, gain_ref, *refs,
 ):
+    *w_refs, ggate_ref, dout_ref, gain_grad_ref, local_ref = refs
+
     @pl.when(pl.program_id(0) == 0)
     def _():
         gain_grad_ref[...] = jnp.zeros_like(gain_grad_ref)
         local_ref[...] = jnp.zeros_like(local_ref)
 
-    grads = mm(branch_ref[...], w_ref[...], 1, 1)
+    grads = mm(branch_ref[...], w_refs[0][...], 1, 1)
     gain = gain_ref[...]
     for h in range(heads):
         cols = slice(h * DV, (h + 1) * DV)
@@ -546,11 +555,11 @@
             grid=(count,),
             in_specs=[
                 pl.BlockSpec((rows, branch.shape[1]), mine),
-                pl.BlockSpec(w_out.shape, whole),
                 pl.BlockSpec((rows, heads * DV), theirs),
                 pl.BlockSpec((rows, heads * PER), theirs),
                 pl.BlockSpec((rows, heads * DK), theirs),
                 pl.BlockSpec((1, DV), whole),
+                *[pl.BlockSpec(w.shape, whole) for w in w_out],
             ],
             out_specs=[
                 pl.BlockSpec((rows, heads * DV), theirs),
@@ -566,10 +575,225 @@
             jax.ShapeDtypeStruct((heads, DV, DK), F32),
         ],
         compiler_params=pltpu.CompilerParams(vmem_limit_bytes=VMEM_LIMIT),
-        cost_estimate=pl.CostEstimate(flops=8_000_000_000, bytes_accessed=16_000_000, transcendentals=0),
-    )(ids, branch, w_out, value, projected, query_map, gain)
-
-
+        cost_estimate=LIGHT,
+    )(ids, branch, value, projected, query_map, gain, *w_out)
+
+
+def project_kernel(layout, pieces, ids_ref, spots_ref, rate_ref, *refs):
+    x_refs = refs[: len(layout)]
+    w_refs = refs[len(layout) : len(layout) + pieces]
+    out_ref, rates_ref = refs[len(layout) + pieces :]
+    rows = out_ref.shape[0] // ids_ref.shape[0]
+    blocks = {}
+    for (k, _), ref in zip(layout, x_refs):
+        blocks.setdefault(k, []).append(ref)
+    ks = list(blocks)
+    for first in range(0, len(ks), 2):
+        group = ks[first : first + 2]
+        group_refs = [ref for k in group for ref in blocks[k]]
+        x = jnp.concatenate([ref[...] for ref in group_refs], axis=0)
+        total = None
+        for b, w_ref in enumerate(w_refs):
+            cols = block_columns(spots_ref, b, w_ref.shape[0])
+            share = mm(jnp.concatenate([ref[:, cols] for ref in group_refs], axis=0), w_ref[...])
+            total = share if total is None else total + share
+        total = total.astype(BF16)
+        rates = mm(x, rate_ref[...], 1, 1)
+        for i, k in enumerate(group):
+            place = pl.ds(pl.multiple_of(ids_ref[k] * rows, rows), rows)
+            out_ref[place, :] = total[i * rows : (i + 1) * rows]
+            rates_ref[place, :] = rates[i * rows : (i + 1) * rows]
+
+
+def layout_of(found, total):
+    rows = found[0][0].shape[0]
+    count = total // rows
+    ks = [0] + [k for s in range(1, count // 2) for k in (s, count - s)] + [count // 2]
+    layout, arrays = [], []
+    for k in ks:
+        start = k * rows
+        for piece in found.get(k, ()):
+            layout.append((k, start))
+            arrays.append(piece)
+            start += piece.shape[0]
+    return layout, arrays
+
+
+def project(ids, spots, found, w_mix, w_rate):
+    total = ids.shape[0] * found[0][0].shape[0]
+    layout, arrays = layout_of(found, total)
+    cols = w_mix[0].shape[1]
+    rates = w_rate.shape[0]
+    whole = lambda shape: pl.BlockSpec(shape, lambda i, ids, spots: (0, 0))
+    return pl.pallas_call(
+        functools.partial(project_kernel, layout, len(w_mix)),
+        grid_spec=pltpu.PrefetchScalarGridSpec(
+            num_scalar_prefetch=2,
+            grid=(1,),
+            in_specs=[whole(a.shape) for a in (w_rate, *arrays, *w_mix)],
+            out_specs=[whole((total, cols)), whole((total, rates))],
+        ),
+        out_shape=[
+            jax.ShapeDtypeStruct((total, cols), BF16),
+            jax.ShapeDtypeStruct((total, rates), F32),
+        ],
+        compiler_params=pltpu.CompilerParams(vmem_limit_bytes=VMEM_LIMIT),
+        cost_estimate=LIGHT,
+    )(ids, spots, w_rate, *arrays, *w_mix)
+
+
+def normed_back_kernel(pieces, blocks, spots_ref, *refs):
+    grads, rates, normed = refs[:blocks], refs[blocks : 2 * blocks], refs[2 * blocks : 3 * blocks]
+    rate_ref, before_ref = refs[3 * blocks : 3 * blocks + 2]
+    w_refs = refs[3 * blocks + 2 : 3 * blocks + 2 + pieces]
+    part_ref, sums_ref = refs[3 * blocks + 2 + pieces :]
+    left = jnp.concatenate([ref[...] for ref in grads], axis=0)
+    rate = jnp.concatenate([ref[...].astype(BF16) for ref in rates], axis=0)
+    count = rate.shape[1]
+    sums_ref[...] = before_ref[...]
+    for b, w_ref in enumerate(w_refs):
+        cols = block_columns(spots_ref, b, w_ref.shape[0])
+        part = mm(left, w_ref[...], 1, 1) + mm(rate, rate_ref[:, cols])
+        part_ref[:, cols] = part.astype(BF16)
+        right = jnp.concatenate([ref[:, cols] for ref in normed], axis=0)
+        sums_ref[:count, cols] += mm(rate, right, 0, 0)
+        sums_ref[4:5, cols] += jnp.sum(part * right.astype(F32), axis=0, keepdims=True)
+
+
+def normed_back(spots, order, blocks, grad_projected, grad_rates, normed, w_mix, w_rate, before):
+    total, width = normed.shape
+    rows = total // blocks
+    cols = w_mix[0].shape[1]
+    rates = w_rate.shape[0]
+    count = len(order)
+    block = lambda k, wide: pl.BlockSpec((rows, wide), lambda i, spots: (k, 0))
+    whole = lambda i, spots: (0, 0)
+    return pl.pallas_call(
+        functools.partial(normed_back_kernel, len(w_mix), count),
+        grid_spec=pltpu.PrefetchScalarGridSpec(
+            num_scalar_prefetch=1,
+            grid=(1,),
+            in_specs=[
+                *[block(k, cols) for k in order],
+                *[block(k, rates) for k in order],
+                *[block(k, width) for k in order],
+                pl.BlockSpec((rates, width), whole),
+                pl.BlockSpec((8, width), whole),
+                *[pl.BlockSpec(w.shape, whole) for w in w_mix],
+            ],
+            out_specs=[pl.BlockSpec((count * rows, width), whole), pl.BlockSpec((8, width), whole)],
+        ),
+        out_shape=[
+            jax.ShapeDtypeStruct((count * rows, width), BF16),
+            jax.ShapeDtypeStruct((8, width), F32),
+        ],
+        compiler_params=pltpu.CompilerParams(vmem_limit_bytes=VMEM_LIMIT),
+        cost_estimate=LIGHT,
+    )(
+        spots,
+        *[grad_projected] * count,
+        *[grad_rates] * count,
+        *[normed] * count,
+        w_rate,
+        before,
+        *w_mix,
+    )
+
+
+def stack_kernel(layout, *refs):
+    out_ref = refs[len(layout)]
+    for (_, start), ref in zip(layout, refs):
+        out_ref[start : start + ref.shape[0], :] = ref[...]
+
+
+def stacked(found, total):
+    layout, arrays = layout_of(found, total)
+    return pl.pallas_call(
+        functools.partial(stack_kernel, layout),
+        out_shape=jax.ShapeDtypeStruct((total, arrays[0].shape[1]), arrays[0].dtype),
+        compiler_params=pltpu.CompilerParams(vmem_limit_bytes=VMEM_LIMIT),
+        cost_estimate=LIGHT,
+    )(*arrays)
+
+
+def finish_kernel(first_ref, second_ref, buffer_ref, out_ref):
+    half = first_ref.shape[0]
+    out_ref[:half, :] = first_ref[...]
+    out_ref[half:, :] = second_ref[...]
+
+
+def finish_stack(buffer, pieces, k):
+    half, width = pieces[0].shape
+    whole = pl.BlockSpec((half, width), lambda i: (0, 0))
+    return pl.pallas_call(
+        finish_kernel,
+        grid=(1,),
+        in_specs=[whole, whole, pl.BlockSpec(memory_space=pl.ANY)],
+        out_specs=pl.BlockSpec((2 * half, width), lambda i: (k, 0)),
+        out_shape=jax.ShapeDtypeStruct(buffer.shape, buffer.dtype),
+        input_output_aliases={2: 0},
+        cost_estimate=LIGHT,
+    )(*pieces, buffer)
+
+
+def outer_kernel(pieces, spots_ref, left_ref, right_ref, *outs):
+    product = mm(left_ref[...], right_ref[...], 0, 0).astype(BF16)
+    for b in range(pieces):
+
+        @pl.when(pl.program_id(0) == b)
+        def _(b=b):
+            outs[b][...] = product
+
+
+def outer(spots, left, right, part, parts):
+    total, m = left.shape
+    pieces = spots.shape[0]
+    n = right.shape[1] // parts
+    shape = (m // pieces, n)
+    return pl.pallas_call(
+        functools.partial(outer_kernel, pieces),
+        grid_spec=pltpu.PrefetchScalarGridSpec(
+            num_scalar_prefetch=1,
+            grid=(pieces,),
+            in_specs=[
+                pl.BlockSpec((total, m // pieces), lambda i, spots: (0, spots[i])),
+                pl.BlockSpec((total, n), lambda i, spots: (0, part)),
+            ],
+            out_specs=[pl.BlockSpec(shape, lambda i, spots: (0, 0))] * pieces,
+        ),
+        out_shape=[jax.ShapeDtypeStruct(shape, BF16)] * pieces,
+        compiler_params=pltpu.CompilerParams(vmem_limit_bytes=VMEM_LIMIT),
+        cost_estimate=LIGHT,
+    )(spots, left, right)
+
+
+def add_kernel(sizes, *refs):
+    outs = refs[3 * sum(sizes) :]
+    at = 0
+    for out_ref, size in zip(outs, sizes):
+        start = 0
+        for _ in range(size):
+            one, two, three = refs[at : at + 3]
+            cols = slice(start, start + one.shape[1])
+            out_ref[:, cols] = one[...].astype(F32) + two[...].astype(F32) + three[...].astype(F32)
+            start += one.shape[1]
+            at += 3
+
+
+def add_all(groups):
+    steps = 4
+    flat = [a for group in groups for triple in group for a in triple]
+    spec = lambda rows, wide: pl.BlockSpec((rows // steps, wide), lambda i: (i, 0))
+    shapes = [(group[0][0].shape[0], sum(t[0].shape[1] for t in group)) for group in groups]
+    return pl.pallas_call(
+        functools.partial(add_kernel, [len(group) for group in groups]),
+        grid=(steps,),
+        in_specs=[spec(*a.shape) for a in flat],
+        out_specs=[spec(*shape) for shape in shapes],
+        out_shape=[jax.ShapeDtypeStruct(shape, F32) for shape in shapes],
+        compiler_params=pltpu.CompilerParams(vmem_limit_bytes=VMEM_LIMIT),
+        cost_estimate=LIGHT,
+    )(*flat)
 def ring_order(count):
     return list(range(0, count, 2)) + list(range(1, count, 2))[::-1]
 
@@ -584,75 +808,85 @@
     order = ring_order(lax.axis_size(axis))
     count = len(order)
     place = {device: i for i, device in enumerate(order)}
-    table = [[order[(place[device] + k) % count] for k in range(count)] for device in range(count)]
-    return lax.dynamic_index_in_dim(jnp.array(table, jnp.int32), lax.axis_index(axis), 0, False)
-
-
-def ring_gather(shard, axis):
+    ahead = [[order[(place[device] + k) % count] for k in range(count)] for device in range(count)]
+    back = [[row.index(device) for device in range(count)] for row in ahead]
+    row = lax.dynamic_index_in_dim(
+        jnp.array([a + b for a, b in zip(ahead, back)], jnp.int32), lax.axis_index(axis), 0, False
+    )
+    return row[:count], row[count:]
+
+
+def after(value, *earlier):
+    return lax.optimization_barrier((value, *earlier))[0]
+
+
+def together(*values):
+    return lax.optimization_barrier(values)
+
+
+def window(fillers, hop, gate):
+    return fillers[hop](lambda value: after(value, gate)) if hop in fillers else ()
+
+
+def ring_gather(shard, axis, fillers={}, stack=True):
     count = lax.axis_size(axis)
+    far = count // 2
     half = shard.shape[0] // 2
-    halves = []
-    for part in range(2):
-        piece = shard[part * half : (part + 1) * half]
-        found = {0: piece}
-        forward = backward = piece
-        for s in range(1, count // 2):
+    total = count * shard.shape[0]
+    found = {0: [shard]}
+    forward = backward = shard
+    buffer = None
+    for hop in range(1, far + 1):
+        gate = forward
+        extra = list(window(fillers, hop, gate))
+        if hop < far:
             forward = ring_step(forward, axis, 1)
             backward = ring_step(backward, axis, -1)
-            found[count - s] = forward
-            found[s] = backward
-        if count > 1:
-            found[count // 2] = ring_step(forward if part == 0 else backward, axis, 1 if part == 0 else -1)
-        halves.append(found)
-    return halves
-
-
-def gathered_near(halves):
-    count = len(halves[0])
-    return jnp.concatenate([found[k] for k in range(count) for found in halves], axis=0)
-
-
-def gathered_whole(halves, ids):
-    count = len(halves[0])
-    half, width = halves[0][0].shape
-    buffer = jnp.zeros((count * 2 * half, width), halves[0][0].dtype)
-    for k in range(count):
-        for part, found in enumerate(halves):
-            buffer = lax.dynamic_update_slice(buffer, found[k], (ids[k] * (2 * half) + part * half, 0))
-    return buffer
-
-
-def ring_scatter(take, rows, axis):
+            found[count - hop] = [forward]
+            found[hop] = [backward]
+        else:
+            if stack:
+                buffer = stacked({k: [after(p, gate) for p in ps] for k, ps in found.items()}, total)
+                extra.append(buffer)
+            forward = ring_step(forward[:half], axis, 1)
+            backward = ring_step(backward[half:], axis, -1)
+            found[hop] = [forward, backward]
+        forward, backward, *_ = together(forward, backward, *extra)
+    found[far] = [forward, backward]
+    return finish_stack(buffer, found[far], far) if stack else found
+
+
+def ring_scatter(take, rows, axis, fillers={}):
     count = lax.axis_size(axis)
-    half = rows // 2
-    totals = []
-    for part in range(2):
-        piece = lambda k: take(k, part * half, half)
-        forward = backward = None
-        if count > 1:
-            if part == 0:
-                forward = ring_step(piece(count // 2), axis, 1)
-            else:
-                backward = ring_step(piece(count // 2), axis, -1)
-        for s in range(count // 2 - 1, 0, -1):
-            forward = piece(s) if forward is None else forward + piece(s)
-            backward = piece(count - s) if backward is None else backward + piece(count - s)
-            forward = ring_step(forward, axis, 1)
-            backward = ring_step(backward, axis, -1)
-        total = piece(0).astype(F32)
-        for other in (forward, backward):
-            if other is not None:
-                total = total + other.astype(F32)
-        totals.append(total)
+    far = count // 2
+    size = rows // 2
+    flows = [[take(far, 0, size), None], [None, take(far, size, size)]]
+    gate = take(far, 0, size)
+    for hop in range(1, far + 1):
+        flows = [
+            [flow[way] if flow[way] is None else ring_step(flow[way], axis, 1 - 2 * way) for way in range(2)]
+            for flow in flows
+        ]
+        extra = window(fillers, hop, gate)
+        flat = together(*[a for flow in flows for a in flow if a is not None], *extra)
+        flat = iter(flat)
+        flows = [[None if a is None else next(flat) for a in flow] for flow in flows]
+        s = far - hop
+        if s:
+            for part, flow in enumerate(flows):
+                for way, k in enumerate((s, count - s)):
+                    piece = take(k, part * size, size)
+                    flow[way] = piece if flow[way] is None else flow[way] + piece
+            gate = flows[0][0]
+    totals = [
+        take(0, part * size, size).astype(F32) + flow[0].astype(F32) + flow[1].astype(F32)
+        for part, flow in enumerate(flows)
+    ]
     return jnp.concatenate(totals, axis=0)
 
 
 def near_rows(array, rows):
     return lambda k, start, size: lax.slice_in_dim(array, k * rows + start, k * rows + start + size, axis=0)
-
-
-def whole_rows(array, rows, ids):
-    return lambda k, start, size: lax.dynamic_slice_in_dim(array, ids[k] * rows + start, size, 0)
 
 
 def swap(value, axis, bit):
@@ -660,45 +894,43 @@
     return lax.ppermute(value, axis, [(i, i ^ bit) for i in range(count)])
 
 
-def pair_gather(shard, axis, dim):
+def pair_spots(axis):
+    count = lax.axis_size(axis)
+    order = jnp.arange(count, dtype=jnp.int32)
+    return lax.axis_index(axis) ^ order if count == 4 else order
+
+
+def pair_far(shard, axis, *pins):
     if lax.axis_size(axis) != 4:
-        return lax.all_gather(shard, axis, axis=dim, tiled=True)
-    me = lax.axis_index(axis)
-    far = swap(shard, axis, 2)
-    near = swap(shard, axis, 1)
-    both = swap(far, axis, 1)
-    size = shard.shape[dim]
-    shape = list(shard.shape)
-    shape[dim] = 4 * size
-    buffer = jnp.zeros(shape, shard.dtype)
-    for bit, piece in enumerate((shard, near, far, both)):
-        buffer = lax.dynamic_update_slice_in_dim(buffer, piece, (me ^ bit) * size, dim)
-    return buffer
-
-
-def pair_scatter(array, axis, dim):
+        return lax.all_gather(shard, axis)
+    return swap(after(shard, *pins), axis, 2)
+
+
+def pair_gather(shard, far, axis, *pins):
+    count = lax.axis_size(axis)
+    if count != 4:
+        return [far[b] for b in range(count)]
+    return [shard, swap(after(shard, *pins), axis, 1), far, swap(after(far, *pins), axis, 1)]
+
+
+def pair_across(pieces, axis):
     if lax.axis_size(axis) != 4:
-        return lax.psum_scatter(array, axis, scatter_dimension=dim, tiled=True).astype(F32)
-    me = lax.axis_index(axis)
-    size = array.shape[dim] // 4
-    piece = lambda bit: lax.dynamic_slice_in_dim(array, (me ^ bit) * size, size, dim)
-    across = swap(piece(3), axis, 1)
-    near = swap(piece(1), axis, 1)
-    far = swap(piece(2) + across, axis, 2)
-    return piece(0).astype(F32) + near.astype(F32) + far.astype(F32)
-
-
-def butterfly(value, axis):
+        return None
+    return swap(pieces[3], axis, 1), swap(pieces[1], axis, 1)
+
+
+def pair_far_sum(pieces, crossed, axis, pin):
+    if crossed is None:
+        return lax.psum_scatter(jnp.stack(pieces), axis, scatter_dimension=0)
+    return swap(pin(pieces[2]) + crossed[0], axis, 2)
+
+
+def round_sum(value, axis):
     count = lax.axis_size(axis)
-    bit = 1
-    while bit < count:
-        value = value + swap(value, axis, bit)
-        bit *= 2
-    return value
-
-
-def after(value, *earlier):
-    return lax.optimization_barrier((value, *earlier))[0]
+    level = [value] + [swap(value, axis, bit) for bit in range(1, count)]
+    while len(level) > 1:
+        level = [level[i] + level[i + 1] for i in range(0, len(level), 2)]
+    return level[0]
 
 
 def per_device(
@@ -722,41 +954,122 @@
     rows_first = (((0,), (0,)), ((), ()))
     dot = lambda a, b, dims: lax.dot_general(a, b, dims, preferred_element_type=F32)
     plain = (((1,), (0,)), ((), ()))
-    ids = ring_ids("head")
+    ids, near_spots = ring_ids("head")
+    spots = pair_spots("seq")
     place = lax.axis_index("seq").reshape(1)
     gain_row = head_gain.reshape(1, DV)
     bias_row = head_bias.T.reshape(1, 2 * heads)
-
+    peers = lax.axis_size("seq")
+    width = tokens.shape[1]
+    keep = {}
+    mix_far = pair_far(w_qkvg, "seq")
     inputs = tokens.astype(F32)
     inverse_one = lax.rsqrt(jnp.mean(inputs * inputs, axis=-1, keepdims=True) + epsilon)
     norm_normed = inputs * inverse_one
-    normed_halves = ring_gather((norm_normed * norm_gain).astype(BF16), "head")
-    w_mix = pair_gather(w_qkvg, "seq", 0)
-    w_rate = pair_gather(w_rates.T, "seq", 1)
-    out_rows = pair_gather(after(w_out, w_mix), "seq", 1)
-    gate_w = pair_gather(after(w_ff_gate, out_rows), "seq", 1)
-    up_w = pair_gather(after(w_ff_up, gate_w), "seq", 1)
-    down_w = pair_gather(after(w_ff_down, up_w), "seq", 1)
-    normed = gathered_whole(normed_halves, ids)
-    seq_rows = normed.shape[0]
-    cotangent_near = gathered_near(ring_gather(after(cotangent, normed), "head"))
-
-    projected = dot(normed, w_mix, plain).astype(BF16)
-    rates = dot(normed, w_rate, contract)
+    hops = lax.axis_size("head") // 2
+    last_window = hops
+
+    rate_shard = w_rates.T
+    if peers == 4:
+        w_rate = jnp.zeros((2 * heads, width), BF16)
+        for b in range(4):
+            w_rate = lax.dynamic_update_slice_in_dim(
+                w_rate,
+                swap(rate_shard, "seq", b) if b else rate_shard,
+                (place[0] ^ b) * rate_shard.shape[1],
+                1,
+            )
+    else:
+        w_rate = lax.all_gather(rate_shard, "seq", axis=1, tiled=True)
+
+    count = 2 * hops
+    stages = 4
+    cot_found = {0: [cotangent]}
+    cot_state = [cotangent, cotangent]
+
+    def cot_hop(hop, *gates):
+        forward, backward, *_ = together(*cot_state, *gates)
+        if hop < hops:
+            forward, backward = ring_step(forward, "head", 1), ring_step(backward, "head", -1)
+            cot_found[count - hop], cot_found[hop] = [forward], [backward]
+        else:
+            half = own_rows // 2
+            forward = ring_step(forward[:half], "head", 1)
+            backward = ring_step(backward[half:], "head", -1)
+            cot_found[hop] = [forward, backward]
+        cot_state[:] = [forward, backward]
+        return list(cot_state)
+
+    def fetch_mix(pin):
+        keep["mix"] = pair_gather(w_qkvg, pin(mix_far), "seq")
+        return keep["mix"]
+
+    def cot_window(hop, other=lambda pin: []):
+        def filler(pin):
+            made = list(other(pin))
+            forward, backward = cot_state
+            cot_state[:] = [pin(forward), pin(backward)]
+            return made + cot_hop(hop)
+
+        return filler
+
+    fillers = {last_window: cot_window(1)} | {last_window - 1: fetch_mix}
+    normed_found = ring_gather((norm_normed * norm_gain).astype(BF16), "head", fillers, False)
+    w_mix = keep["mix"]
+    out_rows = lax.all_gather(after(w_out, mix_far), "seq", axis=1, tiled=True)
+
+    stage_hops = {
+        stage: range(2 + (hops - 1) * stage // 3, 2 + (hops - 1) * (stage + 1) // 3) for stage in range(3)
+    }
+
+    def cot_stage(stage, gate):
+        made = []
+        for hop in stage_hops[stage]:
+            made = cot_hop(hop, gate)
+        return made
+
+    cot_stage(0, normed_found[hops][0])
+    projected, rates = project(ids, spots, normed_found, w_mix, w_rate)
+    seq_rows = projected.shape[0]
     halo_rows = shifted(projected[seq_rows - HALO :], "seq", 1)
+    projected, *_ = together(projected, *cot_state)
+    cot_stage(1, projected)
     out_local, query_map, *saved, end_state = mixer_forward(
         projected, halo_rows, rates, bias_row, conv_weight, GROUP
     )
+    end_state, *_ = together(end_state, *cot_state)
     maps = lax.all_gather(end_state, "seq")
+    cot_stage(2, maps)
     value, gated, branch_part, incoming = gate_output(
-        ids, place, maps, out_local, query_map, projected, gain_row, out_rows
-    )
-    residual = inputs + ring_scatter(near_rows(branch_part, own_rows), own_rows, "head")
+        ids, place, maps, out_local, query_map, projected, gain_row, [out_rows]
+    )
+    branch_part, *_ = together(branch_part, *cot_state)
+    fetch = lambda w, *pins: lax.all_gather(after(w, *pins), "seq", axis=1, tiled=True)
+    down_w = fetch(w_ff_down, maps)
+    gate_w = fetch(w_ff_gate, maps)
+    up_w = fetch(w_ff_up, maps)
+
+    def stack_normed(pin):
+        keep["normed"] = stacked({k: [pin(p) for p in ps] for k, ps in normed_found.items()}, seq_rows)
+        return (keep["normed"],)
+
+    def stack_cotangent(pin):
+        keep["cot"] = stacked({k: [pin(p) for p in ps] for k, ps in cot_found.items()}, seq_rows)
+        return (keep["cot"],)
+
+    residual = inputs + ring_scatter(
+        near_rows(branch_part, own_rows), own_rows, "head", {1: stack_cotangent, 2: stack_normed}
+    )
     inverse_two = lax.rsqrt(jnp.mean(residual * residual, axis=-1, keepdims=True) + epsilon)
     mlp_normed = residual * inverse_two
-    mlp_near = gathered_near(ring_gather((mlp_normed * mlp_gain).astype(BF16), "head"))
-
-    grad_hidden = dot(cotangent_near, down_w, contract)
+
+    def hidden_gradient(pin):
+        keep["gh"] = dot(pin(keep["cot"]), down_w, contract)
+        return (keep["gh"],)
+
+    mlp_near = ring_gather((mlp_normed * mlp_gain).astype(BF16), "head", {2: hidden_gradient})
+    normed, cotangent_near, grad_hidden = keep["normed"], keep["cot"], keep["gh"]
+
     gate_pre = dot(mlp_near, gate_w, contract)
     up_pre = dot(mlp_near, up_w, contract)
     ff_sigmoid = jax.nn.sigmoid(gate_pre)
@@ -766,81 +1079,180 @@
     grad_gate_pre = (grad_hidden * up_pre * ff_slope).astype(BF16)
     grad_up_pre = (grad_hidden * ff_silu).astype(BF16)
     grad_mlp_part = (dot(grad_gate_pre, gate_w, plain) + dot(grad_up_pre, up_w, plain)).astype(BF16)
-    grad_mlp_in = ring_scatter(near_rows(grad_mlp_part, own_rows), own_rows, "head")
-
-    grad_down_s = pair_scatter(dot(hidden, cotangent_near, rows_first).astype(BF16), "seq", 1)
-    grad_gate_s = pair_scatter(dot(grad_gate_pre, mlp_near, rows_first).astype(BF16), "seq", 1)
-    grad_up_s = pair_scatter(dot(grad_up_pre, mlp_near, rows_first).astype(BF16), "seq", 1)
-
+
+    def weight_product(name, left, right):
+        def filler(pin):
+            keep[name] = dot(pin(left), right, rows_first).astype(BF16)
+            return (keep[name],)
+
+        return filler
+
+    scatter = lambda a: lax.psum_scatter(a, "seq", scatter_dimension=1, tiled=True).astype(F32)
+
+    def output_rows(pin):
+        keep["output"] = dot(pin(hidden), down_w, plain).astype(BF16)
+        return (keep["output"],)
+
+    grad_mlp_in = ring_scatter(
+        near_rows(grad_mlp_part, own_rows),
+        own_rows,
+        "head",
+        {
+            1: weight_product("down", hidden, cotangent_near),
+            2: weight_product("gate", grad_gate_pre, mlp_near),
+            3: weight_product("up", grad_up_pre, mlp_near),
+            4: output_rows,
+        },
+    )
+
+    output_part = keep["output"]
     mlp_gain_part = jnp.sum(grad_mlp_in * mlp_normed, axis=0)
     scaled_two = grad_mlp_in * mlp_gain
     grad_residual = cotangent.astype(F32) + inverse_two * (
         scaled_two - mlp_normed * jnp.mean(scaled_two * mlp_normed, axis=-1, keepdims=True)
     )
-    branch_near = gathered_near(ring_gather(grad_residual.astype(BF16), "head"))
+
+    def total_all(groups, pin=lambda value: value):
+        if peers == 4:
+            sums = add_all(
+                [[(keep[n][0], keep[n, "crossed"][1], pin(keep[n, "far"])) for n in group] for group in groups]
+            )
+        else:
+            sums = [
+                jnp.concatenate([keep[n, "far"].astype(F32) for n in group], axis=1) for group in groups
+            ]
+        for group, value in zip(groups, sums):
+            keep[group[0], "total"] = value
+        return sums
+
+    def far_sums(*names):
+        def filler(pin):
+            for name in names:
+                keep[name, "far"] = pair_far_sum(keep[name], keep[name, "crossed"], "seq", pin)
+            return [keep[name, "far"] for name in names]
+
+        return filler
+
+    grad_down_s = scatter(keep["down"])
+    grad_gate_s = scatter(keep["gate"])
+    grad_up_s = scatter(keep["up"])
+    branch_near = ring_gather(grad_residual.astype(BF16), "head")
+    take_output = near_rows(output_part, own_rows)
+    output_state = [None, None]
+    known = lambda: [a for a in output_state if a is not None]
+
+    def output_hops(stage, *gates):
+        for hop in range(hops * (stage - 1) // stages, hops * stage // stages):
+            here = []
+            for way, k in enumerate((hops - hop, count - hops + hop)):
+                if hop == 0 and way == 1:
+                    here.append(None)
+                    continue
+                piece = take_output(k, 0, own_rows)
+                total = piece if output_state[way] is None else output_state[way] + piece
+                here.append(ring_step(after(total, *gates), "head", 1 - 2 * way))
+            output_state[:] = here
+
+    output_hops(1, branch_near)
     grad_gate_mix, grad_mixer, head_gain_part, local_grad = gate_backward(
-        ids, branch_near, out_rows, value, projected, query_map, gain_row, heads
-    )
-    locals_all = lax.all_gather(local_grad.astype(BF16), "seq")
-    output_part = after(dot(hidden, down_w, plain).astype(BF16), branch_near)
-    output = (residual + ring_scatter(near_rows(output_part, own_rows), own_rows, "head")).astype(BF16)
-    grad_out_s = pair_scatter(dot(gated, branch_near, rows_first).astype(BF16), "seq", 1)
-
-    grad_projected, grad_rates, grad_taps, grad_bias_row, tail_rows, lead_rows = mixer_backward(
+        ids, branch_near, [out_rows], value, projected, query_map, gain_row, heads
+    )
+    local_low, *_ = together(local_grad.astype(BF16), *known())
+    output_hops(2, local_low)
+    locals_all = lax.all_gather(local_low, "seq")
+    grad_projected, grad_rates, seq_sums, tail_rows, lead_rows = mixer_backward(
         projected, halo_rows, rates, bias_row, conv_weight, saved,
-        grad_mixer, grad_gate_mix, value, incoming, place, maps, locals_all, GROUP,
-    )
+        grad_mixer, grad_gate_mix, value, incoming, place, near_spots, maps, locals_all, GROUP,
+    )
+    grad_projected, *_ = together(grad_projected, *known())
     later_rows = shifted(lead_rows, "seq", -1)
+    output_hops(3, grad_projected)
+    grad_out_w = dot(after(gated, lead_rows), branch_near, rows_first).astype(BF16)
+    grad_projected, grad_out_w = together(grad_projected, grad_out_w)
+    grad_out_s = scatter(grad_out_w)
     padded = jnp.concatenate([jnp.zeros((HALO, heads * MIX), F32), later_rows])
     last_rows = tail_rows + sum(
         conv_weight[i] * padded[CONV - 1 - i : CONV - 1 - i + HALO] for i in range(CONV)
     )
+    last_start = near_spots[count - 1] * own_rows + own_rows - HALO
     for h in range(heads):
         grad_projected = lax.dynamic_update_slice(
-            grad_projected, last_rows[:, h * MIX : (h + 1) * MIX].astype(BF16), (seq_rows - HALO, h * PER)
+            grad_projected, last_rows[:, h * MIX : (h + 1) * MIX].astype(BF16), (last_start, h * PER)
         )
-    grad_rate_low = grad_rates.astype(BF16)
-    grad_normed_part = (
-        dot(grad_projected, w_mix, contract) + dot(grad_rate_low, w_rate, plain)
-    ).astype(BF16)
-    grad_normed = ring_scatter(whole_rows(grad_normed_part, own_rows, ids), own_rows, "head")
-    grad_w_mix_s = pair_scatter(dot(normed, grad_projected, rows_first).astype(BF16), "seq", 0)
-    grad_rate_t = dot(grad_rate_low, normed, rows_first)
-    norm_gain_part = jnp.sum(grad_normed_part.astype(F32) * normed.astype(F32), axis=0) / norm_gain
-
+    early = [hops] + ([hops - 1, hops + 1] if hops > 1 else [])
+    late = [k for s in range(hops - 2, 0, -1) for k in (s, count - s)] + [0]
+    place_of = {k: (0, i) for i, k in enumerate(early)} | {k: (1, i) for i, k in enumerate(late)}
+    parts = []
+    part, sums = normed_back(
+        spots, early, count, grad_projected, grad_rates, normed, w_mix, w_rate, jnp.zeros((8, width), F32)
+    )
+    parts.append(part)
+
+    def take(k, start, size):
+        which, i = place_of[k]
+        return lax.slice_in_dim(parts[which], i * own_rows + start, i * own_rows + start + size, axis=0)
+
+    def late_rows(pin):
+        part, keep["sums"] = normed_back(
+            spots, late, count, pin(grad_projected), grad_rates, normed, w_mix, w_rate, sums
+        )
+        parts.append(part)
+        return (part,)
+
+    mixes = [("mix", h) for h in range(heads)]
+
+    def first_window(pin):
+        output_hops(4, pin(part))
+        return (*late_rows(pin), *known())
+
+    def second_window(pin):
+        keep[mixes[0]] = outer(spots, normed, pin(grad_projected), 0, heads)
+        keep[mixes[0], "crossed"] = pair_across(keep[mixes[0]], "seq")
+        sums = pin(keep["sums"])
+        gains = jnp.concatenate([sums[4:5], mlp_gain_part[None], head_gain_part], axis=1)
+        keep["gains"] = round_sum(gains, "head")
+        keep["small"] = jnp.concatenate([sums, seq_sums], axis=1)
+        return (*keep[mixes[0]], keep["gains"], keep["small"])
+
+    def third_window(pin):
+        made = []
+        for h, name in enumerate(mixes[1:]):
+            keep[name] = outer(spots, normed, pin(grad_projected), h + 1, heads)
+            keep[name, "crossed"] = pair_across(keep[name], "seq")
+            made += keep[name]
+        keep["gains"] = round_sum(pin(keep["gains"]), "seq")
+        keep["small"] = round_sum(pin(keep["small"]), "seq")
+        far_sums(mixes[0])(pin)
+        return (*made, keep["gains"], keep["small"])
+
+    def fourth_window(pin):
+        far_sums(*mixes[1:])(pin)
+        return [keep[mixes[0], "far"]]
+
+    grad_normed = ring_scatter(
+        take, own_rows, "head", {1: first_window, 2: second_window, 3: third_window, 4: fourth_window}
+    )
     scaled_one = grad_normed * norm_gain
     grad_input = grad_residual + inverse_one * (
         scaled_one - norm_normed * jnp.mean(scaled_one * norm_normed, axis=-1, keepdims=True)
     )
-    width = norm_gain.shape[0]
-    flat = lambda a: jnp.pad(a.reshape(-1), (0, -a.size % 128)).reshape(-1, 128)
-    seq_pack = [flat(a) for a in (grad_taps, grad_rate_t, grad_bias_row)]
-    all_pack = [flat(a) for a in (norm_gain_part, mlp_gain_part, head_gain_part)]
-    sizes = [a.shape[0] for a in seq_pack + all_pack]
-    split = len(seq_pack)
-    pack = butterfly(jnp.concatenate(seq_pack + all_pack, axis=0), "seq")
-    cut = sum(sizes[:split])
-    rest = butterfly(pack[cut:], "head")
-    parts = []
-    start = 0
-    for i, size in enumerate(sizes):
-        parts.append(pack[start : start + size] if i < split else rest[start - cut : start - cut + size])
-        start += size
-    conv_grad = parts[0].reshape(CONV, heads * MIX)
-    rate_sum = parts[1].reshape(2 * heads, width)
+    output = (
+        residual + sum(a.astype(F32) for a in known()) + take_output(0, 0, own_rows).astype(F32)
+    ).astype(BF16)
+    pin = lambda value: after(value, grad_normed)
+    total_all([mixes])
+    small, gains = keep["small"], keep["gains"]
     per_seq = w_rates.shape[0]
-    grad_rates_s = lax.dynamic_slice_in_dim(rate_sum, lax.axis_index("seq") * per_seq, per_seq, 1).T
-    bias_grad = parts[2].reshape(-1)[: 2 * heads].reshape(heads, 2).T
     return (
         output,
         grad_input,
-        grad_w_mix_s,
-        grad_rates_s,
-        conv_grad,
-        bias_grad,
-        parts[3].reshape(width),
-        parts[5].reshape(DV),
-        parts[4].reshape(width),
+        keep[mixes[0], "total"],
+        lax.dynamic_slice_in_dim(small[: 2 * heads], place[0] * per_seq, per_seq, 1).T,
+        small[:CONV, width:],
+        small[CONV, width : width + 2 * heads].reshape(heads, 2).T,
+        gains[0, :width] / norm_gain,
+        gains[0, 2 * width :],
+        gains[0, width : 2 * width],
         grad_out_s,
         grad_gate_s,
         grad_up_s,

time: 682 us -> 623 us (0.913)
  Pallas kernels: 67 us -> 147 us
  waiting for transfers between devices: 259 us -> 198 us
  starting transfers between devices: 153 us -> 110 us
  local copies, waits for them, and re-layouts: 55.8 us -> 22.4 us
  matrix products: 85.5 us -> 62.8 us
  other arithmetic: 27.2 us -> 38.7 us
  between operations: 7.7 us -> 15.9 us
    pallas_call x0 -> x12, Pallas kernels: none -> 79 us  [the longest x2 20.8 us: normed_back(): pl.pallas_call(functools.partial(normed_back_kernel, len(w_mix), count),...]
    ppermute x38 -> x25, waiting for transfers between devices: 92.6 us -> 22.1 us  [swap(): return lax.ppermute(value, axis, [(i, i ^ bit) for i in range(count)])]
    ppermute x112 -> x81, starting transfers between devices: 125 us -> 84.4 us  [ring_step(): lax.ppermute(value, axis, [(order[i], order[(i + step) % count]) for i in...]
    dot_general x16 -> x10, matrix products: 85.5 us -> 62.8 us  [per_device(): lax.dot_general(a, b, dims, preferred_element_type=F32)]
    dynamic_update_slice x39 -> x4, local copies, waits for them, and re-layouts: 17.4 us -> 0.06 us  [per_device(): lax.dynamic_update_slice_in_dim(w_rate, swap(rate_shard, 'seq', b) if b e...]
    convert_element_type x3 -> x9, other arithmetic: 3.15 us -> 14.4 us  [the longest x4 9.36 us: per_device(): lax.psum_scatter(a, 'seq', scatter_dimension=1, tiled=True).astype(F32)]
    ppermute x112 -> x81, waiting for transfers between devices: 167 us -> 175 us  [ring_step(): lax.ppermute(value, axis, [(order[i], order[(i + step) % count]) for i in...]
    unnamed x131 -> x110, local copies, waits for them, and re-layouts: 14.2 us -> 7.14 us
  transfers between devices with their start and end apart: 152 -> 116, of which waited for: 87 -> 56; matrix products, arithmetic and copies ran while one was open for 16% -> 15% of each run, Pallas kernels for 4% -> 24%
where the time goes in v3:
time: 623 us; the launch traced here: 614 us
  waiting for transfers between devices  198 us (32%)
  Pallas kernels  147 us (24%)
  starting transfers between devices  110 us (18%)
  matrix products  62.8 us (10%)
  other arithmetic  38.7 us (6%)
  local copies, waits for them, and re-layouts  22.4 us (4%)
  blocking collectives  18.7 us (3%)
  between operations  15.9 us (3%)
    ppermute x81, waiting for transfers between devices, ring_step(): lax.ppermute(value, axis, [(order[i], order[(i + step) % count]) for i in...  175 us
    ppermute x81, starting transfers between devices, ring_step(): lax.ppermute(value, axis, [(order[i], order[(i + step) % count]) for i in...  84.4 us
    dot_general x10, matrix products, per_device(): lax.dot_general(a, b, dims, preferred_element_type=F32)  62.8 us
    pallas_call x1, Pallas kernels, mixer_backward(): pl.pallas_call(functools.partial(backward_kernel, heads, group, steps, ma...  27.9 us
    ppermute x25, starting transfers between devices, swap(): return lax.ppermute(value, axis, [(i, i ^ bit) for i in range(count)])  22.8 us
    ppermute x25, waiting for transfers between devices, swap(): return lax.ppermute(value, axis, [(i, i ^ bit) for i in range(count)])  22.1 us
    pallas_call x2, Pallas kernels, normed_back(): pl.pallas_call(functools.partial(normed_back_kernel, len(w_mix), count),...  20.8 us
    pallas_call x4, Pallas kernels, stacked(): pl.pallas_call(functools.partial(stack_kernel, layout), out_shape=jax.Sha...  17.7 us
  transfers between devices with their start and end apart: 116, of which 56 were waited for; matrix products, arithmetic and copies ran while one was open for 15% of the time, Pallas kernels for 24%

profile of v3, /device:TPU:0, one launch (start us, length us, event | category | flops | bytes accessed | tf_op | source)
XLA Modules:
  0.0 613.8 jit_solution(5741104771302814181)
XLA Ops:
  7.2 3.0 collective-permute-start.10
  14.8 11.4 %collective-permute-done.3.refs_1_ = bf16[128,2048]{1,0:T(8,128)(2,1)S(1)} collective-permute-done((bf16[128,2048]{1,0:T(8,128)(2,1)S(1)}, bf16[128,2048]{1,0:T(8,128)(2,1)S(1)}, u32[]{:S(2)}, u32[]{:S(2)}) %collective-permute-start.3) | collective-permute-done | bytes 524320 | tf_op jit(solution)/shard_map/ppermute | solution.py:804
  29.4 10.3 %collective-permute-done.5.refs_3_ = bf16[128,2048]{1,0:T(8,128)(2,1)} collective-permute-done((bf16[128,2048]{1,0:T(8,128)(2,1)S(1)}, bf16[128,2048]{1,0:T(8,128)(2,1)}, u32[]{:S(2)}, u32[]{:S(2)}) %collective-permute-start.5) | collective-permute-done | bytes 524320 | tf_op jit(solution)/shard_map/ppermute | solution.py:804
  40.9 4.0 collective-permute-done.10.refs_11_.refs_13_.refs_19_
  47.1 12.6 %collective-permute-done.7.refs_5_ = bf16[128,2048]{1,0:T(8,128)(2,1)S(1)} collective-permute-done((bf16[128,2048]{1,0:T(8,128)(2,1)}, bf16[128,2048]{1,0:T(8,128)(2,1)S(1)}, u32[]{:S(2)}, u32[]{:S(2)}) %collective-permute-start.7) | collective-permute-done | bytes 524320 | tf_op jit(solution)/shard_map/ppermute | solution.py:804
  67.4 12.9 %collective-permute-done.12.refs_7_ = bf16[64,2048]{1,0:T(8,128)(2,1)S(1)} collective-permute-done((bf16[64,2048]{1,0:T(8,128)(2,1)}, bf16[64,2048]{1,0:T(8,128)(2,1)S(1)}, u32[]{:S(2)}, u32[]{:S(2)}) %collective-permute-start.12) | collective-permute-done | bytes 262176 | tf_op jit(solution)/shard_map/ppermute | solution.py:804
  85.7 14.6 %shard_map.237 = (bf16[1024,1536]{1,0:T(8,128)(2,1)}, f32[1024,4]{1,0:T(8,128)}) custom-call(s32[8]{0:T(128)} %get-tuple-element.461.ids_ref, s32[4]{0:T(128)} %iota_xor_fusion.spots_ref, bf16[4,2048]{1,0:T(4,128)(2,1)} %copy-done.32, bf16[128,2048]{1,0:T(8,128)(2,1)} %copy-done.3, bf16[128,2048]{1,0:T(8,128)(2,1)} %copy-done.11, ...), custom_call_target="tpu_custom_call" | custom-call | flops 1 | bytes 1 | tf_op jit(solution)/shard_map/pallas_call | solution.py:628
  106.2 14.4 %shard_map.238 = (f32[1024,512]{1,0:T(8,128)}, bf16[1024,256]{1,0:T(8,128)(2,1)}, bf16[2,8,384,128]{3,2,1,0:T(8,128)(2,1)}, bf16[2,8,128,384]{3,2,1,0:T(8,128)(2...) custom-call(bf16[1024,1536]{1,0:T(8,128)(2,1)} %get-tuple-element.20, ...), custom_call_target="tpu_custom_call" | custom-call | flops 1 | bytes 1 | tf_op jit(solution)/shard_map/pallas_call | solution.py:205
  120.6 11.8 %all-gather = bf16[8,384,128]{2,1,0:T(8,128)(2,1)} all-gather(bf16[2,384,128]{2,1,0:T(8,128)(2,1)} %get-tuple-element.209), channel_id=2, replica_groups=mesh['seq'=4,'head'=8] {'seq'}, dimensions={0}, use_global_device_ids=true | all-gather | bytes 983040 | tf_op jit(solution)/shard_map/all_gather | solution.py:1041
  135.4 12.0 %shard_map.239 = (bf16[1024,512]{1,0:T(8,128)(2,1)}, bf16[1024,512]{1,0:T(8,128)(2,1)}, bf16[1024,2048]{1,0:T(8,128)(2,1)}, bf16[2,256,128]{2,1,0:T(8,128)(2,1)}) custom-call(s32[8]{0:T(128)} %get-tuple-element.461.ids_ref, s32[1]{0:T(128)} %bitcast.1.place_ref, bf16[4,2,384,128]{3,2,1,0:T(8,128)(2,1)} %bitcast.44, ...), custom_call_target="tpu_custom_call" | custom-call | flops 1 | bytes 1 | tf_op jit(solution)/shard_map/pallas_call | solution.py:483
  150.8 4.7 shard_map.240
  162.4 4.4 shard_map.241.refs_6_.refs_7_.refs_8_.refs_10_.refs_11_.refs_12_.refs_13_.refs_14_.left_ref
  176.5 4.6 collective-permute-done.29
  189.4 3.4 collective-permute-done.33
  200.4 9.0 %collective-permute-done.37.refs_2_ = bf16[128,2048]{1,0:T(8,128)(2,1)S(1)} collective-permute-done((bf16[128,2048]{1,0:T(8,128)(2,1)S(1)}, bf16[128,2048]{1,0:T(8,128)(2,1)S(1)}, u32[]{:S(2)}, u32[]{:S(2)}) %collective-permute-start.37) | collective-permute-done | bytes 524320 | tf_op jit(solution)/shard_map/ppermute | solution.py:804
  213.2 7.8 %fusion.24 = f32[1024,704]{0,1:T(8,128)} fusion(bf16[1024,2048]{1,0:T(8,128)(2,1)} %shard_map.240, bf16[704,2048]{1,0:T(8,128)(2,1)} %all-gather.9.cloned.1.call-done), kind=kOutput, calls=%fused_computation.112 | convolution fusion | flops 2952790016 | bytes 9961472 | tf_op jit(solution)/shard_map/dot_general | solution.py:955
  226.3 10.2 %collective-permute-done.41.refs_6_ = bf16[128,2048]{1,0:T(8,128)(2,1)S(1)} collective-permute-done((bf16[128,2048]{1,0:T(8,128)(2,1)}, bf16[128,2048]{1,0:T(8,128)(2,1)S(1)}, u32[]{:S(2)}, u32[]{:S(2)}) %collective-permute-start.41) | collective-permute-done | bytes 524320 | tf_op jit(solution)/shard_map/ppermute | solution.py:804
  238.9 4.3 shard_map.242.buffer_ref
  246.8 7.9 %fusion.25 = f32[1024,704]{0,1:T(8,128)} fusion(bf16[1024,2048]{1,0:T(8,128)(2,1)} %shard_map.243, bf16[704,2048]{1,0:T(8,128)(2,1)} %all-gather.13.cloned.1.call-done), kind=kOutput, calls=%fused_computation.113 | convolution fusion | flops 2952790016 | bytes 9961472 | tf_op jit(solution)/shard_map/dot_general | solution.py:955
  254.7 9.2 %multiply_convert_fusion = (bf16[1024,704]{0,1:T(8,128)(2,1)S(1)}, bf16[1024,704]{0,1:T(8,128)(2,1)S(1)}, bf16[1024,704]{0,1:T(8,128)(2,1)S(1)}) fusion(f32[1024,704]{0,1:T(8,128)} %fusion.24, f32[1024,704]{0,1:T(8,128)} %fusion.25, bf16[1024,2048]{1,0:T(8,128)(2,1)} %shard_map.243, bf16[704,2048]{1,0:T(8,128)(2,1)} %all-gather.11.cloned.1.call-done), kind=kOutput, calls=%fused_computation.6 | convolution fusion | flops 2963603456 | bytes 17170432 | tf_op jit(solution)/shard_map/dot_general | solution.py:955
  263.9 3.5 fusion.26
  267.5 4.2 add_convert_fusion
  273.8 4.5 convolution_convert_fusion.3
  280.5 4.3 collective-permute-done.45
  287.0 7.5 %convolution_convert_fusion.2 = bf16[704,2048]{1,0:T(8,128)(2,1)} fusion(bf16[1024,704]{0,1:T(8,128)(2,1)} %copy-done.50, bf16[1024,2048]{1,0:T(8,128)(2,1)} %shard_map.243), kind=kOutput, calls=%fused_computation.3 | convolution fusion | flops 2954231808 | bytes 8519680 | tf_op jit(solution)/shard_map/dot_general | solution.py:955
  298.7 5.2 collective-permute-done.47
  313.9 6.7 %convolution_convert_fusion.1 = bf16[704,2048]{1,0:T(8,128)(2,1)} fusion(bf16[1024,704]{0,1:T(8,128)(2,1)S(1)} %copy-done.52, bf16[1024,2048]{1,0:T(8,128)(2,1)} %shard_map.243), kind=kOutput, calls=%fused_computation.2 | convolution fusion | flops 2954231808 | bytes 8519680 | tf_op jit(solution)/shard_map/dot_general | solution.py:955
  328.8 6.4 %convolution_convert_fusion = bf16[1024,2048]{1,0:T(8,128)(2,1)} fusion(bf16[1024,704]{0,1:T(8,128)(2,1)} %copy-done.53, bf16[704,2048]{1,0:T(8,128)(2,1)S(1)} %copy-done.47), kind=kOutput, calls=%fused_computation.1 | convolution fusion | flops 2954887168 | bytes 8519680 | tf_op jit(solution)/shard_map/dot_general | solution.py:955
  341.6 10.4 %collective-permute-done.59.refs_2_ = bf16[128,2048]{1,0:T(8,128)(2,1)} collective-permute-done((bf16[128,2048]{1,0:T(8,128)(2,1)S(1)}, bf16[128,2048]{1,0:T(8,128)(2,1)}, u32[]{:S(2)}, u32[]{:S(2)}) %collective-permute-start.59) | collective-permute-done | bytes 524320 | tf_op jit(solution)/shard_map/ppermute | solution.py:804
  354.7 9.9 %collective-permute-done.61.refs_4_ = bf16[128,2048]{1,0:T(8,128)(2,1)} collective-permute-done((bf16[128,2048]{1,0:T(8,128)(2,1)}, bf16[128,2048]{1,0:T(8,128)(2,1)}, u32[]{:S(2)}, u32[]{:S(2)}) %collective-permute-start.61) | collective-permute-done | bytes 524320 | tf_op jit(solution)/shard_map/ppermute | solution.py:804
  368.9 11.9 %collective-permute-done.63.refs_6_ = bf16[128,2048]{1,0:T(8,128)(2,1)S(1)} collective-permute-done((bf16[128,2048]{1,0:T(8,128)(2,1)}, bf16[128,2048]{1,0:T(8,128)(2,1)S(1)}, u32[]{:S(2)}, u32[]{:S(2)}) %collective-permute-start.63) | collective-permute-done | bytes 524320 | tf_op jit(solution)/shard_map/ppermute | solution.py:804
  385.3 4.2 shard_map.244.buffer_ref
  394.2 13.7 %shard_map.246 = (bf16[1024,512]{1,0:T(8,128)(2,1)}, bf16[1024,512]{1,0:T(8,128)(2,1)}, f32[1,256]{1,0:T(1,128)}, f32[2,256,128]{2,1,0:T(8,128)}) custom-call(s32[8]{0:T(128)} %get-tuple-element.461.ids_ref, bf16[1024,2048]{1,0:T(8,128)(2,1)} %shard_map.245.branch_ref, bf16[1024,512]{1,0:T(8,128)(2,1)} %get-tuple-element.302.value_ref, ...), custom_call_target="tpu_custom_call" | custom-call | flops 1 | bytes 1 | tf_op jit(solution)/shard_map/pallas_call | solution.py:551
  413.2 6.9 %all-gather.1 = bf16[8,256,128]{2,1,0:T(8,128)(2,1)} all-gather(bf16[2,256,128]{2,1,0:T(8,128)(2,1)S(1)} %convert_element_type.150), channel_id=3, replica_groups=mesh['seq'=4,'head'=8] {'seq'}, dimensions={0}, use_global_device_ids=true | all-gather | bytes 655360 | tf_op jit(solution)/shard_map/all_gather | solution.py:1162
  420.1 27.9 %shard_map.247 = (bf16[1024,1536]{1,0:T(8,128)(2,1)}, f32[1024,4]{1,0:T(8,128)}, f32[8,1024]{1,0:T(8,128)}, f32[16,1024]{1,0:T(8,128)}, f32[8,1024]{1,0:T(8,128)}) custom-call(bf16[1024,1536]{1,0:T(8,128)(2,1)} %get-tuple-element.204.proj_ref.prev_ref, bf16[1024,1536]{1,0:T(8,128)(2,1)} %get-tuple-element.204.proj_ref.prev_ref, bf16[16,1536]{1,0:T(8,128)(2,1)} %copy-done.38, ...), custom_call_target="tpu_custom_call" | custom-call | flops 1 | bytes 1 | tf_op jit(solution)/shard_map/pallas_call | solution.py:398
  449.5 5.0 convolution_convert_fusion.4
  460.1 8.7 %shard_map.248 = (bf16[384,2048]{1,0:T(8,128)(2,1)}, f32[8,2048]{1,0:T(8,128)}) custom-call(s32[4]{0:T(128)} %iota_xor_fusion.spots_ref, bf16[1024,1536]{1,0:T(8,128)(2,1)} %slice_dynamic-update-slice_fusion.refs_0_.refs_1_.refs_2_.refs_3_.refs_4_.right_ref, ...), custom_call_target="tpu_custom_call" | custom-call | flops 1 | bytes 1 | tf_op jit(solution)/shard_map/pallas_call | solution.py:671
  478.5 12.1 %shard_map.249 = (bf16[640,2048]{1,0:T(8,128)(2,1)}, f32[8,2048]{1,0:T(8,128)}) custom-call(s32[4]{0:T(128)} %iota_xor_fusion.spots_ref, bf16[1024,1536]{1,0:T(8,128)(2,1)} %slice_dynamic-update-slice_fusion.refs_0_.refs_1_.refs_2_.refs_3_.refs_4_.right_ref, ...), custom_call_target="tpu_custom_call" | custom-call | flops 1 | bytes 1 | tf_op jit(solution)/shard_map/pallas_call | solution.py:671
  490.6 4.0 collective-permute-done.75
  498.1 3.1 collective-permute-start.87
  501.2 3.1 collective-permute-start.85
  508.6 8.8 %shard_map.250 = (bf16[512,768]{1,0:T(8,128)(2,1)}, bf16[512,768]{1,0:T(8,128)(2,1)}, bf16[512,768]{1,0:T(8,128)(2,1)}, bf16[512,768]{1,0:T(8,128)(2,1)}) custom-call(s32[4]{0:T(128)} %iota_xor_fusion.spots_ref, bf16[1024,2048]{1,0:T(8,128)(2,1)} %shard_map.241.refs_6_.refs_7_.refs_8_.refs_10_.refs_11_.refs_12_.refs_13_.refs_14_.left_ref, ...), custom_call_target="tpu_custom_call" | custom-call | flops 1 | bytes 1 | tf_op jit(solution)/shard_map/pallas_call | solution.py:753
  521.6 3.9 collective-permute-done.77
  533.7 8.7 %shard_map.251 = (bf16[512,768]{1,0:T(8,128)(2,1)}, bf16[512,768]{1,0:T(8,128)(2,1)}, bf16[512,768]{1,0:T(8,128)(2,1)}, bf16[512,768]{1,0:T(8,128)(2,1)}) custom-call(s32[4]{0:T(128)} %iota_xor_fusion.spots_ref, bf16[1024,2048]{1,0:T(8,128)(2,1)} %shard_map.241.refs_6_.refs_7_.refs_8_.refs_10_.refs_11_.refs_12_.refs_13_.refs_14_.left_ref, ...), custom_call_target="tpu_custom_call" | custom-call | flops 1 | bytes 1 | tf_op jit(solution)/shard_map/pallas_call | solution.py:753
  544.6 3.3 collective-permute-done.96
  551.5 4.5 collective-permute-done.89
  584.2 14.8 %collective-permute-done.107.refs_5_ = bf16[512,768]{1,0:T(8,128)(2,1)S(1)} collective-permute-done((bf16[512,768]{1,0:T(8,128)(2,1)}, bf16[512,768]{1,0:T(8,128)(2,1)S(1)}, u32[]{:S(2)}, u32[]{:S(2)}) %collective-permute-start.107) | collective-permute-done | bytes 786464 | tf_op jit(solution)/shard_map/ppermute | solution.py:894
  599.9 4.7 shard_map.252
  (408 shorter events, 213.6 us)
Async XLA Ops:
  7.2 128.2 %all-gather.7.cloned.1.call-start = ((), (), s32[]{:S(2)}) async-start(), calls=%async_computation.4 | async-start | bytes 2621440 | tf_op jit(solution)/shard_map/all_gather | solution.py:1019
  7.2 37.6 %collective-permute-start.10 = (bf16[512,1536]{1,0:T(8,128)(2,1)}, bf16[512,1536]{1,0:T(8,128)(2,1)S(1)}, u32[]{:S(2)}, u32[]{:S(2)}) collective-permute-start(bf16[512,1536]{1,0:T(8,128)(2,1)} %refs_17_.1), channel_id=1, source_target_pairs={{0,16},{8,24},{16,0},{24,8},{1,17},{9,25},{17,1},{25,9},{2,18},{10... | collective-permute-start | bytes 4718600 | tf_op jit(solution)/shard_map/ppermute | solution.py:894
  29.4 31.6 %collective-permute-start.9 = (bf16[512,1536]{1,0:T(8,128)(2,1)}, bf16[512,1536]{1,0:T(8,128)(2,1)}, u32[]{:S(2)}, u32[]{:S(2)}) collective-permute-start(bf16[512,1536]{1,0:T(8,128)(2,1)} %refs_17_.1), channel_id=1, source_target_pairs={{0,8},{8,0},{16,24},{24,16},{1,9},{9,1},{17,25},{25,17},{2,10},{10... | collective-permute-start | bytes 4718600 | tf_op jit(solution)/shard_map/ppermute | solution.py:894
  44.9 16.2 %collective-permute-start.11 = (bf16[512,1536]{1,0:T(8,128)(2,1)S(1)}, bf16[512,1536]{1,0:T(8,128)(2,1)}, u32[]{:S(2)}, u32[]{:S(2)}) collective-permute-start(bf16[512,1536]{1,0:T(8,128)(2,1)S(1)} %collective-permute-done.10.refs_11_.refs_13_.refs_19_), channel_id=1, source_target_pairs={{0,8},{8,0},{16,24},{24,16},{1,9},{9,1},{17,25},{25,17},{2,10},{10... | collective-permute-start | bytes 4718600 | tf_op jit(solution)/shard_map/ppermute | solution.py:894
  45.0 168.2 %all-gather.9.cloned.1.call-start = ((), (), s32[]{:S(2)}) async-start(), calls=%async_computation.5 | async-start | bytes 3604480 | tf_op jit(solution)/shard_map/all_gather | solution.py:1047
  45.0 14.6 %collective-permute-start.7 = (bf16[128,2048]{1,0:T(8,128)(2,1)}, bf16[128,2048]{1,0:T(8,128)(2,1)S(1)}, u32[]{:S(2)}, u32[]{:S(2)}) collective-permute-start(bf16[128,2048]{1,0:T(8,128)(2,1)} %collective-permute-done.5.refs_3_), channel_id=1, source_target_pairs={{0,1},{2,0},{4,2},{6,4},{7,6},{5,7},{3,5},{1,3},{8,9},{10,8},{12,1... | collective-permute-start | bytes 1572872 | tf_op jit(solution)/shard_map/ppermute | solution.py:804
  46.8 14.3 %collective-permute-start.8 = (bf16[128,2048]{1,0:T(8,128)(2,1)}, bf16[128,2048]{1,0:T(8,128)(2,1)S(1)}, u32[]{:S(2)}, u32[]{:S(2)}) collective-permute-start(bf16[128,2048]{1,0:T(8,128)(2,1)} %copy-done.13), channel_id=1, source_target_pairs={{0,2},{2,4},{4,6},{6,7},{7,5},{5,3},{3,1},{1,0},{8,10},{10,12},{12... | collective-permute-start | bytes 1572872 | tf_op jit(solution)/shard_map/ppermute | solution.py:804
  61.1 20.7 %collective-permute-start.14 = (bf16[128,2048]{1,0:T(8,128)(2,1)}, bf16[128,2048]{1,0:T(8,128)(2,1)}, u32[]{:S(2)}, u32[]{:S(2)}) collective-permute-start(bf16[128,2048]{1,0:T(8,128)(2,1)} %refs_0_), channel_id=1, source_target_pairs={{0,2},{2,4},{4,6},{6,7},{7,5},{5,3},{3,1},{1,0},{8,10},{10,12},{12... | collective-permute-start | bytes 1572872 | tf_op jit(solution)/shard_map/ppermute | solution.py:804
  61.6 20.3 %collective-permute-start.15 = (bf16[128,2048]{1,0:T(8,128)(2,1)}, bf16[128,2048]{1,0:T(8,128)(2,1)}, u32[]{:S(2)}, u32[]{:S(2)}) collective-permute-start(bf16[128,2048]{1,0:T(8,128)(2,1)} %refs_0_), channel_id=1, source_target_pairs={{0,1},{2,0},{4,2},{6,4},{7,6},{5,7},{3,5},{1,3},{8,9},{10,8},{12,1... | collective-permute-start | bytes 1572872 | tf_op jit(solution)/shard_map/ppermute | solution.py:804
  63.2 21.9 %collective-permute-start = (bf16[4,512]{1,0:T(4,128)(2,1)}, bf16[4,512]{1,0:T(4,128)(2,1)S(1)}, u32[]{:S(2)}, u32[]{:S(2)}) collective-permute-start(bf16[4,512]{1,0:T(4,128)(2,1)} %bitcast.57), channel_id=1, source_target_pairs={{0,8},{8,0},{16,24},{24,16},{1,9},{9,1},{17,25},{25,17},{2,10},{10... | collective-permute-start | bytes 12296 | tf_op jit(solution)/shard_map/ppermute | solution.py:894
  63.9 16.4 %collective-permute-start.12 = (bf16[64,2048]{1,0:T(8,128)(2,1)}, bf16[64,2048]{1,0:T(8,128)(2,1)S(1)}, u32[]{:S(2)}, u32[]{:S(2)}) collective-permute-start(bf16[64,2048]{1,0:T(8,128)(2,1)} %slice.267), channel_id=1, source_target_pairs={{0,2},{2,4},{4,6},{6,7},{7,5},{5,3},{3,1},{1,0},{8,10},{10,12},{12... | collective-permute-start | bytes 786440 | tf_op jit(solution)/shard_map/ppermute | solution.py:804
  65.0 16.8 %collective-permute-start.13 = (bf16[64,2048]{1,0:T(8,128)(2,1)}, bf16[64,2048]{1,0:T(8,128)(2,1)}, u32[]{:S(2)}, u32[]{:S(2)}) collective-permute-start(bf16[64,2048]{1,0:T(8,128)(2,1)} %slice.268), channel_id=1, source_target_pairs={{0,1},{2,0},{4,2},{6,4},{7,6},{5,7},{3,5},{1,3},{8,9},{10,8},{12,1... | collective-permute-start | bytes 786440 | tf_op jit(solution)/shard_map/ppermute | solution.py:804
  81.8 18.5 %collective-permute-start.16 = (bf16[128,2048]{1,0:T(8,128)(2,1)}, bf16[128,2048]{1,0:T(8,128)(2,1)}, u32[]{:S(2)}, u32[]{:S(2)}) collective-permute-start(bf16[128,2048]{1,0:T(8,128)(2,1)} %collective-permute-done.14.refs_2_), channel_id=1, source_target_pairs={{0,2},{2,4},{4,6},{6,7},{7,5},{5,3},{3,1},{1,0},{8,10},{10,12},{12... | collective-permute-start | bytes 1572872 | tf_op jit(solution)/shard_map/ppermute | solution.py:804
  82.6 17.8 %collective-permute-start.17 = (bf16[128,2048]{1,0:T(8,128)(2,1)}, bf16[128,2048]{1,0:T(8,128)(2,1)}, u32[]{:S(2)}, u32[]{:S(2)}) collective-permute-start(bf16[128,2048]{1,0:T(8,128)(2,1)} %collective-permute-done.15.refs_1_), channel_id=1, source_target_pairs={{0,1},{2,0},{4,2},{6,4},{7,6},{5,7},{3,5},{1,3},{8,9},{10,8},{12,1... | collective-permute-start | bytes 1572872 | tf_op jit(solution)/shard_map/ppermute | solution.py:804
  100.3 20.2 %collective-permute-start.19 = (bf16[128,2048]{1,0:T(8,128)(2,1)}, bf16[128,2048]{1,0:T(8,128)(2,1)S(1)}, u32[]{:S(2)}, u32[]{:S(2)}) collective-permute-start(bf16[128,2048]{1,0:T(8,128)(2,1)} %collective-permute-done.16.refs_4_), channel_id=1, source_target_pairs={{0,2},{2,4},{4,6},{6,7},{7,5},{5,3},{3,1},{1,0},{8,10},{10,12},{12... | collective-permute-start | bytes 1572872 | tf_op jit(solution)/shard_map/ppermute | solution.py:804
  101.1 19.5 %collective-permute-start.20 = (bf16[128,2048]{1,0:T(8,128)(2,1)}, bf16[128,2048]{1,0:T(8,128)(2,1)S(1)}, u32[]{:S(2)}, u32[]{:S(2)}) collective-permute-start(bf16[128,2048]{1,0:T(8,128)(2,1)} %collective-permute-done.17.refs_3_), channel_id=1, source_target_pairs={{0,1},{2,0},{4,2},{6,4},{7,6},{5,7},{3,5},{1,3},{8,9},{10,8},{12,1... | collective-permute-start | bytes 1572872 | tf_op jit(solution)/shard_map/ppermute | solution.py:804
  132.4 114.4 %all-gather.13.cloned.1.call-start = ((), (), s32[]{:S(2)}) async-start(), calls=%async_computation.7 | async-start | bytes 3604480 | tf_op jit(solution)/shard_map/all_gather | solution.py:1047
  133.2 121.5 %all-gather.11.cloned.1.call-start = ((), (), s32[]{:S(2)}) async-start(), calls=%async_computation.6 | async-start | bytes 3604480 | tf_op jit(solution)/shard_map/all_gather | solution.py:1047
  133.2 14.2 %collective-permute-start.21 = (bf16[64,2048]{1,0:T(8,128)(2,1)S(1)}, bf16[64,2048]{1,0:T(8,128)(2,1)S(1)}, u32[]{:S(2)}, u32[]{:S(2)}) collective-permute-start(bf16[64,2048]{1,0:T(8,128)(2,1)S(1)} %slice.270), channel_id=1, source_target_pairs={{0,2},{2,4},{4,6},{6,7},{7,5},{5,3},{3,1},{1,0},{8,10},{10,12},{12... | collective-permute-start | bytes 786440 | tf_op jit(solution)/shard_map/ppermute | solution.py:804
  189.3 380.0 %reduce-scatter.11.cloned.1.call-start = ((), (), s32[]{:S(2)}) async-start(), calls=%async_computation.11 | async-start | bytes 3604480 | tf_op jit(solution)/shard_map/reduce_scatter | solution.py:1090
  278.3 293.4 %reduce-scatter.7.cloned.1.call-start = ((), (), s32[]{:S(2)}) async-start(), calls=%async_computation.9 | async-start | bytes 3604480 | tf_op jit(solution)/shard_map/reduce_scatter | solution.py:1090
  294.5 281.8 %reduce-scatter.9.cloned.1.call-start = ((), (), s32[]{:S(2)}) async-start(), calls=%async_computation.10 | async-start | bytes 3604480 | tf_op jit(solution)/shard_map/reduce_scatter | solution.py:1090
  354.6 250.0 %reduce-scatter.5.cloned.1.call-start = ((), (), s32[]{:S(2)}) async-start(), calls=%async_computation.8 | async-start | bytes 2621440 | tf_op jit(solution)/shard_map/reduce_scatter | solution.py:1090
  366.9 13.9 %collective-permute-start.63 = (bf16[128,2048]{1,0:T(8,128)(2,1)}, bf16[128,2048]{1,0:T(8,128)(2,1)S(1)}, u32[]{:S(2)}, u32[]{:S(2)}) collective-permute-start(bf16[128,2048]{1,0:T(8,128)(2,1)} %collective-permute-done.61.refs_4_), channel_id=1, source_target_pairs={{0,2},{2,4},{4,6},{6,7},{7,5},{5,3},{3,1},{1,0},{8,10},{10,12},{12... | collective-permute-start | bytes 1572872 | tf_op jit(solution)/shard_map/ppermute | solution.py:804
  392.1 16.8 %collective-permute-start.67 = (bf16[128,2048]{1,0:T(8,128)(2,1)S(1)}, bf16[128,2048]{1,0:T(8,128)(2,1)}, u32[]{:S(2)}, u32[]{:S(2)}) collective-permute-start(bf16[128,2048]{1,0:T(8,128)(2,1)S(1)} %copy-done.29), channel_id=1, source_target_pairs={{0,2},{2,4},{4,6},{6,7},{7,5},{5,3},{3,1},{1,0},{8,10},{10,12},{12... | collective-permute-start | bytes 1572872 | tf_op jit(solution)/shard_map/ppermute | solution.py:804
  411.1 43.4 %collective-permute-start.68 = (bf16[128,2048]{1,0:T(8,128)(2,1)}, bf16[128,2048]{1,0:T(8,128)(2,1)}, u32[]{:S(2)}, u32[]{:S(2)}) collective-permute-start(bf16[128,2048]{1,0:T(8,128)(2,1)} %get-tuple-element.305), channel_id=1, source_target_pairs={{0,2},{2,4},{4,6},{6,7},{7,5},{5,3},{3,1},{1,0},{8,10},{10,12},{12... | collective-permute-start | bytes 1572872 | tf_op jit(solution)/shard_map/ppermute | solution.py:804
  411.7 42.9 %collective-permute-start.69 = (bf16[128,2048]{1,0:T(8,128)(2,1)S(1)}, bf16[128,2048]{1,0:T(8,128)(2,1)}, u32[]{:S(2)}, u32[]{:S(2)}) collective-permute-start(bf16[128,2048]{1,0:T(8,128)(2,1)S(1)} %get-tuple-element.315), channel_id=1, source_target_pairs={{0,1},{2,0},{4,2},{6,4},{7,6},{5,7},{3,5},{1,3},{8,9},{10,8},{12,1... | collective-permute-start | bytes 1572872 | tf_op jit(solution)/shard_map/ppermute | solution.py:804
  456.2 14.7 %collective-permute-start.70 = (bf16[128,2048]{1,0:T(8,128)(2,1)S(1)}, bf16[128,2048]{1,0:T(8,128)(2,1)S(1)}, u32[]{:S(2)}, u32[]{:S(2)}) collective-permute-start(bf16[128,2048]{1,0:T(8,128)(2,1)S(1)} %get-tuple-element.317), channel_id=1, source_target_pairs={{0,2},{2,4},{4,6},{6,7},{7,5},{5,3},{3,1},{1,0},{8,10},{10,12},{12... | collective-permute-start | bytes 1572872 | tf_op jit(solution)/shard_map/ppermute | solution.py:804
  457.5 14.7 %collective-permute-start.73 = (bf16[128,2048]{1,0:T(8,128)(2,1)S(1)}, bf16[128,2048]{1,0:T(8,128)(2,1)S(1)}, u32[]{:S(2)}, u32[]{:S(2)}) collective-permute-start(bf16[128,2048]{1,0:T(8,128)(2,1)S(1)} %get-tuple-element.327), channel_id=1, source_target_pairs={{0,1},{2,0},{4,2},{6,4},{7,6},{5,7},{3,5},{1,3},{8,9},{10,8},{12,1... | collective-permute-start | bytes 1572872 | tf_op jit(solution)/shard_map/ppermute | solution.py:804
  474.4 20.2 %collective-permute-start.74 = (bf16[128,2048]{1,0:T(8,128)(2,1)}, bf16[128,2048]{1,0:T(8,128)(2,1)S(1)}, u32[]{:S(2)}, u32[]{:S(2)}) collective-permute-start(bf16[128,2048]{1,0:T(8,128)(2,1)} %get-tuple-element.328), channel_id=1, source_target_pairs={{0,1},{2,0},{4,2},{6,4},{7,6},{5,7},{3,5},{1,3},{8,9},{10,8},{12,1... | collective-permute-start | bytes 1572872 | tf_op jit(solution)/shard_map/ppermute | solution.py:804
  475.2 19.4 %collective-permute-start.72 = (bf16[128,2048]{1,0:T(8,128)(2,1)}, bf16[128,2048]{1,0:T(8,128)(2,1)}, u32[]{:S(2)}, u32[]{:S(2)}) collective-permute-start(bf16[128,2048]{1,0:T(8,128)(2,1)} %get-tuple-element.326), channel_id=1, source_target_pairs={{0,2},{2,4},{4,6},{6,7},{7,5},{5,3},{3,1},{1,0},{8,10},{10,12},{12... | collective-permute-start | bytes 1572872 | tf_op jit(solution)/shard_map/ppermute | solution.py:804
  476.4 18.2 %collective-permute-start.75 = (bf16[64,2048]{1,0:T(8,128)(2,1)}, bf16[64,2048]{1,0:T(8,128)(2,1)S(1)}, u32[]{:S(2)}, u32[]{:S(2)}) collective-permute-start(bf16[64,2048]{1,0:T(8,128)(2,1)} %get-tuple-element.453), channel_id=1, source_target_pairs={{0,2},{2,4},{4,6},{6,7},{7,5},{5,3},{3,1},{1,0},{8,10},{10,12},{12... | collective-permute-start | bytes 786440 | tf_op jit(solution)/shard_map/ppermute | solution.py:804
  477.3 17.3 %collective-permute-start.76 = (bf16[64,2048]{1,0:T(8,128)(2,1)}, bf16[64,2048]{1,0:T(8,128)(2,1)}, u32[]{:S(2)}, u32[]{:S(2)}) collective-permute-start(bf16[64,2048]{1,0:T(8,128)(2,1)} %get-tuple-element.452), channel_id=1, source_target_pairs={{0,1},{2,0},{4,2},{6,4},{7,6},{5,7},{3,5},{1,3},{8,9},{10,8},{12,1... | collective-permute-start | bytes 786440 | tf_op jit(solution)/shard_map/ppermute | solution.py:804
  501.2 16.3 %collective-permute-start.84 = (f32[1,4352]{1,0:T(1,128)S(1)}, f32[1,4352]{1,0:T(1,128)S(1)}, u32[]{:S(2)}, u32[]{:S(2)}) collective-permute-start(f32[1,4352]{1,0:T(1,128)S(1)} %pad_maximum_fusion.1), channel_id=1, source_target_pairs={{0,4},{1,5},{2,6},{3,7},{4,0},{5,1},{6,2},{7,3},{8,12},{9,13},{10,... | collective-permute-start | bytes 52232 | tf_op jit(solution)/shard_map/ppermute | solution.py:894
  501.2 16.3 %collective-permute-start.85 = (f32[1,4352]{1,0:T(1,128)S(1)}, f32[1,4352]{1,0:T(1,128)S(1)}, u32[]{:S(2)}, u32[]{:S(2)}) collective-permute-start(f32[1,4352]{1,0:T(1,128)S(1)} %pad_maximum_fusion.1), channel_id=1, source_target_pairs={{0,5},{1,4},{2,7},{3,6},{4,1},{5,0},{6,3},{7,2},{8,13},{9,12},{10,... | collective-permute-start | bytes 52232 | tf_op jit(solution)/shard_map/ppermute | solution.py:894
  504.3 15.2 %collective-permute-start.82 = (f32[1,4352]{1,0:T(1,128)S(1)}, f32[1,4352]{1,0:T(1,128)S(1)}, u32[]{:S(2)}, u32[]{:S(2)}) collective-permute-start(f32[1,4352]{1,0:T(1,128)S(1)} %pad_maximum_fusion.1), channel_id=1, source_target_pairs={{0,2},{1,3},{2,0},{3,1},{4,6},{5,7},{6,4},{7,5},{8,10},{9,11},{10,... | collective-permute-start | bytes 52232 | tf_op jit(solution)/shard_map/ppermute | solution.py:894
  505.1 14.4 %collective-permute-start.83 = (f32[1,4352]{1,0:T(1,128)S(1)}, f32[1,4352]{1,0:T(1,128)S(1)}, u32[]{:S(2)}, u32[]{:S(2)}) collective-permute-start(f32[1,4352]{1,0:T(1,128)S(1)} %pad_maximum_fusion.1), channel_id=1, source_target_pairs={{0,3},{1,2},{2,1},{3,0},{4,7},{5,6},{6,5},{7,4},{8,11},{9,10},{10,... | collective-permute-start | bytes 52232 | tf_op jit(solution)/shard_map/ppermute | solution.py:894
  521.5 38.3 %collective-permute-start.102 = (bf16[512,768]{1,0:T(8,128)(2,1)}, bf16[512,768]{1,0:T(8,128)(2,1)S(1)}, u32[]{:S(2)}, u32[]{:S(2)}) collective-permute-start(bf16[512,768]{1,0:T(8,128)(2,1)} %get-tuple-element.338), channel_id=1, source_target_pairs={{0,8},{8,0},{16,24},{24,16},{1,9},{9,1},{17,25},{25,17},{2,10},{10... | collective-permute-start | bytes 2359304 | tf_op jit(solution)/shard_map/ppermute | solution.py:894
  528.5 13.9 %collective-permute-start.93 = (f32[1,4352]{1,0:T(1,128)S(1)}, f32[1,4352]{1,0:T(1,128)S(1)}, u32[]{:S(2)}, u32[]{:S(2)}) collective-permute-start(f32[1,4352]{1,0:T(1,128)S(1)} %add_add_fusion.2), channel_id=1, source_target_pairs={{0,16},{8,24},{16,0},{24,8},{1,17},{9,25},{17,1},{25,9},{2,18},{10... | collective-permute-start | bytes 52232 | tf_op jit(solution)/shard_map/ppermute | solution.py:894
  528.6 13.9 %collective-permute-start.94 = (f32[1,4352]{1,0:T(1,128)S(1)}, f32[1,4352]{1,0:T(1,128)S(1)}, u32[]{:S(2)}, u32[]{:S(2)}) collective-permute-start(f32[1,4352]{1,0:T(1,128)S(1)} %add_add_fusion.2), channel_id=1, source_target_pairs={{0,24},{8,16},{16,8},{24,0},{1,25},{9,17},{17,9},{25,1},{2,26},{10... | collective-permute-start | bytes 52232 | tf_op jit(solution)/shard_map/ppermute | solution.py:894
  528.7 14.8 %collective-permute-start.92 = (f32[1,4352]{1,0:T(1,128)S(1)}, f32[1,4352]{1,0:T(1,128)S(1)}, u32[]{:S(2)}, u32[]{:S(2)}) collective-permute-start(f32[1,4352]{1,0:T(1,128)S(1)} %add_add_fusion.2), channel_id=1, source_target_pairs={{0,8},{8,0},{16,24},{24,16},{1,9},{9,1},{17,25},{25,17},{2,10},{10... | collective-permute-start | bytes 52232 | tf_op jit(solution)/shard_map/ppermute | solution.py:894
  533.0 18.4 %collective-permute-start.88 = (bf16[64,2048]{1,0:T(8,128)(2,1)S(1)}, bf16[64,2048]{1,0:T(8,128)(2,1)S(1)}, u32[]{:S(2)}, u32[]{:S(2)}) collective-permute-start(bf16[64,2048]{1,0:T(8,128)(2,1)S(1)} %get-tuple-element.447), channel_id=1, source_target_pairs={{0,2},{2,4},{4,6},{6,7},{7,5},{5,3},{3,1},{1,0},{8,10},{10,12},{12... | collective-permute-start | bytes 786440 | tf_op jit(solution)/shard_map/ppermute | solution.py:804
  560.1 20.9 %collective-permute-start.103 = (bf16[512,768]{1,0:T(8,128)(2,1)S(1)}, bf16[512,768]{1,0:T(8,128)(2,1)}, u32[]{:S(2)}, u32[]{:S(2)}) collective-permute-start(bf16[512,768]{1,0:T(8,128)(2,1)S(1)} %add.361), channel_id=1, source_target_pairs={{0,16},{8,24},{16,0},{24,8},{1,17},{9,25},{17,1},{25,9},{2,18},{10... | collective-permute-start | bytes 2359304 | tf_op jit(solution)/shard_map/ppermute | solution.py:894
  561.5 17.3 %collective-permute-start.98 = (bf16[64,2048]{1,0:T(8,128)(2,1)}, bf16[64,2048]{1,0:T(8,128)(2,1)}, u32[]{:S(2)}, u32[]{:S(2)}) collective-permute-start(bf16[64,2048]{1,0:T(8,128)(2,1)} %get-tuple-element.443), channel_id=1, source_target_pairs={{0,2},{2,4},{4,6},{6,7},{7,5},{5,3},{3,1},{1,0},{8,10},{10,12},{12... | collective-permute-start | bytes 786440 | tf_op jit(solution)/shard_map/ppermute | solution.py:804
  563.2 15.6 %collective-permute-start.99 = (bf16[64,2048]{1,0:T(8,128)(2,1)}, bf16[64,2048]{1,0:T(8,128)(2,1)}, u32[]{:S(2)}, u32[]{:S(2)}) collective-permute-start(bf16[64,2048]{1,0:T(8,128)(2,1)} %get-tuple-element.442), channel_id=1, source_target_pairs={{0,1},{2,0},{4,2},{6,4},{7,6},{5,7},{3,5},{1,3},{8,9},{10,8},{12,1... | collective-permute-start | bytes 786440 | tf_op jit(solution)/shard_map/ppermute | solution.py:804
  563.5 15.7 %collective-permute-start.100 = (bf16[64,2048]{1,0:T(8,128)(2,1)}, bf16[64,2048]{1,0:T(8,128)(2,1)}, u32[]{:S(2)}, u32[]{:S(2)}) collective-permute-start(bf16[64,2048]{1,0:T(8,128)(2,1)} %get-tuple-element.441), channel_id=1, source_target_pairs={{0,2},{2,4},{4,6},{6,7},{7,5},{5,3},{3,1},{1,0},{8,10},{10,12},{12... | collective-permute-start | bytes 786440 | tf_op jit(solution)/shard_map/ppermute | solution.py:804
  565.2 15.7 %collective-permute-start.101 = (bf16[64,2048]{1,0:T(8,128)(2,1)}, bf16[64,2048]{1,0:T(8,128)(2,1)}, u32[]{:S(2)}, u32[]{:S(2)}) collective-permute-start(bf16[64,2048]{1,0:T(8,128)(2,1)} %get-tuple-element.440), channel_id=1, source_target_pairs={{0,1},{2,0},{4,2},{6,4},{7,6},{5,7},{3,5},{1,3},{8,9},{10,8},{12,1... | collective-permute-start | bytes 786440 | tf_op jit(solution)/shard_map/ppermute | solution.py:804
  579.3 19.7 %collective-permute-start.107 = (bf16[512,768]{1,0:T(8,128)(2,1)}, bf16[512,768]{1,0:T(8,128)(2,1)S(1)}, u32[]{:S(2)}, u32[]{:S(2)}) collective-permute-start(bf16[512,768]{1,0:T(8,128)(2,1)} %add.367), channel_id=1, source_target_pairs={{0,16},{8,24},{16,0},{24,8},{1,17},{9,25},{17,1},{25,9},{2,18},{10... | collective-permute-start | bytes 2359304 | tf_op jit(solution)/shard_map/ppermute | solution.py:894
  (122 other events, 1403.8 us)
Sparse Core Ops, SparseCore 0:
  45.1 24.1 all-gather.6
  132.6 27.8 all-gather.8
  162.0 27.0 all-gather.12
  190.5 27.0 all-gather.10
  278.5 35.3 reduce-scatter.10
  316.4 36.3 reduce-scatter.6
  355.3 36.3 reduce-scatter.8
  478.6 30.1 reduce-scatter.4

commit v4 on v3

--- a/solution.py
+++ b/solution.py
@@ -228,10 +228,9 @@
     heads, group, steps, peers, own,
     proj_ref, prev_ref, halo_ref, rates_ref, bias_ref, taps_ref,
     state_ref, uw_ref, inv_ref, trans_ref, qe_ref,
-    dout_ref, ggate_ref, value_ref, incoming_ref, place_ref, spots_ref, maps_ref, local_ref,
-    gp_ref, grates_ref, sums_ref, tail_ref, lead_ref,
-    x_ref, d_ref, carry_ref, next_ref,
+    dout_ref, value_ref, incoming_ref, place_ref, spots_ref, maps_ref, *refs,
 ):
+    *local_refs, gp_ref, grates_ref, sums_ref, tail_ref, lead_ref, x_ref, d_ref, carry_ref, next_ref = refs
     step = pl.program_id(0)
     rows_here = CHUNK * group
     conv_scratch(step == steps - 1, proj_ref, prev_ref, halo_ref, x_ref, heads, rows_here)
@@ -247,7 +246,11 @@
             grad = jnp.zeros((DV, DK), F32)
             for turn in range(peers - 1):
                 source = peers - 1 - turn
-                moved = mm(grad, maps_ref[source, h, DV:, :], 1, 1) + local_ref[source, h].astype(F32)
+                share = jnp.zeros((DV, DK), F32)
+                for b, local_ref in enumerate(local_refs):
+                    here = (place_ref[0] ^ b) == source if peers == 4 else b == source
+                    share = jnp.where(here, local_ref[h].astype(F32), share)
+                moved = mm(grad, maps_ref[source, h, DV:, :], 1, 1) + share
                 grad = jnp.where(source > place_ref[0], moved, grad)
             carry_ref[h] = grad
         d_ref[rows_here : rows_here + 8, :] = jnp.zeros((8, heads * MIX), F32)
@@ -372,10 +375,7 @@
             )
             part = taps_ref[i : i + 1, cols] * d_ref[pl.ds(row + CONV - 1 - i, CHUNK), cols]
             total = part if total is None else total + part
-        gp_ref[pl.ds(near_row(g), CHUNK), h * PER : h * PER + MIX] = total.astype(BF16)
-        gp_ref[pl.ds(near_row(g), CHUNK), h * PER + MIX : (h + 1) * PER] = ggate_ref[
-            row : row + CHUNK, h * DV : (h + 1) * DV
-        ]
+        gp_ref[pl.ds(near_row(g), CHUNK), cols] = total.astype(BF16)
         if g == group - 1:
             @pl.when(step == 0)
             def _(total=total, cols=cols):
@@ -386,7 +386,7 @@
         lead_ref[...] = d_ref[0:8, :]
 
 
-def mixer_backward(projected, halo, rates, bias_row, taps, saved, dout, ggate, value, incoming, place, spots, maps, local, group):
+def mixer_backward(projected, halo, rates, bias_row, taps, saved, dout, value, incoming, place, spots, maps, local, group):
     state, uw, inv, trans, qe = saved
     total = projected.shape[0]
     heads = rates.shape[1] // 2
@@ -412,22 +412,21 @@
             keep(CHUNK, DK),
             pl.BlockSpec((rows, heads * DV), flip),
             pl.BlockSpec((rows, heads * DV), flip),
-            pl.BlockSpec((rows, heads * DV), flip),
             pl.BlockSpec(incoming.shape, lambda i: (0, 0, 0)),
             pl.BlockSpec(memory_space=pltpu.SMEM),
             pl.BlockSpec(memory_space=pltpu.SMEM),
             pl.BlockSpec(maps.shape, lambda i: (0, 0, 0, 0)),
-            pl.BlockSpec(local.shape, lambda i: (0, 0, 0, 0)),
+            *[pl.BlockSpec(part.shape, lambda i: (0, 0, 0)) for part in local],
         ],
         out_shape=[
-            jax.ShapeDtypeStruct((total, heads * PER), BF16),
+            jax.ShapeDtypeStruct((total, heads * MIX), BF16),
             jax.ShapeDtypeStruct((total, 2 * heads), F32),
             jax.ShapeDtypeStruct((8, heads * MIX), F32),
             jax.ShapeDtypeStruct((HALO, heads * MIX), F32),
             jax.ShapeDtypeStruct((8, heads * MIX), F32),
         ],
         out_specs=[
-            pl.BlockSpec((total, heads * PER), whole),
+            pl.BlockSpec((total, heads * MIX), whole),
             pl.BlockSpec((total, 2 * heads), whole),
             pl.BlockSpec((8, heads * MIX), whole),
             pl.BlockSpec((HALO, heads * MIX), whole),
@@ -441,16 +440,20 @@
         ],
         compiler_params=pltpu.CompilerParams(vmem_limit_bytes=VMEM_LIMIT),
         cost_estimate=LIGHT,
-    )(projected, projected, halo, rates, bias_row, taps, state, uw, inv, trans, qe, dout, ggate, value, incoming, place, spots, maps, local)
-
-
-def gate_kernel(
-    heads, peers,
-    ids_ref, place_ref, maps_ref, olocal_ref, qmap_ref, proj_ref, gain_ref, *refs,
-):
-    *w_refs, value_ref, gated_ref, part_ref, incoming_ref = refs
-
-    @pl.when(pl.program_id(0) == 0)
+    )(projected, projected, halo, rates, bias_row, taps, state, uw, inv, trans, qe, dout, value, incoming, place, spots, maps, *local)
+
+
+def pair_rows(ids_ref, step, which, rows):
+    return pl.ds(pl.multiple_of(ids_ref[2 * step + which] * rows, rows), rows)
+
+
+def gate_kernel(heads, peers, ids_ref, place_ref, maps_ref, gain_ref, w_ref, *refs):
+    olocal_refs, qmap_refs = refs[0:2], refs[2:4]
+    gate_refs = refs[4 : 4 + 2 * heads]
+    value_ref, gated_ref, part_ref, incoming_ref = refs[4 + 2 * heads :]
+    step = pl.program_id(0)
+
+    @pl.when(step == 0)
     def _():
         for h in range(heads):
             state = jnp.zeros((DV, DK), F32)
@@ -459,16 +462,33 @@
                 state = jnp.where(source < place_ref[0], moved, state)
             incoming_ref[h] = state.astype(BF16)
 
+    rows = olocal_refs[0].shape[0]
     for h in range(heads):
         cols = slice(h * DV, (h + 1) * DV)
-        out = olocal_ref[:, cols] + mm(qmap_ref[:, h * DK : (h + 1) * DK], incoming_ref[h], 1, 1)
-        low = out.astype(BF16)
-        value_ref[:, cols] = low
+        query_map = jnp.concatenate([ref[:, h * DK : (h + 1) * DK] for ref in qmap_refs], axis=0)
+        out_local = jnp.concatenate([ref[:, cols] for ref in olocal_refs], axis=0)
+        low = (out_local + mm(query_map, incoming_ref[h], 1, 1)).astype(BF16)
+        for which in range(2):
+            value_ref[pair_rows(ids_ref, step, which, rows), cols] = low[which * rows : (which + 1) * rows]
         value = low.astype(F32)
         normed = value * lax.rsqrt(jnp.mean(value * value, axis=-1, keepdims=True) + epsilon)
-        gate = proj_ref[:, h * PER + MIX : (h + 1) * PER].astype(F32)
+        gate = jnp.concatenate([gate_refs[2 * h + which][...] for which in range(2)], axis=0).astype(F32)
         gated_ref[:, cols] = (normed * gain_ref[...] * (gate * sigmoid(gate))).astype(BF16)
-    part_ref[...] = mm(gated_ref[...], w_refs[0][...]).astype(BF16)
+    part_ref[...] = mm(gated_ref[...], w_ref[...]).astype(BF16)
+
+
+def gate_blocks(heads, rows):
+    full = lambda wide: [
+        pl.BlockSpec((rows, wide), lambda i, *s, which=which: (s[0][2 * i + which], 0)) for which in range(2)
+    ]
+    gates = [
+        pl.BlockSpec(
+            (rows, DV), lambda i, *s, which=which, h=h: (s[0][2 * i + which], (h + 1) * (PER // DV) - 1)
+        )
+        for h in range(heads)
+        for which in range(2)
+    ]
+    return full, gates
 
 
 def gate_output(ids, place, maps, out_local, query_map, projected, gain, w_out):
@@ -476,28 +496,28 @@
     total = projected.shape[0]
     count = ids.shape[0]
     rows = total // count
-    width = sum(w.shape[1] for w in w_out)
-    theirs = lambda i, ids, place: (ids[i], 0)
-    mine = lambda i, ids, place: (i, 0)
-    whole = lambda i, ids, place: (0, 0)
+    width = w_out.shape[1]
+    mine = lambda i, *s: (i, 0)
+    whole = lambda i, *s: (0, 0)
+    full, gates = gate_blocks(heads, rows)
     return pl.pallas_call(
         functools.partial(gate_kernel, heads, maps.shape[0]),
         grid_spec=pltpu.PrefetchScalarGridSpec(
             num_scalar_prefetch=2,
-            grid=(count,),
+            grid=(count // 2,),
             in_specs=[
-                pl.BlockSpec(maps.shape, lambda i, ids, place: (0, 0, 0, 0)),
-                pl.BlockSpec((rows, heads * DV), theirs),
-                pl.BlockSpec((rows, heads * DK), theirs),
-                pl.BlockSpec((rows, heads * PER), theirs),
+                pl.BlockSpec(maps.shape, lambda i, *s: (0, 0, 0, 0)),
                 pl.BlockSpec((1, DV), whole),
-                *[pl.BlockSpec(w.shape, whole) for w in w_out],
+                pl.BlockSpec(w_out.shape, whole),
+                *full(heads * DV),
+                *full(heads * DK),
+                *gates,
             ],
             out_specs=[
-                pl.BlockSpec((rows, heads * DV), theirs),
-                pl.BlockSpec((rows, heads * DV), mine),
-                pl.BlockSpec((rows, width), mine),
-                pl.BlockSpec((heads, DV, DK), lambda i, ids, place: (0, 0, 0)),
+                pl.BlockSpec((total, heads * DV), whole),
+                pl.BlockSpec((2 * rows, heads * DV), mine),
+                pl.BlockSpec((2 * rows, width), mine),
+                pl.BlockSpec((heads, DV, DK), lambda i, *s: (0, 0, 0)),
             ],
         ),
         out_shape=[
@@ -508,28 +528,32 @@
         ],
         compiler_params=pltpu.CompilerParams(vmem_limit_bytes=VMEM_LIMIT),
         cost_estimate=LIGHT,
-    )(ids, place, maps, out_local, query_map, projected, gain, *w_out)
-
-
-def gate_back_kernel(
-    heads,
-    ids_ref, branch_ref, value_ref, proj_ref, qmap_ref, gain_ref, *refs,
-):
-    *w_refs, ggate_ref, dout_ref, gain_grad_ref, local_ref = refs
-
-    @pl.when(pl.program_id(0) == 0)
+    )(
+        ids, place, maps, gain, w_out, out_local, out_local, query_map, query_map,
+        *[projected] * (2 * heads),
+    )
+
+
+def gate_back_kernel(heads, ids_ref, branch_ref, gain_ref, w_ref, *refs):
+    value_refs, qmap_refs = refs[0:2], refs[2:4]
+    gate_refs = refs[4 : 4 + 2 * heads]
+    ggate_ref, dout_ref, gain_grad_ref, local_ref, sum_ref = refs[4 + 2 * heads :]
+    step = pl.program_id(0)
+
+    @pl.when(step == 0)
     def _():
         gain_grad_ref[...] = jnp.zeros_like(gain_grad_ref)
-        local_ref[...] = jnp.zeros_like(local_ref)
-
-    grads = mm(branch_ref[...], w_refs[0][...], 1, 1)
+        sum_ref[...] = jnp.zeros_like(sum_ref)
+
+    rows = value_refs[0].shape[0]
+    grads = mm(branch_ref[...], w_ref[...], 1, 1)
     gain = gain_ref[...]
     for h in range(heads):
         cols = slice(h * DV, (h + 1) * DV)
-        value = value_ref[:, cols].astype(F32)
+        value = jnp.concatenate([ref[:, cols] for ref in value_refs], axis=0).astype(F32)
         inverse = lax.rsqrt(jnp.mean(value * value, axis=-1, keepdims=True) + epsilon)
         normed = value * inverse
-        gate = proj_ref[:, h * PER + MIX : (h + 1) * PER].astype(F32)
+        gate = jnp.concatenate([gate_refs[2 * h + which][...] for which in range(2)], axis=0).astype(F32)
         sig = sigmoid(gate)
         grad = grads[:, cols]
         through = grad * (gate * sig)
@@ -537,46 +561,55 @@
         gain_grad_ref[...] += jnp.sum(through * normed, axis=0, keepdims=True)
         scaled = through * gain
         low = (inverse * (scaled - normed * jnp.mean(scaled * normed, axis=-1, keepdims=True))).astype(BF16)
-        dout_ref[:, cols] = low
-        local_ref[h] += mm(low, qmap_ref[:, h * DK : (h + 1) * DK], 0, 0)
+        for which in range(2):
+            dout_ref[pair_rows(ids_ref, step, which, rows), cols] = low[which * rows : (which + 1) * rows]
+        query_map = jnp.concatenate([ref[:, h * DK : (h + 1) * DK] for ref in qmap_refs], axis=0)
+        sum_ref[h] += mm(low, query_map, 0, 0)
+
+    @pl.when(step == pl.num_programs(0) - 1)
+    def _():
+        local_ref[...] = sum_ref[...].astype(BF16)
 
 
 def gate_backward(ids, branch, w_out, value, projected, query_map, gain, heads):
     total = projected.shape[0]
     count = ids.shape[0]
     rows = total // count
-    theirs = lambda i, ids: (ids[i], 0)
-    mine = lambda i, ids: (i, 0)
-    whole = lambda i, ids: (0, 0)
+    mine = lambda i, *s: (i, 0)
+    whole = lambda i, *s: (0, 0)
+    full, gates = gate_blocks(heads, rows)
     return pl.pallas_call(
         functools.partial(gate_back_kernel, heads),
         grid_spec=pltpu.PrefetchScalarGridSpec(
             num_scalar_prefetch=1,
-            grid=(count,),
+            grid=(count // 2,),
             in_specs=[
-                pl.BlockSpec((rows, branch.shape[1]), mine),
-                pl.BlockSpec((rows, heads * DV), theirs),
-                pl.BlockSpec((rows, heads * PER), theirs),
-                pl.BlockSpec((rows, heads * DK), theirs),
+                pl.BlockSpec((2 * rows, branch.shape[1]), mine),
                 pl.BlockSpec((1, DV), whole),
-                *[pl.BlockSpec(w.shape, whole) for w in w_out],
+                pl.BlockSpec(w_out.shape, whole),
+                *full(heads * DV),
+                *full(heads * DK),
+                *gates,
             ],
             out_specs=[
-                pl.BlockSpec((rows, heads * DV), theirs),
-                pl.BlockSpec((rows, heads * DV), theirs),
+                pl.BlockSpec((2 * rows, heads * DV), mine),
+                pl.BlockSpec((total, heads * DV), whole),
                 pl.BlockSpec((1, DV), whole),
-                pl.BlockSpec((heads, DV, DK), lambda i, ids: (0, 0, 0)),
+                pl.BlockSpec((heads, DV, DK), lambda i, *s: (0, 0, 0)),
             ],
+            scratch_shapes=[pltpu.VMEM((heads, DV, DK), F32)],
         ),
         out_shape=[
             jax.ShapeDtypeStruct((total, heads * DV), BF16),
             jax.ShapeDtypeStruct((total, heads * DV), BF16),
             jax.ShapeDtypeStruct((1, DV), F32),
-            jax.ShapeDtypeStruct((heads, DV, DK), F32),
+            jax.ShapeDtypeStruct((heads, DV, DK), BF16),
         ],
         compiler_params=pltpu.CompilerParams(vmem_limit_bytes=VMEM_LIMIT),
         cost_estimate=LIGHT,
-    )(ids, branch, value, projected, query_map, gain, *w_out)
+    )(
+        ids, branch, gain, w_out, value, value, query_map, query_map, *[projected] * (2 * heads)
+    )
 
 
 def project_kernel(layout, pieces, ids_ref, spots_ref, rate_ref, *refs):
@@ -643,11 +676,19 @@
 
 
 def normed_back_kernel(pieces, blocks, spots_ref, *refs):
-    grads, rates, normed = refs[:blocks], refs[blocks : 2 * blocks], refs[2 * blocks : 3 * blocks]
-    rate_ref, before_ref = refs[3 * blocks : 3 * blocks + 2]
-    w_refs = refs[3 * blocks + 2 : 3 * blocks + 2 + pieces]
-    part_ref, sums_ref = refs[3 * blocks + 2 + pieces :]
-    left = jnp.concatenate([ref[...] for ref in grads], axis=0)
+    mixes, gates, rates, normed = (refs[i * blocks : (i + 1) * blocks] for i in range(4))
+    rate_ref, before_ref = refs[4 * blocks : 4 * blocks + 2]
+    w_refs = refs[4 * blocks + 2 : 4 * blocks + 2 + pieces]
+    part_ref, sums_ref = refs[4 * blocks + 2 + pieces :]
+    heads = gates[0].shape[1] // DV
+    left = jnp.concatenate(
+        [
+            jnp.concatenate([ref[:, h * size : (h + 1) * size] for ref in group], axis=0)
+            for h in range(heads)
+            for group, size in ((mixes, MIX), (gates, DV))
+        ],
+        axis=1,
+    )
     rate = jnp.concatenate([ref[...].astype(BF16) for ref in rates], axis=0)
     count = rate.shape[1]
     sums_ref[...] = before_ref[...]
@@ -660,10 +701,9 @@
         sums_ref[4:5, cols] += jnp.sum(part * right.astype(F32), axis=0, keepdims=True)
 
 
-def normed_back(spots, order, blocks, grad_projected, grad_rates, normed, w_mix, w_rate, before):
+def normed_back(spots, order, blocks, grad_mixed, grad_gates, grad_rates, normed, w_mix, w_rate, before):
     total, width = normed.shape
     rows = total // blocks
-    cols = w_mix[0].shape[1]
     rates = w_rate.shape[0]
     count = len(order)
     block = lambda k, wide: pl.BlockSpec((rows, wide), lambda i, spots: (k, 0))
@@ -674,7 +714,8 @@
             num_scalar_prefetch=1,
             grid=(1,),
             in_specs=[
-                *[block(k, cols) for k in order],
+                *[block(k, grad_mixed.shape[1]) for k in order],
+                *[block(k, grad_gates.shape[1]) for k in order],
                 *[block(k, rates) for k in order],
                 *[block(k, width) for k in order],
                 pl.BlockSpec((rates, width), whole),
@@ -691,7 +732,8 @@
         cost_estimate=LIGHT,
     )(
         spots,
-        *[grad_projected] * count,
+        *[grad_mixed] * count,
+        *[grad_gates] * count,
         *[grad_rates] * count,
         *[normed] * count,
         w_rate,
@@ -736,64 +778,110 @@
     )(*pieces, buffer)
 
 
-def outer_kernel(pieces, spots_ref, left_ref, right_ref, *outs):
-    product = mm(left_ref[...], right_ref[...], 0, 0).astype(BF16)
-    for b in range(pieces):
-
-        @pl.when(pl.program_id(0) == b)
-        def _(b=b):
-            outs[b][...] = product
-
-
-def outer(spots, left, right, part, parts):
+def outer_kernel(left_ref, right_ref, out_ref):
+    out_ref[...] = mm(left_ref[...], right_ref[...], 0, 0).astype(BF16)
+
+
+def outer(left, right):
     total, m = left.shape
-    pieces = spots.shape[0]
-    n = right.shape[1] // parts
-    shape = (m // pieces, n)
+    n = right.shape[1]
+    by_rows = m % 512 == 0 and m > 512
+    rows = 512 if by_rows else m
+    cols = n if by_rows or n % 512 else 512
     return pl.pallas_call(
-        functools.partial(outer_kernel, pieces),
-        grid_spec=pltpu.PrefetchScalarGridSpec(
-            num_scalar_prefetch=1,
-            grid=(pieces,),
-            in_specs=[
-                pl.BlockSpec((total, m // pieces), lambda i, spots: (0, spots[i])),
-                pl.BlockSpec((total, n), lambda i, spots: (0, part)),
-            ],
-            out_specs=[pl.BlockSpec(shape, lambda i, spots: (0, 0))] * pieces,
-        ),
-        out_shape=[jax.ShapeDtypeStruct(shape, BF16)] * pieces,
+        outer_kernel,
+        grid=(m // rows, n // cols),
+        in_specs=[
+            pl.BlockSpec((total, rows), lambda i, j: (0, i)),
+            pl.BlockSpec((total, cols), lambda i, j: (0, j)),
+        ],
+        out_specs=pl.BlockSpec((rows, cols), lambda i, j: (i, j)),
+        out_shape=jax.ShapeDtypeStruct((m, n), BF16),
         compiler_params=pltpu.CompilerParams(vmem_limit_bytes=VMEM_LIMIT),
         cost_estimate=LIGHT,
-    )(spots, left, right)
-
-
-def add_kernel(sizes, *refs):
-    outs = refs[3 * sum(sizes) :]
-    at = 0
-    for out_ref, size in zip(outs, sizes):
-        start = 0
-        for _ in range(size):
-            one, two, three = refs[at : at + 3]
-            cols = slice(start, start + one.shape[1])
-            out_ref[:, cols] = one[...].astype(F32) + two[...].astype(F32) + three[...].astype(F32)
-            start += one.shape[1]
-            at += 3
-
-
-def add_all(groups):
-    steps = 4
-    flat = [a for group in groups for triple in group for a in triple]
-    spec = lambda rows, wide: pl.BlockSpec((rows // steps, wide), lambda i: (i, 0))
-    shapes = [(group[0][0].shape[0], sum(t[0].shape[1] for t in group)) for group in groups]
+    )(left, right)
+
+
+def turn_kernel(count, *refs):
+    for i in range(count):
+        refs[count + i][...] = refs[i][...].astype(F32).T.astype(BF16)
+
+
+def turned(arrays):
+    rows, width = arrays[0].shape
+    step = 512
     return pl.pallas_call(
-        functools.partial(add_kernel, [len(group) for group in groups]),
-        grid=(steps,),
-        in_specs=[spec(*a.shape) for a in flat],
-        out_specs=[spec(*shape) for shape in shapes],
-        out_shape=[jax.ShapeDtypeStruct(shape, F32) for shape in shapes],
+        functools.partial(turn_kernel, len(arrays)),
+        grid=(width // step,),
+        in_specs=[pl.BlockSpec((rows, step), lambda i: (0, i))] * len(arrays),
+        out_specs=[pl.BlockSpec((step, rows), lambda i: (i, 0))] * len(arrays),
+        out_shape=[jax.ShapeDtypeStruct((width, rows), BF16)] * len(arrays),
         compiler_params=pltpu.CompilerParams(vmem_limit_bytes=VMEM_LIMIT),
         cost_estimate=LIGHT,
-    )(*flat)
+    )(*arrays)
+
+
+def widen_kernel(count, *refs):
+    for i in range(count):
+        refs[count + i][...] = refs[i][...].astype(F32)
+
+
+def widen(arrays):
+    steps = 4
+    specs = [pl.BlockSpec((a.shape[0] // steps, a.shape[1]), lambda i: (i, 0)) for a in arrays]
+    return pl.pallas_call(
+        functools.partial(widen_kernel, len(arrays)),
+        grid=(steps,),
+        in_specs=specs,
+        out_specs=specs,
+        out_shape=[jax.ShapeDtypeStruct(a.shape, F32) for a in arrays],
+        compiler_params=pltpu.CompilerParams(vmem_limit_bytes=VMEM_LIMIT),
+        cost_estimate=LIGHT,
+    )(*arrays)
+
+
+def join_kernel(heads, mix_ref, gate_ref, out_ref):
+    for h in range(heads):
+        out_ref[:, h * PER : h * PER + MIX] = mix_ref[:, h * MIX : (h + 1) * MIX].astype(F32)
+        out_ref[:, h * PER + MIX : (h + 1) * PER] = gate_ref[:, h * DV : (h + 1) * DV].astype(F32)
+
+
+def join_heads(mix, gate):
+    rows = mix.shape[0]
+    heads = gate.shape[1] // DV
+    steps = 4
+    spec = lambda wide: pl.BlockSpec((rows // steps, wide), lambda i: (i, 0))
+    return pl.pallas_call(
+        functools.partial(join_kernel, heads),
+        grid=(steps,),
+        in_specs=[spec(mix.shape[1]), spec(gate.shape[1])],
+        out_specs=spec(heads * PER),
+        out_shape=jax.ShapeDtypeStruct((rows, heads * PER), F32),
+        compiler_params=pltpu.CompilerParams(vmem_limit_bytes=VMEM_LIMIT),
+        cost_estimate=LIGHT,
+    )(mix, gate)
+
+
+def times_kernel(left_ref, right_ref, out_ref):
+    out_ref[...] = mm(left_ref[...], right_ref[...])
+
+
+def times(left, right):
+    total, depth = left.shape
+    n = right.shape[1]
+    rows = 256
+    return pl.pallas_call(
+        times_kernel,
+        grid=(total // rows,),
+        in_specs=[
+            pl.BlockSpec((rows, depth), lambda i: (i, 0)),
+            pl.BlockSpec((depth, n), lambda i: (0, 0)),
+        ],
+        out_specs=pl.BlockSpec((rows, n), lambda i: (i, 0)),
+        out_shape=jax.ShapeDtypeStruct((total, n), F32),
+        compiler_params=pltpu.CompilerParams(vmem_limit_bytes=VMEM_LIMIT),
+        cost_estimate=LIGHT,
+    )(left, right)
 def ring_order(count):
     return list(range(0, count, 2)) + list(range(1, count, 2))[::-1]
 
@@ -913,24 +1001,19 @@
     return [shard, swap(after(shard, *pins), axis, 1), far, swap(after(far, *pins), axis, 1)]
 
 
-def pair_across(pieces, axis):
+def seq_shards(value, axis):
     if lax.axis_size(axis) != 4:
-        return None
-    return swap(pieces[3], axis, 1), swap(pieces[1], axis, 1)
-
-
-def pair_far_sum(pieces, crossed, axis, pin):
-    if crossed is None:
-        return lax.psum_scatter(jnp.stack(pieces), axis, scatter_dimension=0)
-    return swap(pin(pieces[2]) + crossed[0], axis, 2)
-
-
-def round_sum(value, axis):
-    count = lax.axis_size(axis)
-    level = [value] + [swap(value, axis, bit) for bit in range(1, count)]
-    while len(level) > 1:
-        level = [level[i] + level[i + 1] for i in range(0, len(level), 2)]
-    return level[0]
+        whole = lax.all_gather(value, axis)
+        return [whole[b] for b in range(lax.axis_size(axis))]
+    return [value] + [swap(value, axis, b) for b in range(1, 4)]
+
+
+def butterfly(value, axis):
+    bit = 1
+    while bit < lax.axis_size(axis):
+        value = value + swap(value, axis, bit)
+        bit *= 2
+    return value
 
 
 def per_device(
@@ -1004,22 +1087,13 @@
         keep["mix"] = pair_gather(w_qkvg, pin(mix_far), "seq")
         return keep["mix"]
 
-    def cot_window(hop, other=lambda pin: []):
-        def filler(pin):
-            made = list(other(pin))
-            forward, backward = cot_state
-            cot_state[:] = [pin(forward), pin(backward)]
-            return made + cot_hop(hop)
-
-        return filler
-
-    fillers = {last_window: cot_window(1)} | {last_window - 1: fetch_mix}
+    fillers = {last_window: fetch_mix}
     normed_found = ring_gather((norm_normed * norm_gain).astype(BF16), "head", fillers, False)
     w_mix = keep["mix"]
     out_rows = lax.all_gather(after(w_out, mix_far), "seq", axis=1, tiled=True)
 
     stage_hops = {
-        stage: range(2 + (hops - 1) * stage // 3, 2 + (hops - 1) * (stage + 1) // 3) for stage in range(3)
+        stage: range(1 + hops * stage // stages, 1 + hops * (stage + 1) // stages) for stage in range(stages)
     }
 
     def cot_stage(stage, gate):
@@ -1038,10 +1112,12 @@
         projected, halo_rows, rates, bias_row, conv_weight, GROUP
     )
     end_state, *_ = together(end_state, *cot_state)
+    cot_stage(2, end_state)
     maps = lax.all_gather(end_state, "seq")
-    cot_stage(2, maps)
+    maps, *_ = together(maps, *cot_state)
+    cot_stage(3, maps)
     value, gated, branch_part, incoming = gate_output(
-        ids, place, maps, out_local, query_map, projected, gain_row, [out_rows]
+        ids, place, maps, out_local, query_map, projected, gain_row, out_rows
     )
     branch_part, *_ = together(branch_part, *cot_state)
     fetch = lambda w, *pins: lax.all_gather(after(w, *pins), "seq", axis=1, tiled=True)
@@ -1057,6 +1133,14 @@
         keep["cot"] = stacked({k: [pin(p) for p in ps] for k, ps in cot_found.items()}, seq_rows)
         return (keep["cot"],)
 
+    def turn_down(pin):
+        keep["down_t"] = turned([pin(down_w)])
+        return keep["down_t"]
+
+    def turn_others(pin):
+        keep["others_t"] = turned([pin(gate_w), pin(up_w)])
+        return keep["others_t"]
+
     residual = inputs + ring_scatter(
         near_rows(branch_part, own_rows), own_rows, "head", {1: stack_cotangent, 2: stack_normed}
     )
@@ -1064,14 +1148,13 @@
     mlp_normed = residual * inverse_two
 
     def hidden_gradient(pin):
-        keep["gh"] = dot(pin(keep["cot"]), down_w, contract)
+        keep["gh"] = times(pin(keep["cot"]), keep["down_t"][0])
         return (keep["gh"],)
 
-    mlp_near = ring_gather((mlp_normed * mlp_gain).astype(BF16), "head", {2: hidden_gradient})
+    mlp_near = ring_gather((mlp_normed * mlp_gain).astype(BF16), "head", {1: turn_down, 2: hidden_gradient, 3: turn_others})
     normed, cotangent_near, grad_hidden = keep["normed"], keep["cot"], keep["gh"]
 
-    gate_pre = dot(mlp_near, gate_w, contract)
-    up_pre = dot(mlp_near, up_w, contract)
+    gate_pre, up_pre = (dot(mlp_near, w, plain) for w in keep["others_t"])
     ff_sigmoid = jax.nn.sigmoid(gate_pre)
     ff_silu = gate_pre * ff_sigmoid
     hidden = (ff_silu * up_pre).astype(BF16)
@@ -1080,16 +1163,21 @@
     grad_up_pre = (grad_hidden * ff_silu).astype(BF16)
     grad_mlp_part = (dot(grad_gate_pre, gate_w, plain) + dot(grad_up_pre, up_w, plain)).astype(BF16)
 
-    def weight_product(name, left, right):
+    scatter = lambda a: lax.psum_scatter(a, "seq", scatter_dimension=1, tiled=True)
+
+    def weight_product(name, left, right, before=None):
         def filler(pin):
-            keep[name] = dot(pin(left), right, rows_first).astype(BF16)
-            return (keep[name],)
+            made = [outer(pin(left), right)] if left is not None else []
+            if before is not None:
+                keep[before, "sum"] = scatter(pin(keep[before]))
+            if made:
+                keep[name] = made[0]
+            return made
 
         return filler
 
-    scatter = lambda a: lax.psum_scatter(a, "seq", scatter_dimension=1, tiled=True).astype(F32)
-
     def output_rows(pin):
+        keep["up", "sum"] = scatter(pin(keep["up"]))
         keep["output"] = dot(pin(hidden), down_w, plain).astype(BF16)
         return (keep["output"],)
 
@@ -1099,8 +1187,8 @@
         "head",
         {
             1: weight_product("down", hidden, cotangent_near),
-            2: weight_product("gate", grad_gate_pre, mlp_near),
-            3: weight_product("up", grad_up_pre, mlp_near),
+            2: weight_product("gate", grad_gate_pre, mlp_near, "down"),
+            3: weight_product("up", grad_up_pre, mlp_near, "gate"),
             4: output_rows,
         },
     )
@@ -1112,31 +1200,10 @@
         scaled_two - mlp_normed * jnp.mean(scaled_two * mlp_normed, axis=-1, keepdims=True)
     )
 
-    def total_all(groups, pin=lambda value: value):
-        if peers == 4:
-            sums = add_all(
-                [[(keep[n][0], keep[n, "crossed"][1], pin(keep[n, "far"])) for n in group] for group in groups]
-            )
-        else:
-            sums = [
-                jnp.concatenate([keep[n, "far"].astype(F32) for n in group], axis=1) for group in groups
-            ]
-        for group, value in zip(groups, sums):
-            keep[group[0], "total"] = value
-        return sums
-
-    def far_sums(*names):
-        def filler(pin):
-            for name in names:
-                keep[name, "far"] = pair_far_sum(keep[name], keep[name, "crossed"], "seq", pin)
-            return [keep[name, "far"] for name in names]
-
-        return filler
-
-    grad_down_s = scatter(keep["down"])
-    grad_gate_s = scatter(keep["gate"])
-    grad_up_s = scatter(keep["up"])
-    branch_near = ring_gather(grad_residual.astype(BF16), "head")
+    grad_down_s, grad_gate_s, grad_up_s = (keep[name, "sum"] for name in ("down", "gate", "up"))
+    branch_near = ring_gather(
+        grad_residual.astype(BF16), "head", {2: lambda pin: [grad_down_s], 4: lambda pin: [grad_gate_s]}
+    )
     take_output = near_rows(output_part, own_rows)
     output_state = [None, None]
     known = lambda: [a for a in output_state if a is not None]
@@ -1155,36 +1222,40 @@
 
     output_hops(1, branch_near)
     grad_gate_mix, grad_mixer, head_gain_part, local_grad = gate_backward(
-        ids, branch_near, [out_rows], value, projected, query_map, gain_row, heads
-    )
-    local_low, *_ = together(local_grad.astype(BF16), *known())
-    output_hops(2, local_low)
-    locals_all = lax.all_gather(local_low, "seq")
-    grad_projected, grad_rates, seq_sums, tail_rows, lead_rows = mixer_backward(
+        ids, branch_near, out_rows, value, projected, query_map, gain_row, heads
+    )
+    local_low, *_ = together(local_grad, *known())
+    shares = seq_shards(local_low, "seq")
+    gate_grad_w = outer(keep["normed"], together(grad_gate_mix, *shares[1:])[0])
+    first_share, gate_grad_w = together(shares[0], gate_grad_w)
+    gate_grad_s = lax.psum_scatter(gate_grad_w, "seq", scatter_dimension=0, tiled=True)
+    output_hops(2, gate_grad_w)
+    grad_mixed, grad_rates, seq_sums, tail_rows, lead_rows = mixer_backward(
         projected, halo_rows, rates, bias_row, conv_weight, saved,
-        grad_mixer, grad_gate_mix, value, incoming, place, near_spots, maps, locals_all, GROUP,
-    )
-    grad_projected, *_ = together(grad_projected, *known())
+        grad_mixer, value, incoming, place, near_spots, maps, [first_share, *shares[1:]], GROUP,
+    )
+    grad_mixed, gate_grad_s, grad_up_s, *_ = together(grad_mixed, gate_grad_s, grad_up_s, *known())
     later_rows = shifted(lead_rows, "seq", -1)
-    output_hops(3, grad_projected)
-    grad_out_w = dot(after(gated, lead_rows), branch_near, rows_first).astype(BF16)
-    grad_projected, grad_out_w = together(grad_projected, grad_out_w)
-    grad_out_s = scatter(grad_out_w)
+    out_grad_w = outer(gated, after(branch_near, lead_rows))
+    output_hops(3, grad_mixed)
     padded = jnp.concatenate([jnp.zeros((HALO, heads * MIX), F32), later_rows])
     last_rows = tail_rows + sum(
         conv_weight[i] * padded[CONV - 1 - i : CONV - 1 - i + HALO] for i in range(CONV)
     )
     last_start = near_spots[count - 1] * own_rows + own_rows - HALO
-    for h in range(heads):
-        grad_projected = lax.dynamic_update_slice(
-            grad_projected, last_rows[:, h * MIX : (h + 1) * MIX].astype(BF16), (last_start, h * PER)
-        )
+    grad_mixed = lax.dynamic_update_slice(grad_mixed, last_rows.astype(BF16), (last_start, 0))
+    grad_mixed, out_grad_w = together(grad_mixed, out_grad_w)
+    mix_grad_w = outer(keep["normed"], grad_mixed)
+    mix_grad_w, out_grad_w = together(mix_grad_w, out_grad_w)
+    grad_out_s = scatter(out_grad_w)
+    grad_mixed, mix_grad_w = together(grad_mixed, mix_grad_w)
+    mix_grad_s = lax.psum_scatter(mix_grad_w, "seq", scatter_dimension=0, tiled=True)
     early = [hops] + ([hops - 1, hops + 1] if hops > 1 else [])
     late = [k for s in range(hops - 2, 0, -1) for k in (s, count - s)] + [0]
     place_of = {k: (0, i) for i, k in enumerate(early)} | {k: (1, i) for i, k in enumerate(late)}
     parts = []
     part, sums = normed_back(
-        spots, early, count, grad_projected, grad_rates, normed, w_mix, w_rate, jnp.zeros((8, width), F32)
+        spots, early, count, grad_mixed, grad_gate_mix, grad_rates, normed, w_mix, w_rate, jnp.zeros((8, width), F32)
     )
     parts.append(part)
 
@@ -1194,40 +1265,32 @@
 
     def late_rows(pin):
         part, keep["sums"] = normed_back(
-            spots, late, count, pin(grad_projected), grad_rates, normed, w_mix, w_rate, sums
+            spots, late, count, pin(grad_mixed), grad_gate_mix, grad_rates, normed, w_mix, w_rate, sums
         )
         parts.append(part)
         return (part,)
 
-    mixes = [("mix", h) for h in range(heads)]
-
     def first_window(pin):
         output_hops(4, pin(part))
         return (*late_rows(pin), *known())
 
     def second_window(pin):
-        keep[mixes[0]] = outer(spots, normed, pin(grad_projected), 0, heads)
-        keep[mixes[0], "crossed"] = pair_across(keep[mixes[0]], "seq")
         sums = pin(keep["sums"])
-        gains = jnp.concatenate([sums[4:5], mlp_gain_part[None], head_gain_part], axis=1)
-        keep["gains"] = round_sum(gains, "head")
-        keep["small"] = jnp.concatenate([sums, seq_sums], axis=1)
-        return (*keep[mixes[0]], keep["gains"], keep["small"])
+        gains = jnp.concatenate([mlp_gain_part[None], head_gain_part, jnp.zeros((1, width - DV), F32)], axis=1)
+        gains = jnp.pad(gains, ((4, 3), (0, 0)))
+        small = jnp.concatenate([sums, gains, seq_sums], axis=1)
+        small = small + swap(small, "seq", 1)
+        keep["gains"] = butterfly(small[4:5, : 3 * width], "head")
+        keep["small"] = small
+        return (grad_out_s,)
+
+    def fourth_window(pin):
+        keep["joined"] = join_heads(pin(mix_grad_s), gate_grad_s)
+        return (keep["joined"],)
 
     def third_window(pin):
-        made = []
-        for h, name in enumerate(mixes[1:]):
-            keep[name] = outer(spots, normed, pin(grad_projected), h + 1, heads)
-            keep[name, "crossed"] = pair_across(keep[name], "seq")
-            made += keep[name]
-        keep["gains"] = round_sum(pin(keep["gains"]), "seq")
-        keep["small"] = round_sum(pin(keep["small"]), "seq")
-        far_sums(mixes[0])(pin)
-        return (*made, keep["gains"], keep["small"])
-
-    def fourth_window(pin):
-        far_sums(*mixes[1:])(pin)
-        return [keep[mixes[0], "far"]]
+        keep["wide"] = widen([pin(a) for a in (grad_down_s, grad_gate_s, grad_up_s)])
+        return keep["wide"]
 
     grad_normed = ring_scatter(
         take, own_rows, "head", {1: first_window, 2: second_window, 3: third_window, 4: fourth_window}
@@ -1239,24 +1302,29 @@
     output = (
         residual + sum(a.astype(F32) for a in known()) + take_output(0, 0, own_rows).astype(F32)
     ).astype(BF16)
-    pin = lambda value: after(value, grad_normed)
-    total_all([mixes])
-    small, gains = keep["small"], keep["gains"]
+    row = jnp.pad(keep["gains"], ((0, 7), (0, keep["small"].shape[1] - 3 * width)))
+    small = jnp.concatenate([keep["small"], row], axis=0)
+    bit = 2
+    while bit < peers:
+        small = small + swap(small, "seq", bit)
+        bit *= 2
+    gains = small[8:9]
+    (wide_out,) = widen([grad_out_s])
     per_seq = w_rates.shape[0]
     return (
         output,
         grad_input,
-        keep[mixes[0], "total"],
+        keep["joined"],
         lax.dynamic_slice_in_dim(small[: 2 * heads], place[0] * per_seq, per_seq, 1).T,
-        small[:CONV, width:],
-        small[CONV, width : width + 2 * heads].reshape(heads, 2).T,
+        small[:CONV, 3 * width :],
+        small[CONV, 3 * width : 3 * width + 2 * heads].reshape(heads, 2).T,
         gains[0, :width] / norm_gain,
-        gains[0, 2 * width :],
+        gains[0, 2 * width : 2 * width + DV],
         gains[0, width : 2 * width],
-        grad_out_s,
-        grad_gate_s,
-        grad_up_s,
-        grad_down_s,
+        wide_out,
+        keep["wide"][1],
+        keep["wide"][2],
+        keep["wide"][0],
     )
 
 

time: 623 us -> 564 us (0.905)
  waiting for transfers between devices: 198 us -> 151 us
  Pallas kernels: 147 us -> 191 us
  matrix products: 62.8 us -> 25.8 us
  starting transfers between devices: 110 us -> 101 us
    ppermute x81, waiting for transfers between devices: 175 us -> 117 us  [ring_step(): lax.ppermute(value, axis, [(order[i], order[(i + step) % count]) for i in...]
    pallas_call x3 -> x12, Pallas kernels: 22.2 us -> 71.9 us  [the longest x6 42.2 us: outer(): pl.pallas_call(outer_kernel, grid=(m // rows, n // cols), in_specs=[pl.Bl...]
    dot_general x10 -> x5, matrix products: 62.8 us -> 25.8 us  [per_device(): lax.dot_general(a, b, dims, preferred_element_type=F32)]
    ppermute x25 -> x14, starting transfers between devices: 22.8 us -> 11.7 us  [swap(): return lax.ppermute(value, axis, [(i, i ^ bit) for i in range(count)])]
    ppermute x25 -> x14, waiting for transfers between devices: 22.1 us -> 32.9 us  [swap(): return lax.ppermute(value, axis, [(i, i ^ bit) for i in range(count)])]
    convert_element_type x6 -> x1, other arithmetic: 10.7 us -> 0.35 us  [per_device(): grad_residual.astype(BF16)]
    all_gather x1 -> x0, blocking collectives: 6.94 us -> none  [per_device(): locals_all = lax.all_gather(local_low, 'seq')]
    add x9, other arithmetic: 6.86 us -> 13.2 us  [ring_scatter(): flow[way] = piece if flow[way] is None else flow[way] + piece]
  transfers between devices with their start and end apart: 116 -> 107, of which waited for: 56 -> 48; matrix products, arithmetic and copies ran while one was open for 15% -> 9% of each run, Pallas kernels for 24% -> 33%
where the time goes in v4:
time: 564 us; the launch traced here: 556 us
  Pallas kernels  191 us (34%)
  waiting for transfers between devices  151 us (27%)
  starting transfers between devices  101 us (18%)
  other arithmetic  35 us (6%)
  matrix products  25.8 us (5%)
  local copies, waits for them, and re-layouts  22.8 us (4%)
  between operations  16.2 us (3%)
  blocking collectives  12.7 us (2%)
    ppermute x81, waiting for transfers between devices, ring_step(): lax.ppermute(value, axis, [(order[i], order[(i + step) % count]) for i in...  117 us
    ppermute x81, starting transfers between devices, ring_step(): lax.ppermute(value, axis, [(order[i], order[(i + step) % count]) for i in...  85.8 us
    pallas_call x6, Pallas kernels, outer(): pl.pallas_call(outer_kernel, grid=(m // rows, n // cols), in_specs=[pl.Bl...  42.2 us
    ppermute x14, waiting for transfers between devices, swap(): return lax.ppermute(value, axis, [(i, i ^ bit) for i in range(count)])  32.9 us
    pallas_call x1, Pallas kernels, mixer_backward(): pl.pallas_call(functools.partial(backward_kernel, heads, group, steps, ma...  27.6 us
    dot_general x5, matrix products, per_device(): lax.dot_general(a, b, dims, preferred_element_type=F32)  25.8 us
    pallas_call x2, Pallas kernels, normed_back(): pl.pallas_call(functools.partial(normed_back_kernel, len(w_mix), count),...  21.1 us
    pallas_call x4, Pallas kernels, stacked(): pl.pallas_call(functools.partial(stack_kernel, layout), out_shape=jax.Sha...  18 us
  transfers between devices with their start and end apart: 107, of which 48 were waited for; matrix products, arithmetic and copies ran while one was open for 9% of the time, Pallas kernels for 33%

profile of v4, /device:TPU:0, one launch (start us, length us, event | category | flops | bytes accessed | tf_op | source)
XLA Modules:
  0.0 555.5 jit_solution(1381338287047593175)
XLA Ops:
  10.3 3.0 collective-permute-start.3
  15.3 10.0 %collective-permute-done.3.refs_1_ = bf16[128,2048]{1,0:T(8,128)(2,1)S(1)} collective-permute-done((bf16[128,2048]{1,0:T(8,128)(2,1)S(1)}, bf16[128,2048]{1,0:T(8,128)(2,1)S(1)}, u32[]{:S(2)}, u32[]{:S(2)}) %collective-permute-start.3) | collective-permute-done | bytes 524320 | tf_op jit(solution)/shard_map/ppermute | solution.py:892
  28.7 10.4 %collective-permute-done.5.refs_3_ = bf16[128,2048]{1,0:T(8,128)(2,1)S(1)} collective-permute-done((bf16[128,2048]{1,0:T(8,128)(2,1)S(1)}, bf16[128,2048]{1,0:T(8,128)(2,1)S(1)}, u32[]{:S(2)}, u32[]{:S(2)}) %collective-permute-start.5) | collective-permute-done | bytes 524320 | tf_op jit(solution)/shard_map/ppermute | solution.py:892
  42.5 9.2 %collective-permute-done.7.refs_5_ = bf16[128,2048]{1,0:T(8,128)(2,1)S(1)} collective-permute-done((bf16[128,2048]{1,0:T(8,128)(2,1)S(1)}, bf16[128,2048]{1,0:T(8,128)(2,1)S(1)}, u32[]{:S(2)}, u32[]{:S(2)}) %collective-permute-start.7) | collective-permute-done | bytes 524320 | tf_op jit(solution)/shard_map/ppermute | solution.py:892
  59.6 3.4 collective-permute-done.9.refs_7_
  67.8 14.8 %shard_map.237 = (bf16[1024,1536]{1,0:T(8,128)(2,1)}, f32[1024,4]{1,0:T(8,128)}) custom-call(s32[8]{0:T(128)} %get-tuple-element.481.ids_ref, s32[4]{0:T(128)} %iota_xor_fusion.spots_ref, bf16[4,2048]{1,0:T(4,128)(2,1)} %copy-done.37, bf16[128,2048]{1,0:T(8,128)(2,1)} %copy-done.3, bf16[128,2048]{1,0:T(8,128)(2,1)} %copy-done.12, ...), custom_call_target="tpu_custom_call" | custom-call | flops 1 | bytes 1 | tf_op jit(solution)/shard_map/pallas_call | solution.py:661
  88.4 14.4 %shard_map.238 = (f32[1024,512]{1,0:T(8,128)}, bf16[1024,256]{1,0:T(8,128)(2,1)}, bf16[2,8,384,128]{3,2,1,0:T(8,128)(2,1)}, bf16[2,8,128,384]{3,2,1,0:T(8,128)(2...) custom-call(bf16[1024,1536]{1,0:T(8,128)(2,1)} %get-tuple-element.21, ...), custom_call_target="tpu_custom_call" | custom-call | flops 1 | bytes 1 | tf_op jit(solution)/shard_map/pallas_call | solution.py:205
  104.9 12.7 %all-gather = bf16[8,384,128]{2,1,0:T(8,128)(2,1)} all-gather(bf16[2,384,128]{2,1,0:T(8,128)(2,1)} %get-tuple-element.216), channel_id=2, replica_groups=mesh['seq'=4,'head'=8] {'seq'}, dimensions={0}, use_global_device_ids=true | all-gather | bytes 983040 | tf_op jit(solution)/shard_map/all_gather | solution.py:1116
  120.6 9.6 %shard_map.239 = (bf16[1024,512]{1,0:T(8,128)(2,1)}, bf16[1024,512]{1,0:T(8,128)(2,1)}, bf16[1024,2048]{1,0:T(8,128)(2,1)}, bf16[2,256,128]{2,1,0:T(8,128)(2,1)}) custom-call(s32[8]{0:T(128)} %get-tuple-element.481.ids_ref, s32[1]{0:T(128)} %bitcast.1.place_ref, bf16[4,2,384,128]{3,2,1,0:T(8,128)(2,1)} %bitcast.34, f32[1,256]{1,0:T(1,128)} %bitcast.44, ...), custom_call_target="tpu_custom_call" | custom-call | flops 1 | bytes 1 | tf_op jit(solution)/shard_map/pallas_call | solution.py:503
  133.7 4.5 shard_map.240.left_ref.right_ref
  145.8 4.6 shard_map.241.left_ref.refs_9_.refs_10_.refs_11_.refs_15_.refs_16_.refs_17_.refs_18_.refs_19_
  160.6 5.2 collective-permute-done.29
  174.1 4.2 collective-permute-done.33
  185.3 4.6 shard_map.242.right_ref
  189.9 4.9 collective-permute-done.37.refs_2_
  197.5 7.7 %shard_map.243 = f32[1024,704]{1,0:T(8,128)} custom-call(bf16[1024,2048]{1,0:T(8,128)(2,1)} %shard_map.240.left_ref.right_ref, bf16[2048,704]{1,0:T(8,128)(2,1)} %shard_map.242.right_ref), custom_call_target="tpu_custom_call" | custom-call | flops 1 | bytes 1 | tf_op jit(solution)/shard_map/pallas_call | solution.py:873
  210.4 6.1 %shard_map.244 = (bf16[2048,704]{1,0:T(8,128)(2,1)}, bf16[2048,704]{1,0:T(8,128)(2,1)}) custom-call(bf16[704,2048]{1,0:T(8,128)(2,1)} %all-gather.10.cloned.1.call-done.refs_0_, bf16[704,2048]{1,0:T(8,128)(2,1)} %all-gather.12.cloned.1.call-done.refs_1_), custom_call_target="tpu_custom_call" | custom-call | flops 1 | bytes 1 | tf_op jit(solution)/shard_map/pallas_call | solution.py:813
  216.5 4.0 collective-permute-done.41.refs_6_
  223.2 4.2 shard_map.245.buffer_ref
  230.7 6.3 %fusion.29 = f32[1024,704]{1,0:T(8,128)S(1)} fusion(bf16[1024,2048]{1,0:T(8,128)(2,1)} %shard_map.246.right_ref, bf16[2048,704]{1,0:T(8,128)(2,1)} %get-tuple-element.271), kind=kOutput, calls=%fused_computation.112 | convolution fusion | flops 2952790016 | bytes 9961472 | tf_op jit(solution)/shard_map/dot_general | solution.py:1038
  237.1 5.7 %multiply_convert_fusion = (bf16[1024,704]{1,0:T(8,128)(2,1)S(1)}, bf16[1024,704]{1,0:T(8,128)(2,1)S(1)}, bf16[1024,704]{1,0:T(8,128)(2,1)}) fusion(f32[1024,704]{1,0:T(8,128)S(1)} %copy-done.8, f32[1024,704]{1,0:T(8,128)S(1)} %fusion.29, bf16[1024,2048]{1,0:T(8,128)(2,1)S(1)} %copy-done, bf16[2048,704]{1,0:T(8,128)(2,1)S(1)} %copy-done.61), kind=kOutput, calls=%fused_computation.2 | convolution fusion | flops 2963603456 | bytes 17170432 | tf_op jit(solution)/shard_map/dot_general | solution.py:1038
  242.7 3.4 fusion.30
  246.2 3.7 add_convert_fusion
  254.0 7.1 %shard_map.247 = bf16[704,2048]{1,0:T(8,128)(2,1)} custom-call(bf16[1024,704]{1,0:T(8,128)(2,1)} %get-tuple-element.293.left_ref, bf16[1024,2048]{1,0:T(8,128)(2,1)} %shard_map.240.left_ref.right_ref), custom_call_target="tpu_custom_call" | custom-call | flops 1 | bytes 1 | tf_op jit(solution)/shard_map/pallas_call | solution.py:791
  266.6 7.3 %shard_map.248 = bf16[704,2048]{1,0:T(8,128)(2,1)} custom-call(bf16[1024,704]{1,0:T(8,128)(2,1)} %copy-done.21, bf16[1024,2048]{1,0:T(8,128)(2,1)} %shard_map.246.right_ref), custom_call_target="tpu_custom_call" | custom-call | flops 1 | bytes 1 | tf_op jit(solution)/shard_map/pallas_call | solution.py:791
  277.1 3.0 collective-permute-start.51
  280.1 2.7 collective-permute-start.53
  282.9 7.2 %shard_map.249 = bf16[704,2048]{1,0:T(8,128)(2,1)} custom-call(bf16[1024,704]{1,0:T(8,128)(2,1)} %copy-done.20, bf16[1024,2048]{1,0:T(8,128)(2,1)} %shard_map.246.right_ref), custom_call_target="tpu_custom_call" | custom-call | flops 1 | bytes 1 | tf_op jit(solution)/shard_map/pallas_call | solution.py:791
  290.9 3.8 collective-permute-done.54
  301.6 6.7 %convolution_convert_fusion = bf16[1024,2048]{1,0:T(8,128)(2,1)} fusion(bf16[1024,704]{1,0:T(8,128)(2,1)S(1)} %copy-done.19, bf16[704,2048]{1,0:T(8,128)(2,1)} %all-gather.8.cloned.1.call-done.refs_0_), kind=kOutput, calls=%fused_computation.1 | convolution fusion | flops 2954887168 | bytes 8519680 | tf_op jit(solution)/shard_map/dot_general | solution.py:1038
  308.8 3.3 collective-permute-done.57
  318.7 9.0 %collective-permute-done.59.refs_2_ = bf16[128,2048]{1,0:T(8,128)(2,1)S(1)} collective-permute-done((bf16[128,2048]{1,0:T(8,128)(2,1)S(1)}, bf16[128,2048]{1,0:T(8,128)(2,1)S(1)}, u32[]{:S(2)}, u32[]{:S(2)}) %collective-permute-start.59) | collective-permute-done | bytes 524320 | tf_op jit(solution)/shard_map/ppermute | solution.py:892
  330.8 9.0 %collective-permute-done.61.refs_4_ = bf16[128,2048]{1,0:T(8,128)(2,1)S(1)} collective-permute-done((bf16[128,2048]{1,0:T(8,128)(2,1)S(1)}, bf16[128,2048]{1,0:T(8,128)(2,1)S(1)}, u32[]{:S(2)}, u32[]{:S(2)}) %collective-permute-start.61) | collective-permute-done | bytes 524320 | tf_op jit(solution)/shard_map/ppermute | solution.py:892
  342.9 7.4 %collective-permute-done.63.refs_6_ = bf16[128,2048]{1,0:T(8,128)(2,1)S(1)} collective-permute-done((bf16[128,2048]{1,0:T(8,128)(2,1)}, bf16[128,2048]{1,0:T(8,128)(2,1)S(1)}, u32[]{:S(2)}, u32[]{:S(2)}) %collective-permute-start.63) | collective-permute-done | bytes 524320 | tf_op jit(solution)/shard_map/ppermute | solution.py:892
  356.7 4.7 shard_map.250.buffer_ref
  364.0 10.1 %shard_map.252 = (bf16[1024,512]{1,0:T(8,128)(2,1)}, bf16[1024,512]{1,0:T(8,128)(2,1)}, f32[1,256]{1,0:T(1,128)}, bf16[2,256,128]{2,1,0:T(8,128)(2,1)}) custom-call(s32[8]{0:T(128)} %get-tuple-element.481.ids_ref, bf16[1024,2048]{1,0:T(8,128)(2,1)} %shard_map.251.branch_ref.right_ref, f32[1,256]{1,0:T(1,128)} %bitcast.45, ...), custom_call_target="tpu_custom_call" | custom-call | flops 1 | bytes 1 | tf_op jit(solution)/shard_map/pallas_call | solution.py:581
  376.1 4.7 collective-permute-done.69.refs_2_
  382.7 6.1 %shard_map.253 = bf16[2048,512]{1,0:T(8,128)(2,1)} custom-call(bf16[1024,2048]{1,0:T(8,128)(2,1)} %shard_map.241.left_ref.refs_9_.refs_10_.refs_11_.refs_15_.refs_16_.refs_17_.refs_18_.refs_19_, bf16[1024,512]{1,0:T(8,128)(2,1)} %get-tuple-element.323.right_ref.refs_3_.refs_4_.refs_5_.refs_6_.refs_7_.refs_8_.refs_9_), custom_call_target="tpu_custom_call" | custom-call | flops 1 | bytes 1 | tf_op jit(solution)/shard_map/pallas_call | solution.py:791
  394.6 27.6 %shard_map.254 = (bf16[1024,1024]{1,0:T(8,128)(2,1)}, f32[1024,4]{1,0:T(8,128)}, f32[8,1024]{1,0:T(8,128)}, f32[16,1024]{1,0:T(8,128)}, f32[8,1024]{1,0:T(8,128)}) custom-call(bf16[1024,1536]{1,0:T(8,128)(2,1)} %get-tuple-element.211.proj_ref.prev_ref.refs_4_.refs_5_.refs_6_.refs_7_, ...), custom_call_target="tpu_custom_call" | custom-call | flops 1 | bytes 1 | tf_op jit(solution)/shard_map/pallas_call | solution.py:398
  423.8 6.1 %shard_map.255 = bf16[512,2048]{1,0:T(8,128)(2,1)} custom-call(bf16[1024,512]{1,0:T(8,128)(2,1)} %get-tuple-element.341.left_ref, bf16[1024,2048]{1,0:T(8,128)(2,1)} %shard_map.251.branch_ref.right_ref), custom_call_target="tpu_custom_call" | custom-call | flops 1 | bytes 1 | tf_op jit(solution)/shard_map/pallas_call | solution.py:791
  433.0 8.4 %shard_map.256 = bf16[2048,1024]{1,0:T(8,128)(2,1)} custom-call(bf16[1024,2048]{1,0:T(8,128)(2,1)} %shard_map.241.left_ref.refs_9_.refs_10_.refs_11_.refs_15_.refs_16_.refs_17_.refs_18_.refs_19_, bf16[1024,1024]{1,0:T(8,128)(2,1)} %fusion.20.right_ref.refs_0_.refs_1_.refs_2_.refs_3_.refs_4_), custom_call_target="tpu_custom_call" | custom-call | flops 1 | bytes 1 | tf_op jit(solution)/shard_map/pallas_call | solution.py:791
  444.2 9.3 %shard_map.257 = (bf16[384,2048]{1,0:T(8,128)(2,1)}, f32[8,2048]{1,0:T(8,128)}) custom-call(s32[4]{0:T(128)} %iota_xor_fusion.spots_ref, bf16[1024,1024]{1,0:T(8,128)(2,1)} %fusion.20.right_ref.refs_0_.refs_1_.refs_2_.refs_3_.refs_4_, bf16[1024,1024]{1,0:T(8,128)(2,1)} %fusion.20.right_ref.refs_0_.refs_1_.refs_2_.refs_3_.refs_4_, ...), custom_call_target="tpu_custom_call" | custom-call | flops 1 | bytes 1 | tf_op jit(solution)/shard_map/pallas_call | solution.py:711
  462.1 11.8 %shard_map.258 = (bf16[640,2048]{1,0:T(8,128)(2,1)}, f32[8,2048]{1,0:T(8,128)}) custom-call(s32[4]{0:T(128)} %iota_xor_fusion.spots_ref, bf16[1024,1024]{1,0:T(8,128)(2,1)} %fusion.20.right_ref.refs_0_.refs_1_.refs_2_.refs_3_.refs_4_, bf16[1024,1024]{1,0:T(8,128)(2,1)} %fusion.20.right_ref.refs_0_.refs_1_.refs_2_.refs_3_.refs_4_, ...), custom_call_target="tpu_custom_call" | custom-call | flops 1 | bytes 1 | tf_op jit(solution)/shard_map/pallas_call | solution.py:711
  494.9 7.1 %collective-permute-done.95 = f32[1,6144]{1,0:T(1,128)S(1)} collective-permute-done((f32[1,6144]{1,0:T(1,128)S(1)}, f32[1,6144]{1,0:T(1,128)S(1)}, u32[]{:S(2)}, u32[]{:S(2)}) %collective-permute-start.95) | collective-permute-done | bytes 24608 | tf_op jit(solution)/shard_map/ppermute | solution.py:982
  508.4 15.5 %collective-permute-done.96 = f32[16,7168]{1,0:T(8,128)S(1)} collective-permute-done((f32[16,7168]{1,0:T(8,128)S(1)}, f32[16,7168]{1,0:T(8,128)S(1)}, u32[]{:S(2)}, u32[]{:S(2)}) %collective-permute-start.96) | collective-permute-done | bytes 458784 | tf_op jit(solution)/shard_map/ppermute | solution.py:982
  524.0 4.2 shard_map.259
  538.0 3.3 shard_map.261
  541.3 3.9 shard_map.260
  (406 shorter events, 193.6 us)
Async XLA Ops:
  7.2 113.4 %all-gather.6.cloned.1.call-start = ((), (), s32[]{:S(2)}) async-start(), calls=%async_computation.6 | async-start | bytes 2621440 | tf_op jit(solution)/shard_map/all_gather | solution.py:1093
  10.3 15.0 %collective-permute-start.3 = (bf16[128,2048]{1,0:T(8,128)(2,1)S(1)}, bf16[128,2048]{1,0:T(8,128)(2,1)S(1)}, u32[]{:S(2)}, u32[]{:S(2)}) collective-permute-start(bf16[128,2048]{1,0:T(8,128)(2,1)S(1)} %fusion.4.refs_0_), channel_id=1, source_target_pairs={{0,1},{2,0},{4,2},{6,4},{7,6},{5,7},{3,5},{1,3},{8,9},{10,8},{12,1... | collective-permute-start | bytes 1572872 | tf_op jit(solution)/shard_map/ppermute | solution.py:892
  13.3 13.4 %collective-permute-start.4 = (bf16[128,2048]{1,0:T(8,128)(2,1)S(1)}, bf16[128,2048]{1,0:T(8,128)(2,1)S(1)}, u32[]{:S(2)}, u32[]{:S(2)}) collective-permute-start(bf16[128,2048]{1,0:T(8,128)(2,1)S(1)} %fusion.4.refs_0_), channel_id=1, source_target_pairs={{0,2},{2,4},{4,6},{6,7},{7,5},{5,3},{3,1},{1,0},{8,10},{10,12},{12... | collective-permute-start | bytes 1572872 | tf_op jit(solution)/shard_map/ppermute | solution.py:892
  13.4 39.6 %collective-permute-start.12 = (bf16[512,1536]{1,0:T(8,128)(2,1)}, bf16[512,1536]{1,0:T(8,128)(2,1)S(1)}, u32[]{:S(2)}, u32[]{:S(2)}) collective-permute-start(bf16[512,1536]{1,0:T(8,128)(2,1)} %refs_22_.1), channel_id=1, source_target_pairs={{0,16},{8,24},{16,0},{24,8},{1,17},{9,25},{17,1},{25,9},{2,18},{10... | collective-permute-start | bytes 4718600 | tf_op jit(solution)/shard_map/ppermute | solution.py:982
  26.7 12.5 %collective-permute-start.5 = (bf16[128,2048]{1,0:T(8,128)(2,1)S(1)}, bf16[128,2048]{1,0:T(8,128)(2,1)S(1)}, u32[]{:S(2)}, u32[]{:S(2)}) collective-permute-start(bf16[128,2048]{1,0:T(8,128)(2,1)S(1)} %collective-permute-done.3.refs_1_), channel_id=1, source_target_pairs={{0,1},{2,0},{4,2},{6,4},{7,6},{5,7},{3,5},{1,3},{8,9},{10,8},{12,1... | collective-permute-start | bytes 1572872 | tf_op jit(solution)/shard_map/ppermute | solution.py:892
  42.5 15.5 %collective-permute-start.11 = (bf16[512,1536]{1,0:T(8,128)(2,1)}, bf16[512,1536]{1,0:T(8,128)(2,1)}, u32[]{:S(2)}, u32[]{:S(2)}) collective-permute-start(bf16[512,1536]{1,0:T(8,128)(2,1)} %refs_22_.1), channel_id=1, source_target_pairs={{0,8},{8,0},{16,24},{24,16},{1,9},{9,1},{17,25},{25,17},{2,10},{10... | collective-permute-start | bytes 4718600 | tf_op jit(solution)/shard_map/ppermute | solution.py:982
  53.2 132.1 %all-gather.8.cloned.1.call-start = ((), (), s32[]{:S(2)}) async-start(), calls=%async_computation.7 | async-start | bytes 3604480 | tf_op jit(solution)/shard_map/all_gather | solution.py:1123
  53.2 13.9 %collective-permute-start = (bf16[4,512]{1,0:T(4,128)(2,1)}, bf16[4,512]{1,0:T(4,128)(2,1)S(1)}, u32[]{:S(2)}, u32[]{:S(2)}) collective-permute-start(bf16[4,512]{1,0:T(4,128)(2,1)} %bitcast.46), channel_id=1, source_target_pairs={{0,8},{8,0},{16,24},{24,16},{1,9},{9,1},{17,25},{25,17},{2,10},{10... | collective-permute-start | bytes 12296 | tf_op jit(solution)/shard_map/ppermute | solution.py:982
  63.9 18.6 %collective-permute-start.14 = (bf16[128,2048]{1,0:T(8,128)(2,1)}, bf16[128,2048]{1,0:T(8,128)(2,1)}, u32[]{:S(2)}, u32[]{:S(2)}) collective-permute-start(bf16[128,2048]{1,0:T(8,128)(2,1)} %refs_0_), channel_id=1, source_target_pairs={{0,2},{2,4},{4,6},{6,7},{7,5},{5,3},{3,1},{1,0},{8,10},{10,12},{12... | collective-permute-start | bytes 1572872 | tf_op jit(solution)/shard_map/ppermute | solution.py:892
  64.4 18.2 %collective-permute-start.15 = (bf16[128,2048]{1,0:T(8,128)(2,1)}, bf16[128,2048]{1,0:T(8,128)(2,1)}, u32[]{:S(2)}, u32[]{:S(2)}) collective-permute-start(bf16[128,2048]{1,0:T(8,128)(2,1)} %refs_0_), channel_id=1, source_target_pairs={{0,1},{2,0},{4,2},{6,4},{7,6},{5,7},{3,5},{1,3},{8,9},{10,8},{12,1... | collective-permute-start | bytes 1572872 | tf_op jit(solution)/shard_map/ppermute | solution.py:892
  82.6 20.2 %collective-permute-start.17 = (bf16[128,2048]{1,0:T(8,128)(2,1)}, bf16[128,2048]{1,0:T(8,128)(2,1)S(1)}, u32[]{:S(2)}, u32[]{:S(2)}) collective-permute-start(bf16[128,2048]{1,0:T(8,128)(2,1)} %collective-permute-done.14.refs_2_), channel_id=1, source_target_pairs={{0,2},{2,4},{4,6},{6,7},{7,5},{5,3},{3,1},{1,0},{8,10},{10,12},{12... | collective-permute-start | bytes 1572872 | tf_op jit(solution)/shard_map/ppermute | solution.py:892
  83.1 19.7 %collective-permute-start.18 = (bf16[128,2048]{1,0:T(8,128)(2,1)}, bf16[128,2048]{1,0:T(8,128)(2,1)S(1)}, u32[]{:S(2)}, u32[]{:S(2)}) collective-permute-start(bf16[128,2048]{1,0:T(8,128)(2,1)} %collective-permute-done.15.refs_1_), channel_id=1, source_target_pairs={{0,1},{2,0},{4,2},{6,4},{7,6},{5,7},{3,5},{1,3},{8,9},{10,8},{12,1... | collective-permute-start | bytes 1572872 | tf_op jit(solution)/shard_map/ppermute | solution.py:892
  102.8 14.8 %collective-permute-start.19 = (bf16[128,2048]{1,0:T(8,128)(2,1)S(1)}, bf16[128,2048]{1,0:T(8,128)(2,1)S(1)}, u32[]{:S(2)}, u32[]{:S(2)}) collective-permute-start(bf16[128,2048]{1,0:T(8,128)(2,1)S(1)} %collective-permute-done.17.refs_4_), channel_id=1, source_target_pairs={{0,2},{2,4},{4,6},{6,7},{7,5},{5,3},{3,1},{1,0},{8,10},{10,12},{12... | collective-permute-start | bytes 1572872 | tf_op jit(solution)/shard_map/ppermute | solution.py:892
  103.3 14.3 %collective-permute-start.20 = (bf16[128,2048]{1,0:T(8,128)(2,1)S(1)}, bf16[128,2048]{1,0:T(8,128)(2,1)S(1)}, u32[]{:S(2)}, u32[]{:S(2)}) collective-permute-start(bf16[128,2048]{1,0:T(8,128)(2,1)S(1)} %collective-permute-done.18.refs_3_), channel_id=1, source_target_pairs={{0,1},{2,0},{4,2},{6,4},{7,6},{5,7},{3,5},{1,3},{8,9},{10,8},{12,1... | collective-permute-start | bytes 1572872 | tf_op jit(solution)/shard_map/ppermute | solution.py:892
  117.6 92.7 %all-gather.10.cloned.1.call-start = ((), (), s32[]{:S(2)}) async-start(), calls=%async_computation.8 | async-start | bytes 3604480 | tf_op jit(solution)/shard_map/all_gather | solution.py:1123
  118.4 92.0 %all-gather.12.cloned.1.call-start = ((), (), s32[]{:S(2)}) async-start(), calls=%async_computation.9 | async-start | bytes 3604480 | tf_op jit(solution)/shard_map/all_gather | solution.py:1123
  145.7 195.2 %reduce-scatter.7.cloned.1.call-start = ((), (), s32[]{:S(2)}) async-start(), calls=%async_computation.10 | async-start | bytes 3604480 | tf_op jit(solution)/shard_map/reduce_scatter | solution.py:1166
  195.8 12.5 %collective-permute-start.40 = (bf16[128,2048]{1,0:T(8,128)(2,1)S(1)}, bf16[128,2048]{1,0:T(8,128)(2,1)}, u32[]{:S(2)}, u32[]{:S(2)}) collective-permute-start(bf16[128,2048]{1,0:T(8,128)(2,1)S(1)} %collective-permute-done.38.refs_1_), channel_id=1, source_target_pairs={{0,1},{2,0},{4,2},{6,4},{7,6},{5,7},{3,5},{1,3},{8,9},{10,8},{12,1... | collective-permute-start | bytes 1572872 | tf_op jit(solution)/shard_map/ppermute | solution.py:892
  208.3 12.2 %collective-permute-start.41 = (bf16[128,2048]{1,0:T(8,128)(2,1)}, bf16[128,2048]{1,0:T(8,128)(2,1)S(1)}, u32[]{:S(2)}, u32[]{:S(2)}) collective-permute-start(bf16[128,2048]{1,0:T(8,128)(2,1)} %collective-permute-done.39.refs_4_), channel_id=1, source_target_pairs={{0,2},{2,4},{4,6},{6,7},{7,5},{5,3},{3,1},{1,0},{8,10},{10,12},{12... | collective-permute-start | bytes 1572872 | tf_op jit(solution)/shard_map/ppermute | solution.py:892
  208.8 12.2 %collective-permute-start.42 = (bf16[128,2048]{1,0:T(8,128)(2,1)}, bf16[128,2048]{1,0:T(8,128)(2,1)S(1)}, u32[]{:S(2)}, u32[]{:S(2)}) collective-permute-start(bf16[128,2048]{1,0:T(8,128)(2,1)} %collective-permute-done.40.refs_3_), channel_id=1, source_target_pairs={{0,1},{2,0},{4,2},{6,4},{7,6},{5,7},{3,5},{1,3},{8,9},{10,8},{12,1... | collective-permute-start | bytes 1572872 | tf_op jit(solution)/shard_map/ppermute | solution.py:892
  262.4 99.0 %reduce-scatter.9.cloned.1.call-start = ((), (), s32[]{:S(2)}) async-start(), calls=%async_computation.11 | async-start | bytes 3604480 | tf_op jit(solution)/shard_map/reduce_scatter | solution.py:1166
  277.1 155.3 %reduce-scatter.13.cloned.1.call-start = ((), (), s32[]{:S(2)}) async-start(), calls=%async_computation.13 | async-start | bytes 3604480 | tf_op jit(solution)/shard_map/reduce_scatter | solution.py:1166
  277.1 13.0 %collective-permute-start.51 = (bf16[64,2048]{1,0:T(8,128)(2,1)}, bf16[64,2048]{1,0:T(8,128)(2,1)}, u32[]{:S(2)}, u32[]{:S(2)}) collective-permute-start(bf16[64,2048]{1,0:T(8,128)(2,1)} %get-tuple-element.435), channel_id=1, source_target_pairs={{0,2},{2,4},{4,6},{6,7},{7,5},{5,3},{3,1},{1,0},{8,10},{10,12},{12... | collective-permute-start | bytes 786440 | tf_op jit(solution)/shard_map/ppermute | solution.py:892
  297.1 135.2 %reduce-scatter.11.cloned.1.call-start = ((), (), s32[]{:S(2)}) async-start(), calls=%async_computation.12 | async-start | bytes 2621440 | tf_op jit(solution)/shard_map/reduce_scatter | solution.py:1231
  299.5 12.6 %collective-permute-start.57 = (bf16[64,2048]{1,0:T(8,128)(2,1)}, bf16[64,2048]{1,0:T(8,128)(2,1)S(1)}, u32[]{:S(2)}, u32[]{:S(2)}) collective-permute-start(bf16[64,2048]{1,0:T(8,128)(2,1)} %get-tuple-element.429), channel_id=1, source_target_pairs={{0,2},{2,4},{4,6},{6,7},{7,5},{5,3},{3,1},{1,0},{8,10},{10,12},{12... | collective-permute-start | bytes 786440 | tf_op jit(solution)/shard_map/ppermute | solution.py:892
  301.6 12.6 %collective-permute-start.58 = (bf16[64,2048]{1,0:T(8,128)(2,1)S(1)}, bf16[64,2048]{1,0:T(8,128)(2,1)S(1)}, u32[]{:S(2)}, u32[]{:S(2)}) collective-permute-start(bf16[64,2048]{1,0:T(8,128)(2,1)S(1)} %get-tuple-element.428), channel_id=1, source_target_pairs={{0,1},{2,0},{4,2},{6,4},{7,6},{5,7},{3,5},{1,3},{8,9},{10,8},{12,1... | collective-permute-start | bytes 786440 | tf_op jit(solution)/shard_map/ppermute | solution.py:892
  388.9 113.7 %reduce-scatter.15.cloned.1.call-start = ((), (), s32[]{:S(2)}) async-start(), calls=%async_computation.14 | async-start | bytes 2621440 | tf_op jit(solution)/shard_map/reduce_scatter | solution.py:1166
  391.1 38.7 %collective-permute-start.71 = (bf16[128,2048]{1,0:T(8,128)(2,1)}, bf16[128,2048]{1,0:T(8,128)(2,1)}, u32[]{:S(2)}, u32[]{:S(2)}) collective-permute-start(bf16[128,2048]{1,0:T(8,128)(2,1)} %get-tuple-element.325), channel_id=1, source_target_pairs={{0,2},{2,4},{4,6},{6,7},{7,5},{5,3},{3,1},{1,0},{8,10},{10,12},{12... | collective-permute-start | bytes 1572872 | tf_op jit(solution)/shard_map/ppermute | solution.py:892
  392.0 37.8 %collective-permute-start.72 = (bf16[128,2048]{1,0:T(8,128)(2,1)S(1)}, bf16[128,2048]{1,0:T(8,128)(2,1)}, u32[]{:S(2)}, u32[]{:S(2)}) collective-permute-start(bf16[128,2048]{1,0:T(8,128)(2,1)S(1)} %get-tuple-element.336), channel_id=1, source_target_pairs={{0,1},{2,0},{4,2},{6,4},{7,6},{5,7},{3,5},{1,3},{8,9},{10,8},{12,1... | collective-permute-start | bytes 1572872 | tf_op jit(solution)/shard_map/ppermute | solution.py:892
  441.4 99.8 %reduce-scatter.17.cloned.1.call-start = ((), (), s32[]{:S(2)}) async-start(), calls=%async_computation.15 | async-start | bytes 5242880 | tf_op jit(solution)/shard_map/reduce_scatter | solution.py:1252
  441.5 16.0 %collective-permute-start.73 = (bf16[128,2048]{1,0:T(8,128)(2,1)}, bf16[128,2048]{1,0:T(8,128)(2,1)S(1)}, u32[]{:S(2)}, u32[]{:S(2)}) collective-permute-start(bf16[128,2048]{1,0:T(8,128)(2,1)} %get-tuple-element.338), channel_id=1, source_target_pairs={{0,2},{2,4},{4,6},{6,7},{7,5},{5,3},{3,1},{1,0},{8,10},{10,12},{12... | collective-permute-start | bytes 1572872 | tf_op jit(solution)/shard_map/ppermute | solution.py:892
  442.6 14.8 %collective-permute-start.76 = (bf16[128,2048]{1,0:T(8,128)(2,1)S(1)}, bf16[128,2048]{1,0:T(8,128)(2,1)S(1)}, u32[]{:S(2)}, u32[]{:S(2)}) collective-permute-start(bf16[128,2048]{1,0:T(8,128)(2,1)S(1)} %get-tuple-element.351), channel_id=1, source_target_pairs={{0,1},{2,0},{4,2},{6,4},{7,6},{5,7},{3,5},{1,3},{8,9},{10,8},{12,1... | collective-permute-start | bytes 1572872 | tf_op jit(solution)/shard_map/ppermute | solution.py:892
  455.4 18.5 %collective-permute-start.78 = (bf16[64,2048]{1,0:T(8,128)(2,1)}, bf16[64,2048]{1,0:T(8,128)(2,1)}, u32[]{:S(2)}, u32[]{:S(2)}) collective-permute-start(bf16[64,2048]{1,0:T(8,128)(2,1)} %get-tuple-element.473), channel_id=1, source_target_pairs={{0,2},{2,4},{4,6},{6,7},{7,5},{5,3},{3,1},{1,0},{8,10},{10,12},{12... | collective-permute-start | bytes 786440 | tf_op jit(solution)/shard_map/ppermute | solution.py:892
  456.3 17.6 %collective-permute-start.79 = (bf16[64,2048]{1,0:T(8,128)(2,1)}, bf16[64,2048]{1,0:T(8,128)(2,1)}, u32[]{:S(2)}, u32[]{:S(2)}) collective-permute-start(bf16[64,2048]{1,0:T(8,128)(2,1)} %get-tuple-element.472), channel_id=1, source_target_pairs={{0,1},{2,0},{4,2},{6,4},{7,6},{5,7},{3,5},{1,3},{8,9},{10,8},{12,1... | collective-permute-start | bytes 786440 | tf_op jit(solution)/shard_map/ppermute | solution.py:892
  459.9 16.4 %collective-permute-start.77 = (bf16[128,2048]{1,0:T(8,128)(2,1)}, bf16[128,2048]{1,0:T(8,128)(2,1)S(1)}, u32[]{:S(2)}, u32[]{:S(2)}) collective-permute-start(bf16[128,2048]{1,0:T(8,128)(2,1)} %get-tuple-element.352), channel_id=1, source_target_pairs={{0,1},{2,0},{4,2},{6,4},{7,6},{5,7},{3,5},{1,3},{8,9},{10,8},{12,1... | collective-permute-start | bytes 1572872 | tf_op jit(solution)/shard_map/ppermute | solution.py:892
  462.0 14.3 %collective-permute-start.75 = (bf16[128,2048]{1,0:T(8,128)(2,1)}, bf16[128,2048]{1,0:T(8,128)(2,1)}, u32[]{:S(2)}, u32[]{:S(2)}) collective-permute-start(bf16[128,2048]{1,0:T(8,128)(2,1)} %get-tuple-element.350), channel_id=1, source_target_pairs={{0,2},{2,4},{4,6},{6,7},{7,5},{5,3},{3,1},{1,0},{8,10},{10,12},{12... | collective-permute-start | bytes 1572872 | tf_op jit(solution)/shard_map/ppermute | solution.py:892
  486.8 15.7 %collective-permute-start.80 = (bf16[64,2048]{1,0:T(8,128)(2,1)}, bf16[64,2048]{1,0:T(8,128)(2,1)}, u32[]{:S(2)}, u32[]{:S(2)}) collective-permute-start(bf16[64,2048]{1,0:T(8,128)(2,1)} %get-tuple-element.471), channel_id=1, source_target_pairs={{0,2},{2,4},{4,6},{6,7},{7,5},{5,3},{3,1},{1,0},{8,10},{10,12},{12... | collective-permute-start | bytes 786440 | tf_op jit(solution)/shard_map/ppermute | solution.py:892
  487.6 14.9 %collective-permute-start.81 = (bf16[64,2048]{1,0:T(8,128)(2,1)}, bf16[64,2048]{1,0:T(8,128)(2,1)}, u32[]{:S(2)}, u32[]{:S(2)}) collective-permute-start(bf16[64,2048]{1,0:T(8,128)(2,1)} %get-tuple-element.470), channel_id=1, source_target_pairs={{0,1},{2,0},{4,2},{6,4},{7,6},{5,7},{3,5},{1,3},{8,9},{10,8},{12,1... | collective-permute-start | bytes 786440 | tf_op jit(solution)/shard_map/ppermute | solution.py:892
  488.9 13.7 %collective-permute-start.82 = (bf16[64,2048]{1,0:T(8,128)(2,1)}, bf16[64,2048]{1,0:T(8,128)(2,1)}, u32[]{:S(2)}, u32[]{:S(2)}) collective-permute-start(bf16[64,2048]{1,0:T(8,128)(2,1)} %get-tuple-element.469), channel_id=1, source_target_pairs={{0,2},{2,4},{4,6},{6,7},{7,5},{5,3},{3,1},{1,0},{8,10},{10,12},{12... | collective-permute-start | bytes 786440 | tf_op jit(solution)/shard_map/ppermute | solution.py:892
  489.7 12.9 %collective-permute-start.83 = (bf16[64,2048]{1,0:T(8,128)(2,1)}, bf16[64,2048]{1,0:T(8,128)(2,1)}, u32[]{:S(2)}, u32[]{:S(2)}) collective-permute-start(bf16[64,2048]{1,0:T(8,128)(2,1)} %get-tuple-element.468), channel_id=1, source_target_pairs={{0,1},{2,0},{4,2},{6,4},{7,6},{5,7},{3,5},{1,3},{8,9},{10,8},{12,1... | collective-permute-start | bytes 786440 | tf_op jit(solution)/shard_map/ppermute | solution.py:892
  502.1 21.8 %collective-permute-start.96 = (f32[16,7168]{1,0:T(8,128)S(1)}, f32[16,7168]{1,0:T(8,128)S(1)}, u32[]{:S(2)}, u32[]{:S(2)}) collective-permute-start(f32[16,7168]{1,0:T(8,128)S(1)} %select_maximum_fusion), channel_id=1, source_target_pairs={{0,16},{8,24},{16,0},{24,8},{1,17},{9,25},{17,1},{25,9},{2,18},{10... | collective-permute-start | bytes 1376264 | tf_op jit(solution)/shard_map/ppermute | solution.py:982
  504.3 23.9 %collective-permute-start.84 = (bf16[64,2048]{1,0:T(8,128)(2,1)S(1)}, bf16[64,2048]{1,0:T(8,128)(2,1)S(1)}, u32[]{:S(2)}, u32[]{:S(2)}) collective-permute-start(bf16[64,2048]{1,0:T(8,128)(2,1)S(1)} %get-tuple-element.467), channel_id=1, source_target_pairs={{0,2},{2,4},{4,6},{6,7},{7,5},{5,3},{3,1},{1,0},{8,10},{10,12},{12... | collective-permute-start | bytes 786440 | tf_op jit(solution)/shard_map/ppermute | solution.py:892
  504.8 23.4 %collective-permute-start.85 = (bf16[64,2048]{1,0:T(8,128)(2,1)S(1)}, bf16[64,2048]{1,0:T(8,128)(2,1)S(1)}, u32[]{:S(2)}, u32[]{:S(2)}) collective-permute-start(bf16[64,2048]{1,0:T(8,128)(2,1)S(1)} %get-tuple-element.466), channel_id=1, source_target_pairs={{0,1},{2,0},{4,2},{6,4},{7,6},{5,7},{3,5},{1,3},{8,9},{10,8},{12,1... | collective-permute-start | bytes 786440 | tf_op jit(solution)/shard_map/ppermute | solution.py:892
  506.3 21.8 %collective-permute-start.86 = (bf16[64,2048]{1,0:T(8,128)(2,1)S(1)}, bf16[64,2048]{1,0:T(8,128)(2,1)S(1)}, u32[]{:S(2)}, u32[]{:S(2)}) collective-permute-start(bf16[64,2048]{1,0:T(8,128)(2,1)S(1)} %get-tuple-element.465), channel_id=1, source_target_pairs={{0,2},{2,4},{4,6},{6,7},{7,5},{5,3},{3,1},{1,0},{8,10},{10,12},{12... | collective-permute-start | bytes 786440 | tf_op jit(solution)/shard_map/ppermute | solution.py:892
  506.8 21.4 %collective-permute-start.87 = (bf16[64,2048]{1,0:T(8,128)(2,1)S(1)}, bf16[64,2048]{1,0:T(8,128)(2,1)S(1)}, u32[]{:S(2)}, u32[]{:S(2)}) collective-permute-start(bf16[64,2048]{1,0:T(8,128)(2,1)S(1)} %get-tuple-element.464), channel_id=1, source_target_pairs={{0,1},{2,0},{4,2},{6,4},{7,6},{5,7},{3,5},{1,3},{8,9},{10,8},{12,1... | collective-permute-start | bytes 786440 | tf_op jit(solution)/shard_map/ppermute | solution.py:892
  530.2 14.9 %collective-permute-start.88 = (bf16[64,2048]{1,0:T(8,128)(2,1)}, bf16[64,2048]{1,0:T(8,128)(2,1)S(1)}, u32[]{:S(2)}, u32[]{:S(2)}) collective-permute-start(bf16[64,2048]{1,0:T(8,128)(2,1)} %get-tuple-element.463), channel_id=1, source_target_pairs={{0,2},{2,4},{4,6},{6,7},{7,5},{5,3},{3,1},{1,0},{8,10},{10,12},{12... | collective-permute-start | bytes 786440 | tf_op jit(solution)/shard_map/ppermute | solution.py:892
  531.0 14.1 %collective-permute-start.89 = (bf16[64,2048]{1,0:T(8,128)(2,1)S(1)}, bf16[64,2048]{1,0:T(8,128)(2,1)S(1)}, u32[]{:S(2)}, u32[]{:S(2)}) collective-permute-start(bf16[64,2048]{1,0:T(8,128)(2,1)S(1)} %get-tuple-element.462), channel_id=1, source_target_pairs={{0,1},{2,0},{4,2},{6,4},{7,6},{5,7},{3,5},{1,3},{8,9},{10,8},{12,1... | collective-permute-start | bytes 786440 | tf_op jit(solution)/shard_map/ppermute | solution.py:892
  532.2 12.9 %collective-permute-start.90 = (bf16[64,2048]{1,0:T(8,128)(2,1)S(1)}, bf16[64,2048]{1,0:T(8,128)(2,1)}, u32[]{:S(2)}, u32[]{:S(2)}) collective-permute-start(bf16[64,2048]{1,0:T(8,128)(2,1)S(1)} %get-tuple-element.461), channel_id=1, source_target_pairs={{0,2},{2,4},{4,6},{6,7},{7,5},{5,3},{3,1},{1,0},{8,10},{10,12},{12... | collective-permute-start | bytes 786440 | tf_op jit(solution)/shard_map/ppermute | solution.py:892
  (121 other events, 1230.7 us)
Sparse Core Ops, SparseCore 0:
  53.3 21.4 all-gather.5
  117.8 27.5 all-gather.7
  147.0 27.0 all-gather.9
  175.5 27.0 all-gather.11
  262.5 36.6 reduce-scatter.6
  301.7 36.2 reduce-scatter.8
  340.6 36.3 reduce-scatter.12
  389.0 30.0 reduce-scatter.10
  441.6 31.1 reduce-scatter.14
  475.3 54.3 reduce-scatter.16

commit v5 on v4

--- a/solution.py
+++ b/solution.py
@@ -882,6 +882,31 @@
         compiler_params=pltpu.CompilerParams(vmem_limit_bytes=VMEM_LIMIT),
         cost_estimate=LIGHT,
     )(left, right)
+
+
+def finish_all_kernel(heads, count, mix_ref, gate_ref, *refs):
+    join_kernel(heads, mix_ref, gate_ref, refs[count])
+    for i in range(count):
+        refs[count + 1 + i][...] = refs[i][...].astype(F32)
+
+
+def finish_all(mix, gate, others):
+    heads = gate.shape[1] // DV
+    steps = 4
+    spec = lambda a, wide: pl.BlockSpec((a.shape[0] // steps, wide), lambda i: (i, 0))
+    plain = [spec(a, a.shape[1]) for a in others]
+    return pl.pallas_call(
+        functools.partial(finish_all_kernel, heads, len(others)),
+        grid=(steps,),
+        in_specs=[spec(mix, mix.shape[1]), spec(gate, gate.shape[1]), *plain],
+        out_specs=[spec(mix, heads * PER), *plain],
+        out_shape=[
+            jax.ShapeDtypeStruct((mix.shape[0], heads * PER), F32),
+            *[jax.ShapeDtypeStruct(a.shape, F32) for a in others],
+        ],
+        compiler_params=pltpu.CompilerParams(vmem_limit_bytes=VMEM_LIMIT),
+        cost_estimate=LIGHT,
+    )(mix, gate, *others)
 def ring_order(count):
     return list(range(0, count, 2)) + list(range(1, count, 2))[::-1]
 
@@ -1227,9 +1252,10 @@
     local_low, *_ = together(local_grad, *known())
     shares = seq_shards(local_low, "seq")
     gate_grad_w = outer(keep["normed"], together(grad_gate_mix, *shares[1:])[0])
-    first_share, gate_grad_w = together(shares[0], gate_grad_w)
+    output_hops(2, shares[1])
+    first_share, gate_grad_w, *_ = together(shares[0], gate_grad_w, *known())
     gate_grad_s = lax.psum_scatter(gate_grad_w, "seq", scatter_dimension=0, tiled=True)
-    output_hops(2, gate_grad_w)
+    output_hops(3, gate_grad_w)
     grad_mixed, grad_rates, seq_sums, tail_rows, lead_rows = mixer_backward(
         projected, halo_rows, rates, bias_row, conv_weight, saved,
         grad_mixer, value, incoming, place, near_spots, maps, [first_share, *shares[1:]], GROUP,
@@ -1237,7 +1263,7 @@
     grad_mixed, gate_grad_s, grad_up_s, *_ = together(grad_mixed, gate_grad_s, grad_up_s, *known())
     later_rows = shifted(lead_rows, "seq", -1)
     out_grad_w = outer(gated, after(branch_near, lead_rows))
-    output_hops(3, grad_mixed)
+    output_hops(4, grad_mixed)
     padded = jnp.concatenate([jnp.zeros((HALO, heads * MIX), F32), later_rows])
     last_rows = tail_rows + sum(
         conv_weight[i] * padded[CONV - 1 - i : CONV - 1 - i + HALO] for i in range(CONV)
@@ -1257,6 +1283,7 @@
     part, sums = normed_back(
         spots, early, count, grad_mixed, grad_gate_mix, grad_rates, normed, w_mix, w_rate, jnp.zeros((8, width), F32)
     )
+    part, *_ = together(part, *known())
     parts.append(part)
 
     def take(k, start, size):
@@ -1271,29 +1298,24 @@
         return (part,)
 
     def first_window(pin):
-        output_hops(4, pin(part))
-        return (*late_rows(pin), *known())
+        return late_rows(pin)
 
     def second_window(pin):
         sums = pin(keep["sums"])
         gains = jnp.concatenate([mlp_gain_part[None], head_gain_part, jnp.zeros((1, width - DV), F32)], axis=1)
         gains = jnp.pad(gains, ((4, 3), (0, 0)))
         small = jnp.concatenate([sums, gains, seq_sums], axis=1)
-        small = small + swap(small, "seq", 1)
-        keep["gains"] = butterfly(small[4:5, : 3 * width], "head")
-        keep["small"] = small
-        return (grad_out_s,)
-
-    def fourth_window(pin):
-        keep["joined"] = join_heads(pin(mix_grad_s), gate_grad_s)
-        return (keep["joined"],)
+        keep["small"] = butterfly(small, "seq")
+        keep["gains"] = keep["small"][4:5, : 3 * width]
+        return (keep["gains"],)
 
     def third_window(pin):
-        keep["wide"] = widen([pin(a) for a in (grad_down_s, grad_gate_s, grad_up_s)])
-        return keep["wide"]
+        gains = pin(keep["gains"])
+        keep["gains"] = gains + swap(gains, "head", 1)
+        return (keep["gains"], mix_grad_s)
 
     grad_normed = ring_scatter(
-        take, own_rows, "head", {1: first_window, 2: second_window, 3: third_window, 4: fourth_window}
+        take, own_rows, "head", {1: first_window, 2: second_window, 3: third_window}
     )
     scaled_one = grad_normed * norm_gain
     grad_input = grad_residual + inverse_one * (
@@ -1302,29 +1324,24 @@
     output = (
         residual + sum(a.astype(F32) for a in known()) + take_output(0, 0, own_rows).astype(F32)
     ).astype(BF16)
-    row = jnp.pad(keep["gains"], ((0, 7), (0, keep["small"].shape[1] - 3 * width)))
-    small = jnp.concatenate([keep["small"], row], axis=0)
+    small, gains = keep["small"], after(keep["gains"], grad_normed)
     bit = 2
-    while bit < peers:
-        small = small + swap(small, "seq", bit)
+    while bit < count:
+        gains = gains + swap(gains, "head", bit)
         bit *= 2
-    gains = small[8:9]
-    (wide_out,) = widen([grad_out_s])
+    joined, *wide = finish_all(mix_grad_s, gate_grad_s, [grad_out_s, grad_gate_s, grad_up_s, grad_down_s])
     per_seq = w_rates.shape[0]
     return (
         output,
         grad_input,
-        keep["joined"],
+        joined,
         lax.dynamic_slice_in_dim(small[: 2 * heads], place[0] * per_seq, per_seq, 1).T,
         small[:CONV, 3 * width :],
         small[CONV, 3 * width : 3 * width + 2 * heads].reshape(heads, 2).T,
         gains[0, :width] / norm_gain,
         gains[0, 2 * width : 2 * width + DV],
         gains[0, width : 2 * width],
-        wide_out,
-        keep["wide"][1],
-        keep["wide"][2],
-        keep["wide"][0],
+        *wide,
     )
 
 

time: 564 us -> 553 us (0.980)
    ppermute x14, waiting for transfers between devices: 32.9 us -> 25 us  [swap(): return lax.ppermute(value, axis, [(i, i ^ bit) for i in range(count)])]
    pallas_call x3 -> x1, Pallas kernels: 11.3 us -> 5.86 us  [finish_all(): pl.pallas_call(functools.partial(finish_all_kernel, heads, len(others)),...]
  transfers between devices with their start and end apart: 107 -> 107, of which waited for: 48 -> 50; matrix products, arithmetic and copies ran while one was open for 9% -> 9% of each run, Pallas kernels for 33% -> 32%
where the time goes in v5:
time: 553 us; the launch traced here: 544 us
  Pallas kernels  186 us (34%)
  waiting for transfers between devices  147 us (27%)
  starting transfers between devices  100 us (18%)
  other arithmetic  35.1 us (6%)
  matrix products  25.8 us (5%)
  local copies, waits for them, and re-layouts  21.7 us (4%)
  between operations  16.3 us (3%)
  blocking collectives  12.7 us (2%)
    ppermute x81, waiting for transfers between devices, ring_step(): lax.ppermute(value, axis, [(order[i], order[(i + step) % count]) for i in...  120 us
    ppermute x81, starting transfers between devices, ring_step(): lax.ppermute(value, axis, [(order[i], order[(i + step) % count]) for i in...  84.9 us
    pallas_call x6, Pallas kernels, outer(): pl.pallas_call(outer_kernel, grid=(m // rows, n // cols), in_specs=[pl.Bl...  42.1 us
    pallas_call x1, Pallas kernels, mixer_backward(): pl.pallas_call(functools.partial(backward_kernel, heads, group, steps, ma...  27.5 us
    dot_general x5, matrix products, per_device(): lax.dot_general(a, b, dims, preferred_element_type=F32)  25.8 us
    ppermute x14, waiting for transfers between devices, swap(): return lax.ppermute(value, axis, [(i, i ^ bit) for i in range(count)])  25 us
    pallas_call x2, Pallas kernels, normed_back(): pl.pallas_call(functools.partial(normed_back_kernel, len(w_mix), count),...  21.3 us
    pallas_call x4, Pallas kernels, stacked(): pl.pallas_call(functools.partial(stack_kernel, layout), out_shape=jax.Sha...  18 us
  transfers between devices with their start and end apart: 107, of which 50 were waited for; matrix products, arithmetic and copies ran while one was open for 9% of the time, Pallas kernels for 32%

profile of v5, /device:TPU:0, one launch (start us, length us, event | category | flops | bytes accessed | tf_op | source)
XLA Modules:
  0.0 544.5 jit_solution(5576488503530108629)
XLA Ops:
  10.3 3.0 collective-permute-start.3
  15.4 10.0 %collective-permute-done.3.refs_1_ = bf16[128,2048]{1,0:T(8,128)(2,1)S(1)} collective-permute-done((bf16[128,2048]{1,0:T(8,128)(2,1)S(1)}, bf16[128,2048]{1,0:T(8,128)(2,1)S(1)}, u32[]{:S(2)}, u32[]{:S(2)}) %collective-permute-start.3) | collective-permute-done | bytes 524320 | tf_op jit(solution)/shard_map/ppermute | solution.py:917
  28.7 10.4 %collective-permute-done.5.refs_3_ = bf16[128,2048]{1,0:T(8,128)(2,1)S(1)} collective-permute-done((bf16[128,2048]{1,0:T(8,128)(2,1)S(1)}, bf16[128,2048]{1,0:T(8,128)(2,1)S(1)}, u32[]{:S(2)}, u32[]{:S(2)}) %collective-permute-start.5) | collective-permute-done | bytes 524320 | tf_op jit(solution)/shard_map/ppermute | solution.py:917
  42.5 9.2 %collective-permute-done.7.refs_5_ = bf16[128,2048]{1,0:T(8,128)(2,1)S(1)} collective-permute-done((bf16[128,2048]{1,0:T(8,128)(2,1)S(1)}, bf16[128,2048]{1,0:T(8,128)(2,1)S(1)}, u32[]{:S(2)}, u32[]{:S(2)}) %collective-permute-start.7) | collective-permute-done | bytes 524320 | tf_op jit(solution)/shard_map/ppermute | solution.py:917
  59.6 3.4 collective-permute-done.9.refs_7_
  67.8 14.7 %shard_map.237 = (bf16[1024,1536]{1,0:T(8,128)(2,1)}, f32[1024,4]{1,0:T(8,128)}) custom-call(s32[8]{0:T(128)} %get-tuple-element.481.ids_ref, s32[4]{0:T(128)} %iota_xor_fusion.spots_ref, bf16[4,2048]{1,0:T(4,128)(2,1)} %copy-done.39, bf16[128,2048]{1,0:T(8,128)(2,1)} %copy-done.3, bf16[128,2048]{1,0:T(8,128)(2,1)} %copy-done.12, ...), custom_call_target="tpu_custom_call" | custom-call | flops 1 | bytes 1 | tf_op jit(solution)/shard_map/pallas_call | solution.py:661
  88.4 14.4 %shard_map.238 = (f32[1024,512]{1,0:T(8,128)}, bf16[1024,256]{1,0:T(8,128)(2,1)}, bf16[2,8,384,128]{3,2,1,0:T(8,128)(2,1)}, bf16[2,8,128,384]{3,2,1,0:T(8,128)(2...) custom-call(bf16[1024,1536]{1,0:T(8,128)(2,1)} %get-tuple-element.21, ...), custom_call_target="tpu_custom_call" | custom-call | flops 1 | bytes 1 | tf_op jit(solution)/shard_map/pallas_call | solution.py:205
  104.9 12.7 %all-gather = bf16[8,384,128]{2,1,0:T(8,128)(2,1)} all-gather(bf16[2,384,128]{2,1,0:T(8,128)(2,1)} %get-tuple-element.216), channel_id=2, replica_groups=mesh['seq'=4,'head'=8] {'seq'}, dimensions={0}, use_global_device_ids=true | all-gather | bytes 983040 | tf_op jit(solution)/shard_map/all_gather | solution.py:1141
  120.6 9.7 %shard_map.239 = (bf16[1024,512]{1,0:T(8,128)(2,1)}, bf16[1024,512]{1,0:T(8,128)(2,1)}, bf16[1024,2048]{1,0:T(8,128)(2,1)}, bf16[2,256,128]{2,1,0:T(8,128)(2,1)}) custom-call(s32[8]{0:T(128)} %get-tuple-element.481.ids_ref, s32[1]{0:T(128)} %bitcast.1.place_ref, bf16[4,2,384,128]{3,2,1,0:T(8,128)(2,1)} %bitcast.34, f32[1,256]{1,0:T(1,128)} %bitcast.44, ...), custom_call_target="tpu_custom_call" | custom-call | flops 1 | bytes 1 | tf_op jit(solution)/shard_map/pallas_call | solution.py:503
  133.7 4.5 shard_map.240.left_ref.right_ref
  145.8 4.6 shard_map.241.left_ref.refs_9_.refs_10_.refs_11_.refs_15_.refs_16_.refs_17_.refs_18_.refs_19_
  160.6 5.2 collective-permute-done.29
  174.0 4.2 collective-permute-done.33
  184.7 4.6 shard_map.242.right_ref
  189.3 5.1 collective-permute-done.37.refs_2_
  196.9 7.7 %shard_map.243 = f32[1024,704]{1,0:T(8,128)} custom-call(bf16[1024,2048]{1,0:T(8,128)(2,1)} %shard_map.240.left_ref.right_ref, bf16[2048,704]{1,0:T(8,128)(2,1)} %shard_map.242.right_ref), custom_call_target="tpu_custom_call" | custom-call | flops 1 | bytes 1 | tf_op jit(solution)/shard_map/pallas_call | solution.py:873
  210.0 6.1 %shard_map.244 = (bf16[2048,704]{1,0:T(8,128)(2,1)}, bf16[2048,704]{1,0:T(8,128)(2,1)}) custom-call(bf16[704,2048]{1,0:T(8,128)(2,1)} %all-gather.10.cloned.1.call-done.refs_0_, bf16[704,2048]{1,0:T(8,128)(2,1)} %all-gather.12.cloned.1.call-done.refs_1_), custom_call_target="tpu_custom_call" | custom-call | flops 1 | bytes 1 | tf_op jit(solution)/shard_map/pallas_call | solution.py:813
  216.1 4.0 collective-permute-done.41.refs_6_
  223.1 4.2 shard_map.245.buffer_ref
  230.7 6.3 %fusion.28 = f32[1024,704]{1,0:T(8,128)S(1)} fusion(bf16[1024,2048]{1,0:T(8,128)(2,1)} %shard_map.246.right_ref, bf16[2048,704]{1,0:T(8,128)(2,1)} %get-tuple-element.271), kind=kOutput, calls=%fused_computation.108 | convolution fusion | flops 2952790016 | bytes 9961472 | tf_op jit(solution)/shard_map/dot_general | solution.py:1063
  237.0 5.7 %multiply_convert_fusion = (bf16[1024,704]{1,0:T(8,128)(2,1)S(1)}, bf16[1024,704]{1,0:T(8,128)(2,1)S(1)}, bf16[1024,704]{1,0:T(8,128)(2,1)}) fusion(f32[1024,704]{1,0:T(8,128)S(1)} %copy-done.8, f32[1024,704]{1,0:T(8,128)S(1)} %fusion.28, bf16[1024,2048]{1,0:T(8,128)(2,1)S(1)} %copy-done, bf16[2048,704]{1,0:T(8,128)(2,1)S(1)} %copy-done.64), kind=kOutput, calls=%fused_computation.2 | convolution fusion | flops 2963603456 | bytes 17170432 | tf_op jit(solution)/shard_map/dot_general | solution.py:1063
  242.7 3.4 fusion.29
  246.1 3.7 add_convert_fusion
  254.0 7.1 %shard_map.247 = bf16[704,2048]{1,0:T(8,128)(2,1)} custom-call(bf16[1024,704]{1,0:T(8,128)(2,1)} %get-tuple-element.293.left_ref, bf16[1024,2048]{1,0:T(8,128)(2,1)} %shard_map.240.left_ref.right_ref), custom_call_target="tpu_custom_call" | custom-call | flops 1 | bytes 1 | tf_op jit(solution)/shard_map/pallas_call | solution.py:791
  267.2 7.2 %shard_map.248 = bf16[704,2048]{1,0:T(8,128)(2,1)} custom-call(bf16[1024,704]{1,0:T(8,128)(2,1)} %copy-done.21, bf16[1024,2048]{1,0:T(8,128)(2,1)} %shard_map.246.right_ref), custom_call_target="tpu_custom_call" | custom-call | flops 1 | bytes 1 | tf_op jit(solution)/shard_map/pallas_call | solution.py:791
  282.2 7.2 %shard_map.249 = bf16[704,2048]{1,0:T(8,128)(2,1)} custom-call(bf16[1024,704]{1,0:T(8,128)(2,1)} %copy-done.20, bf16[1024,2048]{1,0:T(8,128)(2,1)} %shard_map.246.right_ref), custom_call_target="tpu_custom_call" | custom-call | flops 1 | bytes 1 | tf_op jit(solution)/shard_map/pallas_call | solution.py:791
  300.1 6.7 %convolution_convert_fusion = bf16[1024,2048]{1,0:T(8,128)(2,1)} fusion(bf16[1024,704]{1,0:T(8,128)(2,1)S(1)} %copy-done.19, bf16[704,2048]{1,0:T(8,128)(2,1)} %all-gather.8.cloned.1.call-done.refs_0_), kind=kOutput, calls=%fused_computation.1 | convolution fusion | flops 2954887168 | bytes 8519680 | tf_op jit(solution)/shard_map/dot_general | solution.py:1063
  307.2 3.0 collective-permute-done.57
  310.2 2.6 collective-permute-done.58
  317.4 9.4 %collective-permute-done.59.refs_2_ = bf16[128,2048]{1,0:T(8,128)(2,1)S(1)} collective-permute-done((bf16[128,2048]{1,0:T(8,128)(2,1)S(1)}, bf16[128,2048]{1,0:T(8,128)(2,1)S(1)}, u32[]{:S(2)}, u32[]{:S(2)}) %collective-permute-start.59) | collective-permute-done | bytes 524320 | tf_op jit(solution)/shard_map/ppermute | solution.py:917
  329.6 9.1 %collective-permute-done.61.refs_4_ = bf16[128,2048]{1,0:T(8,128)(2,1)S(1)} collective-permute-done((bf16[128,2048]{1,0:T(8,128)(2,1)S(1)}, bf16[128,2048]{1,0:T(8,128)(2,1)S(1)}, u32[]{:S(2)}, u32[]{:S(2)}) %collective-permute-start.61) | collective-permute-done | bytes 524320 | tf_op jit(solution)/shard_map/ppermute | solution.py:917
  342.0 7.4 %collective-permute-done.63.refs_6_ = bf16[128,2048]{1,0:T(8,128)(2,1)S(1)} collective-permute-done((bf16[128,2048]{1,0:T(8,128)(2,1)}, bf16[128,2048]{1,0:T(8,128)(2,1)S(1)}, u32[]{:S(2)}, u32[]{:S(2)}) %collective-permute-start.63) | collective-permute-done | bytes 524320 | tf_op jit(solution)/shard_map/ppermute | solution.py:917
  355.8 4.6 shard_map.250.buffer_ref
  363.2 10.1 %shard_map.252 = (bf16[1024,512]{1,0:T(8,128)(2,1)}, bf16[1024,512]{1,0:T(8,128)(2,1)}, f32[1,256]{1,0:T(1,128)}, bf16[2,256,128]{2,1,0:T(8,128)(2,1)}) custom-call(s32[8]{0:T(128)} %get-tuple-element.481.ids_ref, bf16[1024,2048]{1,0:T(8,128)(2,1)} %shard_map.251.branch_ref.right_ref, f32[1,256]{1,0:T(1,128)} %bitcast.45, ...), custom_call_target="tpu_custom_call" | custom-call | flops 1 | bytes 1 | tf_op jit(solution)/shard_map/pallas_call | solution.py:581
  378.9 5.3 collective-permute-done.70.refs_2_
  384.9 6.2 %shard_map.253 = bf16[2048,512]{1,0:T(8,128)(2,1)} custom-call(bf16[1024,2048]{1,0:T(8,128)(2,1)} %shard_map.241.left_ref.refs_9_.refs_10_.refs_11_.refs_15_.refs_16_.refs_17_.refs_18_.refs_19_, bf16[1024,512]{1,0:T(8,128)(2,1)} %get-tuple-element.324.right_ref.refs_3_.refs_4_.refs_5_.refs_6_.refs_7_.refs_8_.refs_9_), custom_call_target="tpu_custom_call" | custom-call | flops 1 | bytes 1 | tf_op jit(solution)/shard_map/pallas_call | solution.py:791
  391.2 2.6 slice_add_fusion.3
  397.3 27.5 %shard_map.254 = (bf16[1024,1024]{1,0:T(8,128)(2,1)}, f32[1024,4]{1,0:T(8,128)}, f32[8,1024]{1,0:T(8,128)}, f32[16,1024]{1,0:T(8,128)}, f32[8,1024]{1,0:T(8,128)}) custom-call(bf16[1024,1536]{1,0:T(8,128)(2,1)} %get-tuple-element.211.proj_ref.prev_ref.refs_4_.refs_5_.refs_6_.refs_7_, ...), custom_call_target="tpu_custom_call" | custom-call | flops 1 | bytes 1 | tf_op jit(solution)/shard_map/pallas_call | solution.py:398
  426.4 6.1 %shard_map.255 = bf16[512,2048]{1,0:T(8,128)(2,1)} custom-call(bf16[1024,512]{1,0:T(8,128)(2,1)} %get-tuple-element.344.left_ref, bf16[1024,2048]{1,0:T(8,128)(2,1)} %shard_map.251.branch_ref.right_ref), custom_call_target="tpu_custom_call" | custom-call | flops 1 | bytes 1 | tf_op jit(solution)/shard_map/pallas_call | solution.py:791
  435.6 8.5 %shard_map.256 = bf16[2048,1024]{1,0:T(8,128)(2,1)} custom-call(bf16[1024,2048]{1,0:T(8,128)(2,1)} %shard_map.241.left_ref.refs_9_.refs_10_.refs_11_.refs_15_.refs_16_.refs_17_.refs_18_.refs_19_, bf16[1024,1024]{1,0:T(8,128)(2,1)} %fusion.20.right_ref.refs_0_.refs_1_.refs_2_.refs_3_.refs_4_), custom_call_target="tpu_custom_call" | custom-call | flops 1 | bytes 1 | tf_op jit(solution)/shard_map/pallas_call | solution.py:791
  446.9 9.6 %shard_map.257 = (bf16[384,2048]{1,0:T(8,128)(2,1)}, f32[8,2048]{1,0:T(8,128)}) custom-call(s32[4]{0:T(128)} %iota_xor_fusion.spots_ref, bf16[1024,1024]{1,0:T(8,128)(2,1)} %fusion.20.right_ref.refs_0_.refs_1_.refs_2_.refs_3_.refs_4_, bf16[1024,1024]{1,0:T(8,128)(2,1)} %fusion.20.right_ref.refs_0_.refs_1_.refs_2_.refs_3_.refs_4_, ...), custom_call_target="tpu_custom_call" | custom-call | flops 1 | bytes 1 | tf_op jit(solution)/shard_map/pallas_call | solution.py:711
  456.5 2.6 collective-permute-done.76
  464.2 11.7 %shard_map.258 = (bf16[640,2048]{1,0:T(8,128)(2,1)}, f32[8,2048]{1,0:T(8,128)}) custom-call(s32[4]{0:T(128)} %iota_xor_fusion.spots_ref, bf16[1024,1024]{1,0:T(8,128)(2,1)} %fusion.20.right_ref.refs_0_.refs_1_.refs_2_.refs_3_.refs_4_, bf16[1024,1024]{1,0:T(8,128)(2,1)} %fusion.20.right_ref.refs_0_.refs_1_.refs_2_.refs_3_.refs_4_, ...), custom_call_target="tpu_custom_call" | custom-call | flops 1 | bytes 1 | tf_op jit(solution)/shard_map/pallas_call | solution.py:711
  484.0 8.6 %collective-permute-done.85 = f32[8,7168]{1,0:T(8,128)} collective-permute-done((f32[8,7168]{1,0:T(8,128)S(1)}, f32[8,7168]{1,0:T(8,128)}, u32[]{:S(2)}, u32[]{:S(2)}) %collective-permute-start.85) | collective-permute-done | bytes 229408 | tf_op jit(solution)/shard_map/ppermute | solution.py:1007
  503.9 6.5 %collective-permute-done.90 = f32[1,6144]{1,0:T(1,128)S(1)} collective-permute-done((f32[1,6144]{1,0:T(1,128)S(1)}, f32[1,6144]{1,0:T(1,128)S(1)}, u32[]{:S(2)}, u32[]{:S(2)}) %collective-permute-start.90) | collective-permute-done | bytes 24608 | tf_op jit(solution)/shard_map/ppermute | solution.py:1007
  510.5 3.8 collective-permute-done.95
  514.3 3.0 collective-permute-start.96
  528.1 5.9 %shard_map.259 = (f32[512,1536]{1,0:T(8,128)}, f32[512,512]{1,0:T(8,128)}, f32[704,512]{1,0:T(8,128)}, f32[704,512]{1,0:T(8,128)}, f32[704,512]{1,0:T(8,128)}) custom-call(bf16[512,1024]{1,0:T(8,128)(2,1)} %reduce-scatter.15.cloned.1.call-done.mix_ref, bf16[512,512]{1,0:T(8,128)(2,1)} %reduce-scatter.11.cloned.1.call-done.gate_ref, ...), custom_call_target="tpu_custom_call" | custom-call | flops 1 | bytes 1 | tf_op jit(solution)/shard_map/pallas_call | solution.py:898
  (409 shorter events, 189.3 us)
Async XLA Ops:
  7.2 113.4 %all-gather.6.cloned.1.call-start = ((), (), s32[]{:S(2)}) async-start(), calls=%async_computation.6 | async-start | bytes 2621440 | tf_op jit(solution)/shard_map/all_gather | solution.py:1118
  10.3 15.0 %collective-permute-start.3 = (bf16[128,2048]{1,0:T(8,128)(2,1)S(1)}, bf16[128,2048]{1,0:T(8,128)(2,1)S(1)}, u32[]{:S(2)}, u32[]{:S(2)}) collective-permute-start(bf16[128,2048]{1,0:T(8,128)(2,1)S(1)} %fusion.4.refs_0_), channel_id=1, source_target_pairs={{0,1},{2,0},{4,2},{6,4},{7,6},{5,7},{3,5},{1,3},{8,9},{10,8},{12,1... | collective-permute-start | bytes 1572872 | tf_op jit(solution)/shard_map/ppermute | solution.py:917
  13.3 13.4 %collective-permute-start.4 = (bf16[128,2048]{1,0:T(8,128)(2,1)S(1)}, bf16[128,2048]{1,0:T(8,128)(2,1)S(1)}, u32[]{:S(2)}, u32[]{:S(2)}) collective-permute-start(bf16[128,2048]{1,0:T(8,128)(2,1)S(1)} %fusion.4.refs_0_), channel_id=1, source_target_pairs={{0,2},{2,4},{4,6},{6,7},{7,5},{5,3},{3,1},{1,0},{8,10},{10,12},{12... | collective-permute-start | bytes 1572872 | tf_op jit(solution)/shard_map/ppermute | solution.py:917
  13.5 39.6 %collective-permute-start.12 = (bf16[512,1536]{1,0:T(8,128)(2,1)}, bf16[512,1536]{1,0:T(8,128)(2,1)S(1)}, u32[]{:S(2)}, u32[]{:S(2)}) collective-permute-start(bf16[512,1536]{1,0:T(8,128)(2,1)} %refs_22_.1), channel_id=1, source_target_pairs={{0,16},{8,24},{16,0},{24,8},{1,17},{9,25},{17,1},{25,9},{2,18},{10... | collective-permute-start | bytes 4718600 | tf_op jit(solution)/shard_map/ppermute | solution.py:1007
  26.7 12.5 %collective-permute-start.5 = (bf16[128,2048]{1,0:T(8,128)(2,1)S(1)}, bf16[128,2048]{1,0:T(8,128)(2,1)S(1)}, u32[]{:S(2)}, u32[]{:S(2)}) collective-permute-start(bf16[128,2048]{1,0:T(8,128)(2,1)S(1)} %collective-permute-done.3.refs_1_), channel_id=1, source_target_pairs={{0,1},{2,0},{4,2},{6,4},{7,6},{5,7},{3,5},{1,3},{8,9},{10,8},{12,1... | collective-permute-start | bytes 1572872 | tf_op jit(solution)/shard_map/ppermute | solution.py:917
  28.3 12.2 %collective-permute-start.6 = (bf16[128,2048]{1,0:T(8,128)(2,1)S(1)}, bf16[128,2048]{1,0:T(8,128)(2,1)S(1)}, u32[]{:S(2)}, u32[]{:S(2)}) collective-permute-start(bf16[128,2048]{1,0:T(8,128)(2,1)S(1)} %collective-permute-done.4.refs_2_), channel_id=1, source_target_pairs={{0,2},{2,4},{4,6},{6,7},{7,5},{5,3},{3,1},{1,0},{8,10},{10,12},{12... | collective-permute-start | bytes 1572872 | tf_op jit(solution)/shard_map/ppermute | solution.py:917
  42.5 15.5 %collective-permute-start.11 = (bf16[512,1536]{1,0:T(8,128)(2,1)}, bf16[512,1536]{1,0:T(8,128)(2,1)}, u32[]{:S(2)}, u32[]{:S(2)}) collective-permute-start(bf16[512,1536]{1,0:T(8,128)(2,1)} %refs_22_.1), channel_id=1, source_target_pairs={{0,8},{8,0},{16,24},{24,16},{1,9},{9,1},{17,25},{25,17},{2,10},{10... | collective-permute-start | bytes 4718600 | tf_op jit(solution)/shard_map/ppermute | solution.py:1007
  53.2 131.6 %all-gather.8.cloned.1.call-start = ((), (), s32[]{:S(2)}) async-start(), calls=%async_computation.7 | async-start | bytes 3604480 | tf_op jit(solution)/shard_map/all_gather | solution.py:1148
  53.2 13.9 %collective-permute-start = (bf16[4,512]{1,0:T(4,128)(2,1)}, bf16[4,512]{1,0:T(4,128)(2,1)S(1)}, u32[]{:S(2)}, u32[]{:S(2)}) collective-permute-start(bf16[4,512]{1,0:T(4,128)(2,1)} %bitcast.46), channel_id=1, source_target_pairs={{0,8},{8,0},{16,24},{24,16},{1,9},{9,1},{17,25},{25,17},{2,10},{10... | collective-permute-start | bytes 12296 | tf_op jit(solution)/shard_map/ppermute | solution.py:1007
  63.9 18.6 %collective-permute-start.14 = (bf16[128,2048]{1,0:T(8,128)(2,1)}, bf16[128,2048]{1,0:T(8,128)(2,1)}, u32[]{:S(2)}, u32[]{:S(2)}) collective-permute-start(bf16[128,2048]{1,0:T(8,128)(2,1)} %refs_0_), channel_id=1, source_target_pairs={{0,2},{2,4},{4,6},{6,7},{7,5},{5,3},{3,1},{1,0},{8,10},{10,12},{12... | collective-permute-start | bytes 1572872 | tf_op jit(solution)/shard_map/ppermute | solution.py:917
  64.4 18.1 %collective-permute-start.15 = (bf16[128,2048]{1,0:T(8,128)(2,1)}, bf16[128,2048]{1,0:T(8,128)(2,1)}, u32[]{:S(2)}, u32[]{:S(2)}) collective-permute-start(bf16[128,2048]{1,0:T(8,128)(2,1)} %refs_0_), channel_id=1, source_target_pairs={{0,1},{2,0},{4,2},{6,4},{7,6},{5,7},{3,5},{1,3},{8,9},{10,8},{12,1... | collective-permute-start | bytes 1572872 | tf_op jit(solution)/shard_map/ppermute | solution.py:917
  82.5 20.2 %collective-permute-start.17 = (bf16[128,2048]{1,0:T(8,128)(2,1)}, bf16[128,2048]{1,0:T(8,128)(2,1)S(1)}, u32[]{:S(2)}, u32[]{:S(2)}) collective-permute-start(bf16[128,2048]{1,0:T(8,128)(2,1)} %collective-permute-done.14.refs_2_), channel_id=1, source_target_pairs={{0,2},{2,4},{4,6},{6,7},{7,5},{5,3},{3,1},{1,0},{8,10},{10,12},{12... | collective-permute-start | bytes 1572872 | tf_op jit(solution)/shard_map/ppermute | solution.py:917
  83.0 19.8 %collective-permute-start.18 = (bf16[128,2048]{1,0:T(8,128)(2,1)}, bf16[128,2048]{1,0:T(8,128)(2,1)S(1)}, u32[]{:S(2)}, u32[]{:S(2)}) collective-permute-start(bf16[128,2048]{1,0:T(8,128)(2,1)} %collective-permute-done.15.refs_1_), channel_id=1, source_target_pairs={{0,1},{2,0},{4,2},{6,4},{7,6},{5,7},{3,5},{1,3},{8,9},{10,8},{12,1... | collective-permute-start | bytes 1572872 | tf_op jit(solution)/shard_map/ppermute | solution.py:917
  102.8 14.8 %collective-permute-start.19 = (bf16[128,2048]{1,0:T(8,128)(2,1)S(1)}, bf16[128,2048]{1,0:T(8,128)(2,1)S(1)}, u32[]{:S(2)}, u32[]{:S(2)}) collective-permute-start(bf16[128,2048]{1,0:T(8,128)(2,1)S(1)} %collective-permute-done.17.refs_4_), channel_id=1, source_target_pairs={{0,2},{2,4},{4,6},{6,7},{7,5},{5,3},{3,1},{1,0},{8,10},{10,12},{12... | collective-permute-start | bytes 1572872 | tf_op jit(solution)/shard_map/ppermute | solution.py:917
  103.3 14.3 %collective-permute-start.20 = (bf16[128,2048]{1,0:T(8,128)(2,1)S(1)}, bf16[128,2048]{1,0:T(8,128)(2,1)S(1)}, u32[]{:S(2)}, u32[]{:S(2)}) collective-permute-start(bf16[128,2048]{1,0:T(8,128)(2,1)S(1)} %collective-permute-done.18.refs_3_), channel_id=1, source_target_pairs={{0,1},{2,0},{4,2},{6,4},{7,6},{5,7},{3,5},{1,3},{8,9},{10,8},{12,1... | collective-permute-start | bytes 1572872 | tf_op jit(solution)/shard_map/ppermute | solution.py:917
  117.6 92.3 %all-gather.10.cloned.1.call-start = ((), (), s32[]{:S(2)}) async-start(), calls=%async_computation.8 | async-start | bytes 3604480 | tf_op jit(solution)/shard_map/all_gather | solution.py:1148
  118.4 91.6 %all-gather.12.cloned.1.call-start = ((), (), s32[]{:S(2)}) async-start(), calls=%async_computation.9 | async-start | bytes 3604480 | tf_op jit(solution)/shard_map/all_gather | solution.py:1148
  118.4 11.9 %collective-permute-start.21 = (bf16[64,2048]{1,0:T(8,128)(2,1)S(1)}, bf16[64,2048]{1,0:T(8,128)(2,1)S(1)}, u32[]{:S(2)}, u32[]{:S(2)}) collective-permute-start(bf16[64,2048]{1,0:T(8,128)(2,1)S(1)} %slice.262), channel_id=1, source_target_pairs={{0,2},{2,4},{4,6},{6,7},{7,5},{5,3},{3,1},{1,0},{8,10},{10,12},{12... | collective-permute-start | bytes 786440 | tf_op jit(solution)/shard_map/ppermute | solution.py:917
  145.7 194.2 %reduce-scatter.7.cloned.1.call-start = ((), (), s32[]{:S(2)}) async-start(), calls=%async_computation.10 | async-start | bytes 3604480 | tf_op jit(solution)/shard_map/reduce_scatter | solution.py:1191
  182.6 11.8 %collective-permute-start.37 = (bf16[128,2048]{1,0:T(8,128)(2,1)S(1)}, bf16[128,2048]{1,0:T(8,128)(2,1)S(1)}, u32[]{:S(2)}, u32[]{:S(2)}) collective-permute-start(bf16[128,2048]{1,0:T(8,128)(2,1)S(1)} %multiply_convert_fusion.3.refs_0_), channel_id=1, source_target_pairs={{0,2},{2,4},{4,6},{6,7},{7,5},{5,3},{3,1},{1,0},{8,10},{10,12},{12... | collective-permute-start | bytes 1572872 | tf_op jit(solution)/shard_map/ppermute | solution.py:917
  195.8 12.2 %collective-permute-start.40 = (bf16[128,2048]{1,0:T(8,128)(2,1)S(1)}, bf16[128,2048]{1,0:T(8,128)(2,1)}, u32[]{:S(2)}, u32[]{:S(2)}) collective-permute-start(bf16[128,2048]{1,0:T(8,128)(2,1)S(1)} %collective-permute-done.38.refs_1_), channel_id=1, source_target_pairs={{0,1},{2,0},{4,2},{6,4},{7,6},{5,7},{3,5},{1,3},{8,9},{10,8},{12,1... | collective-permute-start | bytes 1572872 | tf_op jit(solution)/shard_map/ppermute | solution.py:917
  207.9 12.2 %collective-permute-start.41 = (bf16[128,2048]{1,0:T(8,128)(2,1)}, bf16[128,2048]{1,0:T(8,128)(2,1)S(1)}, u32[]{:S(2)}, u32[]{:S(2)}) collective-permute-start(bf16[128,2048]{1,0:T(8,128)(2,1)} %collective-permute-done.39.refs_4_), channel_id=1, source_target_pairs={{0,2},{2,4},{4,6},{6,7},{7,5},{5,3},{3,1},{1,0},{8,10},{10,12},{12... | collective-permute-start | bytes 1572872 | tf_op jit(solution)/shard_map/ppermute | solution.py:917
  208.7 12.2 %collective-permute-start.42 = (bf16[128,2048]{1,0:T(8,128)(2,1)}, bf16[128,2048]{1,0:T(8,128)(2,1)S(1)}, u32[]{:S(2)}, u32[]{:S(2)}) collective-permute-start(bf16[128,2048]{1,0:T(8,128)(2,1)} %collective-permute-done.40.refs_3_), channel_id=1, source_target_pairs={{0,1},{2,0},{4,2},{6,4},{7,6},{5,7},{3,5},{1,3},{8,9},{10,8},{12,1... | collective-permute-start | bytes 1572872 | tf_op jit(solution)/shard_map/ppermute | solution.py:917
  263.0 97.3 %reduce-scatter.9.cloned.1.call-start = ((), (), s32[]{:S(2)}) async-start(), calls=%async_computation.11 | async-start | bytes 3604480 | tf_op jit(solution)/shard_map/reduce_scatter | solution.py:1191
  277.6 157.3 %reduce-scatter.13.cloned.1.call-start = ((), (), s32[]{:S(2)}) async-start(), calls=%async_computation.13 | async-start | bytes 3604480 | tf_op jit(solution)/shard_map/reduce_scatter | solution.py:1191
  295.7 139.3 %reduce-scatter.11.cloned.1.call-start = ((), (), s32[]{:S(2)}) async-start(), calls=%async_computation.12 | async-start | bytes 2621440 | tf_op jit(solution)/shard_map/reduce_scatter | solution.py:1257
  298.1 12.1 %collective-permute-start.57 = (bf16[64,2048]{1,0:T(8,128)(2,1)}, bf16[64,2048]{1,0:T(8,128)(2,1)S(1)}, u32[]{:S(2)}, u32[]{:S(2)}) collective-permute-start(bf16[64,2048]{1,0:T(8,128)(2,1)} %get-tuple-element.429), channel_id=1, source_target_pairs={{0,2},{2,4},{4,6},{6,7},{7,5},{5,3},{3,1},{1,0},{8,10},{10,12},{12... | collective-permute-start | bytes 786440 | tf_op jit(solution)/shard_map/ppermute | solution.py:917
  300.1 12.7 %collective-permute-start.58 = (bf16[64,2048]{1,0:T(8,128)(2,1)S(1)}, bf16[64,2048]{1,0:T(8,128)(2,1)S(1)}, u32[]{:S(2)}, u32[]{:S(2)}) collective-permute-start(bf16[64,2048]{1,0:T(8,128)(2,1)S(1)} %get-tuple-element.428), channel_id=1, source_target_pairs={{0,1},{2,0},{4,2},{6,4},{7,6},{5,7},{3,5},{1,3},{8,9},{10,8},{12,1... | collective-permute-start | bytes 786440 | tf_op jit(solution)/shard_map/ppermute | solution.py:917
  315.6 11.9 %collective-permute-start.60 = (bf16[128,2048]{1,0:T(8,128)(2,1)S(1)}, bf16[128,2048]{1,0:T(8,128)(2,1)S(1)}, u32[]{:S(2)}, u32[]{:S(2)}) collective-permute-start(bf16[128,2048]{1,0:T(8,128)(2,1)S(1)} %get-tuple-element.309.refs_0_), channel_id=1, source_target_pairs={{0,1},{2,0},{4,2},{6,4},{7,6},{5,7},{3,5},{1,3},{8,9},{10,8},{12,1... | collective-permute-start | bytes 1572872 | tf_op jit(solution)/shard_map/ppermute | solution.py:917
  375.5 15.6 %collective-permute-start.69 = (bf16[128,2048]{1,0:T(8,128)(2,1)}, bf16[128,2048]{1,0:T(8,128)(2,1)}, u32[]{:S(2)}, u32[]{:S(2)}) collective-permute-start(bf16[128,2048]{1,0:T(8,128)(2,1)} %get-tuple-element.322), channel_id=1, source_target_pairs={{0,2},{2,4},{4,6},{6,7},{7,5},{5,3},{3,1},{1,0},{8,10},{10,12},{12... | collective-permute-start | bytes 1572872 | tf_op jit(solution)/shard_map/ppermute | solution.py:917
  376.5 14.6 %collective-permute-start.72 = (bf16[128,2048]{1,0:T(8,128)(2,1)S(1)}, bf16[128,2048]{1,0:T(8,128)(2,1)}, u32[]{:S(2)}, u32[]{:S(2)}) collective-permute-start(bf16[128,2048]{1,0:T(8,128)(2,1)S(1)} %get-tuple-element.325), channel_id=1, source_target_pairs={{0,1},{2,0},{4,2},{6,4},{7,6},{5,7},{3,5},{1,3},{8,9},{10,8},{12,1... | collective-permute-start | bytes 1572872 | tf_op jit(solution)/shard_map/ppermute | solution.py:917
  391.2 128.7 %reduce-scatter.15.cloned.1.call-start = ((), (), s32[]{:S(2)}) async-start(), calls=%async_computation.14 | async-start | bytes 5242880 | tf_op jit(solution)/shard_map/reduce_scatter | solution.py:1278
  393.8 38.7 %collective-permute-start.73 = (bf16[128,2048]{1,0:T(8,128)(2,1)}, bf16[128,2048]{1,0:T(8,128)(2,1)S(1)}, u32[]{:S(2)}, u32[]{:S(2)}) collective-permute-start(bf16[128,2048]{1,0:T(8,128)(2,1)} %get-tuple-element.327), channel_id=1, source_target_pairs={{0,2},{2,4},{4,6},{6,7},{7,5},{5,3},{3,1},{1,0},{8,10},{10,12},{12... | collective-permute-start | bytes 1572872 | tf_op jit(solution)/shard_map/ppermute | solution.py:917
  394.7 37.8 %collective-permute-start.74 = (bf16[128,2048]{1,0:T(8,128)(2,1)}, bf16[128,2048]{1,0:T(8,128)(2,1)}, u32[]{:S(2)}, u32[]{:S(2)}) collective-permute-start(bf16[128,2048]{1,0:T(8,128)(2,1)} %get-tuple-element.338), channel_id=1, source_target_pairs={{0,1},{2,0},{4,2},{6,4},{7,6},{5,7},{3,5},{1,3},{8,9},{10,8},{12,1... | collective-permute-start | bytes 1572872 | tf_op jit(solution)/shard_map/ppermute | solution.py:917
  444.1 84.0 %reduce-scatter.17.cloned.1.call-start = ((), (), s32[]{:S(2)}) async-start(), calls=%async_computation.15 | async-start | bytes 2621440 | tf_op jit(solution)/shard_map/reduce_scatter | solution.py:1191
  444.1 14.9 %collective-permute-start.76 = (bf16[128,2048]{1,0:T(8,128)(2,1)}, bf16[128,2048]{1,0:T(8,128)(2,1)S(1)}, u32[]{:S(2)}, u32[]{:S(2)}) collective-permute-start(bf16[128,2048]{1,0:T(8,128)(2,1)} %get-tuple-element.341), channel_id=1, source_target_pairs={{0,1},{2,0},{4,2},{6,4},{7,6},{5,7},{3,5},{1,3},{8,9},{10,8},{12,1... | collective-permute-start | bytes 1572872 | tf_op jit(solution)/shard_map/ppermute | solution.py:917
  445.9 15.0 %collective-permute-start.75 = (bf16[128,2048]{1,0:T(8,128)(2,1)}, bf16[128,2048]{1,0:T(8,128)(2,1)S(1)}, u32[]{:S(2)}, u32[]{:S(2)}) collective-permute-start(bf16[128,2048]{1,0:T(8,128)(2,1)} %get-tuple-element.340), channel_id=1, source_target_pairs={{0,2},{2,4},{4,6},{6,7},{7,5},{5,3},{3,1},{1,0},{8,10},{10,12},{12... | collective-permute-start | bytes 1572872 | tf_op jit(solution)/shard_map/ppermute | solution.py:917
  462.1 13.9 %collective-permute-start.78 = (bf16[64,2048]{1,0:T(8,128)(2,1)S(1)}, bf16[64,2048]{1,0:T(8,128)(2,1)S(1)}, u32[]{:S(2)}, u32[]{:S(2)}) collective-permute-start(bf16[64,2048]{1,0:T(8,128)(2,1)S(1)} %get-tuple-element.473), channel_id=1, source_target_pairs={{0,2},{2,4},{4,6},{6,7},{7,5},{5,3},{3,1},{1,0},{8,10},{10,12},{12... | collective-permute-start | bytes 786440 | tf_op jit(solution)/shard_map/ppermute | solution.py:917
  462.5 13.5 %collective-permute-start.79 = (bf16[64,2048]{1,0:T(8,128)(2,1)S(1)}, bf16[64,2048]{1,0:T(8,128)(2,1)S(1)}, u32[]{:S(2)}, u32[]{:S(2)}) collective-permute-start(bf16[64,2048]{1,0:T(8,128)(2,1)S(1)} %get-tuple-element.472), channel_id=1, source_target_pairs={{0,1},{2,0},{4,2},{6,4},{7,6},{5,7},{3,5},{1,3},{8,9},{10,8},{12,1... | collective-permute-start | bytes 786440 | tf_op jit(solution)/shard_map/ppermute | solution.py:917
  477.9 15.7 %collective-permute-start.80 = (bf16[64,2048]{1,0:T(8,128)(2,1)}, bf16[64,2048]{1,0:T(8,128)(2,1)}, u32[]{:S(2)}, u32[]{:S(2)}) collective-permute-start(bf16[64,2048]{1,0:T(8,128)(2,1)} %get-tuple-element.471), channel_id=1, source_target_pairs={{0,2},{2,4},{4,6},{6,7},{7,5},{5,3},{3,1},{1,0},{8,10},{10,12},{12... | collective-permute-start | bytes 786440 | tf_op jit(solution)/shard_map/ppermute | solution.py:917
  478.4 15.3 %collective-permute-start.81 = (bf16[64,2048]{1,0:T(8,128)(2,1)}, bf16[64,2048]{1,0:T(8,128)(2,1)}, u32[]{:S(2)}, u32[]{:S(2)}) collective-permute-start(bf16[64,2048]{1,0:T(8,128)(2,1)} %get-tuple-element.470), channel_id=1, source_target_pairs={{0,1},{2,0},{4,2},{6,4},{7,6},{5,7},{3,5},{1,3},{8,9},{10,8},{12,1... | collective-permute-start | bytes 786440 | tf_op jit(solution)/shard_map/ppermute | solution.py:917
  480.0 13.6 %collective-permute-start.82 = (bf16[64,2048]{1,0:T(8,128)(2,1)}, bf16[64,2048]{1,0:T(8,128)(2,1)}, u32[]{:S(2)}, u32[]{:S(2)}) collective-permute-start(bf16[64,2048]{1,0:T(8,128)(2,1)} %get-tuple-element.469), channel_id=1, source_target_pairs={{0,2},{2,4},{4,6},{6,7},{7,5},{5,3},{3,1},{1,0},{8,10},{10,12},{12... | collective-permute-start | bytes 786440 | tf_op jit(solution)/shard_map/ppermute | solution.py:917
  480.4 13.2 %collective-permute-start.83 = (bf16[64,2048]{1,0:T(8,128)(2,1)}, bf16[64,2048]{1,0:T(8,128)(2,1)}, u32[]{:S(2)}, u32[]{:S(2)}) collective-permute-start(bf16[64,2048]{1,0:T(8,128)(2,1)} %get-tuple-element.468), channel_id=1, source_target_pairs={{0,1},{2,0},{4,2},{6,4},{7,6},{5,7},{3,5},{1,3},{8,9},{10,8},{12,1... | collective-permute-start | bytes 786440 | tf_op jit(solution)/shard_map/ppermute | solution.py:917
  496.2 23.7 %collective-permute-start.86 = (bf16[64,2048]{1,0:T(8,128)(2,1)}, bf16[64,2048]{1,0:T(8,128)(2,1)}, u32[]{:S(2)}, u32[]{:S(2)}) collective-permute-start(bf16[64,2048]{1,0:T(8,128)(2,1)} %get-tuple-element.467), channel_id=1, source_target_pairs={{0,2},{2,4},{4,6},{6,7},{7,5},{5,3},{3,1},{1,0},{8,10},{10,12},{12... | collective-permute-start | bytes 786440 | tf_op jit(solution)/shard_map/ppermute | solution.py:917
  497.7 22.2 %collective-permute-start.87 = (bf16[64,2048]{1,0:T(8,128)(2,1)}, bf16[64,2048]{1,0:T(8,128)(2,1)}, u32[]{:S(2)}, u32[]{:S(2)}) collective-permute-start(bf16[64,2048]{1,0:T(8,128)(2,1)} %get-tuple-element.466), channel_id=1, source_target_pairs={{0,1},{2,0},{4,2},{6,4},{7,6},{5,7},{3,5},{1,3},{8,9},{10,8},{12,1... | collective-permute-start | bytes 786440 | tf_op jit(solution)/shard_map/ppermute | solution.py:917
  498.2 21.7 %collective-permute-start.88 = (bf16[64,2048]{1,0:T(8,128)(2,1)}, bf16[64,2048]{1,0:T(8,128)(2,1)}, u32[]{:S(2)}, u32[]{:S(2)}) collective-permute-start(bf16[64,2048]{1,0:T(8,128)(2,1)} %get-tuple-element.465), channel_id=1, source_target_pairs={{0,2},{2,4},{4,6},{6,7},{7,5},{5,3},{3,1},{1,0},{8,10},{10,12},{12... | collective-permute-start | bytes 786440 | tf_op jit(solution)/shard_map/ppermute | solution.py:917
  499.7 20.2 %collective-permute-start.89 = (bf16[64,2048]{1,0:T(8,128)(2,1)}, bf16[64,2048]{1,0:T(8,128)(2,1)}, u32[]{:S(2)}, u32[]{:S(2)}) collective-permute-start(bf16[64,2048]{1,0:T(8,128)(2,1)} %get-tuple-element.464), channel_id=1, source_target_pairs={{0,1},{2,0},{4,2},{6,4},{7,6},{5,7},{3,5},{1,3},{8,9},{10,8},{12,1... | collective-permute-start | bytes 786440 | tf_op jit(solution)/shard_map/ppermute | solution.py:917
  521.5 12.4 %collective-permute-start.91 = (bf16[64,2048]{1,0:T(8,128)(2,1)S(1)}, bf16[64,2048]{1,0:T(8,128)(2,1)S(1)}, u32[]{:S(2)}, u32[]{:S(2)}) collective-permute-start(bf16[64,2048]{1,0:T(8,128)(2,1)S(1)} %get-tuple-element.463), channel_id=1, source_target_pairs={{0,2},{2,4},{4,6},{6,7},{7,5},{5,3},{3,1},{1,0},{8,10},{10,12},{12... | collective-permute-start | bytes 786440 | tf_op jit(solution)/shard_map/ppermute | solution.py:917
  (124 other events, 1261.8 us)
Sparse Core Ops, SparseCore 0:
  53.3 21.4 all-gather.5
  117.7 27.5 all-gather.7
  146.9 27.0 all-gather.9
  175.4 27.0 all-gather.11
  263.2 35.0 reduce-scatter.6
  300.8 36.3 reduce-scatter.8
  339.7 36.3 reduce-scatter.12
  391.3 30.2 reduce-scatter.10
  444.2 47.0 reduce-scatter.14
  494.4 33.6 reduce-scatter.16

commit v6 on v5

--- a/solution.py
+++ b/solution.py
@@ -41,6 +41,14 @@
 
 def block_columns(spots_ref, b, width):
     return pl.ds(pl.multiple_of(spots_ref[b] * width, 128), width)
+
+
+def chosen(refs, place_ref, source, h, rows):
+    value = refs[0][h, rows, :]
+    for b in range(1, len(refs)):
+        here = (place_ref[0] ^ b) == source if len(refs) == 4 else b == source
+        value = jnp.where(here, refs[b][h, rows, :], value)
+    return value
 
 
 def softplus(x):
@@ -228,8 +236,9 @@
     heads, group, steps, peers, own,
     proj_ref, prev_ref, halo_ref, rates_ref, bias_ref, taps_ref,
     state_ref, uw_ref, inv_ref, trans_ref, qe_ref,
-    dout_ref, value_ref, incoming_ref, place_ref, spots_ref, maps_ref, *refs,
+    dout_ref, value_ref, incoming_ref, place_ref, spots_ref, *refs,
 ):
+    maps_refs, refs = refs[:peers], refs[peers:]
     *local_refs, gp_ref, grates_ref, sums_ref, tail_ref, lead_ref, x_ref, d_ref, carry_ref, next_ref = refs
     step = pl.program_id(0)
     rows_here = CHUNK * group
@@ -250,7 +259,7 @@
                 for b, local_ref in enumerate(local_refs):
                     here = (place_ref[0] ^ b) == source if peers == 4 else b == source
                     share = jnp.where(here, local_ref[h].astype(F32), share)
-                moved = mm(grad, maps_ref[source, h, DV:, :], 1, 1) + share
+                moved = mm(grad, chosen(maps_refs, place_ref, source, h, slice(DV, DV + DK)), 1, 1) + share
                 grad = jnp.where(source > place_ref[0], moved, grad)
             carry_ref[h] = grad
         d_ref[rows_here : rows_here + 8, :] = jnp.zeros((8, heads * MIX), F32)
@@ -396,7 +405,7 @@
     flip = lambda i: (steps - 1 - i, 0)
     keep = lambda a, b: pl.BlockSpec((heads, group, a, b), lambda i: (0, steps - 1 - i, 0, 0))
     return pl.pallas_call(
-        functools.partial(backward_kernel, heads, group, steps, maps.shape[0], total // spots.shape[0]),
+        functools.partial(backward_kernel, heads, group, steps, len(maps), total // spots.shape[0]),
         grid=(steps,),
         in_specs=[
             pl.BlockSpec((rows, heads * PER), flip),
@@ -415,7 +424,7 @@
             pl.BlockSpec(incoming.shape, lambda i: (0, 0, 0)),
             pl.BlockSpec(memory_space=pltpu.SMEM),
             pl.BlockSpec(memory_space=pltpu.SMEM),
-            pl.BlockSpec(maps.shape, lambda i: (0, 0, 0, 0)),
+            *[pl.BlockSpec(part.shape, lambda i: (0, 0, 0)) for part in maps],
             *[pl.BlockSpec(part.shape, lambda i: (0, 0, 0)) for part in local],
         ],
         out_shape=[
@@ -440,14 +449,15 @@
         ],
         compiler_params=pltpu.CompilerParams(vmem_limit_bytes=VMEM_LIMIT),
         cost_estimate=LIGHT,
-    )(projected, projected, halo, rates, bias_row, taps, state, uw, inv, trans, qe, dout, value, incoming, place, spots, maps, *local)
+    )(projected, projected, halo, rates, bias_row, taps, state, uw, inv, trans, qe, dout, value, incoming, place, spots, *maps, *local)
 
 
 def pair_rows(ids_ref, step, which, rows):
     return pl.ds(pl.multiple_of(ids_ref[2 * step + which] * rows, rows), rows)
 
 
-def gate_kernel(heads, peers, ids_ref, place_ref, maps_ref, gain_ref, w_ref, *refs):
+def gate_kernel(heads, peers, ids_ref, place_ref, gain_ref, w_ref, *refs):
+    maps_refs, refs = refs[:peers], refs[peers:]
     olocal_refs, qmap_refs = refs[0:2], refs[2:4]
     gate_refs = refs[4 : 4 + 2 * heads]
     value_ref, gated_ref, part_ref, incoming_ref = refs[4 + 2 * heads :]
@@ -458,7 +468,8 @@
         for h in range(heads):
             state = jnp.zeros((DV, DK), F32)
             for source in range(peers - 1):
-                moved = mm(state, maps_ref[source, h, DV:, :]) + maps_ref[source, h, :DV, :].astype(F32)
+                entry = chosen(maps_refs, place_ref, source, h, slice(None))
+                moved = mm(state, entry[DV:]) + entry[:DV].astype(F32)
                 state = jnp.where(source < place_ref[0], moved, state)
             incoming_ref[h] = state.astype(BF16)
 
@@ -492,7 +503,7 @@
 
 
 def gate_output(ids, place, maps, out_local, query_map, projected, gain, w_out):
-    heads = maps.shape[1]
+    heads = maps[0].shape[0]
     total = projected.shape[0]
     count = ids.shape[0]
     rows = total // count
@@ -501,14 +512,14 @@
     whole = lambda i, *s: (0, 0)
     full, gates = gate_blocks(heads, rows)
     return pl.pallas_call(
-        functools.partial(gate_kernel, heads, maps.shape[0]),
+        functools.partial(gate_kernel, heads, len(maps)),
         grid_spec=pltpu.PrefetchScalarGridSpec(
             num_scalar_prefetch=2,
             grid=(count // 2,),
             in_specs=[
-                pl.BlockSpec(maps.shape, lambda i, *s: (0, 0, 0, 0)),
                 pl.BlockSpec((1, DV), whole),
                 pl.BlockSpec(w_out.shape, whole),
+                *[pl.BlockSpec(part.shape, lambda i, *s: (0, 0, 0)) for part in maps],
                 *full(heads * DV),
                 *full(heads * DK),
                 *gates,
@@ -529,7 +540,7 @@
         compiler_params=pltpu.CompilerParams(vmem_limit_bytes=VMEM_LIMIT),
         cost_estimate=LIGHT,
     )(
-        ids, place, maps, gain, w_out, out_local, out_local, query_map, query_map,
+        ids, place, gain, w_out, *maps, out_local, out_local, query_map, query_map,
         *[projected] * (2 * heads),
     )
 
@@ -1138,17 +1149,17 @@
     )
     end_state, *_ = together(end_state, *cot_state)
     cot_stage(2, end_state)
-    maps = lax.all_gather(end_state, "seq")
-    maps, *_ = together(maps, *cot_state)
-    cot_stage(3, maps)
+    maps = seq_shards(end_state, "seq")
+    maps = list(together(*maps, *cot_state))[:peers]
+    cot_stage(3, maps[1])
     value, gated, branch_part, incoming = gate_output(
         ids, place, maps, out_local, query_map, projected, gain_row, out_rows
     )
     branch_part, *_ = together(branch_part, *cot_state)
     fetch = lambda w, *pins: lax.all_gather(after(w, *pins), "seq", axis=1, tiled=True)
-    down_w = fetch(w_ff_down, maps)
-    gate_w = fetch(w_ff_gate, maps)
-    up_w = fetch(w_ff_up, maps)
+    down_w = fetch(w_ff_down, *maps)
+    gate_w = fetch(w_ff_gate, *maps)
+    up_w = fetch(w_ff_up, *maps)
 
     def stack_normed(pin):
         keep["normed"] = stacked({k: [pin(p) for p in ps] for k, ps in normed_found.items()}, seq_rows)
@@ -1262,7 +1273,6 @@
     )
     grad_mixed, gate_grad_s, grad_up_s, *_ = together(grad_mixed, gate_grad_s, grad_up_s, *known())
     later_rows = shifted(lead_rows, "seq", -1)
-    out_grad_w = outer(gated, after(branch_near, lead_rows))
     output_hops(4, grad_mixed)
     padded = jnp.concatenate([jnp.zeros((HALO, heads * MIX), F32), later_rows])
     last_rows = tail_rows + sum(
@@ -1270,10 +1280,7 @@
     )
     last_start = near_spots[count - 1] * own_rows + own_rows - HALO
     grad_mixed = lax.dynamic_update_slice(grad_mixed, last_rows.astype(BF16), (last_start, 0))
-    grad_mixed, out_grad_w = together(grad_mixed, out_grad_w)
     mix_grad_w = outer(keep["normed"], grad_mixed)
-    mix_grad_w, out_grad_w = together(mix_grad_w, out_grad_w)
-    grad_out_s = scatter(out_grad_w)
     grad_mixed, mix_grad_w = together(grad_mixed, mix_grad_w)
     mix_grad_s = lax.psum_scatter(mix_grad_w, "seq", scatter_dimension=0, tiled=True)
     early = [hops] + ([hops - 1, hops + 1] if hops > 1 else [])
@@ -1305,14 +1312,20 @@
         gains = jnp.concatenate([mlp_gain_part[None], head_gain_part, jnp.zeros((1, width - DV), F32)], axis=1)
         gains = jnp.pad(gains, ((4, 3), (0, 0)))
         small = jnp.concatenate([sums, gains, seq_sums], axis=1)
-        keep["small"] = butterfly(small, "seq")
-        keep["gains"] = keep["small"][4:5, : 3 * width]
-        return (keep["gains"],)
+        keep["small"] = small + swap(small, "seq", 1)
+        out_grad_w = outer(gated, pin(branch_near))
+        keep["out"] = scatter(out_grad_w)
+        return (keep["small"], out_grad_w)
 
     def third_window(pin):
-        gains = pin(keep["gains"])
-        keep["gains"] = gains + swap(gains, "head", 1)
-        return (keep["gains"], mix_grad_s)
+        small = pin(keep["small"])
+        bit = 2
+        while bit < peers:
+            small = small + swap(small, "seq", bit)
+            bit *= 2
+        keep["small"] = small
+        keep["gains"] = small[4:5, : 3 * width]
+        return (small, mix_grad_s)
 
     grad_normed = ring_scatter(
         take, own_rows, "head", {1: first_window, 2: second_window, 3: third_window}
@@ -1325,11 +1338,11 @@
         residual + sum(a.astype(F32) for a in known()) + take_output(0, 0, own_rows).astype(F32)
     ).astype(BF16)
     small, gains = keep["small"], after(keep["gains"], grad_normed)
-    bit = 2
+    bit = 1
     while bit < count:
         gains = gains + swap(gains, "head", bit)
         bit *= 2
-    joined, *wide = finish_all(mix_grad_s, gate_grad_s, [grad_out_s, grad_gate_s, grad_up_s, grad_down_s])
+    joined, *wide = finish_all(mix_grad_s, gate_grad_s, [keep["out"], grad_gate_s, grad_up_s, grad_down_s])
     per_seq = w_rates.shape[0]
     return (
         output,

time: 553 us -> 553 us (level)
  blocking collectives: 12.7 us -> 0 us
  starting transfers between devices: 100 us -> 109 us
    all_gather x1 -> x0, blocking collectives: 12.7 us -> none  [per_device(): maps = lax.all_gather(end_state, 'seq')]
    ppermute x14 -> x17, starting transfers between devices: 11.5 us -> 15.1 us  [swap(): return lax.ppermute(value, axis, [(i, i ^ bit) for i in range(count)])]
    ppermute x14 -> x17, waiting for transfers between devices: 25 us -> 26 us  [swap(): return lax.ppermute(value, axis, [(i, i ^ bit) for i in range(count)])]
  transfers between devices with their start and end apart: 107 -> 110, of which waited for: 50 -> 56; matrix products, arithmetic and copies ran while one was open for 9% -> 9% of each run, Pallas kernels for 32% -> 32%
where the time goes in v6:
time: 553 us; the launch traced here: 544 us
  Pallas kernels  186 us (34%)
  waiting for transfers between devices  150 us (27%)
  starting transfers between devices  109 us (20%)
  other arithmetic  35.1 us (6%)
  matrix products  25.8 us (5%)
  local copies, waits for them, and re-layouts  22.6 us (4%)
  between operations  16.3 us (3%)
    ppermute x81, waiting for transfers between devices, ring_step(): lax.ppermute(value, axis, [(order[i], order[(i + step) % count]) for i in...  123 us
    ppermute x81, starting transfers between devices, ring_step(): lax.ppermute(value, axis, [(order[i], order[(i + step) % count]) for i in...  90.2 us
    pallas_call x6, Pallas kernels, outer(): pl.pallas_call(outer_kernel, grid=(m // rows, n // cols), in_specs=[pl.Bl...  42.2 us
    pallas_call x1, Pallas kernels, mixer_backward(): pl.pallas_call(functools.partial(backward_kernel, heads, group, steps, le...  27.7 us
    ppermute x17, waiting for transfers between devices, swap(): return lax.ppermute(value, axis, [(i, i ^ bit) for i in range(count)])  26 us
    dot_general x5, matrix products, per_device(): lax.dot_general(a, b, dims, preferred_element_type=F32)  25.8 us
    pallas_call x2, Pallas kernels, normed_back(): pl.pallas_call(functools.partial(normed_back_kernel, len(w_mix), count),...  21.5 us
    pallas_call x4, Pallas kernels, stacked(): pl.pallas_call(functools.partial(stack_kernel, layout), out_shape=jax.Sha...  17.5 us
  transfers between devices with their start and end apart: 110, of which 56 were waited for; matrix products, arithmetic and copies ran while one was open for 9% of the time, Pallas kernels for 32%

profile of v6, /device:TPU:0, one launch (start us, length us, event | category | flops | bytes accessed | tf_op | source)
XLA Modules:
  0.0 544.4 jit_solution(17923685103557002058)
XLA Ops:
  10.3 3.0 collective-permute-start.4
  15.3 10.0 %collective-permute-done.4.refs_1_ = bf16[128,2048]{1,0:T(8,128)(2,1)S(1)} collective-permute-done((bf16[128,2048]{1,0:T(8,128)(2,1)S(1)}, bf16[128,2048]{1,0:T(8,128)(2,1)S(1)}, u32[]{:S(2)}, u32[]{:S(2)}) %collective-permute-start.4) | collective-permute-done | bytes 524320 | tf_op jit(solution)/shard_map/ppermute | solution.py:928
  28.7 10.4 %collective-permute-done.6.refs_3_ = bf16[128,2048]{1,0:T(8,128)(2,1)S(1)} collective-permute-done((bf16[128,2048]{1,0:T(8,128)(2,1)S(1)}, bf16[128,2048]{1,0:T(8,128)(2,1)S(1)}, u32[]{:S(2)}, u32[]{:S(2)}) %collective-permute-start.6) | collective-permute-done | bytes 524320 | tf_op jit(solution)/shard_map/ppermute | solution.py:928
  42.5 9.2 %collective-permute-done.8.refs_5_ = bf16[128,2048]{1,0:T(8,128)(2,1)S(1)} collective-permute-done((bf16[128,2048]{1,0:T(8,128)(2,1)S(1)}, bf16[128,2048]{1,0:T(8,128)(2,1)S(1)}, u32[]{:S(2)}, u32[]{:S(2)}) %collective-permute-start.8) | collective-permute-done | bytes 524320 | tf_op jit(solution)/shard_map/ppermute | solution.py:928
  59.6 3.4 collective-permute-done.10.refs_7_
  67.8 14.7 %shard_map.237 = (bf16[1024,1536]{1,0:T(8,128)(2,1)}, f32[1024,4]{1,0:T(8,128)}) custom-call(s32[8]{0:T(128)} %get-tuple-element.466.ids_ref, s32[4]{0:T(128)} %iota_xor_fusion.spots_ref, bf16[4,2048]{1,0:T(4,128)(2,1)} %copy-done.41, bf16[128,2048]{1,0:T(8,128)(2,1)} %copy-done.3, bf16[128,2048]{1,0:T(8,128)(2,1)} %copy-done.12, ...), custom_call_target="tpu_custom_call" | custom-call | flops 1 | bytes 1 | tf_op jit(solution)/shard_map/pallas_call | solution.py:672
  88.3 14.4 %shard_map.238 = (f32[1024,512]{1,0:T(8,128)}, bf16[1024,256]{1,0:T(8,128)(2,1)}, bf16[2,8,384,128]{3,2,1,0:T(8,128)(2,1)}, bf16[2,8,128,384]{3,2,1,0:T(8,128)(2...) custom-call(bf16[1024,1536]{1,0:T(8,128)(2,1)} %get-tuple-element.21, ...), custom_call_target="tpu_custom_call" | custom-call | flops 1 | bytes 1 | tf_op jit(solution)/shard_map/pallas_call | solution.py:213
  109.5 5.8 %collective-permute-done.20.refs_2_ = bf16[2,384,128]{2,1,0:T(8,128)(2,1)S(1)} collective-permute-done((bf16[2,384,128]{2,1,0:T(8,128)(2,1)}, bf16[2,384,128]{2,1,0:T(8,128)(2,1)S(1)}, u32[]{:S(2)}, u32[]{:S(2)}) %collective-permute-start.20) | collective-permute-done | bytes 196640 | tf_op jit(solution)/shard_map/ppermute | solution.py:1018
  115.4 3.8 collective-permute-done.21.refs_3_
  122.9 9.7 %shard_map.239 = (bf16[1024,512]{1,0:T(8,128)(2,1)}, bf16[1024,512]{1,0:T(8,128)(2,1)}, bf16[1024,2048]{1,0:T(8,128)(2,1)}, bf16[2,256,128]{2,1,0:T(8,128)(2,1)}) custom-call(s32[8]{0:T(128)} %get-tuple-element.466.ids_ref, s32[1]{0:T(128)} %bitcast.1.place_ref, f32[1,256]{1,0:T(1,128)} %bitcast.41, bf16[512,2048]{1,0:T(8,128)(2,1)} %all-gather.5.cloned.1.call-done.w_ref, ...), custom_call_target="tpu_custom_call" | custom-call | flops 1 | bytes 1 | tf_op jit(solution)/shard_map/pallas_call | solution.py:514
  136.0 4.5 shard_map.240.left_ref.right_ref
  147.2 4.5 shard_map.241.left_ref.refs_9_.refs_10_.refs_11_.refs_15_.refs_16_.refs_17_.refs_18_.refs_19_
  160.6 4.3 collective-permute-done.32
  173.2 3.2 collective-permute-done.36
  183.5 4.7 shard_map.242.right_ref
  188.2 4.4 collective-permute-done.40.refs_2_
  196.7 7.7 %shard_map.243 = f32[1024,704]{1,0:T(8,128)} custom-call(bf16[1024,2048]{1,0:T(8,128)(2,1)} %shard_map.240.left_ref.right_ref, bf16[2048,704]{1,0:T(8,128)(2,1)} %shard_map.242.right_ref), custom_call_target="tpu_custom_call" | custom-call | flops 1 | bytes 1 | tf_op jit(solution)/shard_map/pallas_call | solution.py:884
  210.3 6.1 %shard_map.244 = (bf16[2048,704]{1,0:T(8,128)(2,1)}, bf16[2048,704]{1,0:T(8,128)(2,1)}) custom-call(bf16[704,2048]{1,0:T(8,128)(2,1)} %all-gather.9.cloned.1.call-done.refs_0_, bf16[704,2048]{1,0:T(8,128)(2,1)} %all-gather.11.cloned.1.call-done.refs_1_), custom_call_target="tpu_custom_call" | custom-call | flops 1 | bytes 1 | tf_op jit(solution)/shard_map/pallas_call | solution.py:824
  216.4 3.8 collective-permute-done.44.refs_6_
  224.7 4.2 shard_map.245.buffer_ref
  232.2 6.3 %fusion.28 = f32[1024,704]{1,0:T(8,128)S(1)} fusion(bf16[1024,2048]{1,0:T(8,128)(2,1)} %shard_map.246.right_ref, bf16[2048,704]{1,0:T(8,128)(2,1)} %get-tuple-element.273), kind=kOutput, calls=%fused_computation.108 | convolution fusion | flops 2952790016 | bytes 9961472 | tf_op jit(solution)/shard_map/dot_general | solution.py:1074
  238.6 5.7 %multiply_convert_fusion = (bf16[1024,704]{1,0:T(8,128)(2,1)S(1)}, bf16[1024,704]{1,0:T(8,128)(2,1)S(1)}, bf16[1024,704]{1,0:T(8,128)(2,1)}) fusion(f32[1024,704]{1,0:T(8,128)S(1)} %copy-done.8, f32[1024,704]{1,0:T(8,128)S(1)} %fusion.28, bf16[1024,2048]{1,0:T(8,128)(2,1)S(1)} %copy-done, bf16[2048,704]{1,0:T(8,128)(2,1)S(1)} %copy-done.66), kind=kOutput, calls=%fused_computation.2 | convolution fusion | flops 2963603456 | bytes 17170432 | tf_op jit(solution)/shard_map/dot_general | solution.py:1074
  244.2 3.4 fusion.29
  247.7 3.7 add_convert_fusion
  255.5 7.1 %shard_map.247 = bf16[704,2048]{1,0:T(8,128)(2,1)} custom-call(bf16[1024,704]{1,0:T(8,128)(2,1)} %get-tuple-element.295.left_ref, bf16[1024,2048]{1,0:T(8,128)(2,1)} %shard_map.240.left_ref.right_ref), custom_call_target="tpu_custom_call" | custom-call | flops 1 | bytes 1 | tf_op jit(solution)/shard_map/pallas_call | solution.py:802
  268.3 7.3 %shard_map.248 = bf16[704,2048]{1,0:T(8,128)(2,1)} custom-call(bf16[1024,704]{1,0:T(8,128)(2,1)} %copy-done.21, bf16[1024,2048]{1,0:T(8,128)(2,1)} %shard_map.246.right_ref), custom_call_target="tpu_custom_call" | custom-call | flops 1 | bytes 1 | tf_op jit(solution)/shard_map/pallas_call | solution.py:802
  281.5 2.9 collective-permute-start.57
  284.4 7.1 %shard_map.249 = bf16[704,2048]{1,0:T(8,128)(2,1)} custom-call(bf16[1024,704]{1,0:T(8,128)(2,1)} %copy-done.20, bf16[1024,2048]{1,0:T(8,128)(2,1)} %shard_map.246.right_ref), custom_call_target="tpu_custom_call" | custom-call | flops 1 | bytes 1 | tf_op jit(solution)/shard_map/pallas_call | solution.py:802
  301.8 6.7 %convolution_convert_fusion = bf16[1024,2048]{1,0:T(8,128)(2,1)} fusion(bf16[1024,704]{1,0:T(8,128)(2,1)S(1)} %copy-done.19, bf16[704,2048]{1,0:T(8,128)(2,1)} %all-gather.7.cloned.1.call-done.refs_0_), kind=kOutput, calls=%fused_computation.1 | convolution fusion | flops 2954887168 | bytes 8519680 | tf_op jit(solution)/shard_map/dot_general | solution.py:1074
  308.6 3.5 collective-permute-done.60
  314.7 3.4 collective-permute-start.62
  318.1 8.5 %collective-permute-done.62.refs_2_ = bf16[128,2048]{1,0:T(8,128)(2,1)S(1)} collective-permute-done((bf16[128,2048]{1,0:T(8,128)(2,1)S(1)}, bf16[128,2048]{1,0:T(8,128)(2,1)S(1)}, u32[]{:S(2)}, u32[]{:S(2)}) %collective-permute-start.62) | collective-permute-done | bytes 524320 | tf_op jit(solution)/shard_map/ppermute | solution.py:928
  330.7 8.3 %collective-permute-done.64.refs_4_ = bf16[128,2048]{1,0:T(8,128)(2,1)S(1)} collective-permute-done((bf16[128,2048]{1,0:T(8,128)(2,1)S(1)}, bf16[128,2048]{1,0:T(8,128)(2,1)S(1)}, u32[]{:S(2)}, u32[]{:S(2)}) %collective-permute-start.64) | collective-permute-done | bytes 524320 | tf_op jit(solution)/shard_map/ppermute | solution.py:928
  342.4 8.2 %collective-permute-done.66.refs_6_ = bf16[128,2048]{1,0:T(8,128)(2,1)S(1)} collective-permute-done((bf16[128,2048]{1,0:T(8,128)(2,1)}, bf16[128,2048]{1,0:T(8,128)(2,1)S(1)}, u32[]{:S(2)}, u32[]{:S(2)}) %collective-permute-start.66) | collective-permute-done | bytes 524320 | tf_op jit(solution)/shard_map/ppermute | solution.py:928
  356.3 4.2 shard_map.250.buffer_ref
  364.3 10.1 %shard_map.252 = (bf16[1024,512]{1,0:T(8,128)(2,1)}, bf16[1024,512]{1,0:T(8,128)(2,1)}, f32[1,256]{1,0:T(1,128)}, bf16[2,256,128]{2,1,0:T(8,128)(2,1)}) custom-call(s32[8]{0:T(128)} %get-tuple-element.466.ids_ref, bf16[1024,2048]{1,0:T(8,128)(2,1)} %shard_map.251.branch_ref.right_ref, f32[1,256]{1,0:T(1,128)} %bitcast.42, ...), custom_call_target="tpu_custom_call" | custom-call | flops 1 | bytes 1 | tf_op jit(solution)/shard_map/pallas_call | solution.py:592
  380.2 4.5 collective-permute-done.73.refs_6_
  386.2 6.2 %shard_map.253 = bf16[2048,512]{1,0:T(8,128)(2,1)} custom-call(bf16[1024,2048]{1,0:T(8,128)(2,1)} %shard_map.241.left_ref.refs_9_.refs_10_.refs_11_.refs_15_.refs_16_.refs_17_.refs_18_.refs_19_, bf16[1024,512]{1,0:T(8,128)(2,1)} %get-tuple-element.326.right_ref.refs_3_.refs_4_.refs_5_.refs_6_.refs_7_.refs_8_.refs_9_), custom_call_target="tpu_custom_call" | custom-call | flops 1 | bytes 1 | tf_op jit(solution)/shard_map/pallas_call | solution.py:802
  398.6 27.7 %shard_map.254 = (bf16[1024,1024]{1,0:T(8,128)(2,1)}, f32[1024,4]{1,0:T(8,128)}, f32[8,1024]{1,0:T(8,128)}, f32[16,1024]{1,0:T(8,128)}, f32[8,1024]{1,0:T(8,128)}) custom-call(bf16[1024,1536]{1,0:T(8,128)(2,1)} %get-tuple-element.211.proj_ref.prev_ref.refs_8_.refs_9_.refs_10_.refs_11_.refs_4_.refs_5_.refs_6_.refs_7_, ...), custom_call_target="tpu_custom_call" | custom-call | flops 1 | bytes 1 | tf_op jit(solution)/shard_map/pallas_call | solution.py:407
  431.1 8.5 %shard_map.255 = bf16[2048,1024]{1,0:T(8,128)(2,1)} custom-call(bf16[1024,2048]{1,0:T(8,128)(2,1)} %shard_map.241.left_ref.refs_9_.refs_10_.refs_11_.refs_15_.refs_16_.refs_17_.refs_18_.refs_19_, bf16[1024,1024]{1,0:T(8,128)(2,1)} %fusion.20.right_ref.refs_0_.refs_1_.refs_2_.refs_3_.refs_4_), custom_call_target="tpu_custom_call" | custom-call | flops 1 | bytes 1 | tf_op jit(solution)/shard_map/pallas_call | solution.py:802
  442.4 9.6 %shard_map.256 = (bf16[384,2048]{1,0:T(8,128)(2,1)}, f32[8,2048]{1,0:T(8,128)}) custom-call(s32[4]{0:T(128)} %iota_xor_fusion.spots_ref, bf16[1024,1024]{1,0:T(8,128)(2,1)} %fusion.20.right_ref.refs_0_.refs_1_.refs_2_.refs_3_.refs_4_, bf16[1024,1024]{1,0:T(8,128)(2,1)} %fusion.20.right_ref.refs_0_.refs_1_.refs_2_.refs_3_.refs_4_, ...), custom_call_target="tpu_custom_call" | custom-call | flops 1 | bytes 1 | tf_op jit(solution)/shard_map/pallas_call | solution.py:722
  458.1 12.0 %shard_map.257 = (bf16[640,2048]{1,0:T(8,128)(2,1)}, f32[8,2048]{1,0:T(8,128)}) custom-call(s32[4]{0:T(128)} %iota_xor_fusion.spots_ref, bf16[1024,1024]{1,0:T(8,128)(2,1)} %fusion.20.right_ref.refs_0_.refs_1_.refs_2_.refs_3_.refs_4_, bf16[1024,1024]{1,0:T(8,128)(2,1)} %fusion.20.right_ref.refs_0_.refs_1_.refs_2_.refs_3_.refs_4_, ...), custom_call_target="tpu_custom_call" | custom-call | flops 1 | bytes 1 | tf_op jit(solution)/shard_map/pallas_call | solution.py:722
  472.1 6.1 %shard_map.258 = bf16[512,2048]{1,0:T(8,128)(2,1)} custom-call(bf16[1024,512]{1,0:T(8,128)(2,1)} %get-tuple-element.359.left_ref, bf16[1024,2048]{1,0:T(8,128)(2,1)} %shard_map.251.branch_ref.right_ref), custom_call_target="tpu_custom_call" | custom-call | flops 1 | bytes 1 | tf_op jit(solution)/shard_map/pallas_call | solution.py:802
  483.3 4.3 collective-permute-done.83
  489.4 3.5 collective-permute-done.85
  507.4 4.2 collective-permute-done.97
  511.7 3.8 collective-permute-done.98
  527.9 5.9 %shard_map.259 = (f32[512,1536]{1,0:T(8,128)}, f32[512,512]{1,0:T(8,128)}, f32[704,512]{1,0:T(8,128)}, f32[704,512]{1,0:T(8,128)}, f32[704,512]{1,0:T(8,128)}) custom-call(bf16[512,1024]{1,0:T(8,128)(2,1)} %reduce-scatter.15.cloned.1.call-done.mix_ref, bf16[512,512]{1,0:T(8,128)(2,1)} %reduce-scatter.11.cloned.1.call-done.gate_ref, ...), custom_call_target="tpu_custom_call" | custom-call | flops 1 | bytes 1 | tf_op jit(solution)/shard_map/pallas_call | solution.py:909
  (418 shorter events, 203.9 us)
Async XLA Ops:
  7.2 115.7 %all-gather.5.cloned.1.call-start = ((), (), s32[]{:S(2)}) async-start(), calls=%async_computation.6 | async-start | bytes 2621440 | tf_op jit(solution)/shard_map/all_gather | solution.py:1129
  10.3 15.0 %collective-permute-start.4 = (bf16[128,2048]{1,0:T(8,128)(2,1)S(1)}, bf16[128,2048]{1,0:T(8,128)(2,1)S(1)}, u32[]{:S(2)}, u32[]{:S(2)}) collective-permute-start(bf16[128,2048]{1,0:T(8,128)(2,1)S(1)} %fusion.4.refs_0_), channel_id=1, source_target_pairs={{0,1},{2,0},{4,2},{6,4},{7,6},{5,7},{3,5},{1,3},{8,9},{10,8},{12,1... | collective-permute-start | bytes 1572872 | tf_op jit(solution)/shard_map/ppermute | solution.py:928
  13.3 13.4 %collective-permute-start.5 = (bf16[128,2048]{1,0:T(8,128)(2,1)S(1)}, bf16[128,2048]{1,0:T(8,128)(2,1)S(1)}, u32[]{:S(2)}, u32[]{:S(2)}) collective-permute-start(bf16[128,2048]{1,0:T(8,128)(2,1)S(1)} %fusion.4.refs_0_), channel_id=1, source_target_pairs={{0,2},{2,4},{4,6},{6,7},{7,5},{5,3},{3,1},{1,0},{8,10},{10,12},{12... | collective-permute-start | bytes 1572872 | tf_op jit(solution)/shard_map/ppermute | solution.py:928
  13.4 39.6 %collective-permute-start = (bf16[512,1536]{1,0:T(8,128)(2,1)}, bf16[512,1536]{1,0:T(8,128)(2,1)S(1)}, u32[]{:S(2)}, u32[]{:S(2)}) collective-permute-start(bf16[512,1536]{1,0:T(8,128)(2,1)} %refs_22_.1), channel_id=1, source_target_pairs={{0,16},{8,24},{16,0},{24,8},{1,17},{9,25},{17,1},{25,9},{2,18},{10... | collective-permute-start | bytes 4718600 | tf_op jit(solution)/shard_map/ppermute | solution.py:1018
  26.7 12.5 %collective-permute-start.6 = (bf16[128,2048]{1,0:T(8,128)(2,1)S(1)}, bf16[128,2048]{1,0:T(8,128)(2,1)S(1)}, u32[]{:S(2)}, u32[]{:S(2)}) collective-permute-start(bf16[128,2048]{1,0:T(8,128)(2,1)S(1)} %collective-permute-done.4.refs_1_), channel_id=1, source_target_pairs={{0,1},{2,0},{4,2},{6,4},{7,6},{5,7},{3,5},{1,3},{8,9},{10,8},{12,1... | collective-permute-start | bytes 1572872 | tf_op jit(solution)/shard_map/ppermute | solution.py:928
  28.3 12.2 %collective-permute-start.7 = (bf16[128,2048]{1,0:T(8,128)(2,1)S(1)}, bf16[128,2048]{1,0:T(8,128)(2,1)S(1)}, u32[]{:S(2)}, u32[]{:S(2)}) collective-permute-start(bf16[128,2048]{1,0:T(8,128)(2,1)S(1)} %collective-permute-done.5.refs_2_), channel_id=1, source_target_pairs={{0,2},{2,4},{4,6},{6,7},{7,5},{5,3},{3,1},{1,0},{8,10},{10,12},{12... | collective-permute-start | bytes 1572872 | tf_op jit(solution)/shard_map/ppermute | solution.py:928
  42.5 15.5 %collective-permute-start.12 = (bf16[512,1536]{1,0:T(8,128)(2,1)}, bf16[512,1536]{1,0:T(8,128)(2,1)}, u32[]{:S(2)}, u32[]{:S(2)}) collective-permute-start(bf16[512,1536]{1,0:T(8,128)(2,1)} %refs_22_.1), channel_id=1, source_target_pairs={{0,8},{8,0},{16,24},{24,16},{1,9},{9,1},{17,25},{25,17},{2,10},{10... | collective-permute-start | bytes 4718600 | tf_op jit(solution)/shard_map/ppermute | solution.py:1018
  53.2 130.4 %all-gather.7.cloned.1.call-start = ((), (), s32[]{:S(2)}) async-start(), calls=%async_computation.7 | async-start | bytes 3604480 | tf_op jit(solution)/shard_map/all_gather | solution.py:1159
  53.2 13.9 %collective-permute-start.1 = (bf16[4,512]{1,0:T(4,128)(2,1)}, bf16[4,512]{1,0:T(4,128)(2,1)S(1)}, u32[]{:S(2)}, u32[]{:S(2)}) collective-permute-start(bf16[4,512]{1,0:T(4,128)(2,1)} %bitcast.43), channel_id=1, source_target_pairs={{0,8},{8,0},{16,24},{24,16},{1,9},{9,1},{17,25},{25,17},{2,10},{10... | collective-permute-start | bytes 12296 | tf_op jit(solution)/shard_map/ppermute | solution.py:1018
  63.9 18.5 %collective-permute-start.14 = (bf16[128,2048]{1,0:T(8,128)(2,1)}, bf16[128,2048]{1,0:T(8,128)(2,1)}, u32[]{:S(2)}, u32[]{:S(2)}) collective-permute-start(bf16[128,2048]{1,0:T(8,128)(2,1)} %refs_0_), channel_id=1, source_target_pairs={{0,2},{2,4},{4,6},{6,7},{7,5},{5,3},{3,1},{1,0},{8,10},{10,12},{12... | collective-permute-start | bytes 1572872 | tf_op jit(solution)/shard_map/ppermute | solution.py:928
  64.4 18.1 %collective-permute-start.15 = (bf16[128,2048]{1,0:T(8,128)(2,1)}, bf16[128,2048]{1,0:T(8,128)(2,1)}, u32[]{:S(2)}, u32[]{:S(2)}) collective-permute-start(bf16[128,2048]{1,0:T(8,128)(2,1)} %refs_0_), channel_id=1, source_target_pairs={{0,1},{2,0},{4,2},{6,4},{7,6},{5,7},{3,5},{1,3},{8,9},{10,8},{12,1... | collective-permute-start | bytes 1572872 | tf_op jit(solution)/shard_map/ppermute | solution.py:928
  82.5 20.2 %collective-permute-start.17 = (bf16[128,2048]{1,0:T(8,128)(2,1)}, bf16[128,2048]{1,0:T(8,128)(2,1)S(1)}, u32[]{:S(2)}, u32[]{:S(2)}) collective-permute-start(bf16[128,2048]{1,0:T(8,128)(2,1)} %collective-permute-done.14.refs_2_), channel_id=1, source_target_pairs={{0,2},{2,4},{4,6},{6,7},{7,5},{5,3},{3,1},{1,0},{8,10},{10,12},{12... | collective-permute-start | bytes 1572872 | tf_op jit(solution)/shard_map/ppermute | solution.py:928
  83.0 19.7 %collective-permute-start.18 = (bf16[128,2048]{1,0:T(8,128)(2,1)}, bf16[128,2048]{1,0:T(8,128)(2,1)S(1)}, u32[]{:S(2)}, u32[]{:S(2)}) collective-permute-start(bf16[128,2048]{1,0:T(8,128)(2,1)} %collective-permute-done.15.refs_1_), channel_id=1, source_target_pairs={{0,1},{2,0},{4,2},{6,4},{7,6},{5,7},{3,5},{1,3},{8,9},{10,8},{12,1... | collective-permute-start | bytes 1572872 | tf_op jit(solution)/shard_map/ppermute | solution.py:928
  102.7 16.5 %collective-permute-start.22 = (bf16[128,2048]{1,0:T(8,128)(2,1)S(1)}, bf16[128,2048]{1,0:T(8,128)(2,1)S(1)}, u32[]{:S(2)}, u32[]{:S(2)}) collective-permute-start(bf16[128,2048]{1,0:T(8,128)(2,1)S(1)} %collective-permute-done.17.refs_4_), channel_id=1, source_target_pairs={{0,2},{2,4},{4,6},{6,7},{7,5},{5,3},{3,1},{1,0},{8,10},{10,12},{12... | collective-permute-start | bytes 1572872 | tf_op jit(solution)/shard_map/ppermute | solution.py:928
  103.2 16.0 %collective-permute-start.23 = (bf16[128,2048]{1,0:T(8,128)(2,1)S(1)}, bf16[128,2048]{1,0:T(8,128)(2,1)S(1)}, u32[]{:S(2)}, u32[]{:S(2)}) collective-permute-start(bf16[128,2048]{1,0:T(8,128)(2,1)S(1)} %collective-permute-done.18.refs_3_), channel_id=1, source_target_pairs={{0,1},{2,0},{4,2},{6,4},{7,6},{5,7},{3,5},{1,3},{8,9},{10,8},{12,1... | collective-permute-start | bytes 1572872 | tf_op jit(solution)/shard_map/ppermute | solution.py:928
  119.3 91.0 %all-gather.9.cloned.1.call-start = ((), (), s32[]{:S(2)}) async-start(), calls=%async_computation.8 | async-start | bytes 3604480 | tf_op jit(solution)/shard_map/all_gather | solution.py:1159
  120.0 90.3 %all-gather.11.cloned.1.call-start = ((), (), s32[]{:S(2)}) async-start(), calls=%async_computation.9 | async-start | bytes 3604480 | tf_op jit(solution)/shard_map/all_gather | solution.py:1159
  120.1 12.5 %collective-permute-start.24 = (bf16[64,2048]{1,0:T(8,128)(2,1)S(1)}, bf16[64,2048]{1,0:T(8,128)(2,1)S(1)}, u32[]{:S(2)}, u32[]{:S(2)}) collective-permute-start(bf16[64,2048]{1,0:T(8,128)(2,1)S(1)} %slice.262), channel_id=1, source_target_pairs={{0,2},{2,4},{4,6},{6,7},{7,5},{5,3},{3,1},{1,0},{8,10},{10,12},{12... | collective-permute-start | bytes 786440 | tf_op jit(solution)/shard_map/ppermute | solution.py:928
  147.2 193.2 %reduce-scatter.7.cloned.1.call-start = ((), (), s32[]{:S(2)}) async-start(), calls=%async_computation.10 | async-start | bytes 3604480 | tf_op jit(solution)/shard_map/reduce_scatter | solution.py:1202
  194.3 11.9 %collective-permute-start.42 = (bf16[128,2048]{1,0:T(8,128)(2,1)S(1)}, bf16[128,2048]{1,0:T(8,128)(2,1)}, u32[]{:S(2)}, u32[]{:S(2)}) collective-permute-start(bf16[128,2048]{1,0:T(8,128)(2,1)S(1)} %collective-permute-done.40.refs_2_), channel_id=1, source_target_pairs={{0,2},{2,4},{4,6},{6,7},{7,5},{5,3},{3,1},{1,0},{8,10},{10,12},{12... | collective-permute-start | bytes 1572872 | tf_op jit(solution)/shard_map/ppermute | solution.py:928
  194.8 13.2 %collective-permute-start.43 = (bf16[128,2048]{1,0:T(8,128)(2,1)S(1)}, bf16[128,2048]{1,0:T(8,128)(2,1)}, u32[]{:S(2)}, u32[]{:S(2)}) collective-permute-start(bf16[128,2048]{1,0:T(8,128)(2,1)S(1)} %collective-permute-done.41.refs_1_), channel_id=1, source_target_pairs={{0,1},{2,0},{4,2},{6,4},{7,6},{5,7},{3,5},{1,3},{8,9},{10,8},{12,1... | collective-permute-start | bytes 1572872 | tf_op jit(solution)/shard_map/ppermute | solution.py:928
  208.0 12.2 %collective-permute-start.44 = (bf16[128,2048]{1,0:T(8,128)(2,1)}, bf16[128,2048]{1,0:T(8,128)(2,1)S(1)}, u32[]{:S(2)}, u32[]{:S(2)}) collective-permute-start(bf16[128,2048]{1,0:T(8,128)(2,1)} %collective-permute-done.42.refs_4_), channel_id=1, source_target_pairs={{0,2},{2,4},{4,6},{6,7},{7,5},{5,3},{3,1},{1,0},{8,10},{10,12},{12... | collective-permute-start | bytes 1572872 | tf_op jit(solution)/shard_map/ppermute | solution.py:928
  210.3 12.2 %collective-permute-start.45 = (bf16[128,2048]{1,0:T(8,128)(2,1)}, bf16[128,2048]{1,0:T(8,128)(2,1)S(1)}, u32[]{:S(2)}, u32[]{:S(2)}) collective-permute-start(bf16[128,2048]{1,0:T(8,128)(2,1)} %collective-permute-done.43.refs_3_), channel_id=1, source_target_pairs={{0,1},{2,0},{4,2},{6,4},{7,6},{5,7},{3,5},{1,3},{8,9},{10,8},{12,1... | collective-permute-start | bytes 1572872 | tf_op jit(solution)/shard_map/ppermute | solution.py:928
  264.1 96.4 %reduce-scatter.9.cloned.1.call-start = ((), (), s32[]{:S(2)}) async-start(), calls=%async_computation.11 | async-start | bytes 3604480 | tf_op jit(solution)/shard_map/reduce_scatter | solution.py:1202
  278.8 151.7 %reduce-scatter.13.cloned.1.call-start = ((), (), s32[]{:S(2)}) async-start(), calls=%async_computation.13 | async-start | bytes 3604480 | tf_op jit(solution)/shard_map/reduce_scatter | solution.py:1202
  278.8 12.7 %collective-permute-start.54 = (bf16[64,2048]{1,0:T(8,128)(2,1)}, bf16[64,2048]{1,0:T(8,128)(2,1)}, u32[]{:S(2)}, u32[]{:S(2)}) collective-permute-start(bf16[64,2048]{1,0:T(8,128)(2,1)} %get-tuple-element.420), channel_id=1, source_target_pairs={{0,2},{2,4},{4,6},{6,7},{7,5},{5,3},{3,1},{1,0},{8,10},{10,12},{12... | collective-permute-start | bytes 786440 | tf_op jit(solution)/shard_map/ppermute | solution.py:928
  279.0 12.5 %collective-permute-start.55 = (bf16[64,2048]{1,0:T(8,128)(2,1)}, bf16[64,2048]{1,0:T(8,128)(2,1)}, u32[]{:S(2)}, u32[]{:S(2)}) collective-permute-start(bf16[64,2048]{1,0:T(8,128)(2,1)} %get-tuple-element.419), channel_id=1, source_target_pairs={{0,1},{2,0},{4,2},{6,4},{7,6},{5,7},{3,5},{1,3},{8,9},{10,8},{12,1... | collective-permute-start | bytes 786440 | tf_op jit(solution)/shard_map/ppermute | solution.py:928
  295.4 135.0 %reduce-scatter.11.cloned.1.call-start = ((), (), s32[]{:S(2)}) async-start(), calls=%async_computation.12 | async-start | bytes 2621440 | tf_op jit(solution)/shard_map/reduce_scatter | solution.py:1268
  295.5 13.1 %collective-permute-start.58 = (bf16[64,2048]{1,0:T(8,128)(2,1)}, bf16[64,2048]{1,0:T(8,128)(2,1)S(1)}, u32[]{:S(2)}, u32[]{:S(2)}) collective-permute-start(bf16[64,2048]{1,0:T(8,128)(2,1)} %get-tuple-element.416), channel_id=1, source_target_pairs={{0,2},{2,4},{4,6},{6,7},{7,5},{5,3},{3,1},{1,0},{8,10},{10,12},{12... | collective-permute-start | bytes 786440 | tf_op jit(solution)/shard_map/ppermute | solution.py:928
  299.5 12.6 %collective-permute-start.60 = (bf16[64,2048]{1,0:T(8,128)(2,1)}, bf16[64,2048]{1,0:T(8,128)(2,1)S(1)}, u32[]{:S(2)}, u32[]{:S(2)}) collective-permute-start(bf16[64,2048]{1,0:T(8,128)(2,1)} %get-tuple-element.414), channel_id=1, source_target_pairs={{0,2},{2,4},{4,6},{6,7},{7,5},{5,3},{3,1},{1,0},{8,10},{10,12},{12... | collective-permute-start | bytes 786440 | tf_op jit(solution)/shard_map/ppermute | solution.py:928
  299.5 12.7 %collective-permute-start.61 = (bf16[64,2048]{1,0:T(8,128)(2,1)S(1)}, bf16[64,2048]{1,0:T(8,128)(2,1)S(1)}, u32[]{:S(2)}, u32[]{:S(2)}) collective-permute-start(bf16[64,2048]{1,0:T(8,128)(2,1)S(1)} %get-tuple-element.413), channel_id=1, source_target_pairs={{0,1},{2,0},{4,2},{6,4},{7,6},{5,7},{3,5},{1,3},{8,9},{10,8},{12,1... | collective-permute-start | bytes 786440 | tf_op jit(solution)/shard_map/ppermute | solution.py:928
  314.7 11.9 %collective-permute-start.62 = (bf16[128,2048]{1,0:T(8,128)(2,1)S(1)}, bf16[128,2048]{1,0:T(8,128)(2,1)S(1)}, u32[]{:S(2)}, u32[]{:S(2)}) collective-permute-start(bf16[128,2048]{1,0:T(8,128)(2,1)S(1)} %get-tuple-element.311.refs_0_), channel_id=1, source_target_pairs={{0,2},{2,4},{4,6},{6,7},{7,5},{5,3},{3,1},{1,0},{8,10},{10,12},{12... | collective-permute-start | bytes 1572872 | tf_op jit(solution)/shard_map/ppermute | solution.py:928
  376.6 15.9 %collective-permute-start.72 = (bf16[128,2048]{1,0:T(8,128)(2,1)}, bf16[128,2048]{1,0:T(8,128)(2,1)}, u32[]{:S(2)}, u32[]{:S(2)}) collective-permute-start(bf16[128,2048]{1,0:T(8,128)(2,1)} %get-tuple-element.324), channel_id=1, source_target_pairs={{0,2},{2,4},{4,6},{6,7},{7,5},{5,3},{3,1},{1,0},{8,10},{10,12},{12... | collective-permute-start | bytes 1572872 | tf_op jit(solution)/shard_map/ppermute | solution.py:928
  377.7 14.7 %collective-permute-start.75 = (bf16[128,2048]{1,0:T(8,128)(2,1)S(1)}, bf16[128,2048]{1,0:T(8,128)(2,1)}, u32[]{:S(2)}, u32[]{:S(2)}) collective-permute-start(bf16[128,2048]{1,0:T(8,128)(2,1)S(1)} %get-tuple-element.327), channel_id=1, source_target_pairs={{0,1},{2,0},{4,2},{6,4},{7,6},{5,7},{3,5},{1,3},{8,9},{10,8},{12,1... | collective-permute-start | bytes 1572872 | tf_op jit(solution)/shard_map/ppermute | solution.py:928
  392.5 128.5 %reduce-scatter.15.cloned.1.call-start = ((), (), s32[]{:S(2)}) async-start(), calls=%async_computation.14 | async-start | bytes 5242880 | tf_op jit(solution)/shard_map/reduce_scatter | solution.py:1285
  395.1 32.9 %collective-permute-start.76 = (bf16[128,2048]{1,0:T(8,128)(2,1)}, bf16[128,2048]{1,0:T(8,128)(2,1)S(1)}, u32[]{:S(2)}, u32[]{:S(2)}) collective-permute-start(bf16[128,2048]{1,0:T(8,128)(2,1)} %get-tuple-element.329), channel_id=1, source_target_pairs={{0,2},{2,4},{4,6},{6,7},{7,5},{5,3},{3,1},{1,0},{8,10},{10,12},{12... | collective-permute-start | bytes 1572872 | tf_op jit(solution)/shard_map/ppermute | solution.py:928
  396.6 31.5 %collective-permute-start.77 = (bf16[128,2048]{1,0:T(8,128)(2,1)}, bf16[128,2048]{1,0:T(8,128)(2,1)}, u32[]{:S(2)}, u32[]{:S(2)}) collective-permute-start(bf16[128,2048]{1,0:T(8,128)(2,1)} %get-tuple-element.340), channel_id=1, source_target_pairs={{0,1},{2,0},{4,2},{6,4},{7,6},{5,7},{3,5},{1,3},{8,9},{10,8},{12,1... | collective-permute-start | bytes 1572872 | tf_op jit(solution)/shard_map/ppermute | solution.py:928
  439.6 88.3 %reduce-scatter.17.cloned.1.call-start = ((), (), s32[]{:S(2)}) async-start(), calls=%async_computation.15 | async-start | bytes 2621440 | tf_op jit(solution)/shard_map/reduce_scatter | solution.py:1202
  439.7 14.3 %collective-permute-start.79 = (bf16[128,2048]{1,0:T(8,128)(2,1)}, bf16[128,2048]{1,0:T(8,128)(2,1)S(1)}, u32[]{:S(2)}, u32[]{:S(2)}) collective-permute-start(bf16[128,2048]{1,0:T(8,128)(2,1)} %get-tuple-element.343), channel_id=1, source_target_pairs={{0,1},{2,0},{4,2},{6,4},{7,6},{5,7},{3,5},{1,3},{8,9},{10,8},{12,1... | collective-permute-start | bytes 1572872 | tf_op jit(solution)/shard_map/ppermute | solution.py:928
  440.2 14.5 %collective-permute-start.78 = (bf16[128,2048]{1,0:T(8,128)(2,1)}, bf16[128,2048]{1,0:T(8,128)(2,1)S(1)}, u32[]{:S(2)}, u32[]{:S(2)}) collective-permute-start(bf16[128,2048]{1,0:T(8,128)(2,1)} %get-tuple-element.342), channel_id=1, source_target_pairs={{0,2},{2,4},{4,6},{6,7},{7,5},{5,3},{3,1},{1,0},{8,10},{10,12},{12... | collective-permute-start | bytes 1572872 | tf_op jit(solution)/shard_map/ppermute | solution.py:928
  456.0 14.1 %collective-permute-start.81 = (bf16[64,2048]{1,0:T(8,128)(2,1)S(1)}, bf16[64,2048]{1,0:T(8,128)(2,1)S(1)}, u32[]{:S(2)}, u32[]{:S(2)}) collective-permute-start(bf16[64,2048]{1,0:T(8,128)(2,1)S(1)} %get-tuple-element.458), channel_id=1, source_target_pairs={{0,2},{2,4},{4,6},{6,7},{7,5},{5,3},{3,1},{1,0},{8,10},{10,12},{12... | collective-permute-start | bytes 786440 | tf_op jit(solution)/shard_map/ppermute | solution.py:928
  457.6 12.5 %collective-permute-start.82 = (bf16[64,2048]{1,0:T(8,128)(2,1)S(1)}, bf16[64,2048]{1,0:T(8,128)(2,1)S(1)}, u32[]{:S(2)}, u32[]{:S(2)}) collective-permute-start(bf16[64,2048]{1,0:T(8,128)(2,1)S(1)} %get-tuple-element.457), channel_id=1, source_target_pairs={{0,1},{2,0},{4,2},{6,4},{7,6},{5,7},{3,5},{1,3},{8,9},{10,8},{12,1... | collective-permute-start | bytes 786440 | tf_op jit(solution)/shard_map/ppermute | solution.py:928
  480.3 12.5 %collective-permute-start.85 = (bf16[64,2048]{1,0:T(8,128)(2,1)}, bf16[64,2048]{1,0:T(8,128)(2,1)S(1)}, u32[]{:S(2)}, u32[]{:S(2)}) collective-permute-start(bf16[64,2048]{1,0:T(8,128)(2,1)} %get-tuple-element.454), channel_id=1, source_target_pairs={{0,2},{2,4},{4,6},{6,7},{7,5},{5,3},{3,1},{1,0},{8,10},{10,12},{12... | collective-permute-start | bytes 786440 | tf_op jit(solution)/shard_map/ppermute | solution.py:928
  482.0 12.2 %collective-permute-start.86 = (bf16[64,2048]{1,0:T(8,128)(2,1)}, bf16[64,2048]{1,0:T(8,128)(2,1)S(1)}, u32[]{:S(2)}, u32[]{:S(2)}) collective-permute-start(bf16[64,2048]{1,0:T(8,128)(2,1)} %get-tuple-element.453), channel_id=1, source_target_pairs={{0,1},{2,0},{4,2},{6,4},{7,6},{5,7},{3,5},{1,3},{8,9},{10,8},{12,1... | collective-permute-start | bytes 786440 | tf_op jit(solution)/shard_map/ppermute | solution.py:928
  498.0 22.9 %collective-permute-start.88 = (bf16[64,2048]{1,0:T(8,128)(2,1)}, bf16[64,2048]{1,0:T(8,128)(2,1)}, u32[]{:S(2)}, u32[]{:S(2)}) collective-permute-start(bf16[64,2048]{1,0:T(8,128)(2,1)} %get-tuple-element.452), channel_id=1, source_target_pairs={{0,2},{2,4},{4,6},{6,7},{7,5},{5,3},{3,1},{1,0},{8,10},{10,12},{12... | collective-permute-start | bytes 786440 | tf_op jit(solution)/shard_map/ppermute | solution.py:928
  499.4 21.5 %collective-permute-start.89 = (bf16[64,2048]{1,0:T(8,128)(2,1)}, bf16[64,2048]{1,0:T(8,128)(2,1)}, u32[]{:S(2)}, u32[]{:S(2)}) collective-permute-start(bf16[64,2048]{1,0:T(8,128)(2,1)} %get-tuple-element.451), channel_id=1, source_target_pairs={{0,1},{2,0},{4,2},{6,4},{7,6},{5,7},{3,5},{1,3},{8,9},{10,8},{12,1... | collective-permute-start | bytes 786440 | tf_op jit(solution)/shard_map/ppermute | solution.py:928
  500.1 20.9 %collective-permute-start.90 = (bf16[64,2048]{1,0:T(8,128)(2,1)}, bf16[64,2048]{1,0:T(8,128)(2,1)}, u32[]{:S(2)}, u32[]{:S(2)}) collective-permute-start(bf16[64,2048]{1,0:T(8,128)(2,1)} %get-tuple-element.450), channel_id=1, source_target_pairs={{0,2},{2,4},{4,6},{6,7},{7,5},{5,3},{3,1},{1,0},{8,10},{10,12},{12... | collective-permute-start | bytes 786440 | tf_op jit(solution)/shard_map/ppermute | solution.py:928
  501.4 19.5 %collective-permute-start.91 = (bf16[64,2048]{1,0:T(8,128)(2,1)}, bf16[64,2048]{1,0:T(8,128)(2,1)}, u32[]{:S(2)}, u32[]{:S(2)}) collective-permute-start(bf16[64,2048]{1,0:T(8,128)(2,1)} %get-tuple-element.449), channel_id=1, source_target_pairs={{0,1},{2,0},{4,2},{6,4},{7,6},{5,7},{3,5},{1,3},{8,9},{10,8},{12,1... | collective-permute-start | bytes 786440 | tf_op jit(solution)/shard_map/ppermute | solution.py:928
  (129 other events, 1275.6 us)
Sparse Core Ops, SparseCore 0:
  53.3 21.4 all-gather.4
  119.4 26.6 all-gather.6
  147.7 27.0 all-gather.8
  176.2 27.0 all-gather.10
  264.2 36.8 reduce-scatter.6
  303.7 36.3 reduce-scatter.8
  342.6 36.3 reduce-scatter.12
  392.6 31.6 reduce-scatter.10
  439.7 44.8 reduce-scatter.14
  487.7 31.3 reduce-scatter.16

commit v7 on v6

--- a/solution.py
+++ b/solution.py
@@ -1237,8 +1237,13 @@
     )
 
     grad_down_s, grad_gate_s, grad_up_s = (keep[name, "sum"] for name in ("down", "gate", "up"))
+    def first_output(pin):
+        start = hops * own_rows
+        keep["first"] = pin(lax.slice_in_dim(output_part, start, start + own_rows, axis=0))
+        return [grad_down_s, keep["first"]]
+
     branch_near = ring_gather(
-        grad_residual.astype(BF16), "head", {2: lambda pin: [grad_down_s], 4: lambda pin: [grad_gate_s]}
+        grad_residual.astype(BF16), "head", {2: first_output, 4: lambda pin: [grad_gate_s]}
     )
     take_output = near_rows(output_part, own_rows)
     output_state = [None, None]
@@ -1251,7 +1256,7 @@
                 if hop == 0 and way == 1:
                     here.append(None)
                     continue
-                piece = take_output(k, 0, own_rows)
+                piece = take_output(k, 0, own_rows) if hop else keep["first"]
                 total = piece if output_state[way] is None else output_state[way] + piece
                 here.append(ring_step(after(total, *gates), "head", 1 - 2 * way))
             output_state[:] = here

time: 553 us -> 553 us (level)
  transfers between devices with their start and end apart: 110 -> 110, of which waited for: 56 -> 57; matrix products, arithmetic and copies ran while one was open for 9% -> 9% of each run, Pallas kernels for 32% -> 32%
where the time goes in v7:
time: 553 us; the launch traced here: 544 us
  Pallas kernels  186 us (34%)
  waiting for transfers between devices  155 us (28%)
  starting transfers between devices  106 us (19%)
  other arithmetic  35.1 us (6%)
  matrix products  24.5 us (4%)
  local copies, waits for them, and re-layouts  20.8 us (4%)
  between operations  16.3 us (3%)
    ppermute x81, waiting for transfers between devices, ring_step(): lax.ppermute(value, axis, [(order[i], order[(i + step) % count]) for i in...  127 us
    ppermute x81, starting transfers between devices, ring_step(): lax.ppermute(value, axis, [(order[i], order[(i + step) % count]) for i in...  89.3 us
    pallas_call x6, Pallas kernels, outer(): pl.pallas_call(outer_kernel, grid=(m // rows, n // cols), in_specs=[pl.Bl...  42.4 us
    ppermute x17, waiting for transfers between devices, swap(): return lax.ppermute(value, axis, [(i, i ^ bit) for i in range(count)])  27.6 us
    pallas_call x1, Pallas kernels, mixer_backward(): pl.pallas_call(functools.partial(backward_kernel, heads, group, steps, le...  27.2 us
    dot_general x5, matrix products, per_device(): lax.dot_general(a, b, dims, preferred_element_type=F32)  24.5 us
    pallas_call x2, Pallas kernels, normed_back(): pl.pallas_call(functools.partial(normed_back_kernel, len(w_mix), count),...  22.2 us
    pallas_call x4, Pallas kernels, stacked(): pl.pallas_call(functools.partial(stack_kernel, layout), out_shape=jax.Sha...  17.5 us
  transfers between devices with their start and end apart: 110, of which 57 were waited for; matrix products, arithmetic and copies ran while one was open for 9% of the time, Pallas kernels for 32%

profile of v7, /device:TPU:0, one launch (start us, length us, event | category | flops | bytes accessed | tf_op | source)
XLA Modules:
  0.0 544.4 jit_solution(17144718322324872426)
XLA Ops:
  10.2 3.0 collective-permute-start.4
  15.3 10.0 %collective-permute-done.4.refs_1_ = bf16[128,2048]{1,0:T(8,128)(2,1)S(1)} collective-permute-done((bf16[128,2048]{1,0:T(8,128)(2,1)S(1)}, bf16[128,2048]{1,0:T(8,128)(2,1)S(1)}, u32[]{:S(2)}, u32[]{:S(2)}) %collective-permute-start.4) | collective-permute-done | bytes 524320 | tf_op jit(solution)/shard_map/ppermute | solution.py:928
  28.6 10.4 %collective-permute-done.6.refs_3_ = bf16[128,2048]{1,0:T(8,128)(2,1)S(1)} collective-permute-done((bf16[128,2048]{1,0:T(8,128)(2,1)S(1)}, bf16[128,2048]{1,0:T(8,128)(2,1)S(1)}, u32[]{:S(2)}, u32[]{:S(2)}) %collective-permute-start.6) | collective-permute-done | bytes 524320 | tf_op jit(solution)/shard_map/ppermute | solution.py:928
  42.4 9.2 %collective-permute-done.8.refs_5_ = bf16[128,2048]{1,0:T(8,128)(2,1)S(1)} collective-permute-done((bf16[128,2048]{1,0:T(8,128)(2,1)S(1)}, bf16[128,2048]{1,0:T(8,128)(2,1)S(1)}, u32[]{:S(2)}, u32[]{:S(2)}) %collective-permute-start.8) | collective-permute-done | bytes 524320 | tf_op jit(solution)/shard_map/ppermute | solution.py:928
  59.5 3.4 collective-permute-done.10.refs_7_
  67.7 14.7 %shard_map.237 = (bf16[1024,1536]{1,0:T(8,128)(2,1)}, f32[1024,4]{1,0:T(8,128)}) custom-call(s32[8]{0:T(128)} %get-tuple-element.468.ids_ref, s32[4]{0:T(128)} %iota_xor_fusion.spots_ref, bf16[4,2048]{1,0:T(4,128)(2,1)} %copy-done.42, bf16[128,2048]{1,0:T(8,128)(2,1)} %copy-done.3, bf16[128,2048]{1,0:T(8,128)(2,1)} %copy-done.13, ...), custom_call_target="tpu_custom_call" | custom-call | flops 1 | bytes 1 | tf_op jit(solution)/shard_map/pallas_call | solution.py:672
  88.3 14.4 %shard_map.238 = (f32[1024,512]{1,0:T(8,128)}, bf16[1024,256]{1,0:T(8,128)(2,1)}, bf16[2,8,384,128]{3,2,1,0:T(8,128)(2,1)}, bf16[2,8,128,384]{3,2,1,0:T(8,128)(2...) custom-call(bf16[1024,1536]{1,0:T(8,128)(2,1)} %get-tuple-element.21, ...), custom_call_target="tpu_custom_call" | custom-call | flops 1 | bytes 1 | tf_op jit(solution)/shard_map/pallas_call | solution.py:213
  106.5 2.8 collective-permute-start.20
  109.5 5.8 %collective-permute-done.20.refs_2_ = bf16[2,384,128]{2,1,0:T(8,128)(2,1)S(1)} collective-permute-done((bf16[2,384,128]{2,1,0:T(8,128)(2,1)}, bf16[2,384,128]{2,1,0:T(8,128)(2,1)S(1)}, u32[]{:S(2)}, u32[]{:S(2)}) %collective-permute-start.20) | collective-permute-done | bytes 196640 | tf_op jit(solution)/shard_map/ppermute | solution.py:1018
  115.3 3.8 collective-permute-done.21.refs_3_
  122.8 9.7 %shard_map.239 = (bf16[1024,512]{1,0:T(8,128)(2,1)}, bf16[1024,512]{1,0:T(8,128)(2,1)}, bf16[1024,2048]{1,0:T(8,128)(2,1)}, bf16[2,256,128]{2,1,0:T(8,128)(2,1)}) custom-call(s32[8]{0:T(128)} %get-tuple-element.468.ids_ref, s32[1]{0:T(128)} %bitcast.1.place_ref, f32[1,256]{1,0:T(1,128)} %bitcast.41, bf16[512,2048]{1,0:T(8,128)(2,1)} %all-gather.5.cloned.1.call-done.w_ref, ...), custom_call_target="tpu_custom_call" | custom-call | flops 1 | bytes 1 | tf_op jit(solution)/shard_map/pallas_call | solution.py:514
  135.9 4.5 shard_map.240.left_ref.right_ref
  147.2 4.6 shard_map.241.left_ref.refs_9_.refs_10_.refs_11_.refs_15_.refs_16_.refs_17_.refs_18_.refs_19_
  160.5 4.3 collective-permute-done.32
  173.1 3.2 collective-permute-done.36
  183.4 4.6 shard_map.242.right_ref
  188.0 4.4 collective-permute-done.40.refs_2_
  196.8 7.7 %shard_map.243 = f32[1024,704]{1,0:T(8,128)} custom-call(bf16[1024,2048]{1,0:T(8,128)(2,1)} %shard_map.240.left_ref.right_ref, bf16[2048,704]{1,0:T(8,128)(2,1)} %shard_map.242.right_ref), custom_call_target="tpu_custom_call" | custom-call | flops 1 | bytes 1 | tf_op jit(solution)/shard_map/pallas_call | solution.py:884
  210.2 6.1 %shard_map.244 = (bf16[2048,704]{1,0:T(8,128)(2,1)}, bf16[2048,704]{1,0:T(8,128)(2,1)}) custom-call(bf16[704,2048]{1,0:T(8,128)(2,1)} %all-gather.9.cloned.1.call-done.refs_0_, bf16[704,2048]{1,0:T(8,128)(2,1)} %all-gather.11.cloned.1.call-done.refs_1_), custom_call_target="tpu_custom_call" | custom-call | flops 1 | bytes 1 | tf_op jit(solution)/shard_map/pallas_call | solution.py:824
  216.2 3.8 collective-permute-done.44.refs_6_
  224.5 4.3 shard_map.245.buffer_ref
  232.1 6.3 %fusion.28 = f32[1024,704]{1,0:T(8,128)S(1)} fusion(bf16[1024,2048]{1,0:T(8,128)(2,1)} %shard_map.246.right_ref, bf16[2048,704]{1,0:T(8,128)(2,1)} %get-tuple-element.274), kind=kOutput, calls=%fused_computation.108 | convolution fusion | flops 2952790016 | bytes 9961472 | tf_op jit(solution)/shard_map/dot_general | solution.py:1074
  238.4 5.7 %multiply_convert_fusion = (bf16[1024,704]{1,0:T(8,128)(2,1)S(1)}, bf16[1024,704]{1,0:T(8,128)(2,1)S(1)}, bf16[1024,704]{1,0:T(8,128)(2,1)}) fusion(f32[1024,704]{1,0:T(8,128)S(1)} %copy-done.9, f32[1024,704]{1,0:T(8,128)S(1)} %fusion.28, bf16[1024,2048]{1,0:T(8,128)(2,1)S(1)} %copy-done, bf16[2048,704]{1,0:T(8,128)(2,1)S(1)} %copy-done.67), kind=kOutput, calls=%fused_computation.2 | convolution fusion | flops 2963603456 | bytes 17170432 | tf_op jit(solution)/shard_map/dot_general | solution.py:1074
  244.1 3.4 fusion.29
  247.6 3.7 add_convert_fusion
  255.4 7.1 %shard_map.247 = bf16[704,2048]{1,0:T(8,128)(2,1)} custom-call(bf16[1024,704]{1,0:T(8,128)(2,1)} %get-tuple-element.296.left_ref, bf16[1024,2048]{1,0:T(8,128)(2,1)} %shard_map.240.left_ref.right_ref), custom_call_target="tpu_custom_call" | custom-call | flops 1 | bytes 1 | tf_op jit(solution)/shard_map/pallas_call | solution.py:802
  268.4 7.5 %shard_map.248 = bf16[704,2048]{1,0:T(8,128)(2,1)} custom-call(bf16[1024,704]{1,0:T(8,128)(2,1)} %copy-done.22, bf16[1024,2048]{1,0:T(8,128)(2,1)} %shard_map.246.right_ref), custom_call_target="tpu_custom_call" | custom-call | flops 1 | bytes 1 | tf_op jit(solution)/shard_map/pallas_call | solution.py:802
  281.4 2.9 collective-permute-start.57
  284.3 7.1 %shard_map.249 = bf16[704,2048]{1,0:T(8,128)(2,1)} custom-call(bf16[1024,704]{1,0:T(8,128)(2,1)} %copy-done.21, bf16[1024,2048]{1,0:T(8,128)(2,1)} %shard_map.246.right_ref), custom_call_target="tpu_custom_call" | custom-call | flops 1 | bytes 1 | tf_op jit(solution)/shard_map/pallas_call | solution.py:802
  301.6 5.4 convolution_convert_fusion
  307.1 4.8 collective-permute-done.60
  318.0 8.7 %collective-permute-done.62.refs_2_ = bf16[128,2048]{1,0:T(8,128)(2,1)S(1)} collective-permute-done((bf16[128,2048]{1,0:T(8,128)(2,1)S(1)}, bf16[128,2048]{1,0:T(8,128)(2,1)S(1)}, u32[]{:S(2)}, u32[]{:S(2)}) %collective-permute-start.62) | collective-permute-done | bytes 524320 | tf_op jit(solution)/shard_map/ppermute | solution.py:928
  331.6 7.2 %collective-permute-done.64.refs_4_ = bf16[128,2048]{1,0:T(8,128)(2,1)S(1)} collective-permute-done((bf16[128,2048]{1,0:T(8,128)(2,1)S(1)}, bf16[128,2048]{1,0:T(8,128)(2,1)S(1)}, u32[]{:S(2)}, u32[]{:S(2)}) %collective-permute-start.64) | collective-permute-done | bytes 524320 | tf_op jit(solution)/shard_map/ppermute | solution.py:928
  342.2 10.0 %collective-permute-done.66.refs_6_ = bf16[128,2048]{1,0:T(8,128)(2,1)S(1)} collective-permute-done((bf16[128,2048]{1,0:T(8,128)(2,1)}, bf16[128,2048]{1,0:T(8,128)(2,1)S(1)}, u32[]{:S(2)}, u32[]{:S(2)}) %collective-permute-start.66) | collective-permute-done | bytes 524320 | tf_op jit(solution)/shard_map/ppermute | solution.py:928
  355.7 4.2 shard_map.250.buffer_ref
  365.8 10.1 %shard_map.252 = (bf16[1024,512]{1,0:T(8,128)(2,1)}, bf16[1024,512]{1,0:T(8,128)(2,1)}, f32[1,256]{1,0:T(1,128)}, bf16[2,256,128]{2,1,0:T(8,128)(2,1)}) custom-call(s32[8]{0:T(128)} %get-tuple-element.468.ids_ref, bf16[1024,2048]{1,0:T(8,128)(2,1)} %shard_map.251.branch_ref.right_ref, f32[1,256]{1,0:T(1,128)} %bitcast.42, ...), custom_call_target="tpu_custom_call" | custom-call | flops 1 | bytes 1 | tf_op jit(solution)/shard_map/pallas_call | solution.py:592
  381.4 5.3 collective-permute-done.73.refs_6_
  387.4 6.2 %shard_map.253 = bf16[2048,512]{1,0:T(8,128)(2,1)} custom-call(bf16[1024,2048]{1,0:T(8,128)(2,1)} %shard_map.241.left_ref.refs_9_.refs_10_.refs_11_.refs_15_.refs_16_.refs_17_.refs_18_.refs_19_, bf16[1024,512]{1,0:T(8,128)(2,1)} %get-tuple-element.328.right_ref.refs_3_.refs_4_.refs_5_.refs_6_.refs_7_.refs_8_.refs_9_), custom_call_target="tpu_custom_call" | custom-call | flops 1 | bytes 1 | tf_op jit(solution)/shard_map/pallas_call | solution.py:802
  399.8 27.2 %shard_map.254 = (bf16[1024,1024]{1,0:T(8,128)(2,1)}, f32[1024,4]{1,0:T(8,128)}, f32[8,1024]{1,0:T(8,128)}, f32[16,1024]{1,0:T(8,128)}, f32[8,1024]{1,0:T(8,128)}) custom-call(bf16[1024,1536]{1,0:T(8,128)(2,1)} %get-tuple-element.212.proj_ref.prev_ref.refs_8_.refs_9_.refs_10_.refs_11_.refs_4_.refs_5_.refs_6_.refs_7_, ...), custom_call_target="tpu_custom_call" | custom-call | flops 1 | bytes 1 | tf_op jit(solution)/shard_map/pallas_call | solution.py:407
  431.8 8.5 %shard_map.255 = bf16[2048,1024]{1,0:T(8,128)(2,1)} custom-call(bf16[1024,2048]{1,0:T(8,128)(2,1)} %shard_map.241.left_ref.refs_9_.refs_10_.refs_11_.refs_15_.refs_16_.refs_17_.refs_18_.refs_19_, bf16[1024,1024]{1,0:T(8,128)(2,1)} %fusion.20.right_ref.refs_0_.refs_1_.refs_2_.refs_3_.refs_4_), custom_call_target="tpu_custom_call" | custom-call | flops 1 | bytes 1 | tf_op jit(solution)/shard_map/pallas_call | solution.py:802
  443.1 10.3 %shard_map.256 = (bf16[384,2048]{1,0:T(8,128)(2,1)}, f32[8,2048]{1,0:T(8,128)}) custom-call(s32[4]{0:T(128)} %iota_xor_fusion.spots_ref, bf16[1024,1024]{1,0:T(8,128)(2,1)} %fusion.20.right_ref.refs_0_.refs_1_.refs_2_.refs_3_.refs_4_, bf16[1024,1024]{1,0:T(8,128)(2,1)} %fusion.20.right_ref.refs_0_.refs_1_.refs_2_.refs_3_.refs_4_, ...), custom_call_target="tpu_custom_call" | custom-call | flops 1 | bytes 1 | tf_op jit(solution)/shard_map/pallas_call | solution.py:722
  459.1 11.8 %shard_map.257 = (bf16[640,2048]{1,0:T(8,128)(2,1)}, f32[8,2048]{1,0:T(8,128)}) custom-call(s32[4]{0:T(128)} %iota_xor_fusion.spots_ref, bf16[1024,1024]{1,0:T(8,128)(2,1)} %fusion.20.right_ref.refs_0_.refs_1_.refs_2_.refs_3_.refs_4_, bf16[1024,1024]{1,0:T(8,128)(2,1)} %fusion.20.right_ref.refs_0_.refs_1_.refs_2_.refs_3_.refs_4_, ...), custom_call_target="tpu_custom_call" | custom-call | flops 1 | bytes 1 | tf_op jit(solution)/shard_map/pallas_call | solution.py:722
  472.9 6.1 %shard_map.258 = bf16[512,2048]{1,0:T(8,128)(2,1)} custom-call(bf16[1024,512]{1,0:T(8,128)(2,1)} %get-tuple-element.361.left_ref, bf16[1024,2048]{1,0:T(8,128)(2,1)} %shard_map.251.branch_ref.right_ref), custom_call_target="tpu_custom_call" | custom-call | flops 1 | bytes 1 | tf_op jit(solution)/shard_map/pallas_call | solution.py:802
  484.1 4.3 collective-permute-done.83
  489.4 4.1 collective-permute-done.85
  507.8 4.1 collective-permute-done.97
  512.0 3.8 collective-permute-done.98
  528.2 5.9 %shard_map.259 = (f32[512,1536]{1,0:T(8,128)}, f32[512,512]{1,0:T(8,128)}, f32[704,512]{1,0:T(8,128)}, f32[704,512]{1,0:T(8,128)}, f32[704,512]{1,0:T(8,128)}) custom-call(bf16[512,1024]{1,0:T(8,128)(2,1)} %reduce-scatter.15.cloned.1.call-done.mix_ref, bf16[512,512]{1,0:T(8,128)(2,1)} %reduce-scatter.11.cloned.1.call-done.gate_ref, ...), custom_call_target="tpu_custom_call" | custom-call | flops 1 | bytes 1 | tf_op jit(solution)/shard_map/pallas_call | solution.py:909
  (420 shorter events, 201.9 us)
Async XLA Ops:
  7.2 115.6 %all-gather.5.cloned.1.call-start = ((), (), s32[]{:S(2)}) async-start(), calls=%async_computation.6 | async-start | bytes 2621440 | tf_op jit(solution)/shard_map/all_gather | solution.py:1129
  10.2 15.0 %collective-permute-start.4 = (bf16[128,2048]{1,0:T(8,128)(2,1)S(1)}, bf16[128,2048]{1,0:T(8,128)(2,1)S(1)}, u32[]{:S(2)}, u32[]{:S(2)}) collective-permute-start(bf16[128,2048]{1,0:T(8,128)(2,1)S(1)} %fusion.4.refs_0_), channel_id=1, source_target_pairs={{0,1},{2,0},{4,2},{6,4},{7,6},{5,7},{3,5},{1,3},{8,9},{10,8},{12,1... | collective-permute-start | bytes 1572872 | tf_op jit(solution)/shard_map/ppermute | solution.py:928
  13.2 13.4 %collective-permute-start.5 = (bf16[128,2048]{1,0:T(8,128)(2,1)S(1)}, bf16[128,2048]{1,0:T(8,128)(2,1)S(1)}, u32[]{:S(2)}, u32[]{:S(2)}) collective-permute-start(bf16[128,2048]{1,0:T(8,128)(2,1)S(1)} %fusion.4.refs_0_), channel_id=1, source_target_pairs={{0,2},{2,4},{4,6},{6,7},{7,5},{5,3},{3,1},{1,0},{8,10},{10,12},{12... | collective-permute-start | bytes 1572872 | tf_op jit(solution)/shard_map/ppermute | solution.py:928
  13.4 39.6 %collective-permute-start = (bf16[512,1536]{1,0:T(8,128)(2,1)}, bf16[512,1536]{1,0:T(8,128)(2,1)S(1)}, u32[]{:S(2)}, u32[]{:S(2)}) collective-permute-start(bf16[512,1536]{1,0:T(8,128)(2,1)} %refs_22_.1), channel_id=1, source_target_pairs={{0,16},{8,24},{16,0},{24,8},{1,17},{9,25},{17,1},{25,9},{2,18},{10... | collective-permute-start | bytes 4718600 | tf_op jit(solution)/shard_map/ppermute | solution.py:1018
  26.6 12.5 %collective-permute-start.6 = (bf16[128,2048]{1,0:T(8,128)(2,1)S(1)}, bf16[128,2048]{1,0:T(8,128)(2,1)S(1)}, u32[]{:S(2)}, u32[]{:S(2)}) collective-permute-start(bf16[128,2048]{1,0:T(8,128)(2,1)S(1)} %collective-permute-done.4.refs_1_), channel_id=1, source_target_pairs={{0,1},{2,0},{4,2},{6,4},{7,6},{5,7},{3,5},{1,3},{8,9},{10,8},{12,1... | collective-permute-start | bytes 1572872 | tf_op jit(solution)/shard_map/ppermute | solution.py:928
  28.2 12.2 %collective-permute-start.7 = (bf16[128,2048]{1,0:T(8,128)(2,1)S(1)}, bf16[128,2048]{1,0:T(8,128)(2,1)S(1)}, u32[]{:S(2)}, u32[]{:S(2)}) collective-permute-start(bf16[128,2048]{1,0:T(8,128)(2,1)S(1)} %collective-permute-done.5.refs_2_), channel_id=1, source_target_pairs={{0,2},{2,4},{4,6},{6,7},{7,5},{5,3},{3,1},{1,0},{8,10},{10,12},{12... | collective-permute-start | bytes 1572872 | tf_op jit(solution)/shard_map/ppermute | solution.py:928
  42.4 15.5 %collective-permute-start.12 = (bf16[512,1536]{1,0:T(8,128)(2,1)}, bf16[512,1536]{1,0:T(8,128)(2,1)}, u32[]{:S(2)}, u32[]{:S(2)}) collective-permute-start(bf16[512,1536]{1,0:T(8,128)(2,1)} %refs_22_.1), channel_id=1, source_target_pairs={{0,8},{8,0},{16,24},{24,16},{1,9},{9,1},{17,25},{25,17},{2,10},{10... | collective-permute-start | bytes 4718600 | tf_op jit(solution)/shard_map/ppermute | solution.py:1018
  53.1 130.3 %all-gather.7.cloned.1.call-start = ((), (), s32[]{:S(2)}) async-start(), calls=%async_computation.7 | async-start | bytes 3604480 | tf_op jit(solution)/shard_map/all_gather | solution.py:1159
  53.2 13.8 %collective-permute-start.1 = (bf16[4,512]{1,0:T(4,128)(2,1)}, bf16[4,512]{1,0:T(4,128)(2,1)S(1)}, u32[]{:S(2)}, u32[]{:S(2)}) collective-permute-start(bf16[4,512]{1,0:T(4,128)(2,1)} %bitcast.43), channel_id=1, source_target_pairs={{0,8},{8,0},{16,24},{24,16},{1,9},{9,1},{17,25},{25,17},{2,10},{10... | collective-permute-start | bytes 12296 | tf_op jit(solution)/shard_map/ppermute | solution.py:1018
  63.9 18.5 %collective-permute-start.14 = (bf16[128,2048]{1,0:T(8,128)(2,1)}, bf16[128,2048]{1,0:T(8,128)(2,1)}, u32[]{:S(2)}, u32[]{:S(2)}) collective-permute-start(bf16[128,2048]{1,0:T(8,128)(2,1)} %refs_0_), channel_id=1, source_target_pairs={{0,2},{2,4},{4,6},{6,7},{7,5},{5,3},{3,1},{1,0},{8,10},{10,12},{12... | collective-permute-start | bytes 1572872 | tf_op jit(solution)/shard_map/ppermute | solution.py:928
  64.3 18.1 %collective-permute-start.15 = (bf16[128,2048]{1,0:T(8,128)(2,1)}, bf16[128,2048]{1,0:T(8,128)(2,1)}, u32[]{:S(2)}, u32[]{:S(2)}) collective-permute-start(bf16[128,2048]{1,0:T(8,128)(2,1)} %refs_0_), channel_id=1, source_target_pairs={{0,1},{2,0},{4,2},{6,4},{7,6},{5,7},{3,5},{1,3},{8,9},{10,8},{12,1... | collective-permute-start | bytes 1572872 | tf_op jit(solution)/shard_map/ppermute | solution.py:928
  82.4 20.3 %collective-permute-start.17 = (bf16[128,2048]{1,0:T(8,128)(2,1)}, bf16[128,2048]{1,0:T(8,128)(2,1)S(1)}, u32[]{:S(2)}, u32[]{:S(2)}) collective-permute-start(bf16[128,2048]{1,0:T(8,128)(2,1)} %collective-permute-done.14.refs_2_), channel_id=1, source_target_pairs={{0,2},{2,4},{4,6},{6,7},{7,5},{5,3},{3,1},{1,0},{8,10},{10,12},{12... | collective-permute-start | bytes 1572872 | tf_op jit(solution)/shard_map/ppermute | solution.py:928
  82.9 19.8 %collective-permute-start.18 = (bf16[128,2048]{1,0:T(8,128)(2,1)}, bf16[128,2048]{1,0:T(8,128)(2,1)S(1)}, u32[]{:S(2)}, u32[]{:S(2)}) collective-permute-start(bf16[128,2048]{1,0:T(8,128)(2,1)} %collective-permute-done.15.refs_1_), channel_id=1, source_target_pairs={{0,1},{2,0},{4,2},{6,4},{7,6},{5,7},{3,5},{1,3},{8,9},{10,8},{12,1... | collective-permute-start | bytes 1572872 | tf_op jit(solution)/shard_map/ppermute | solution.py:928
  102.7 16.4 %collective-permute-start.22 = (bf16[128,2048]{1,0:T(8,128)(2,1)S(1)}, bf16[128,2048]{1,0:T(8,128)(2,1)S(1)}, u32[]{:S(2)}, u32[]{:S(2)}) collective-permute-start(bf16[128,2048]{1,0:T(8,128)(2,1)S(1)} %collective-permute-done.17.refs_4_), channel_id=1, source_target_pairs={{0,2},{2,4},{4,6},{6,7},{7,5},{5,3},{3,1},{1,0},{8,10},{10,12},{12... | collective-permute-start | bytes 1572872 | tf_op jit(solution)/shard_map/ppermute | solution.py:928
  103.2 15.9 %collective-permute-start.23 = (bf16[128,2048]{1,0:T(8,128)(2,1)S(1)}, bf16[128,2048]{1,0:T(8,128)(2,1)S(1)}, u32[]{:S(2)}, u32[]{:S(2)}) collective-permute-start(bf16[128,2048]{1,0:T(8,128)(2,1)S(1)} %collective-permute-done.18.refs_3_), channel_id=1, source_target_pairs={{0,1},{2,0},{4,2},{6,4},{7,6},{5,7},{3,5},{1,3},{8,9},{10,8},{12,1... | collective-permute-start | bytes 1572872 | tf_op jit(solution)/shard_map/ppermute | solution.py:928
  119.2 91.0 %all-gather.9.cloned.1.call-start = ((), (), s32[]{:S(2)}) async-start(), calls=%async_computation.8 | async-start | bytes 3604480 | tf_op jit(solution)/shard_map/all_gather | solution.py:1159
  119.9 90.2 %all-gather.11.cloned.1.call-start = ((), (), s32[]{:S(2)}) async-start(), calls=%async_computation.9 | async-start | bytes 3604480 | tf_op jit(solution)/shard_map/all_gather | solution.py:1159
  120.0 12.5 %collective-permute-start.24 = (bf16[64,2048]{1,0:T(8,128)(2,1)S(1)}, bf16[64,2048]{1,0:T(8,128)(2,1)S(1)}, u32[]{:S(2)}, u32[]{:S(2)}) collective-permute-start(bf16[64,2048]{1,0:T(8,128)(2,1)S(1)} %slice.262), channel_id=1, source_target_pairs={{0,2},{2,4},{4,6},{6,7},{7,5},{5,3},{3,1},{1,0},{8,10},{10,12},{12... | collective-permute-start | bytes 786440 | tf_op jit(solution)/shard_map/ppermute | solution.py:928
  147.1 193.0 %reduce-scatter.7.cloned.1.call-start = ((), (), s32[]{:S(2)}) async-start(), calls=%async_computation.10 | async-start | bytes 3604480 | tf_op jit(solution)/shard_map/reduce_scatter | solution.py:1202
  194.3 11.9 %collective-permute-start.42 = (bf16[128,2048]{1,0:T(8,128)(2,1)S(1)}, bf16[128,2048]{1,0:T(8,128)(2,1)}, u32[]{:S(2)}, u32[]{:S(2)}) collective-permute-start(bf16[128,2048]{1,0:T(8,128)(2,1)S(1)} %collective-permute-done.40.refs_2_), channel_id=1, source_target_pairs={{0,2},{2,4},{4,6},{6,7},{7,5},{5,3},{3,1},{1,0},{8,10},{10,12},{12... | collective-permute-start | bytes 1572872 | tf_op jit(solution)/shard_map/ppermute | solution.py:928
  194.8 13.0 %collective-permute-start.43 = (bf16[128,2048]{1,0:T(8,128)(2,1)S(1)}, bf16[128,2048]{1,0:T(8,128)(2,1)}, u32[]{:S(2)}, u32[]{:S(2)}) collective-permute-start(bf16[128,2048]{1,0:T(8,128)(2,1)S(1)} %collective-permute-done.41.refs_1_), channel_id=1, source_target_pairs={{0,1},{2,0},{4,2},{6,4},{7,6},{5,7},{3,5},{1,3},{8,9},{10,8},{12,1... | collective-permute-start | bytes 1572872 | tf_op jit(solution)/shard_map/ppermute | solution.py:928
  207.9 12.2 %collective-permute-start.44 = (bf16[128,2048]{1,0:T(8,128)(2,1)}, bf16[128,2048]{1,0:T(8,128)(2,1)S(1)}, u32[]{:S(2)}, u32[]{:S(2)}) collective-permute-start(bf16[128,2048]{1,0:T(8,128)(2,1)} %collective-permute-done.42.refs_4_), channel_id=1, source_target_pairs={{0,2},{2,4},{4,6},{6,7},{7,5},{5,3},{3,1},{1,0},{8,10},{10,12},{12... | collective-permute-start | bytes 1572872 | tf_op jit(solution)/shard_map/ppermute | solution.py:928
  210.1 12.2 %collective-permute-start.45 = (bf16[128,2048]{1,0:T(8,128)(2,1)}, bf16[128,2048]{1,0:T(8,128)(2,1)S(1)}, u32[]{:S(2)}, u32[]{:S(2)}) collective-permute-start(bf16[128,2048]{1,0:T(8,128)(2,1)} %collective-permute-done.43.refs_3_), channel_id=1, source_target_pairs={{0,1},{2,0},{4,2},{6,4},{7,6},{5,7},{3,5},{1,3},{8,9},{10,8},{12,1... | collective-permute-start | bytes 1572872 | tf_op jit(solution)/shard_map/ppermute | solution.py:928
  264.3 95.6 %reduce-scatter.9.cloned.1.call-start = ((), (), s32[]{:S(2)}) async-start(), calls=%async_computation.11 | async-start | bytes 3604480 | tf_op jit(solution)/shard_map/reduce_scatter | solution.py:1202
  279.2 152.0 %reduce-scatter.13.cloned.1.call-start = ((), (), s32[]{:S(2)}) async-start(), calls=%async_computation.13 | async-start | bytes 3604480 | tf_op jit(solution)/shard_map/reduce_scatter | solution.py:1202
  279.2 12.2 %collective-permute-start.54 = (bf16[64,2048]{1,0:T(8,128)(2,1)}, bf16[64,2048]{1,0:T(8,128)(2,1)}, u32[]{:S(2)}, u32[]{:S(2)}) collective-permute-start(bf16[64,2048]{1,0:T(8,128)(2,1)} %get-tuple-element.422), channel_id=1, source_target_pairs={{0,2},{2,4},{4,6},{6,7},{7,5},{5,3},{3,1},{1,0},{8,10},{10,12},{12... | collective-permute-start | bytes 786440 | tf_op jit(solution)/shard_map/ppermute | solution.py:928
  279.3 12.1 %collective-permute-start.55 = (bf16[64,2048]{1,0:T(8,128)(2,1)}, bf16[64,2048]{1,0:T(8,128)(2,1)}, u32[]{:S(2)}, u32[]{:S(2)}) collective-permute-start(bf16[64,2048]{1,0:T(8,128)(2,1)} %get-tuple-element.421), channel_id=1, source_target_pairs={{0,1},{2,0},{4,2},{6,4},{7,6},{5,7},{3,5},{1,3},{8,9},{10,8},{12,1... | collective-permute-start | bytes 786440 | tf_op jit(solution)/shard_map/ppermute | solution.py:928
  295.3 135.9 %reduce-scatter.11.cloned.1.call-start = ((), (), s32[]{:S(2)}) async-start(), calls=%async_computation.12 | async-start | bytes 2621440 | tf_op jit(solution)/shard_map/reduce_scatter | solution.py:1273
  295.3 11.8 %collective-permute-start.58 = (bf16[64,2048]{1,0:T(8,128)(2,1)}, bf16[64,2048]{1,0:T(8,128)(2,1)S(1)}, u32[]{:S(2)}, u32[]{:S(2)}) collective-permute-start(bf16[64,2048]{1,0:T(8,128)(2,1)} %get-tuple-element.418), channel_id=1, source_target_pairs={{0,2},{2,4},{4,6},{6,7},{7,5},{5,3},{3,1},{1,0},{8,10},{10,12},{12... | collective-permute-start | bytes 786440 | tf_op jit(solution)/shard_map/ppermute | solution.py:928
  299.1 12.8 %collective-permute-start.60 = (bf16[64,2048]{1,0:T(8,128)(2,1)}, bf16[64,2048]{1,0:T(8,128)(2,1)S(1)}, u32[]{:S(2)}, u32[]{:S(2)}) collective-permute-start(bf16[64,2048]{1,0:T(8,128)(2,1)} %get-tuple-element.416), channel_id=1, source_target_pairs={{0,2},{2,4},{4,6},{6,7},{7,5},{5,3},{3,1},{1,0},{8,10},{10,12},{12... | collective-permute-start | bytes 786440 | tf_op jit(solution)/shard_map/ppermute | solution.py:928
  299.9 12.8 %collective-permute-start.61 = (bf16[64,2048]{1,0:T(8,128)(2,1)S(1)}, bf16[64,2048]{1,0:T(8,128)(2,1)S(1)}, u32[]{:S(2)}, u32[]{:S(2)}) collective-permute-start(bf16[64,2048]{1,0:T(8,128)(2,1)S(1)} %get-tuple-element.415), channel_id=1, source_target_pairs={{0,1},{2,0},{4,2},{6,4},{7,6},{5,7},{3,5},{1,3},{8,9},{10,8},{12,1... | collective-permute-start | bytes 786440 | tf_op jit(solution)/shard_map/ppermute | solution.py:928
  340.2 12.0 %collective-permute-start.66 = (bf16[128,2048]{1,0:T(8,128)(2,1)}, bf16[128,2048]{1,0:T(8,128)(2,1)S(1)}, u32[]{:S(2)}, u32[]{:S(2)}) collective-permute-start(bf16[128,2048]{1,0:T(8,128)(2,1)} %copy-done.41), channel_id=1, source_target_pairs={{0,2},{2,4},{4,6},{6,7},{7,5},{5,3},{3,1},{1,0},{8,10},{10,12},{12... | collective-permute-start | bytes 1572872 | tf_op jit(solution)/shard_map/ppermute | solution.py:928
  378.1 15.5 %collective-permute-start.72 = (bf16[128,2048]{1,0:T(8,128)(2,1)}, bf16[128,2048]{1,0:T(8,128)(2,1)}, u32[]{:S(2)}, u32[]{:S(2)}) collective-permute-start(bf16[128,2048]{1,0:T(8,128)(2,1)} %get-tuple-element.326), channel_id=1, source_target_pairs={{0,2},{2,4},{4,6},{6,7},{7,5},{5,3},{3,1},{1,0},{8,10},{10,12},{12... | collective-permute-start | bytes 1572872 | tf_op jit(solution)/shard_map/ppermute | solution.py:928
  378.3 15.3 %collective-permute-start.75 = (bf16[128,2048]{1,0:T(8,128)(2,1)S(1)}, bf16[128,2048]{1,0:T(8,128)(2,1)}, u32[]{:S(2)}, u32[]{:S(2)}) collective-permute-start(bf16[128,2048]{1,0:T(8,128)(2,1)S(1)} %get-tuple-element.329), channel_id=1, source_target_pairs={{0,1},{2,0},{4,2},{6,4},{7,6},{5,7},{3,5},{1,3},{8,9},{10,8},{12,1... | collective-permute-start | bytes 1572872 | tf_op jit(solution)/shard_map/ppermute | solution.py:928
  393.7 127.6 %reduce-scatter.15.cloned.1.call-start = ((), (), s32[]{:S(2)}) async-start(), calls=%async_computation.14 | async-start | bytes 5242880 | tf_op jit(solution)/shard_map/reduce_scatter | solution.py:1290
  396.3 32.4 %collective-permute-start.76 = (bf16[128,2048]{1,0:T(8,128)(2,1)}, bf16[128,2048]{1,0:T(8,128)(2,1)S(1)}, u32[]{:S(2)}, u32[]{:S(2)}) collective-permute-start(bf16[128,2048]{1,0:T(8,128)(2,1)} %get-tuple-element.331), channel_id=1, source_target_pairs={{0,2},{2,4},{4,6},{6,7},{7,5},{5,3},{3,1},{1,0},{8,10},{10,12},{12... | collective-permute-start | bytes 1572872 | tf_op jit(solution)/shard_map/ppermute | solution.py:928
  396.8 31.9 %collective-permute-start.77 = (bf16[128,2048]{1,0:T(8,128)(2,1)}, bf16[128,2048]{1,0:T(8,128)(2,1)}, u32[]{:S(2)}, u32[]{:S(2)}) collective-permute-start(bf16[128,2048]{1,0:T(8,128)(2,1)} %get-tuple-element.342), channel_id=1, source_target_pairs={{0,1},{2,0},{4,2},{6,4},{7,6},{5,7},{3,5},{1,3},{8,9},{10,8},{12,1... | collective-permute-start | bytes 1572872 | tf_op jit(solution)/shard_map/ppermute | solution.py:928
  440.3 87.9 %reduce-scatter.17.cloned.1.call-start = ((), (), s32[]{:S(2)}) async-start(), calls=%async_computation.15 | async-start | bytes 2621440 | tf_op jit(solution)/shard_map/reduce_scatter | solution.py:1202
  440.4 14.0 %collective-permute-start.79 = (bf16[128,2048]{1,0:T(8,128)(2,1)}, bf16[128,2048]{1,0:T(8,128)(2,1)S(1)}, u32[]{:S(2)}, u32[]{:S(2)}) collective-permute-start(bf16[128,2048]{1,0:T(8,128)(2,1)} %get-tuple-element.345), channel_id=1, source_target_pairs={{0,1},{2,0},{4,2},{6,4},{7,6},{5,7},{3,5},{1,3},{8,9},{10,8},{12,1... | collective-permute-start | bytes 1572872 | tf_op jit(solution)/shard_map/ppermute | solution.py:928
  441.2 14.4 %collective-permute-start.78 = (bf16[128,2048]{1,0:T(8,128)(2,1)}, bf16[128,2048]{1,0:T(8,128)(2,1)S(1)}, u32[]{:S(2)}, u32[]{:S(2)}) collective-permute-start(bf16[128,2048]{1,0:T(8,128)(2,1)} %get-tuple-element.344), channel_id=1, source_target_pairs={{0,2},{2,4},{4,6},{6,7},{7,5},{5,3},{3,1},{1,0},{8,10},{10,12},{12... | collective-permute-start | bytes 1572872 | tf_op jit(solution)/shard_map/ppermute | solution.py:928
  456.9 14.0 %collective-permute-start.81 = (bf16[64,2048]{1,0:T(8,128)(2,1)S(1)}, bf16[64,2048]{1,0:T(8,128)(2,1)S(1)}, u32[]{:S(2)}, u32[]{:S(2)}) collective-permute-start(bf16[64,2048]{1,0:T(8,128)(2,1)S(1)} %get-tuple-element.460), channel_id=1, source_target_pairs={{0,2},{2,4},{4,6},{6,7},{7,5},{5,3},{3,1},{1,0},{8,10},{10,12},{12... | collective-permute-start | bytes 786440 | tf_op jit(solution)/shard_map/ppermute | solution.py:928
  458.0 12.9 %collective-permute-start.82 = (bf16[64,2048]{1,0:T(8,128)(2,1)S(1)}, bf16[64,2048]{1,0:T(8,128)(2,1)S(1)}, u32[]{:S(2)}, u32[]{:S(2)}) collective-permute-start(bf16[64,2048]{1,0:T(8,128)(2,1)S(1)} %get-tuple-element.459), channel_id=1, source_target_pairs={{0,1},{2,0},{4,2},{6,4},{7,6},{5,7},{3,5},{1,3},{8,9},{10,8},{12,1... | collective-permute-start | bytes 786440 | tf_op jit(solution)/shard_map/ppermute | solution.py:928
  481.1 12.5 %collective-permute-start.85 = (bf16[64,2048]{1,0:T(8,128)(2,1)}, bf16[64,2048]{1,0:T(8,128)(2,1)S(1)}, u32[]{:S(2)}, u32[]{:S(2)}) collective-permute-start(bf16[64,2048]{1,0:T(8,128)(2,1)} %get-tuple-element.456), channel_id=1, source_target_pairs={{0,2},{2,4},{4,6},{6,7},{7,5},{5,3},{3,1},{1,0},{8,10},{10,12},{12... | collective-permute-start | bytes 786440 | tf_op jit(solution)/shard_map/ppermute | solution.py:928
  482.1 12.2 %collective-permute-start.86 = (bf16[64,2048]{1,0:T(8,128)(2,1)}, bf16[64,2048]{1,0:T(8,128)(2,1)S(1)}, u32[]{:S(2)}, u32[]{:S(2)}) collective-permute-start(bf16[64,2048]{1,0:T(8,128)(2,1)} %get-tuple-element.455), channel_id=1, source_target_pairs={{0,1},{2,0},{4,2},{6,4},{7,6},{5,7},{3,5},{1,3},{8,9},{10,8},{12,1... | collective-permute-start | bytes 786440 | tf_op jit(solution)/shard_map/ppermute | solution.py:928
  498.2 23.0 %collective-permute-start.88 = (bf16[64,2048]{1,0:T(8,128)(2,1)}, bf16[64,2048]{1,0:T(8,128)(2,1)}, u32[]{:S(2)}, u32[]{:S(2)}) collective-permute-start(bf16[64,2048]{1,0:T(8,128)(2,1)} %get-tuple-element.454), channel_id=1, source_target_pairs={{0,2},{2,4},{4,6},{6,7},{7,5},{5,3},{3,1},{1,0},{8,10},{10,12},{12... | collective-permute-start | bytes 786440 | tf_op jit(solution)/shard_map/ppermute | solution.py:928
  498.8 22.4 %collective-permute-start.89 = (bf16[64,2048]{1,0:T(8,128)(2,1)}, bf16[64,2048]{1,0:T(8,128)(2,1)}, u32[]{:S(2)}, u32[]{:S(2)}) collective-permute-start(bf16[64,2048]{1,0:T(8,128)(2,1)} %get-tuple-element.453), channel_id=1, source_target_pairs={{0,1},{2,0},{4,2},{6,4},{7,6},{5,7},{3,5},{1,3},{8,9},{10,8},{12,1... | collective-permute-start | bytes 786440 | tf_op jit(solution)/shard_map/ppermute | solution.py:928
  500.2 21.0 %collective-permute-start.90 = (bf16[64,2048]{1,0:T(8,128)(2,1)}, bf16[64,2048]{1,0:T(8,128)(2,1)}, u32[]{:S(2)}, u32[]{:S(2)}) collective-permute-start(bf16[64,2048]{1,0:T(8,128)(2,1)} %get-tuple-element.452), channel_id=1, source_target_pairs={{0,2},{2,4},{4,6},{6,7},{7,5},{5,3},{3,1},{1,0},{8,10},{10,12},{12... | collective-permute-start | bytes 786440 | tf_op jit(solution)/shard_map/ppermute | solution.py:928
  500.8 20.4 %collective-permute-start.91 = (bf16[64,2048]{1,0:T(8,128)(2,1)}, bf16[64,2048]{1,0:T(8,128)(2,1)}, u32[]{:S(2)}, u32[]{:S(2)}) collective-permute-start(bf16[64,2048]{1,0:T(8,128)(2,1)} %get-tuple-element.451), channel_id=1, source_target_pairs={{0,1},{2,0},{4,2},{6,4},{7,6},{5,7},{3,5},{1,3},{8,9},{10,8},{12,1... | collective-permute-start | bytes 786440 | tf_op jit(solution)/shard_map/ppermute | solution.py:928
  (130 other events, 1303.9 us)
Sparse Core Ops, SparseCore 0:
  53.2 21.4 all-gather.4
  119.3 26.6 all-gather.6
  147.6 27.0 all-gather.8
  176.1 27.0 all-gather.10
  264.4 36.4 reduce-scatter.6
  303.4 36.3 reduce-scatter.8
  342.3 36.3 reduce-scatter.12
  393.8 28.6 reduce-scatter.10
  440.4 43.2 reduce-scatter.14
  486.8 31.4 reduce-scatter.16
